TPU v7x, 32 devices: a whole 2x2x4 slice. The times are simulated.
32 devices in a mesh: seq: 8 (over z, y), batch: 4 (over x, core).
Axes of the slice: x: 2, y: 2, z: 4, core: 2. Of those that a mesh axis runs over, the one named last changes fastest.
Arguments:
- tokens: bfloat16 [2, 4, 2048, 1024], P(None, 'batch', 'seq'), may hold values from -6 to 6
- ln_gain: float32 [1024], replicated, may hold values from 0.1 to 1.9
- w_up: bfloat16 [1024, 4096], replicated, may hold values from -0.1875 to 0.1875
- conv_w: float32 [4, 2048], replicated, may hold values from -3 to 3
- conv_b: float32 [2048], replicated, may hold values from -1.2 to 1.2
- w_query: bfloat16 [4, 512, 512], replicated, may hold values from -0.25 to 0.25
- w_key: bfloat16 [4, 512, 512], replicated, may hold values from -0.25 to 0.25
- w_value: bfloat16 [4, 512, 512], replicated, may hold values from -0.25 to 0.25
- gate_w: float32 [6144, 8], replicated, may hold values from -0.0546875 to 0.0546875
- gate_b: float32 [4], replicated, may hold values from 1 to 12
- out_gain: float32 [2048], replicated, may hold values from 0.1 to 1.9
- skip_gain: float32 [2048], replicated, may hold values from 0.5 to 1.5
- w_down: bfloat16 [2048, 1024], replicated, may hold values from -0.125 to 0.125
- d_out: bfloat16 [2, 4, 2048, 1024], P(None, 'batch', 'seq'), may hold values from -6 to 6
Outputs:
- block_out: bfloat16 [2, 4, 2048, 1024], P(None, 'batch', 'seq')
- grad_tokens: bfloat16 [2, 4, 2048, 1024], P(None, 'batch', 'seq')
- grad_ln_gain: float32 [1024], replicated
- grad_w_up: float32 [1024, 4096], P('seq', 'batch')
- grad_conv_w: float32 [4, 2048], replicated
- grad_conv_b: float32 [2048], replicated
- grad_w_query: float32 [4, 512, 512], P(None, 'seq', 'batch')
- grad_w_key: float32 [4, 512, 512], P(None, 'seq', 'batch')
- grad_w_value: float32 [4, 512, 512], P(None, 'seq', 'batch')
- grad_gate_w: float32 [6144, 8], replicated
- grad_gate_b: float32 [4], replicated
- grad_out_gain: float32 [2048], replicated
- grad_skip_gain: float32 [2048], replicated
- grad_w_down: float32 [2048, 1024], P('seq', 'batch')
All inputs are finite; a program needn't handle non-finite values.
Results may differ from a plain program's by a relative error of at most 0.023.
The roundings to bfloat16 on the way count: a program that leaves them out, or rounds other values in their place, can miss the bound.
Values may be sent and summed in bfloat16 or wider, within the bound.
A program may use at most 576 MiB of HBM per device.

v0:
```python
from functools import partial

import jax
import jax.numpy as jnp
from jax import lax
from jax.sharding import PartitionSpec as P

highest_mode = lax.Precision.HIGHEST
norm_epsilon = 1e-05
floor_value = -1e30


def shifted(value, axis, steps):
    count = lax.axis_size(axis)
    initial, last = (max(0, -steps), min(count, count - steps))
    return lax.ppermute(value, axis, [(source, source + steps) for source in range(initial, last)])


def entering(x, axis, combine, identity, reverse):
    count, index = (lax.axis_size(axis), lax.axis_index(axis))
    everything = jax.tree.map(lambda part: lax.all_gather(part, axis), x)
    start = jax.tree.map(
        lambda part, zero: jnp.broadcast_to(jnp.asarray(zero, part.dtype), part.shape), x, identity
    )

    def step(k, before):
        at = count - 1 - k if reverse else k
        reached = at > index if reverse else at < index
        new = combine(before, jax.tree.map(lambda part: part[at], everything))
        return jax.tree.map(lambda a, b: jnp.where(reached, a, b), new, before)

    return lax.fori_loop(0, count, step, start)


def layer_norm(row_data, gain_vec):
    centre = row_data - jnp.mean(row_data, axis=-1, keepdims=True)
    spread = jnp.mean(centre * centre, axis=-1, keepdims=True)
    return centre * lax.rsqrt(spread + norm_epsilon) * gain_vec


def conv_silu(extended, conv_w, conv_b):
    conv_width = conv_w.shape[0]
    out_len = extended.shape[0] - conv_width + 1
    summed = conv_b + conv_w[0] * extended[0:out_len]
    for j in range(1, conv_width):
        summed = summed + conv_w[j] * extended[j : j + out_len]
    return jax.nn.silu(summed)


def head_product(features, matrices):
    token_count = features.shape[0]
    by_head = features.reshape(token_count, matrices.shape[0], -1)
    return jnp.einsum(
        "thd,hde->the", by_head, matrices, preferred_element_type=jnp.float32
    ).reshape(token_count, -1)


def head_back(grad_rows, matrices):
    token_count = grad_rows.shape[0]
    by_head = grad_rows.reshape(token_count, matrices.shape[0], -1)
    return jnp.einsum(
        "the,hde->thd", by_head, matrices, preferred_element_type=jnp.float32
    ).reshape(token_count, -1)


def head_weight(features, grad_rows, head_count):
    token_count = features.shape[0]
    left_side = features.reshape(token_count, head_count, -1)
    right_side = grad_rows.reshape(token_count, head_count, -1)
    return jnp.einsum("thd,the->hde", left_side, right_side, preferred_element_type=jnp.float32)


def to_heads(features, head_count):
    return features.reshape(features.shape[0], head_count, -1).transpose(1, 0, 2)


def cell_hidden(queries, key_rows, value_rows, in_gate, log_forget, state_c, state_n, state_m):
    head_size = queries.shape[-1]
    length = queries.shape[1]
    scaled = queries * head_size ** (-0.5)
    running = jnp.cumsum(log_forget, axis=1)
    causal = jnp.arange(length)[:, None] >= jnp.arange(length)[None, :]
    decays = running[:, :, None] - running[:, None, :] + in_gate[:, None, :]
    decays = jnp.where(causal[None], decays, floor_value)
    carried = running + state_m[:, None]
    stable = jnp.maximum(carried, jnp.max(decays, axis=2))
    scores = jnp.einsum("htd,hsd->hts", scaled, key_rows, precision=highest_mode)
    weights = jnp.exp(decays - stable[:, :, None]) * scores
    from_state = jnp.exp(carried - stable)
    numerator = jnp.einsum("hts,hsd->htd", weights, value_rows, precision=highest_mode)
    numerator = numerator + from_state[:, :, None] * jnp.einsum(
        "htd,hde->hte", scaled, state_c, precision=highest_mode
    )
    denominator = jnp.sum(weights, axis=2) + from_state * jnp.einsum(
        "htd,hd->ht", scaled, state_n, precision=highest_mode
    )
    return numerator / jnp.maximum(jnp.abs(denominator), jnp.exp(-stable))[:, :, None]


def cell_state(key_rows, value_rows, in_gate, log_forget, state_c, state_n, state_m):
    running = jnp.cumsum(log_forget, axis=1)
    seg_total = running[:, -1]
    exponent = seg_total[:, None] - running + in_gate
    local_top = jnp.max(exponent, axis=1)
    new_m = jnp.maximum(seg_total + state_m, local_top)
    key_weight = jnp.exp(exponent - new_m[:, None])
    weighted = key_rows * key_weight[:, :, None]
    keep_old = jnp.exp(seg_total + state_m - new_m)
    new_c = keep_old[:, None, None] * state_c + jnp.einsum(
        "hsd,hse->hde", weighted, value_rows, precision=highest_mode
    )
    new_n = keep_old[:, None] * state_n + jnp.sum(weighted, axis=1)
    return (new_c, new_n, new_m)


def local_summary(key_rows, value_rows, in_gate, log_forget):
    running = jnp.cumsum(log_forget, axis=1)
    seg_total = running[:, -1]
    exponent = seg_total[:, None] - running + in_gate
    local_top = jnp.max(exponent, axis=1)
    key_weight = jnp.exp(exponent - local_top[:, None])
    weighted = key_rows * key_weight[:, :, None]
    state_c = jnp.einsum("hsd,hse->hde", weighted, value_rows, precision=highest_mode)
    state_n = jnp.sum(weighted, axis=1)
    return (state_c, state_n, local_top, seg_total)


def combine_states(earlier, later):
    top = jnp.maximum(later[3] + earlier[2], later[2])
    keep_first = jnp.exp(later[3] + earlier[2] - top)
    keep_second = jnp.exp(later[2] - top)
    merged_c = keep_first[..., None, None] * earlier[0] + keep_second[..., None, None] * later[0]
    merged_n = keep_first[..., None] * earlier[1] + keep_second[..., None] * later[1]
    return (merged_c, merged_n, top, earlier[3] + later[3])


def state_identity(template):
    return (
        jnp.zeros_like(template[0]),
        jnp.zeros_like(template[1]),
        jnp.full_like(template[2], floor_value),
        jnp.zeros_like(template[3]),
    )


def head_output(hidden, out_gain, skip_gain, conv_out, gate_z):
    centre = hidden - jnp.mean(hidden, axis=-1, keepdims=True)
    spread = jnp.mean(centre * centre, axis=-1, keepdims=True)
    normed = centre * lax.rsqrt(spread + norm_epsilon)
    flat_out = normed.transpose(1, 0, 2).reshape(hidden.shape[1], -1) * out_gain
    return (flat_out + skip_gain * conv_out) * jax.nn.silu(gate_z)


def output_tail(
    query_f,
    key_f,
    value_f,
    gate_pre,
    conv_f,
    gate_z,
    out_gain,
    skip_gain,
    state_c,
    state_n,
    state_m,
):
    head_count = gate_pre.shape[1] // 2
    in_gate = gate_pre[:, :head_count].T
    log_forget = jax.nn.log_sigmoid(gate_pre[:, head_count:]).T
    hidden = cell_hidden(
        to_heads(query_f, head_count),
        to_heads(key_f, head_count),
        to_heads(value_f, head_count),
        in_gate,
        log_forget,
        state_c,
        state_n,
        state_m,
    )
    return head_output(hidden, out_gain, skip_gain, conv_f, gate_z)


def state_tail(key_f, value_f, gate_pre, state_c, state_n, state_m):
    head_count = gate_pre.shape[1] // 2
    in_gate = gate_pre[:, :head_count].T
    log_forget = jax.nn.log_sigmoid(gate_pre[:, head_count:]).T
    return cell_state(
        to_heads(key_f, head_count),
        to_heads(value_f, head_count),
        in_gate,
        log_forget,
        state_c,
        state_n,
        state_m,
    )


def to_device_blocks(grad_full, seq_count, batch_count):
    if grad_full.ndim == 2:
        rows, cols = grad_full.shape
        split = grad_full.reshape(seq_count, rows // seq_count, batch_count, cols // batch_count)
        return split.transpose(0, 2, 1, 3).reshape(
            seq_count * batch_count, rows // seq_count, cols // batch_count
        )
    heads, rows, cols = grad_full.shape
    split = grad_full.reshape(heads, seq_count, rows // seq_count, batch_count, cols // batch_count)
    return split.transpose(1, 3, 0, 2, 4).reshape(
        seq_count * batch_count, heads, rows // seq_count, cols // batch_count
    )


def per_device(
    tokens,
    ln_gain,
    w_up,
    conv_w,
    conv_b,
    w_query,
    w_key,
    w_value,
    gate_w,
    gate_b,
    out_gain,
    skip_gain,
    w_down,
    d_out,
):
    micro_count = tokens.shape[0]
    token_count = tokens.shape[2]
    inner = w_down.shape[0]
    head_count = w_query.shape[0]
    halo_len = conv_w.shape[0] - 1
    bias_row = jnp.concatenate([jnp.zeros((head_count,), jnp.float32), gate_b])
    kept = []
    summaries = []
    for micro_step in range(micro_count):
        row_f = tokens[micro_step, 0].astype(jnp.float32)
        normed, ln_back = jax.vjp(layer_norm, row_f, ln_gain)
        normed_low = normed.astype(jnp.bfloat16)
        lifted = jnp.dot(normed_low, w_up, preferred_element_type=jnp.float32)
        mix_in = lifted[:, :inner].astype(jnp.bfloat16)
        gate_z = lifted[:, inner:]
        before = shifted(mix_in[token_count - halo_len :], "seq", 1)
        extended = jnp.concatenate([before, mix_in], axis=0).astype(jnp.float32)
        conv_f, conv_back = jax.vjp(conv_silu, extended, conv_w, conv_b)
        conv_low = conv_f.astype(jnp.bfloat16)
        queries = head_product(conv_low, w_query).astype(jnp.bfloat16)
        key_rows = head_product(conv_low, w_key).astype(jnp.bfloat16)
        value_rows = head_product(mix_in, w_value).astype(jnp.bfloat16)
        joined = jnp.concatenate([queries, key_rows, value_rows], axis=1).astype(jnp.float32)
        gate_pre = jnp.dot(joined, gate_w, precision=highest_mode) + bias_row
        summary = local_summary(
            to_heads(joined[:, inner : 2 * inner], head_count),
            to_heads(joined[:, 2 * inner :], head_count),
            gate_pre[:, :head_count].T,
            jax.nn.log_sigmoid(gate_pre[:, head_count:]).T,
        )
        summaries.append(summary)
        kept.append(
            (row_f, ln_back, normed_low, mix_in, gate_z, conv_back, conv_low, joined, gate_pre)
        )
    incoming = [entering(s, "seq", combine_states, state_identity(s), False) for s in summaries]
    g_down = jnp.zeros((inner, w_down.shape[1]), jnp.float32)
    tails = []
    reverse_items = []
    for micro_step in range(micro_count):
        row_f, ln_back, normed_low, mix_in, gate_z, conv_back, conv_low, joined, gate_pre = kept[
            micro_step
        ]
        state_c, state_n, state_m, unused_total = incoming[micro_step]
        out_fn = partial(output_tail, state_m=state_m)
        gated, out_back = jax.vjp(
            out_fn,
            joined[:, :inner],
            joined[:, inner : 2 * inner],
            joined[:, 2 * inner :],
            gate_pre,
            conv_low.astype(jnp.float32),
            gate_z,
            out_gain,
            skip_gain,
            state_c,
            state_n,
        )
        state_fn = partial(state_tail, state_m=state_m)
        new_state, state_back = jax.vjp(
            state_fn,
            joined[:, inner : 2 * inner],
            joined[:, 2 * inner :],
            gate_pre,
            state_c,
            state_n,
        )
        out_c, out_n, out_m = new_state
        gated_low = gated.astype(jnp.bfloat16)
        block_rows = (
            row_f + jnp.dot(gated_low, w_down, preferred_element_type=jnp.float32)
        ).astype(jnp.bfloat16)
        cotangent = d_out[micro_step, 0]
        d_gated = jnp.dot(cotangent, w_down.T, preferred_element_type=jnp.float32)
        g_down = g_down + jnp.dot(gated_low.T, cotangent, preferred_element_type=jnp.float32)
        first = out_back(d_gated)
        grad_scale = jnp.where(state_m > -1e29, -state_m, floor_value)
        reverse_items.append((first[8], first[9], grad_scale, summaries[micro_step][3]))
        tails.append((state_back, first, out_c, out_n, out_m, block_rows, cotangent))
    returned = [entering(s, "seq", combine_states, state_identity(s), True) for s in reverse_items]
    g_up = jnp.zeros(w_up.shape, jnp.float32)
    g_query = jnp.zeros(w_query.shape, jnp.float32)
    g_key = jnp.zeros(w_key.shape, jnp.float32)
    g_value = jnp.zeros(w_value.shape, jnp.float32)
    g_ln = jnp.zeros(ln_gain.shape, jnp.float32)
    g_conv_w = jnp.zeros(conv_w.shape, jnp.float32)
    g_conv_b = jnp.zeros(conv_b.shape, jnp.float32)
    g_gate_w = jnp.zeros(gate_w.shape, jnp.float32)
    g_gate_b = jnp.zeros(gate_b.shape, jnp.float32)
    g_out_gain = jnp.zeros(out_gain.shape, jnp.float32)
    g_skip = jnp.zeros(skip_gain.shape, jnp.float32)
    out_rows = []
    grad_rows_all = []
    for micro_step in range(micro_count):
        row_f, ln_back, normed_low, mix_in, gate_z, conv_back, conv_low, joined, gate_pre = kept[
            micro_step
        ]
        state_back, first, out_c, out_n, out_m, block_rows, cotangent = tails[micro_step]
        later_c, later_n, later_m, unused_sum = returned[micro_step]
        scale_out = jnp.exp(out_m + later_m)
        cot_c = scale_out[:, None, None] * later_c
        cot_n = scale_out[:, None] * later_n
        cot_m = jnp.sum(cot_c * out_c, axis=(1, 2)) + jnp.sum(cot_n * out_n, axis=1)
        second = state_back((cot_c, cot_n, cot_m))
        d_query = first[0]
        d_key = first[1] + second[0]
        d_value = first[2] + second[1]
        d_gate_pre = first[3] + second[2]
        d_conv_skip = first[4]
        d_gate_z = first[5]
        g_out_step = first[6]
        g_skip_step = first[7]
        d_joined = jnp.dot(d_gate_pre, gate_w.T, precision=highest_mode)
        g_gate_w = g_gate_w + jnp.dot(joined.T, d_gate_pre, precision=highest_mode)
        g_gate_b = g_gate_b + jnp.sum(d_gate_pre[:, head_count:], axis=0)
        g_out_gain = g_out_gain + g_out_step
        g_skip = g_skip + g_skip_step
        query_low = (d_query + d_joined[:, :inner]).astype(jnp.bfloat16)
        key_low = (d_key + d_joined[:, inner : 2 * inner]).astype(jnp.bfloat16)
        value_low = (d_value + d_joined[:, 2 * inner :]).astype(jnp.bfloat16)
        d_conv = d_conv_skip + head_back(query_low, w_query) + head_back(key_low, w_key)
        g_query = g_query + head_weight(conv_low, query_low, head_count)
        g_key = g_key + head_weight(conv_low, key_low, head_count)
        g_value = g_value + head_weight(mix_in, value_low, head_count)
        d_extended, g_conv_w_step, g_conv_b_step = conv_back(d_conv)
        g_conv_w = g_conv_w + g_conv_w_step
        g_conv_b = g_conv_b + g_conv_b_step
        sent_back = shifted(d_extended[:halo_len], "seq", -1)
        d_mix = (
            d_extended[halo_len:]
            + head_back(value_low, w_value)
            + jnp.pad(sent_back, ((token_count - halo_len, 0), (0, 0)))
        )
        d_lifted = jnp.concatenate([d_mix, d_gate_z], axis=1).astype(jnp.bfloat16)
        g_up = g_up + jnp.dot(normed_low.T, d_lifted, preferred_element_type=jnp.float32)
        d_normed = jnp.dot(d_lifted, w_up.T, preferred_element_type=jnp.float32)
        d_row, g_ln_step = ln_back(d_normed)
        g_ln = g_ln + g_ln_step
        out_rows.append(block_rows)
        grad_rows_all.append((cotangent.astype(jnp.float32) + d_row).astype(jnp.bfloat16))
    seq_count = lax.axis_size("seq")
    batch_count = lax.axis_size("batch")
    blocks = tuple(
        (
            to_device_blocks(g, seq_count, batch_count)
            for g in (g_up, g_query, g_key, g_value, g_down)
        )
    )
    pieces = lax.psum_scatter(blocks, ("seq", "batch"), scatter_dimension=0, tiled=True)
    s_up, s_query, s_key, s_value, s_down = tuple((p[0] for p in pieces))
    s_ln, s_conv_w, s_conv_b, s_gate_w, s_gate_b, s_out_gain, s_skip = lax.psum(
        (g_ln, g_conv_w, g_conv_b, g_gate_w, g_gate_b, g_out_gain, g_skip), ("seq", "batch")
    )
    block_out = jnp.stack(out_rows)[:, None]
    grad_tokens = jnp.stack(grad_rows_all)[:, None]
    return (
        block_out,
        grad_tokens,
        s_ln,
        s_up,
        s_conv_w,
        s_conv_b,
        s_query,
        s_key,
        s_value,
        s_gate_w,
        s_gate_b,
        s_out_gain,
        s_skip,
        s_down,
    )


def solution(mesh):
    placed = (
        P(None, "batch", "seq", None),
        P(),
        P(),
        P(),
        P(),
        P(),
        P(),
        P(),
        P(),
        P(),
        P(),
        P(),
        P(),
        P(None, "batch", "seq", None),
    )
    return jax.shard_map(
        per_device,
        mesh=mesh,
        in_specs=placed,
        out_specs=(
            P(None, "batch", "seq", None),
            P(None, "batch", "seq", None),
            P(),
            P("seq", "batch"),
            P(),
            P(),
            P(None, "seq", "batch"),
            P(None, "seq", "batch"),
            P(None, "seq", "batch"),
            P(),
            P(),
            P(),
            P(),
            P("seq", "batch"),
        ),
        check_vma=False,
    )
```

profile of v0, /device:TPU:24, one launch (start us, length us, event | category | flops | bytes accessed | tf_op | source)
XLA Modules:
  0.0 3782.8 jit_solution(15267126343681386025)
XLA Ops:
  10.7 8.0 fusion.363
  115.8 7.1 broadcast_multiply_fusion.1
  123.8 17.4 all-reduce.37
  146.1 40.8 %all-gather.14 = f32[8,4,512]{2,1,0:T(4,128)S(1)} all-gather(f32[1,4,512]{2,1,0:T(4,128)S(1)} %bitcast.892), channel_id=5, replica_groups=mesh['seq'=8,'batch'=4] {'seq'}, dimensions={0}, use_global_device_ids=true | all-gather | bytes 73728 | tf_op jit(solution)/shard_map/all_gather | solution.py:21
  187.3 530.4 %all-gather.23.cloned.1.call-done = f32[32,512,512]{2,1,0:T(8,128)} async-done(((f32[4,512,512]{2,1,0:T(8,128)}), f32[32,512,512]{2,1,0:T(8,128)}) %all-gather.23.cloned.1.call-update) | async-done | bytes 33554448 | tf_op jit(solution)/shard_map/all_gather | solution.py:21
  717.6 53.9 %while.76 = (s32[]{:T(128)}, f32[4,512,512]{2,1,0:T(8,128)}, f32[4,512]{1,0:T(4,128)S(1)}, f32[4]{0:T(128)S(1)}, s32[]{:T(128)}, /*index=5*/f32[8,4]{1,0:T(8,128...) while((s32[]{:T(128)}, f32[4,512,512]{2,1,0:T(8,128)}, ...), condition=%wide.region_9.11_spmd.clone, body=%wide.region_8.10_spmd.clone.sunk | while | flops 5253152 | bytes 12607853 | solution.py:32
  723.4 7.1 fusion.435
  730.6 6.7 fusion.435
  737.4 6.7 fusion.435
  744.2 6.7 fusion.435
  751.1 6.7 fusion.435
  757.9 6.7 fusion.435
  764.7 6.7 fusion.435
  807.8 42.1 %all-gather.15 = f32[8,4,512]{2,1,0:T(4,128)S(1)} all-gather(f32[1,4,512]{2,1,0:T(4,128)S(1)} %bitcast.893), channel_id=9, replica_groups=mesh['seq'=8,'batch'=4] {'seq'}, dimensions={0}, use_global_device_ids=true | all-gather | bytes 73728 | tf_op jit(solution)/shard_map/all_gather | solution.py:21
  876.0 482.1 %all-gather.25.cloned.1.call-done = f32[32,512,512]{2,1,0:T(8,128)} async-done(((f32[4,512,512]{2,1,0:T(8,128)}), f32[32,512,512]{2,1,0:T(8,128)}) %all-gather.25.cloned.1.call-update) | async-done | bytes 33554448 | tf_op jit(solution)/shard_map/all_gather | solution.py:21
  1358.1 64.1 %while.77 = (s32[]{:T(128)}, f32[4,512,512]{2,1,0:T(8,128)}, f32[4,512]{1,0:T(4,128)S(1)}, f32[4]{0:T(128)S(1)}, s32[]{:T(128)}, /*index=5*/f32[8,4]{1,0:T(8,128...) while((s32[]{:T(128)}, f32[4,512,512]{2,1,0:T(8,128)}, ...), condition=%wide.region_23.25_spmd.clone, body=%wide.region_22.24_spmd.clone.sunk | while | flops 5253152 | bytes 12607853 | solution.py:32
  1366.3 7.4 fusion.437
  1423.5 24.5 all-reduce.36
  1458.6 55.2 %all-gather.16 = f32[8,4,512]{2,1,0:T(4,128)S(1)} all-gather(f32[1,4,512]{2,1,0:T(4,128)} %bitcast.894), channel_id=12, replica_groups=mesh['seq'=8,'batch'=4] {'seq'}, dimensions={0}, use_global_device_ids=true | all-gather | bytes 73728 | tf_op jit(solution)/shard_map/all_gather | solution.py:21
  1537.5 461.7 %all-gather.27.cloned.1.call-done = f32[32,512,512]{2,1,0:T(8,128)} async-done(((f32[4,512,512]{2,1,0:T(8,128)}), f32[32,512,512]{2,1,0:T(8,128)}) %all-gather.27.cloned.1.call-update) | async-done | bytes 33554448 | tf_op jit(solution)/shard_map/all_gather | solution.py:21
  1999.2 68.6 %while.78 = (s32[]{:T(128)}, f32[4,512,512]{2,1,0:T(8,128)}, f32[4,512]{1,0:T(4,128)S(1)}, f32[4]{0:T(128)}, s32[]{:T(128)}, /*index=5*/f32[8,4]{1,0:T(8,128)}, ...) while((s32[]{:T(128)}, f32[4,512,512]{2,1,0:T(8,128)}, ...), condition=%wide.region_40.42_spmd.clone, body=%wide.region_39.41_spmd.clone.sunk | while | flops 5253156 | bytes 12607915 | solution.py:32
  2008.6 6.7 fusion.439
  2017.4 6.7 fusion.439
  2026.1 6.7 fusion.439
  2034.8 6.7 fusion.439
  2043.6 6.7 fusion.439
  2052.3 6.7 fusion.439
  2061.0 6.7 fusion.439
  2088.1 11.8 fusion.124
  2128.4 9.6 fusion.37
  2179.3 52.2 %all-gather.17 = f32[8,4,512]{2,1,0:T(4,128)S(1)} all-gather(f32[1,4,512]{2,1,0:T(4,128)} %bitcast.895), channel_id=15, replica_groups=mesh['seq'=8,'batch'=4] {'seq'}, dimensions={0}, use_global_device_ids=true | all-gather | bytes 73728 | tf_op jit(solution)/shard_map/all_gather | solution.py:21
  2245.1 541.1 %all-gather.29.cloned.1.call-done = f32[32,512,512]{2,1,0:T(8,128)} async-done(((f32[4,512,512]{2,1,0:T(8,128)}), f32[32,512,512]{2,1,0:T(8,128)}) %all-gather.29.cloned.1.call-update) | async-done | bytes 33554448 | tf_op jit(solution)/shard_map/all_gather | solution.py:21
  2786.2 57.6 %while.79 = (s32[]{:T(128)}, f32[4,512,512]{2,1,0:T(8,128)}, f32[4,512]{1,0:T(4,128)S(1)}, f32[4]{0:T(128)S(1)}, s32[]{:T(128)}, /*index=5*/f32[8,4]{1,0:T(8,128...) while((s32[]{:T(128)}, f32[4,512,512]{2,1,0:T(8,128)}, ...), condition=%wide.region_66.68_spmd.clone, body=%wide.region_65.67_spmd.clone.sunk | while | flops 5253156 | bytes 12607915 | solution.py:32
  2863.1 11.7 fusion.127
  2889.7 7.2 fusion.291
  2900.2 7.2 fusion.60
  2965.2 6.6 fusion.39
  2977.6 10.6 reshape.765
  2988.2 8.1 copy.292
  3023.5 8.3 fusion.133
  3031.8 10.8 convolution_add_fusion
  3042.6 20.4 reshape.749
  3063.1 17.9 copy.276
  3099.0 41.5 %all-reduce.35 = (f32[1024]{0:T(1024)}, f32[4,2048]{1,0:T(4,128)}, f32[2048]{0:T(1024)}, f32[4]{0:T(128)}, f32[2048]{0:T(1024)}, /*index=5*/f32[2048]{0:T(1024)}) all-reduce(f32[1024]{0:T(1024)S(1)} %add.739, f32[4,2048]{1,0:T(4,128)S(1)} %add_add_fusion.4, f32[2048]{0:T(1024)S(1)} %add.742, ...), channel_id=1, replica_groups=mesh['seq'=8,'batch'=4] {'seq','batch'}, use_global_device_ids=true, to_apply=%region_82.84 | all-reduce | flops 15364 | bytes 122912 | tf_op jit(solution)/shard_map/psum | solution.py:377
  3149.9 139.9 %reduce-scatter.10.cloned.1.call-done = f32[1,4,64,128]{3,2,1,0:T(8,128)} async-done(((f32[32,4,64,128]{3,2,1,0:T(8,128)}), f32[1,4,64,128]{3,2,1,0:T(8,128)}) %reduce-scatter.10.cloned.1.call-update) | async-done | bytes 131088 | tf_op jit(solution)/shard_map/reduce_scatter | solution.py:375
  3289.8 139.7 %reduce-scatter.12.cloned.1.call-done = f32[1,4,64,128]{3,2,1,0:T(8,128)} async-done(((f32[32,4,64,128]{3,2,1,0:T(8,128)}), f32[1,4,64,128]{3,2,1,0:T(8,128)}) %reduce-scatter.12.cloned.1.call-update) | async-done | bytes 131088 | tf_op jit(solution)/shard_map/reduce_scatter | solution.py:375
  3429.4 148.5 %reduce-scatter.14.cloned.1.call-done = f32[1,256,256]{2,1,0:T(8,128)} async-done(((f32[32,256,256]{2,1,0:T(8,128)}), f32[1,256,256]{2,1,0:T(8,128)}) %reduce-scatter.14.cloned.1.call-update) | async-done | bytes 262160 | tf_op jit(solution)/shard_map/reduce_scatter | solution.py:375
  3578.0 196.1 %reduce-scatter.6.cloned.1.call-done = f32[1,128,1024]{2,1,0:T(8,128)} async-done(((f32[32,128,1024]{2,1,0:T(8,128)}), f32[1,128,1024]{2,1,0:T(8,128)}) %reduce-scatter.6.cloned.1.call-update) | async-done | bytes 524304 | tf_op jit(solution)/shard_map/reduce_scatter | solution.py:375
  (900 shorter events, 604.3 us)
Async XLA Ops:
  7.2 36.6 copy-start
  7.2 710.4 %all-gather.23.cloned.1.call-start = ((), (), s32[]{:S(2)}) async-start(), calls=%async_computation.11 | async-start | bytes 37748736 | tf_op jit(solution)/shard_map/all_gather | solution.py:21
  8.8 9.9 copy-start.121
  8.8 13.3 copy-start.169
  8.9 13.3 slice-start
  10.6 11.5 copy-start.201
  10.7 11.5 slice-start.1
  18.7 17.1 collective-permute-start
  26.8 10.7 collective-permute-start.1
  61.5 61.8 %copy-start.211 = (f32[4]{0:T(128)}, f32[4]{0:T(128)S(1)}, u32[]{:S(2)}) copy-start(f32[4]{0:T(128)S(1)} %slice_reduce_fusion.1) | copy-start | bytes 52
  61.7 61.8 %copy-start.195 = (f32[4]{0:T(128)}, f32[4]{0:T(128)S(1)}, u32[]{:S(2)}) copy-start(f32[4]{0:T(128)S(1)} %get-tuple-element.1151) | copy-start | bytes 52
  76.4 1281.7 %all-gather.25.cloned.1.call-start = ((), (), s32[]{:S(2)}) async-start(), calls=%async_computation.12 | async-start | bytes 37748736 | tf_op jit(solution)/shard_map/all_gather | solution.py:21
  106.5 16.4 copy-start.210
  106.7 16.4 copy-start.193
  113.9 1885.4 %all-gather.27.cloned.1.call-start = ((), (), s32[]{:S(2)}) async-start(), calls=%async_computation.13 | async-start | bytes 37748736 | tf_op jit(solution)/shard_map/all_gather | solution.py:21
  780.0 81.2 %copy-start.127 = (f32[4,256]{1,0:T(4,128)}, f32[4,256]{1,0:T(4,128)S(1)}, u32[]{:S(2)}) copy-start(f32[4,256]{1,0:T(4,128)S(1)} %get-tuple-element.1142) | copy-start | bytes 12292
  796.2 1990.0 %all-gather.29.cloned.1.call-start = ((), (), s32[]{:S(2)}) async-start(), calls=%async_computation.14 | async-start | bytes 37748736 | tf_op jit(solution)/shard_map/all_gather | solution.py:21
  805.8 44.1 %copy-start.38 = (f32[4,256,512]{2,1,0:T(8,128)S(1)}, f32[4,256,512]{2,1,0:T(8,128)}, u32[]{:S(2)}) copy-start(f32[4,256,512]{2,1,0:T(8,128)} %copy-done.37) | copy-start | bytes 6291460
  805.8 44.1 %copy-start.177 = (f32[256,4]{0,1:T(4,128)S(1)}, f32[256,4]{0,1:T(4,128)}, u32[]{:S(2)}) copy-start(f32[256,4]{0,1:T(4,128)} %get-tuple-element.1238) | copy-start | bytes 12292
  805.8 44.1 %copy-start.178 = (f32[256,4]{0,1:T(4,128)S(1)}, f32[256,4]{0,1:T(4,128)}, u32[]{:S(2)}) copy-start(f32[256,4]{0,1:T(4,128)} %get-tuple-element.1240) | copy-start | bytes 12292
  1358.1 90.6 %copy-start.145 = (f32[4,256]{1,0:T(4,128)S(1)}, f32[4,256]{1,0:T(4,128)}, u32[]{:S(2)}) copy-start(f32[4,256]{1,0:T(4,128)} %copy-done.144) | copy-start | bytes 12292
  1422.2 30.0 copy-start.130
  1422.2 30.0 copy-start.134
  1422.2 30.0 copy-start.143
  1422.2 30.0 copy-start.172
  1422.2 30.0 copy-start.189
  1422.2 30.0 copy-start.215
  1422.2 30.0 copy-start.216
  1453.2 778.3 %copy-start.119 = (f32[4,256]{1,0:T(4,128)}, f32[4,256]{1,0:T(4,128)S(1)}, u32[]{:S(2)}) copy-start(f32[4,256]{1,0:T(4,128)S(1)} %get-tuple-element.983) | copy-start | bytes 12292
  1458.6 61.3 %copy-start.15 = (f32[256,4,512]{2,0,1:T(8,128)S(1)}, f32[256,4,512]{2,0,1:T(8,128)}, u32[]{:S(2)}) copy-start(f32[256,4,512]{2,0,1:T(8,128)} %copy.227) | copy-start | bytes 6291460
  2082.5 149.0 %copy-start.139 = (f32[256,4]{0,1:T(4,128)}, f32[256,4]{0,1:T(4,128)S(1)}, u32[]{:S(2)}) copy-start(f32[256,4]{0,1:T(4,128)S(1)} %get-tuple-element.1232) | copy-start | bytes 12292
  2115.4 116.1 %copy-start.135 = (f32[256,4]{0,1:T(4,128)}, f32[256,4]{0,1:T(4,128)S(1)}, u32[]{:S(2)}) copy-start(f32[256,4]{0,1:T(4,128)S(1)} %get-tuple-element.1223) | copy-start | bytes 12292
  2115.4 116.1 %copy-start.137 = (f32[256,4]{0,1:T(4,128)}, f32[256,4]{0,1:T(4,128)S(1)}, u32[]{:S(2)}) copy-start(f32[256,4]{0,1:T(4,128)S(1)} %get-tuple-element.1224) | copy-start | bytes 12292
  2140.1 17.1 copy-start.184
  2147.1 997.3 %all-reduce.40.cloned.1.call-start = ((), (), s32[]{:S(2)}) async-start(), calls=%async_computation.9 | async-start | bytes 393216 | tf_op jit(solution)/shard_map/psum | solution.py:377
  2239.7 546.5 %copy-start.198 = (f32[4]{0:T(128)S(1)}, f32[4]{0:T(128)}, u32[]{:S(2)}) copy-start(f32[4]{0:T(128)} %custom-call.11) | copy-start | bytes 52
  2786.2 57.6 %copy-start.207 = (f32[4]{0:T(128)S(1)}, f32[4]{0:T(128)}, u32[]{:S(2)}) copy-start(f32[4]{0:T(128)} %get-tuple-element.1118) | copy-start | bytes 52
  2900.2 249.7 %reduce-scatter.8.cloned.1.call-start = ((), (), s32[]{:S(2)}) async-start(), calls=%async_computation.6 | async-start | bytes 4325376 | tf_op jit(solution)/shard_map/reduce_scatter | solution.py:375
  2921.4 368.3 %reduce-scatter.10.cloned.1.call-start = ((), (), s32[]{:S(2)}) async-start(), calls=%async_computation.7 | async-start | bytes 4325376 | tf_op jit(solution)/shard_map/reduce_scatter | solution.py:375
  2936.6 492.8 %reduce-scatter.12.cloned.1.call-start = ((), (), s32[]{:S(2)}) async-start(), calls=%async_computation.8 | async-start | bytes 4325376 | tf_op jit(solution)/shard_map/reduce_scatter | solution.py:375
  2952.9 625.1 %reduce-scatter.14.cloned.1.call-start = ((), (), s32[]{:S(2)}) async-start(), calls=%async_computation.10 | async-start | bytes 8650752 | tf_op jit(solution)/shard_map/reduce_scatter | solution.py:375
  2996.4 777.7 %reduce-scatter.6.cloned.1.call-start = ((), (), s32[]{:S(2)}) async-start(), calls=%async_computation.5 | async-start | bytes 17301504 | tf_op jit(solution)/shard_map/reduce_scatter | solution.py:375
  3009.1 10.1 collective-permute-start.3
  3015.8 5.8 collective-permute-start.2
  3019.6 12.2 copy-start.82
  3022.1 9.7 copy-start.84
  3095.5 45.1 %copy-start.204 = (f32[256]{0:T(256)S(1)}, f32[256]{0:T(256)}, u32[]{:S(2)}) copy-start(f32[256]{0:T(256)} %copy-done.203) | copy-start | bytes 3076
  3095.5 45.1 %copy-start.202 = (f32[256]{0:T(256)S(1)}, f32[256]{0:T(256)}, u32[]{:S(2)}) copy-start(f32[256]{0:T(256)} %copy-done.201) | copy-start | bytes 3076
  (202 other events, 712.1 us)
Sparse Core Ops, SparseCore 0:
  76.6 641.0 all-gather.22
  719.1 638.9 all-gather.24
  1359.7 639.5 all-gather.26
  2147.2 638.9 all-gather.28
  2900.3 123.8 all-reduce.39
  3026.9 122.9 reduce-scatter.7
  3152.7 137.0 reduce-scatter.9
  3292.6 136.7 reduce-scatter.11
  3432.3 145.6 reduce-scatter.13
  3580.7 193.3 reduce-scatter.5
where the time goes:
time: 3800 us; the launch traced here: 3780 us
  waiting for transfers between devices  2650 us (70%)
  other arithmetic  375 us (10%)
  blocking collectives  274 us (7%)
  matrix products  265 us (7%)
  local copies, waits for them, and re-layouts  191 us (5%)
    all_gather x4, waiting for transfers between devices, entering(): everything = jax.tree.map(lambda part: lax.all_gather(part, axis), x)  2020 us
    reduce_scatter x5, waiting for transfers between devices, per_device(): lax.psum_scatter(blocks, ('seq', 'batch'), scatter_dimension=0, tiled=True)  630 us
    select_n x96, other arithmetic, step(): return jax.tree.map(lambda a, b: jnp.where(reached, a, b), new, before)  233 us
    all_gather x4, blocking collectives, entering(): everything = jax.tree.map(lambda part: lax.all_gather(part, axis), x)  190 us
  transfers between devices with their start and end apart: 14, of which 10 were waited for; matrix products, arithmetic and copies ran while one was open for 13% of the time, Pallas kernels for 0%

commit v1 on v0

v1 whole, which is shorter than its diff:
```python
from functools import partial

import jax
import jax.numpy as jnp
from jax import lax
from jax.experimental import pallas as pl
from jax.experimental.pallas import tpu as pltpu
from jax.sharding import PartitionSpec as P

norm_epsilon = 1e-05
floor_value = -1e30


def shifted(value, axis, steps):
    count = lax.axis_size(axis)
    initial, last = (max(0, -steps), min(count, count - steps))
    return lax.ppermute(value, axis, [(source, source + steps) for source in range(initial, last)])


def combine_states(earlier, later):
    top = jnp.maximum(later[3] + earlier[2], later[2])
    keep_first = jnp.exp(later[3] + earlier[2] - top)
    keep_second = jnp.exp(later[2] - top)
    merged_c = keep_first[..., None, None] * earlier[0] + keep_second[..., None, None] * later[0]
    merged_n = keep_first[..., None] * earlier[1] + keep_second[..., None] * later[1]
    return (merged_c, merged_n, top, earlier[3] + later[3])


def state_identity(template):
    return (
        jnp.zeros_like(template[0]),
        jnp.zeros_like(template[1]),
        jnp.full_like(template[2], floor_value),
        jnp.zeros_like(template[3]),
    )


def head_output(hidden, out_gain, skip_gain, conv_out, gate_z):
    centre = hidden - jnp.mean(hidden, axis=-1, keepdims=True)
    spread = jnp.mean(centre * centre, axis=-1, keepdims=True)
    normed = centre * lax.rsqrt(spread + norm_epsilon)
    flat_out = normed.transpose(1, 0, 2).reshape(hidden.shape[1], -1) * out_gain
    return (flat_out + skip_gain * conv_out) * jax.nn.silu(gate_z)


def output_tail(
    query_f,
    key_f,
    value_f,
    gate_pre,
    conv_f,
    gate_z,
    out_gain,
    skip_gain,
    state_c,
    state_n,
    state_m,
):
    head_count = gate_pre.shape[1] // 2
    in_gate = gate_pre[:, :head_count].T
    log_forget = jax.nn.log_sigmoid(gate_pre[:, head_count:]).T
    hidden = cell_hidden(
        to_heads(query_f, head_count),
        to_heads(key_f, head_count),
        to_heads(value_f, head_count),
        in_gate,
        log_forget,
        state_c,
        state_n,
        state_m,
    )
    return head_output(hidden, out_gain, skip_gain, conv_f, gate_z)


def state_tail(key_f, value_f, gate_pre, state_c, state_n, state_m):
    head_count = gate_pre.shape[1] // 2
    in_gate = gate_pre[:, :head_count].T
    log_forget = jax.nn.log_sigmoid(gate_pre[:, head_count:]).T
    return cell_state(
        to_heads(key_f, head_count),
        to_heads(value_f, head_count),
        in_gate,
        log_forget,
        state_c,
        state_n,
        state_m,
    )


def to_device_blocks(grad_full, seq_count, batch_count):
    if grad_full.ndim == 2:
        rows, cols = grad_full.shape
        split = grad_full.reshape(seq_count, rows // seq_count, batch_count, cols // batch_count)
        return split.transpose(0, 2, 1, 3).reshape(
            seq_count * batch_count, rows // seq_count, cols // batch_count
        )
    heads, rows, cols = grad_full.shape
    split = grad_full.reshape(heads, seq_count, rows // seq_count, batch_count, cols // batch_count)
    return split.transpose(1, 3, 0, 2, 4).reshape(
        seq_count * batch_count, heads, rows // seq_count, cols // batch_count
    )


f32 = jnp.float32
bf16 = jnp.bfloat16
chunk_len = 256
wide_len = 512
vmem_bytes = 56 * 1024 * 1024


def mm(a, b):
    return lax.dot_general(a, b, (((1,), (0,)), ((), ())), preferred_element_type=f32)


def mm_nt(a, b):
    return lax.dot_general(a, b, (((1,), (1,)), ((), ())), preferred_element_type=f32)


def mm_tn(a, b):
    return lax.dot_general(a, b, (((0,), (0,)), ((), ())), preferred_element_type=f32)


def split_three(value):
    high = value.astype(bf16)
    rest = value - high.astype(f32)
    middle = rest.astype(bf16)
    low = (rest - middle.astype(f32)).astype(bf16)
    return high, middle, low


def conv_taps(ext, length):
    return [pltpu.roll(ext, 3 - j, 0)[8 : 8 + length] if j < 3 else ext[8 : 8 + length] for j in range(4)]


def lift_kernel(chained, head_ref, normed, w_mix, w_gate, w_q, w_k, w_v, conv_w, conv_b, gate_w, *refs):
    if chained:
        rows_before, *refs, halo_out, carry = refs
    else:
        *refs, carry = refs
    mix_out, conv_out, q_out, k_out, v_out, z_out, gate_out = refs
    length = normed.shape[0]

    @pl.when(pl.program_id(0) == 0)
    def _():
        if chained:
            mix_before = mm(rows_before[...], w_mix[...]).astype(bf16)
            halo_out[...] = mix_before
            carry[...] = mix_before[8:16].astype(f32)
        else:
            carry[...] = jnp.zeros_like(carry)

    rows = normed[...]
    mix = mm(rows, w_mix[...]).astype(bf16)
    mix_out[...] = mix
    z_out[...] = mm(rows, w_gate[...])
    mix_f = mix.astype(f32)
    taps = conv_taps(jnp.concatenate([carry[...], mix_f], axis=0), length)
    carry[...] = mix_f[length - 8 :]
    summed = conv_b[...]
    for j in range(4):
        summed = summed + conv_w[j : j + 1, :] * taps[j]
    conv = (summed * jax.nn.sigmoid(summed)).astype(bf16)
    conv_out[...] = conv
    q = mm(conv, w_q[0]).astype(bf16)
    k = mm(conv, w_k[0]).astype(bf16)
    v = mm(mix, w_v[0]).astype(bf16)
    q_out[...] = q
    k_out[...] = k
    v_out[...] = v
    parts = mm_nt(gate_w[0], q) + mm_nt(gate_w[1], k) + mm_nt(gate_w[2], v)
    gate_out[...] = parts[0:8] + parts[8:16] + parts[16:24]


def gate_rows(gates, causal, diagonal):
    in_row = gates[0:1, :]
    pre = gates[1:2, :]
    log_forget = jnp.minimum(pre, 0.0) - jnp.log1p(jnp.exp(-jnp.abs(pre)))
    run_col = jnp.sum(jnp.where(causal, log_forget, 0.0), axis=1, keepdims=True)
    run_row = jnp.sum(jnp.where(diagonal, run_col, 0.0), axis=0, keepdims=True)
    return in_row - run_row, run_col, log_forget


def masks(length):
    row = lax.broadcasted_iota(jnp.int32, (length, length), 0)
    col = lax.broadcasted_iota(jnp.int32, (length, length), 1)
    return row >= col, row == col


def cell_forward_kernel(
    chained, head_ref, gates, q_ref, k_ref, v_ref, conv_ref, z_ref, out_gain, skip_gain, w_down, *refs
):
    if chained:
        *first, part_out, normed_out, state_out, norm_out, weight_out, col_out, row_out = refs[:10]
        *final, state, norm, level = refs[10:]
    else:
        part_out, normed_out, state_out, norm_out, weight_out, col_out, row_out = refs[:7]
        state, norm, level = refs[7:]
    length = q_ref.shape[0]
    head_size = q_ref.shape[1]
    scale = head_size ** (-0.5)

    @pl.when(pl.program_id(0) == 0)
    def _():
        if chained:
            for ref, value in zip((state, norm, level), first):
                ref[...] = value[...]
        else:
            state[...] = jnp.zeros_like(state)
            norm[...] = jnp.zeros_like(norm)
            level[...] = jnp.full_like(level, floor_value)

    causal, diagonal = masks(length)
    a_row, run_col, log_forget = gate_rows(gates[...], causal, diagonal)
    before = level[0:1, 0:1]
    top = jnp.maximum(
        before, jnp.max(jnp.where(causal, a_row, floor_value), axis=1, keepdims=True)
    )
    decay = jnp.exp(jnp.where(causal, a_row - top, floor_value))
    q = q_ref[...]
    k = k_ref[...]
    v = v_ref[...]
    q_f = q.astype(f32)
    weights = decay * (mm_nt(q, k) * scale)
    weights_low = weights.astype(bf16)
    weight_out[...] = weights_low
    from_state = jnp.exp(before - top)
    state_low = state[...].astype(bf16)
    state_out[0] = state_low
    norm_row = norm[0:1, :]
    norm_out[0] = norm[...]
    numerator = mm(weights_low, v) + (from_state * scale) * mm(q, state_low)
    denominator = jnp.sum(weights, axis=1, keepdims=True) + (from_state * scale) * jnp.sum(
        q_f * norm_row, axis=1, keepdims=True
    )
    floor = jnp.exp(-(run_col + top))
    size = jnp.abs(denominator)
    inverse = 1.0 / jnp.maximum(size, floor)
    hidden = numerator * inverse
    centre = hidden - jnp.mean(hidden, axis=1, keepdims=True)
    spread = jnp.mean(centre * centre, axis=1, keepdims=True)
    rstd = lax.rsqrt(spread + norm_epsilon)
    normed = centre * rstd
    normed_out[...] = normed
    gate_z = z_ref[...]
    gated = (normed * out_gain[...] + skip_gain[...] * conv_ref[...].astype(f32)) * (
        gate_z * jax.nn.sigmoid(gate_z)
    )
    part_out[...] = mm(gated.astype(bf16), w_down[...]).astype(bf16)
    factor = jnp.where(
        size > floor,
        jnp.where(denominator > 0, 1.0, -1.0) * inverse * (norm_epsilon * rstd * rstd),
        0.0,
    )
    lane = lax.broadcasted_iota(jnp.int32, (length, 128), 1)
    packed = jnp.where(lane == 0, rstd, inverse)
    packed = jnp.where(lane == 2, from_state, packed)
    packed = jnp.where(lane == 3, top, packed)
    col_out[...] = jnp.where(lane == 4, factor, packed)
    sub = lax.broadcasted_iota(jnp.int32, (8, length), 0)
    row_out[...] = jnp.where(sub == 0, a_row, 1.0 - jnp.exp(log_forget))
    last = top[length - 1 : length, :]
    a_col = jnp.sum(jnp.where(diagonal, a_row, 0.0), axis=1, keepdims=True)
    weighted = k.astype(f32) * jnp.exp(a_col - last)
    keep = jnp.exp(before - last)
    state[...] = keep * state[...] + mm_tn(weighted.astype(bf16), v)
    norm[...] = keep * norm[...] + jnp.sum(weighted, axis=0, keepdims=True)
    level[...] = jnp.broadcast_to(run_col[length - 1 : length, :] + last, level.shape)
    if chained:
        for ref, value in zip(final, (state, norm, level)):
            ref[...] = value[...]


def cell_backward_kernel(
    chained, head_ref, rows_ref, q_ref, k_ref, v_ref, conv_ref, z_ref, normed_ref, state_ref, norm_ref,
    weight_ref, col_ref, cot_ref, out_gain, skip_gain, w_down, *refs
):
    if chained:
        *first, dq_out, dk_out, dv_out, dskip_out, dz_out, gate_out, g_down_out, g_gain_out = refs[:10]
        *final, d_state, d_norm, g_down, g_gain = refs[10:]
    else:
        dq_out, dk_out, dv_out, dskip_out, dz_out, gate_out, g_down_out, g_gain_out = refs[:8]
        d_state, d_norm, g_down, g_gain = refs[8:]
    length = q_ref.shape[0]
    head_size = q_ref.shape[1]
    scale = head_size ** (-0.5)

    @pl.when(pl.program_id(0) == 0)
    def _():
        if chained:
            d_state[...] = first[0][...]
            d_norm[...] = first[1][...]
        else:
            d_state[...] = jnp.zeros_like(d_state)
            d_norm[...] = jnp.zeros_like(d_norm)
        g_down[...] = jnp.zeros_like(g_down)
        g_gain[...] = jnp.zeros_like(g_gain)

    causal, diagonal = masks(length)
    rstd = col_ref[:, 0:1]
    inverse = col_ref[:, 1:2]
    from_state = col_ref[:, 2:3]
    top = col_ref[:, 3:4]
    factor = col_ref[:, 4:5]
    a_row = rows_ref[0:1, :]
    q = q_ref[...]
    k = k_ref[...]
    v = v_ref[...]
    q_f = q.astype(f32)
    k_f = k.astype(f32)
    conv = conv_ref[...].astype(f32)
    normed = normed_ref[...]
    gate_z = z_ref[...]
    cot = cot_ref[...]
    opened = jax.nn.sigmoid(gate_z)
    silu = gate_z * opened
    head_in = normed * out_gain[...] + skip_gain[...] * conv
    g_down[...] += mm_tn((head_in * silu).astype(bf16), cot)
    d_gated = mm_nt(cot, w_down[...])
    dz_out[...] = (d_gated * head_in * (opened * (1.0 + gate_z * (1.0 - opened)))).astype(bf16)
    d_head = d_gated * silu
    g_gain[0:1, :] += jnp.sum(d_head * normed, axis=0, keepdims=True)
    g_gain[1:2, :] += jnp.sum(d_head * conv, axis=0, keepdims=True)
    dskip_out[...] = skip_gain[...] * d_head
    d_hat = d_head * out_gain[...]
    along = jnp.sum(d_hat * normed, axis=1, keepdims=True)
    d_hidden = rstd * (
        d_hat - jnp.mean(d_hat, axis=1, keepdims=True) - normed * (along / head_size)
    )
    d_num = d_hidden * inverse
    d_den = -along * factor
    d_num_low = d_num.astype(bf16)
    decay = jnp.exp(jnp.where(causal, a_row - top, floor_value))
    d_scores = ((mm_nt(d_num_low, v) + d_den) * (decay * scale)).astype(bf16)
    through = from_state * scale
    dq_near = mm(d_scores, k)
    dq_far = (
        mm_nt((d_num * through).astype(bf16), state_ref[0])
        + (through * d_den) * norm_ref[0, 0:1, :]
    )
    last = top[length - 1 : length, :]
    keep = from_state[length - 1 : length, :]
    a_col = jnp.sum(jnp.where(diagonal, a_row, 0.0), axis=1, keepdims=True)
    key_weight = jnp.exp(a_col - last)
    d_state_low = d_state[...].astype(bf16)
    dk_near = mm_tn(d_scores, q)
    dk_far = key_weight * (mm_nt(v, d_state_low) + d_norm[0:1, :])
    dv = mm_tn(weight_ref[...], d_num_low) + mm((k_f * key_weight).astype(bf16), d_state_low)
    dq_out[...] = dq_near + dq_far
    dk_out[...] = dk_near + dk_far
    dv_out[...] = dv
    held = state_ref[0].astype(f32) * d_state[...]
    held = jnp.sum(jnp.sum(held, axis=0, keepdims=True) + norm_ref[0, 0:1, :] * d_norm[0:1, :])
    q_state = q_f * through
    d_state[...] = keep * d_state[...] + mm_tn(q_state.astype(bf16), d_num_low)
    d_norm[...] = keep * d_norm[...] + jnp.sum(q_state * d_den, axis=0, keepdims=True)
    q_dot = jnp.sum(q_f * (dq_near + dq_far), axis=1, keepdims=True)
    k_near = jnp.sum(k_f * dk_near, axis=1, keepdims=True)
    k_far = jnp.sum(k_f * dk_far, axis=1, keepdims=True)
    d_in = jnp.sum(jnp.where(diagonal, k_near + k_far, 0.0), axis=0, keepdims=True)
    d_log = jnp.sum(
        jnp.where(causal, q_dot - k_near, jnp.where(diagonal, 0.0, k_far)), axis=0, keepdims=True
    )
    d_log = d_log + keep * held
    sub = lax.broadcasted_iota(jnp.int32, (8, length), 0)
    gate_out[...] = jnp.where(sub == 0, d_in, d_log * rows_ref[1:2, :])

    @pl.when(pl.program_id(0) == pl.num_programs(0) - 1)
    def _():
        if chained:
            final[0][...] = d_state[...]
            final[1][...] = d_norm[...]
        g_down_out[...] = g_down[...].astype(bf16)
        g_gain_out[...] = g_gain[...]


def lower_kernel(
    chained, head_ref, d_gate, dq_ref, dk_ref, dv_ref, dskip_ref, dz_ref, mix_ref, mix_before, conv_ref,
    q_ref, k_ref, v_ref, normed, w_q, w_k, w_v, w_mix, w_gate, conv_w, conv_b, gate_w, *refs
):
    if chained:
        first_halo, first_later, *refs = refs
        later_out = refs.pop(7)
    part_out, gq_out, gk_out, gv_out, gm_out, gz_out, small_out = refs[:7]
    g_q, g_k, g_v, g_m, g_z, g_small, later = refs[7:]
    length = q_ref.shape[0]
    step = pl.program_id(0)

    @pl.when(step == 0)
    def _():
        for ref in (g_q, g_k, g_v, g_m, g_z, g_small, later):
            ref[...] = jnp.zeros_like(ref)
        if chained:
            later[...] = first_later[...]

    high, middle, low = split_three(d_gate[...])
    left = jnp.concatenate([high, middle, low, high, middle, high], axis=0)
    d_joined = mm_tn(left, gate_w[...])
    size = q_ref.shape[1]
    query_low = (dq_ref[...] + d_joined[:, :size]).astype(bf16)
    key_low = (dk_ref[...] + d_joined[:, size : 2 * size]).astype(bf16)
    value_low = (dv_ref[...] + d_joined[:, 2 * size :]).astype(bf16)
    conv = conv_ref[...]
    mix = mix_ref[...]
    g_q[...] += mm_tn(conv, query_low)
    g_k[...] += mm_tn(conv, key_low)
    g_v[...] += mm_tn(mix, value_low)
    three = jnp.concatenate([high, middle, low], axis=0)
    for at, ref in enumerate((q_ref, k_ref, v_ref)):
        got = mm(three, ref[...])
        g_small[8 * at : 8 * at + 8, :] += got[0:8] + got[8:16] + got[16:24]
    d_conv = dskip_ref[...] + mm_nt(query_low, w_q[0]) + mm_nt(key_low, w_k[0])
    halo = mix_before[8:16, :].astype(f32)
    edge = first_halo[8:16, :].astype(f32) if chained else 0.0
    halo = jnp.where(step == pl.num_programs(0) - 1, edge, halo)
    taps = conv_taps(jnp.concatenate([halo, mix.astype(f32)], axis=0), length)
    summed = conv_b[...]
    for j in range(4):
        summed = summed + conv_w[j : j + 1, :] * taps[j]
    opened = jax.nn.sigmoid(summed)
    d_summed = d_conv * (opened * (1.0 + summed * (1.0 - opened)))
    for j in range(4):
        g_small[24 + j : 25 + j, :] += jnp.sum(d_summed * taps[j], axis=0, keepdims=True)
    g_small[28:29, :] += jnp.sum(d_summed, axis=0, keepdims=True)
    ext = jnp.concatenate([d_summed, later[...]], axis=0)
    later[...] = d_summed[0:8]
    d_mix = conv_w[3:4, :] * d_summed
    for j in range(3):
        d_mix = d_mix + conv_w[j : j + 1, :] * pltpu.roll(ext, length + 8 - (3 - j), 0)[0:length]
    d_mix = (d_mix + mm_nt(value_low, w_v[0])).astype(bf16)
    d_z = dz_ref[...]
    rows = normed[...]
    g_m[...] += mm_tn(rows, d_mix)
    g_z[...] += mm_tn(rows, d_z)
    part_out[...] = (mm_nt(d_mix, w_mix[...]) + mm_nt(d_z, w_gate[...])).astype(bf16)

    @pl.when(step == pl.num_programs(0) - 1)
    def _():
        gq_out[...] = g_q[...].astype(bf16)
        gk_out[...] = g_k[...].astype(bf16)
        gv_out[...] = g_v[...].astype(bf16)
        gm_out[...] = g_m[...].astype(bf16)
        gz_out[...] = g_z[...].astype(bf16)
        small_out[...] = g_small[...]
        if chained:
            later_out[...] = later[...]


def struct(shape, dtype):
    return jax.ShapeDtypeStruct(shape, dtype)


def run_kernel(body, head, grid, inputs, in_specs, outs, out_specs, scratch, name, flops, nbytes):
    return pl.pallas_call(
        body,
        grid_spec=pltpu.PrefetchScalarGridSpec(
            num_scalar_prefetch=1,
            grid=(grid,),
            in_specs=in_specs,
            out_specs=out_specs,
            scratch_shapes=scratch,
        ),
        out_shape=outs,
        compiler_params=pltpu.CompilerParams(
            dimension_semantics=("arbitrary",), vmem_limit_bytes=vmem_bytes
        ),
        cost_estimate=pl.CostEstimate(flops=flops, bytes_accessed=nbytes, transcendentals=0),
        name=name,
    )(head, *inputs)


def fixed(shape, *index):
    return pl.BlockSpec(shape, lambda g, h: tuple(h[0] if i == "h" else i for i in index))


def lift(head, normed, w_up, w_query, w_key, w_value, conv_w, conv_b, gate_parts, *first):
    tokens, width = normed.shape
    heads, size, _ = w_query.shape
    length = wide_len
    by_row = lambda cols: pl.BlockSpec((length, cols), lambda g, h: (g, 0))
    weight = pl.BlockSpec((1, size, size), lambda g, h: (h[0], 0, 0))
    chained = len(first) > 0
    halo = [pl.BlockSpec((16, size), lambda g, h: (0, 0))] * chained
    return run_kernel(
        partial(lift_kernel, chained), head, tokens // length,
        (normed, w_up, w_up, w_query, w_key, w_value, conv_w, conv_b, gate_parts, *first),
        [
            by_row(width),
            pl.BlockSpec((width, size), lambda g, h: (0, h[0])),
            pl.BlockSpec((width, size), lambda g, h: (0, heads + h[0])),
            weight, weight, weight,
            pl.BlockSpec((4, size), lambda g, h: (0, h[0])),
            pl.BlockSpec((1, size), lambda g, h: (0, h[0])),
            pl.BlockSpec(gate_parts.shape, lambda g, h: (0, 0, 0)),
        ]
        + [pl.BlockSpec((16, width), lambda g, h: (0, 0))] * chained,
        [struct((tokens, size), bf16)] * 5
        + [struct((tokens, size), f32), struct((8, tokens), f32)]
        + [struct((16, size), bf16)] * chained,
        [by_row(size)] * 6 + [pl.BlockSpec((8, length), lambda g, h: (0, g))] + halo,
        [pltpu.VMEM((8, size), f32)],
        "lift", 2 * tokens * size * (2 * width + 3 * size), 24 * 2**20,
    )


def cell_forward(head, gates, q, k, v, conv, gate_z, out_gain, skip_gain, w_down, *first):
    tokens, size = q.shape
    width = w_down.shape[1]
    length = chunk_len
    steps = tokens // length
    by_row = lambda cols: pl.BlockSpec((length, cols), lambda g, h: (g, 0))
    gain = pl.BlockSpec((1, size), lambda g, h: (0, h[0]))
    carried = [struct(value.shape, f32) for value in first]
    carried_specs = [pl.BlockSpec(value.shape, lambda g, h: (0, 0)) for value in first]
    return run_kernel(
        partial(cell_forward_kernel, len(first) > 0), head, steps,
        (gates, q, k, v, conv, gate_z, out_gain, skip_gain, w_down, *first),
        [pl.BlockSpec((2, length), lambda g, h: (0, g))]
        + [by_row(size)] * 5
        + [gain, gain, pl.BlockSpec((size, width), lambda g, h: (h[0], 0))]
        + carried_specs,
        [
            struct((tokens, width), bf16),
            struct((tokens, size), f32),
            struct((steps, size, size), bf16),
            struct((steps, 8, size), f32),
            struct((tokens, length), bf16),
            struct((tokens, 128), f32),
            struct((8, tokens), f32),
        ]
        + carried,
        [
            by_row(width),
            by_row(size),
            pl.BlockSpec((1, size, size), lambda g, h: (g, 0, 0)),
            pl.BlockSpec((1, 8, size), lambda g, h: (g, 0, 0)),
            by_row(length),
            by_row(128),
            pl.BlockSpec((8, length), lambda g, h: (0, g)),
        ]
        + carried_specs,
        [pltpu.VMEM((size, size), f32), pltpu.VMEM((8, size), f32), pltpu.VMEM((8, 128), f32)],
        "cell_forward", 2 * tokens * size * (2 * length + 2 * size + width), 28 * 2**20,
    )


def cell_backward(
    head, rows, q, k, v, conv, gate_z, normed, states, norms, weights, cols, cot,
    out_gain, skip_gain, w_down, *first,
):
    tokens, size = q.shape
    width = w_down.shape[1]
    length = chunk_len
    steps = tokens // length
    end = steps - 1
    by_row = lambda n: pl.BlockSpec((length, n), lambda g, h: (end - g, 0))
    gain = pl.BlockSpec((1, size), lambda g, h: (0, h[0]))
    whole = lambda shape: pl.BlockSpec(shape, lambda g, h: (0, 0))
    carried = [struct(value.shape, f32) for value in first]
    carried_specs = [whole(value.shape) for value in first]
    return run_kernel(
        partial(cell_backward_kernel, len(first) > 0), head, steps,
        (rows, q, k, v, conv, gate_z, normed, states, norms, weights, cols, cot,
         out_gain, skip_gain, w_down, *first),
        [pl.BlockSpec((8, length), lambda g, h: (0, end - g))]
        + [by_row(size)] * 6
        + [
            pl.BlockSpec((1, size, size), lambda g, h: (end - g, 0, 0)),
            pl.BlockSpec((1, 8, size), lambda g, h: (end - g, 0, 0)),
            by_row(length),
            by_row(128),
            by_row(width),
            gain, gain,
            pl.BlockSpec((size, width), lambda g, h: (h[0], 0)),
        ]
        + carried_specs,
        [struct((tokens, size), f32)] * 4
        + [
            struct((tokens, size), bf16),
            struct((8, tokens), f32),
            struct((size, width), bf16),
            struct((8, size), f32),
        ]
        + carried,
        [by_row(size)] * 5
        + [
            pl.BlockSpec((8, length), lambda g, h: (0, end - g)),
            whole((size, width)),
            whole((8, size)),
        ]
        + carried_specs,
        [
            pltpu.VMEM((size, size), f32),
            pltpu.VMEM((8, size), f32),
            pltpu.VMEM((size, width), f32),
            pltpu.VMEM((8, size), f32),
        ],
        "cell_backward", 2 * tokens * size * (4 * length + 4 * size + 2 * width), 44 * 2**20,
    )


def lower(
    head, d_gate, dq, dk, dv, dskip, dz, mix, conv, q, k, v, normed,
    w_query, w_key, w_value, w_up, conv_w, conv_b, gate_pairs, *first,
):
    tokens, size = q.shape
    width = normed.shape[1]
    heads = w_query.shape[0]
    length = wide_len
    steps = tokens // length
    end = steps - 1
    by_row = lambda n: pl.BlockSpec((length, n), lambda g, h: (end - g, 0))
    weight = pl.BlockSpec((1, size, size), lambda g, h: (h[0], 0, 0))
    whole = lambda shape: pl.BlockSpec(shape, lambda g, h: (0, 0))
    chained = len(first) > 0
    return run_kernel(
        partial(lower_kernel, chained), head, steps,
        (d_gate, dq, dk, dv, dskip, dz, mix, mix, conv, q, k, v, normed,
         w_query, w_key, w_value, w_up, w_up, conv_w, conv_b, gate_pairs, *first),
        [pl.BlockSpec((8, length), lambda g, h: (0, end - g))]
        + [by_row(size)] * 6
        + [
            pl.BlockSpec(
                (16, size),
                lambda g, h: (jnp.maximum((end - g) * (length // 16) - 1, 0), 0),
            )
        ]
        + [by_row(size)] * 4
        + [by_row(width), weight, weight, weight]
        + [
            pl.BlockSpec((width, size), lambda g, h: (0, h[0])),
            pl.BlockSpec((width, size), lambda g, h: (0, heads + h[0])),
            pl.BlockSpec((4, size), lambda g, h: (0, h[0])),
            pl.BlockSpec((1, size), lambda g, h: (0, h[0])),
            whole(gate_pairs.shape),
        ]
        + [whole(value.shape) for value in first],
        [struct((tokens, width), bf16)]
        + [struct((size, size), bf16)] * 3
        + [struct((width, size), bf16)] * 2
        + [struct((32, size), f32)]
        + [struct((8, size), f32)] * chained,
        [by_row(width)]
        + [whole((size, size))] * 3
        + [whole((width, size))] * 2
        + [whole((32, size))]
        + [whole((8, size))] * chained,
        [pltpu.VMEM((size, size), f32)] * 3
        + [pltpu.VMEM((width, size), f32)] * 2
        + [pltpu.VMEM((32, size), f32), pltpu.VMEM((8, size), f32)],
        "lower", 2 * tokens * size * (6 * size + 4 * width), 48 * 2**20,
    )


def swap(value, axis, mask):
    count = lax.axis_size(axis)
    return lax.ppermute(value, axis, [(s, s ^ mask) for s in range(count)])


def part_of(value, at, count, axis):
    size = value.shape[axis] // count
    return lax.dynamic_slice_in_dim(value, at * size, size, axis)


def halved(value, bit, dim, axis, mask):
    kept = part_of(value, bit, 2, dim).astype(f32)
    return kept + swap(part_of(value, 1 - bit, 2, dim), axis, mask).astype(f32)


def paired(mine, other, bit, dim):
    return jnp.where(
        bit == 0, jnp.concatenate([mine, other], dim), jnp.concatenate([other, mine], dim)
    )


def place():
    at_seq, at_batch = lax.axis_index("seq"), lax.axis_index("batch")
    return (at_seq % 8) // 2, at_seq % 2, at_batch // 2, at_batch % 2


def across(blocks, z):
    got = [lax.dynamic_index_in_dim(blocks, z, 0, keepdims=False)]
    for k in range(1, 4):
        got.append(swap(lax.dynamic_index_in_dim(blocks, z ^ k, 0, keepdims=False), "seq", 2 * k))
    got = jnp.stack(got)
    return jnp.stack([lax.dynamic_index_in_dim(got, z ^ k, 0, keepdims=False) for k in range(4)])


def gather_sequence(own):
    z, y, x, c = place()
    micro, rows, width = own.shape
    slots = paired(own, swap(own, "batch", 1), c, 0)
    blocks = across(part_of(slots, c, 2, 2), z)[:, None]
    both = paired(blocks, swap(blocks, "seq", 1), y, 1)
    return paired(both, swap(both, "batch", 1), c, 3).reshape(8 * rows, width)


def scatter_sequence(parts):
    z, y, x, c = place()
    width = parts.shape[1]
    blocks = parts.reshape(4, 2, -1, width)
    blocks = halved(blocks, c, 2, "batch", 1).astype(bf16)
    blocks = halved(blocks, y, 1, "seq", 1).astype(bf16)[:, 0]
    slots = across(blocks, z)
    other = swap(part_of(slots, 1 - c, 2, 0), "batch", 1)
    return paired(part_of(slots, c, 2, 0), other, c, 1).astype(f32)


def total_over_heads(value):
    value = value + swap(value, "batch", 1)
    return value + swap(value, "seq", 1)


def reduce_up(pair):
    z, y, x, c = place()
    kept = halved(pair, x, 0, "batch", 2)[0].astype(bf16)
    kept = halved(kept, z // 2, 0, "seq", 4).astype(bf16)
    kept = halved(kept, z % 2, 0, "seq", 2).astype(bf16)
    other = swap(part_of(kept, 1 - y, 2, 0), "seq", 1)
    return paired(part_of(kept, y, 2, 0), other, y, 1).astype(f32)


def reduce_square(stack):
    z, y, x, c = place()
    kept = halved(stack, x, 2, "batch", 2).astype(bf16)
    kept = halved(kept, z // 2, 1, "seq", 4).astype(bf16)
    kept = halved(kept, z % 2, 1, "seq", 2).astype(bf16)
    other = swap(part_of(kept, 1 - y, 2, 1), "seq", 1)
    kept = paired(part_of(kept, y, 2, 1)[None], other[None], y, 0)
    other = swap(part_of(kept, 1 - c, 2, 3), "batch", 1)
    return paired(part_of(kept, c, 2, 3), other, c, 0).astype(f32)


def reduce_down(value):
    z, y, x, c = place()
    kept = halved(value, x, 1, "batch", 2).astype(bf16)
    kept = (kept.astype(f32) + swap(kept, "seq", 4).astype(f32)).astype(bf16)
    kept = kept.astype(f32) + swap(kept, "seq", 2).astype(f32)
    kept = jnp.where(z == 2 * c + y, kept, 0.0).astype(bf16)
    kept = halved(kept, y, 0, "seq", 1).astype(bf16)
    return halved(kept, c, 1, "batch", 1)


def over_ranges(value, count):
    size = lax.axis_size("seq")
    groups = [[first + 8 * k for k in range(count)] for first in range(8)]
    return lax.all_gather(value, "seq", axis_index_groups=groups) if size > 8 else value[None]


def state_before(state, norm, level, total, ranges):
    index = lax.axis_index("seq") // 8
    summary = (state, norm[0], level[0, 0], total)
    everything = jax.tree.map(lambda part: over_ranges(part, ranges), summary)
    before = state_identity(summary)
    for k in range(ranges - 1):
        new = combine_states(before, jax.tree.map(lambda part: part[k], everything))
        before = jax.tree.map(lambda a, b: jnp.where(k < index, a, b), new, before)
    return (
        before[0],
        jnp.broadcast_to(before[1], norm.shape),
        jnp.broadcast_to(before[2], level.shape),
    )


def cotangent_after(d_state, d_norm, keep, ranges):
    index = lax.axis_index("seq") // 8
    own = (d_state, d_norm)
    everything = jax.tree.map(lambda part: over_ranges(part, ranges), own)
    keeps = over_ranges(keep, ranges)
    after = jax.tree.map(jnp.zeros_like, own)
    for k in range(ranges - 1, 0, -1):
        new = jax.tree.map(lambda a, b: a[k] + keeps[k] * b, everything, after)
        after = jax.tree.map(lambda a, b: jnp.where(k > index, a, b), new, after)
    return after


def reduce_blocks(at, g_m, g_z, squares, g_down, heads):
    count, batch_count = lax.axis_size("seq"), lax.axis_size("batch")
    width, size = g_m.shape
    inner = heads * size
    up = jnp.zeros((width, 2 * inner), f32)
    up = lax.dynamic_update_slice_in_dim(up, g_m.astype(f32), at * size, 1)
    up = lax.dynamic_update_slice_in_dim(up, g_z.astype(f32), inner + at * size, 1)
    down = lax.dynamic_update_slice_in_dim(
        jnp.zeros((inner, width), f32), g_down.astype(f32), at * size, 0
    )
    full = [up, down]
    for g in squares:
        full.append(
            lax.dynamic_update_slice_in_dim(
                jnp.zeros((heads, size, size), f32), g.astype(f32)[None], at, 0
            )
        )
    blocks = tuple(to_device_blocks(g, count, batch_count) for g in full)
    pieces = lax.psum_scatter(blocks, ("seq", "batch"), scatter_dimension=0, tiled=True)
    s_up, s_down, s_query, s_key, s_value = tuple(p[0] for p in pieces)
    return s_up, jnp.stack([s_query, s_key, s_value], 1), s_down


def head_device(
    tokens, ln_gain, w_up, conv_w, conv_b, w_query, w_key, w_value, gate_w, gate_b,
    out_gain, skip_gain, w_down, d_out,
):
    z, y, x, c = place()
    at = 2 * c + y
    ranges = lax.axis_size("seq") // 8
    direct = ranges == 1 and lax.axis_size("batch") == 4
    head = jnp.reshape(at, (1,)).astype(jnp.int32)
    heads, size, _ = w_query.shape
    inner = heads * size
    conv_row = conv_b.reshape(1, inner)
    out_row = out_gain.reshape(1, inner)
    skip_row = skip_gain.reshape(1, inner)

    row_f = tokens[:, 0].astype(f32)
    centre = row_f - jnp.mean(row_f, axis=-1, keepdims=True)
    rstd = lax.rsqrt(jnp.mean(centre * centre, axis=-1, keepdims=True) + norm_epsilon)
    row_hat = centre * rstd
    normed = gather_sequence((row_hat * ln_gain).astype(bf16))
    cot = gather_sequence(d_out[:, 0])

    gate_own = lax.dynamic_index_in_dim(
        gate_w.reshape(3, heads, size, 8), at, 1, keepdims=False
    ).transpose(0, 2, 1)
    high = lax.reduce_precision(gate_own, 8, 7)
    middle = lax.reduce_precision(gate_own - high, 8, 7)
    low = lax.reduce_precision(gate_own - high - middle, 8, 7)
    gate_parts = jnp.concatenate([high, middle, low, jnp.zeros_like(high)], 1).astype(bf16)
    gate_pairs = (
        jnp.concatenate([high, high, high, middle, middle, low], 1)
        .astype(bf16)
        .transpose(1, 0, 2)
        .reshape(48, 3 * size)
    )

    first = () if ranges == 1 else (shifted(normed[-16:], "seq", 8),)
    mix, conv, q, k, v, gate_z, gates, *halo = lift(
        head, normed, w_up, w_query, w_key, w_value, conv_w, conv_row, gate_parts, *first
    )
    gates = total_over_heads(gates)
    gates = jnp.concatenate(
        [
            lax.dynamic_slice_in_dim(gates, at, 1, 0),
            lax.dynamic_slice_in_dim(gates, heads + at, 1, 0)
            + lax.dynamic_slice_in_dim(gate_b, at, 1, 0)[:, None],
        ]
    )
    first = ()
    if ranges > 1:
        first = (
            jnp.zeros((size, size), f32),
            jnp.zeros((8, size), f32),
            jnp.full((8, 128), floor_value, f32),
        )
        *_, state, norm, level = cell_forward(
            head, gates, q, k, v, conv, gate_z, out_row, skip_row, w_down, *first
        )
        total = jnp.sum(jax.nn.log_sigmoid(gates[1]))
        first = state_before(state, norm, level, total, ranges)
    part, head_normed, states, norms, weights, cols, rows, *last = cell_forward(
        head, gates, q, k, v, conv, gate_z, out_row, skip_row, w_down, *first
    )
    block_rows = (row_f + scatter_sequence(part)).astype(bf16)
    after = ()
    if ranges > 1:
        after = (jnp.zeros((size, size), f32), jnp.zeros((8, size), f32))
        *_, d_state, d_norm = cell_backward(
            head, rows, q, k, v, conv, gate_z, head_normed, states, norms, weights, cols, cot,
            out_row, skip_row, w_down, *after,
        )
        keep = jnp.exp(total + first[2][0, 0] - last[2][0, 0])
        after = cotangent_after(d_state, d_norm, keep, ranges)
    dq, dk, dv, dskip, dz, d_rows, g_down, g_gain, *_ = cell_backward(
        head, rows, q, k, v, conv, gate_z, head_normed, states, norms, weights, cols, cot,
        out_row, skip_row, w_down, *after,
    )
    if direct:
        s_down = reduce_down(g_down)
    index = jnp.arange(2 * heads)[:, None]
    d_gate = jnp.where(index == at, d_rows[0:1], jnp.where(index == heads + at, d_rows[1:2], 0.0))
    d_gate = total_over_heads(d_gate)
    first = ()
    if ranges > 1:
        *_, later = lower(
            head, d_gate, dq, dk, dv, dskip, dz, mix, conv, q, k, v, normed,
            w_query, w_key, w_value, w_up, conv_w, conv_row, gate_pairs,
            halo[0], jnp.zeros((8, size), f32),
        )
        first = (halo[0], shifted(later, "seq", -8))
    d_part, g_q, g_k, g_v, g_m, g_z, small, *_ = lower(
        head, d_gate, dq, dk, dv, dskip, dz, mix, conv, q, k, v, normed,
        w_query, w_key, w_value, w_up, conv_w, conv_row, gate_pairs, *first,
    )
    d_normed = scatter_sequence(d_part)
    scaled = d_normed * ln_gain
    d_row = rstd * (
        scaled
        - jnp.mean(scaled, axis=-1, keepdims=True)
        - row_hat * jnp.mean(scaled * row_hat, axis=-1, keepdims=True)
    )
    grad_rows = (d_out[:, 0].astype(f32) + d_row).astype(bf16)
    g_ln = jnp.sum(d_normed * row_hat, axis=(0, 1))
    if direct:
        s_up = reduce_up(jnp.stack([g_m, g_z]))
        squares = reduce_square(jnp.stack([g_q, g_k, g_v]))
    else:
        s_up, squares, s_down = reduce_blocks(at, g_m, g_z, (g_q, g_k, g_v), g_down, heads)
    bias = jnp.broadcast_to(jnp.sum(d_rows[1]), (1, size))
    small = jnp.concatenate([small[:29], g_gain[0:2], bias])[None]
    small = jnp.where(jnp.arange(heads)[:, None, None] == at, small, 0.0)
    small, s_ln = lax.psum((small, g_ln), ("seq", "batch"))
    s_gate_w = small[:, :24].reshape(heads, 3, 8, size).transpose(1, 0, 3, 2).reshape(3 * inner, 8)
    s_conv_w = small[:, 24:28].transpose(1, 0, 2).reshape(4, inner)
    return (
        block_rows[:, None],
        grad_rows[:, None],
        s_ln,
        s_up,
        s_conv_w,
        small[:, 28].reshape(inner),
        squares[:, 0],
        squares[:, 1],
        squares[:, 2],
        s_gate_w,
        small[:, 31, 0],
        small[:, 29].reshape(inner),
        small[:, 30].reshape(inner),
        s_down,
    )


def solution(mesh):
    placed = (P(None, "batch", "seq", None),) + (P(),) * 12 + (P(None, "batch", "seq", None),)
    return jax.shard_map(
        head_device,
        mesh=mesh,
        in_specs=placed,
        out_specs=(
            P(None, "batch", "seq", None),
            P(None, "batch", "seq", None),
            P(),
            P("seq", "batch"),
            P(),
            P(),
            P(None, "seq", "batch"),
            P(None, "seq", "batch"),
            P(None, "seq", "batch"),
            P(),
            P(),
            P(),
            P(),
            P("seq", "batch"),
        ),
        check_vma=False,
    )
```

time: 3800 us -> 574 us (0.15)
  waiting for transfers between devices: 2650 us -> 310 us
  other arithmetic: 375 us -> 48.3 us
  matrix products: 265 us -> 0 us
  blocking collectives: 274 us -> 37.8 us
  local copies, waits for them, and re-layouts: 191 us -> 23.1 us
  Pallas kernels: 0 us -> 89.8 us
    all_gather x4 -> x0, waiting for transfers between devices: 2020 us -> none  [entering(): everything = jax.tree.map(lambda part: lax.all_gather(part, axis), x)]
    reduce_scatter x5 -> x0, waiting for transfers between devices: 630 us -> none  [per_device(): lax.psum_scatter(blocks, ('seq', 'batch'), scatter_dimension=0, tiled=True)]
    dot_general x66 -> x0, matrix products: 265 us -> none  [the longest x6 38.4 us: cell_state(): jnp.einsum('hsd,hse->hde', weighted, value_rows, precision=highest_mode)]
    select_n x96 -> x9, other arithmetic: 233 us -> 16.3 us  [the longest x7 15.4 us: paired(): jnp.where(bit == 0, jnp.concatenate([mine, other], dim), jnp.concatenate(...]
    ppermute x4 -> x42, waiting for transfers between devices: 2.04 us -> 193 us  [swap(): return lax.ppermute(value, axis, [(s, s ^ mask) for s in range(count)])]
    all_gather x4 -> x0, blocking collectives: 190 us -> none  [entering(): everything = jax.tree.map(lambda part: lax.all_gather(part, axis), x)]
    psum x1, waiting for transfers between devices: 0.01 us -> 118 us  [head_device(): small, s_ln = lax.psum((small, g_ln), ('seq', 'batch'))]
    pallas_call x0 -> x4, Pallas kernels: none -> 89.8 us  [run_kernel(): pl.pallas_call(body, grid_spec=pltpu.PrefetchScalarGridSpec(num_scalar_pr...]
  transfers between devices with their start and end apart: 14 -> 43, of which waited for: 10 -> 19; matrix products, arithmetic and copies ran while one was open for 13% -> 11% of each run, Pallas kernels for 0% -> 8%
where the time goes in v1:
time: 574 us; the launch traced here: 570 us
  waiting for transfers between devices  310 us (54%)
  Pallas kernels  89.8 us (16%)
  other arithmetic  48.3 us (8%)
  starting transfers between devices  45.1 us (8%)
  blocking collectives  37.8 us (7%)
  local copies, waits for them, and re-layouts  23.1 us (4%)
  between operations  15 us (3%)
    ppermute x42, waiting for transfers between devices, swap(): return lax.ppermute(value, axis, [(s, s ^ mask) for s in range(count)])  193 us
    psum x1, waiting for transfers between devices, head_device(): small, s_ln = lax.psum((small, g_ln), ('seq', 'batch'))  118 us
    pallas_call x4, Pallas kernels, run_kernel(): pl.pallas_call(body, grid_spec=pltpu.PrefetchScalarGridSpec(num_scalar_pr...  89.8 us
    ppermute x42, starting transfers between devices, swap(): return lax.ppermute(value, axis, [(s, s ^ mask) for s in range(count)])  45.1 us
    psum x1, blocking collectives, head_device(): small, s_ln = lax.psum((small, g_ln), ('seq', 'batch'))  37.8 us
    select_n x7, other arithmetic, paired(): jnp.where(bit == 0, jnp.concatenate([mine, other], dim), jnp.concatenate(...  15.4 us
  transfers between devices with their start and end apart: 43, of which 19 were waited for; matrix products, arithmetic and copies ran while one was open for 11% of the time, Pallas kernels for 8%

profile of v1, /device:TPU:24, one launch (start us, length us, event | category | flops | bytes accessed | tf_op | source)
XLA Modules:
  0.0 569.6 jit_solution(16054344703878142344)
XLA Ops:
  7.3 1.6 convert_reduce_fusion
  8.8 1.6 fusion.9
  11.5 2.3 collective-permute-done
  13.7 2.0 maximum_select_fusion.2
  16.4 1.9 collective-permute-start.2
  18.3 2.5 collective-permute-start.1
  20.8 6.7 %collective-permute-done.3 = bf16[256,512]{1,0:T(8,128)(2,1)S(1)} collective-permute-done((bf16[256,512]{1,0:T(8,128)(2,1)S(1)}, bf16[256,512]{1,0:T(8,128)(2,1)S(1)}, u32[]{:S(2)}, u32[]{:S(2)}) %collective-permute-start.3) | collective-permute-done | bytes 262176 | tf_op jit(solution)/shard_map/ppermute | solution.py:656
  27.5 14.0 %collective-permute-done.2 = bf16[256,512]{1,0:T(8,128)(2,1)S(1)} collective-permute-done((bf16[256,512]{1,0:T(8,128)(2,1)S(1)}, bf16[256,512]{1,0:T(8,128)(2,1)S(1)}, u32[]{:S(2)}, u32[]{:S(2)}) %collective-permute-start.2) | collective-permute-done | bytes 262176 | tf_op jit(solution)/shard_map/ppermute | solution.py:656
  41.8 1.6 collective-permute-start.4
  43.4 1.9 maximum_select_fusion.4
  47.3 3.0 collective-permute-start.15
  50.4 6.8 %collective-permute-done.17 = bf16[256,512]{1,0:T(8,128)(2,1)S(1)} collective-permute-done((bf16[256,512]{1,0:T(8,128)(2,1)S(1)}, bf16[256,512]{1,0:T(8,128)(2,1)S(1)}, u32[]{:S(2)}, u32[]{:S(2)}) %collective-permute-start.17) | collective-permute-done | bytes 262176 | tf_op jit(solution)/shard_map/ppermute | solution.py:656
  57.1 11.0 %collective-permute-done.16 = bf16[256,512]{1,0:T(8,128)(2,1)} collective-permute-done((bf16[256,512]{1,0:T(8,128)(2,1)S(1)}, bf16[256,512]{1,0:T(8,128)(2,1)}, u32[]{:S(2)}, u32[]{:S(2)}) %collective-permute-start.16) | collective-permute-done | bytes 262176 | tf_op jit(solution)/shard_map/ppermute | solution.py:656
  71.0 2.0 maximum_select_fusion.3
  73.9 20.5 %collective-permute-done.18 = bf16[4,1,256,512]{3,2,0,1:T(8,128)(2,1)} collective-permute-done((bf16[4,1,256,512]{3,2,0,1:T(8,128)(2,1)}, bf16[4,1,256,512]{3,2,0,1:T(8,128)(2,1)}, u32[]{:S(2)}, u32[]{:S(2)}) %collective-permute-start.18) | collective-permute-done | bytes 1048608 | tf_op jit(solution)/shard_map/ppermute | solution.py:656
  94.4 3.9 maximum_select_fusion.5
  100.0 1.7 copy.44
  101.7 2.9 maximum_select_fusion.normed
  104.6 14.1 %lift.1 = (bf16[2048,512]{1,0:T(8,128)(2,1)}, bf16[2048,512]{1,0:T(8,128)(2,1)}, bf16[2048,512]{1,0:T(8,128)(2,1)}, bf16[2048,512]{1,0:T(8,128)(2,1)}, bf16[2048...) custom-call(s32[1]{0:T(128)} %bitcast.head_ref, bf16[2048,1024]{1,0:T(8,128)(2,1)} %maximum_select_fusion.normed, ...), custom_call_target="tpu_custom_call" | custom-call | flops 7516192768 | bytes 25165824 | tf_op jit(solution)/shard_map/lift/pallas_call | solution.py:453
  119.3 1.7 copy.46
  121.0 1.8 copy.47
  123.4 2.7 maximum_select_fusion.1.cot_ref
  128.5 16.6 %cell_forward.1 = (bf16[2048,1024]{1,0:T(8,128)(2,1)}, f32[2048,512]{1,0:T(8,128)}, bf16[8,512,512]{2,1,0:T(8,128)(2,1)}, f32[8,8,512]{2,1,0:T(8,128)}, bf16[204...) custom-call(s32[1]{0:T(128)} %bitcast.head_ref, f32[2,2048]{1,0:T(2,128)} %pad_maximum_fusion.7.gates, ...), custom_call_target="tpu_custom_call" | custom-call | flops 5368709120 | bytes 29360128 | tf_op jit(solution)/shard_map/cell_forward/pallas_call | solution.py:453
  145.0 26.4 %cell_backward.1 = (f32[2048,512]{1,0:T(8,128)}, f32[2048,512]{1,0:T(8,128)}, f32[2048,512]{1,0:T(8,128)}, f32[2048,512]{1,0:T(8,128)}, bf16[2048,512]{1,0:T(8,1...) custom-call(s32[1]{0:T(128)} %bitcast.head_ref, f32[8,2048]{1,0:T(8,128)} %get-tuple-element.50.rows_ref, ...), custom_call_target="tpu_custom_call" | custom-call | flops 10737418240 | bytes 46137344 | tf_op jit(solution)/shard_map/cell_backward/pallas_call | solution.py:453
  180.9 32.8 %lower.1 = (bf16[2048,1024]{1,0:T(8,128)(2,1)}, bf16[512,512]{1,0:T(8,128)(2,1)}, bf16[512,512]{1,0:T(8,128)(2,1)}, bf16[512,512]{1,0:T(8,128)(2,1)}, bf16[1024,...) custom-call(s32[1]{0:T(128)} %bitcast.head_ref, f32[8,2048]{1,0:T(8,128)} %fusion.27.d_gate, ...), custom_call_target="tpu_custom_call" | custom-call | flops 15032385536 | bytes 50331648 | tf_op jit(solution)/shard_map/lower/pallas_call | solution.py:453
  213.7 1.6 pad_maximum_fusion
  218.7 2.6 fusion.17
  221.8 3.1 constant_dynamic-slice_fusion.19
  224.9 117.5 %all-reduce.2.cloned.1.call-done = f32[4,32,512]{2,0,1:T(4,128)} async-done(((f32[4,32,512]{2,0,1:T(4,128)}), f32[4,32,512]{2,0,1:T(4,128)}) %all-reduce.2.cloned.1.call-update) | async-done | bytes 262160 | tf_op jit(solution)/shard_map/psum | solution.py:910
  344.6 1.6 collective-permute-start.38
  351.8 26.0 %collective-permute-done.38 = bf16[512,512]{1,0:T(8,128)(2,1)S(1)} collective-permute-done((bf16[512,512]{1,0:T(8,128)(2,1)S(1)}, bf16[512,512]{1,0:T(8,128)(2,1)S(1)}, u32[]{:S(2)}, u32[]{:S(2)}) %collective-permute-start.38) | collective-permute-done | bytes 524320 | tf_op jit(solution)/shard_map/ppermute | solution.py:656
  378.0 7.9 %collective-permute-done.33 = bf16[3,256,256]{2,1,0:T(8,128)(2,1)S(1)} collective-permute-done((bf16[3,256,256]{2,1,0:T(8,128)(2,1)S(1)}, bf16[3,256,256]{2,1,0:T(8,128)(2,1)S(1)}, u32[]{:S(2)}, u32[]{:S(2)}) %collective-permute-start.33) | collective-permute-done | bytes 393248 | tf_op jit(solution)/shard_map/ppermute | solution.py:656
  386.1 1.8 add_convert_fusion.2
  387.9 2.7 collective-permute-start.29
  390.6 15.5 %collective-permute-done.34 = bf16[3,128,256]{2,1,0:T(8,128)(2,1)S(1)} collective-permute-done((bf16[3,128,256]{2,1,0:T(8,128)(2,1)S(1)}, bf16[3,128,256]{2,1,0:T(8,128)(2,1)S(1)}, u32[]{:S(2)}, u32[]{:S(2)}) %collective-permute-start.34) | collective-permute-done | bytes 196640 | tf_op jit(solution)/shard_map/ppermute | solution.py:656
  408.5 3.2 collective-permute-done.35
  411.8 1.8 collective-permute-done.29
  414.7 1.9 collective-permute-done.40
  416.8 2.7 add_convert_fusion
  421.1 2.6 add_convert_fusion.1
  426.8 43.7 %collective-permute-done.31 = bf16[128,512]{1,0:T(8,128)(2,1)S(1)} collective-permute-done((bf16[128,512]{1,0:T(8,128)(2,1)S(1)}, bf16[128,512]{1,0:T(8,128)(2,1)S(1)}, u32[]{:S(2)}, u32[]{:S(2)}) %collective-permute-start.31) | collective-permute-done | bytes 131104 | tf_op jit(solution)/shard_map/ppermute | solution.py:656
  473.5 2.8 collective-permute-start.24
  478.4 4.7 collective-permute-done.26
  483.1 9.7 %collective-permute-start.10 = (bf16[128,1024]{1,0:T(8,128)(2,1)S(1)}, bf16[128,1024]{1,0:T(8,128)(2,1)S(1)}, u32[]{:S(2)}, u32[]{:S(2)}) collective-permute-start(bf16[128,1024]{1,0:T(8,128)(2,1)S(1)} %get-tuple-element.114), channel_id=1, source_target_pairs={{0,8},{4,12},{8,0},{12,4},{16,24},{20,28},{24,16},{28,20},{1,9},{5... | collective-permute-start | bytes 786440 | tf_op jit(solution)/shard_map/ppermute | solution.py:656
  492.8 16.0 %collective-permute-done.25 = bf16[128,1024]{1,0:T(8,128)(2,1)S(1)} collective-permute-done((bf16[128,1024]{1,0:T(8,128)(2,1)S(1)}, bf16[128,1024]{1,0:T(8,128)(2,1)S(1)}, u32[]{:S(2)}, u32[]{:S(2)}) %collective-permute-start.25) | collective-permute-done | bytes 262176 | tf_op jit(solution)/shard_map/ppermute | solution.py:656
  509.4 9.4 %collective-permute-done.11 = bf16[128,1024]{1,0:T(8,128)(2,1)S(1)} collective-permute-done((bf16[128,1024]{1,0:T(8,128)(2,1)S(1)}, bf16[128,1024]{1,0:T(8,128)(2,1)S(1)}, u32[]{:S(2)}, u32[]{:S(2)}) %collective-permute-start.11) | collective-permute-done | bytes 262176 | tf_op jit(solution)/shard_map/ppermute | solution.py:656
  521.3 37.8 %psum.14 = f32[1024]{0:T(1024)} all-reduce(f32[1024]{0:T(1024)S(1)} %get-tuple-element.72), channel_id=1, replica_groups=mesh['seq'=8,'batch'=4] {'seq','batch'}, use_global_device_ids=true, to_apply=%region_5.6 | all-reduce | flops 1024 | bytes 8192 | tf_op jit(solution)/shard_map/psum | solution.py:910
  559.0 3.7 fusion.16
  (186 shorter events, 50.8 us)
Async XLA Ops:
  7.2 335.3 %all-reduce.2.cloned.1.call-start = ((), (), s32[]{:S(2)}) async-start(), calls=%async_computation | async-start | bytes 524288 | tf_op jit(solution)/shard_map/psum | solution.py:910
  10.9 2.9 collective-permute-start
  11.0 32.4 %collective-permute-start.14 = (bf16[2,256,1024]{2,1,0:T(8,128)(2,1)S(1)}, bf16[2,256,1024]{2,1,0:T(8,128)(2,1)}, u32[]{:S(2)}, u32[]{:S(2)}) collective-permute-start(bf16[2,256,1024]{2,1,0:T(8,128)(2,1)S(1)} %bitcast.153), channel_id=1, source_target_pairs={{0,1},{1,0},{2,3},{3,2},{4,5},{5,4},{6,7},{7,6},{8,9},{9,8},{10,11... | collective-permute-start | bytes 3145736 | tf_op jit(solution)/shard_map/ppermute | solution.py:656
  16.3 11.2 %collective-permute-start.3 = (bf16[256,512]{1,0:T(8,128)(2,1)S(1)}, bf16[256,512]{1,0:T(8,128)(2,1)S(1)}, u32[]{:S(2)}, u32[]{:S(2)}) collective-permute-start(bf16[256,512]{1,0:T(8,128)(2,1)S(1)} %get-tuple-element.86), channel_id=1, source_target_pairs={{0,24},{4,28},{8,16},{12,20},{16,8},{20,12},{24,0},{28,4},{1,25},{... | collective-permute-start | bytes 786440 | tf_op jit(solution)/shard_map/ppermute | solution.py:656
  16.4 25.1 %collective-permute-start.2 = (bf16[256,512]{1,0:T(8,128)(2,1)S(1)}, bf16[256,512]{1,0:T(8,128)(2,1)S(1)}, u32[]{:S(2)}, u32[]{:S(2)}) collective-permute-start(bf16[256,512]{1,0:T(8,128)(2,1)S(1)} %get-tuple-element.87), channel_id=1, source_target_pairs={{0,16},{4,20},{8,24},{12,28},{16,0},{20,4},{24,8},{28,12},{1,17},{... | collective-permute-start | bytes 786440 | tf_op jit(solution)/shard_map/ppermute | solution.py:656
  18.3 23.2 %collective-permute-start.1 = (bf16[256,512]{1,0:T(8,128)(2,1)S(1)}, bf16[256,512]{1,0:T(8,128)(2,1)S(1)}, u32[]{:S(2)}, u32[]{:S(2)}) collective-permute-start(bf16[256,512]{1,0:T(8,128)(2,1)S(1)} %get-tuple-element.88), channel_id=1, source_target_pairs={{0,8},{4,12},{8,0},{12,4},{16,24},{20,28},{24,16},{28,20},{1,9},{5... | collective-permute-start | bytes 786440 | tf_op jit(solution)/shard_map/ppermute | solution.py:656
  41.8 29.2 %collective-permute-start.4 = (bf16[4,1,256,512]{3,2,0,1:T(8,128)(2,1)S(1)}, bf16[4,1,256,512]{3,2,0,1:T(8,128)(2,1)}, u32[]{:S(2)}, u32[]{:S(2)}) collective-permute-start(bf16[4,1,256,512]{3,2,0,1:T(8,128)(2,1)S(1)} %maximum_bitcast_fusion), channel_id=1, source_target_pairs={{0,4},{4,0},{8,12},{12,8},{16,20},{20,16},{24,28},{28,24},{1,5},{5... | collective-permute-start | bytes 3145736 | tf_op jit(solution)/shard_map/ppermute | solution.py:656
  45.9 11.2 %collective-permute-start.17 = (bf16[256,512]{1,0:T(8,128)(2,1)S(1)}, bf16[256,512]{1,0:T(8,128)(2,1)S(1)}, u32[]{:S(2)}, u32[]{:S(2)}) collective-permute-start(bf16[256,512]{1,0:T(8,128)(2,1)S(1)} %get-tuple-element.82), channel_id=1, source_target_pairs={{0,24},{4,28},{8,16},{12,20},{16,8},{20,12},{24,0},{28,4},{1,25},{... | collective-permute-start | bytes 786440 | tf_op jit(solution)/shard_map/ppermute | solution.py:656
  47.3 20.8 %collective-permute-start.16 = (bf16[256,512]{1,0:T(8,128)(2,1)S(1)}, bf16[256,512]{1,0:T(8,128)(2,1)}, u32[]{:S(2)}, u32[]{:S(2)}) collective-permute-start(bf16[256,512]{1,0:T(8,128)(2,1)S(1)} %get-tuple-element.83), channel_id=1, source_target_pairs={{0,16},{4,20},{8,24},{12,28},{16,0},{20,4},{24,8},{28,12},{1,17},{... | collective-permute-start | bytes 786440 | tf_op jit(solution)/shard_map/ppermute | solution.py:656
  47.3 20.8 %collective-permute-start.15 = (bf16[256,512]{1,0:T(8,128)(2,1)S(1)}, bf16[256,512]{1,0:T(8,128)(2,1)}, u32[]{:S(2)}, u32[]{:S(2)}) collective-permute-start(bf16[256,512]{1,0:T(8,128)(2,1)S(1)} %get-tuple-element.84), channel_id=1, source_target_pairs={{0,8},{4,12},{8,0},{12,4},{16,24},{20,28},{24,16},{28,20},{1,9},{5... | collective-permute-start | bytes 786440 | tf_op jit(solution)/shard_map/ppermute | solution.py:656
  70.5 23.9 %collective-permute-start.18 = (bf16[4,1,256,512]{3,2,0,1:T(8,128)(2,1)}, bf16[4,1,256,512]{3,2,0,1:T(8,128)(2,1)}, u32[]{:S(2)}, u32[]{:S(2)}) collective-permute-start(bf16[4,1,256,512]{3,2,0,1:T(8,128)(2,1)} %maximum_bitcast_fusion.1), channel_id=1, source_target_pairs={{0,4},{4,0},{8,12},{12,8},{16,20},{20,16},{24,28},{28,24},{1,5},{5... | collective-permute-start | bytes 3145736 | tf_op jit(solution)/shard_map/ppermute | solution.py:656
  73.0 27.0 %collective-permute-start.5 = (bf16[4,2,256,512]{3,2,0,1:T(8,128)(2,1)S(1)}, bf16[4,2,256,512]{3,2,0,1:T(8,128)(2,1)}, u32[]{:S(2)}, u32[]{:S(2)}) collective-permute-start(bf16[4,2,256,512]{3,2,0,1:T(8,128)(2,1)S(1)} %maximum_select_fusion.3), channel_id=1, source_target_pairs={{0,1},{1,0},{2,3},{3,2},{4,5},{5,4},{6,7},{7,6},{8,9},{9,8},{10,11... | collective-permute-start | bytes 6291464 | tf_op jit(solution)/shard_map/ppermute | solution.py:656
  98.3 22.7 %collective-permute-start.19 = (bf16[4,2,256,512]{3,2,0,1:T(8,128)(2,1)}, bf16[4,2,256,512]{3,2,0,1:T(8,128)(2,1)}, u32[]{:S(2)}, u32[]{:S(2)}) collective-permute-start(bf16[4,2,256,512]{3,2,0,1:T(8,128)(2,1)} %maximum_select_fusion.5), channel_id=1, source_target_pairs={{0,1},{1,0},{2,3},{3,2},{4,5},{5,4},{6,7},{7,6},{8,9},{9,8},{10,11... | collective-permute-start | bytes 6291464 | tf_op jit(solution)/shard_map/ppermute | solution.py:656
  118.7 4.1 collective-permute-start.6
  122.8 4.3 collective-permute-start.7
  145.0 28.1 %copy-start.1 = (bf16[2048,1024]{1,0:T(8,128)(2,1)S(1)}, bf16[2048,1024]{1,0:T(8,128)(2,1)}, u32[]{:S(2)}) copy-start(bf16[2048,1024]{1,0:T(8,128)(2,1)} %get-tuple-element.49) | copy-start | bytes 12582916
  173.0 2.7 collective-permute-start.20
  174.6 246.5 %collective-permute-start.8 = (bf16[4,2,128,1024]{3,2,1,0:T(8,128)(2,1)}, bf16[4,2,128,1024]{3,2,1,0:T(8,128)(2,1)}, u32[]{:S(2)}, u32[]{:S(2)}) collective-permute-start(bf16[4,2,128,1024]{3,2,1,0:T(8,128)(2,1)} %constant_dynamic-slice_fusion.31), channel_id=1, source_target_pairs={{0,1},{1,0},{2,3},{3,2},{4,5},{5,4},{6,7},{7,6},{8,9},{9,8},{10,11... | collective-permute-start | bytes 6291464 | tf_op jit(solution)/shard_map/ppermute | solution.py:656
  175.9 4.3 collective-permute-start.21
  177.3 166.0 %collective-permute-start.37 = (bf16[512,512]{1,0:T(8,128)(2,1)}, bf16[512,512]{1,0:T(8,128)(2,1)}, u32[]{:S(2)}, u32[]{:S(2)}) collective-permute-start(bf16[512,512]{1,0:T(8,128)(2,1)} %constant_dynamic-slice_fusion.2), channel_id=1, source_target_pairs={{0,2},{1,3},{2,0},{3,1},{4,6},{5,7},{6,4},{7,5},{8,10},{9,11},{10,... | collective-permute-start | bytes 1572872 | tf_op jit(solution)/shard_map/ppermute | solution.py:656
  216.3 129.9 %collective-permute-start.32 = (bf16[3,512,256]{2,1,0:T(8,128)(2,1)}, bf16[3,512,256]{2,1,0:T(8,128)(2,1)S(1)}, u32[]{:S(2)}, u32[]{:S(2)}) collective-permute-start(bf16[3,512,256]{2,1,0:T(8,128)(2,1)} %constant_dynamic-slice_fusion.8), channel_id=1, source_target_pairs={{0,2},{1,3},{2,0},{3,1},{4,6},{5,7},{6,4},{7,5},{8,10},{9,11},{10,... | collective-permute-start | bytes 2359304 | tf_op jit(solution)/shard_map/ppermute | solution.py:656
  221.3 164.8 %collective-permute-start.28 = (bf16[1,1024,512]{2,1,0:T(8,128)(2,1)}, bf16[1,1024,512]{2,1,0:T(8,128)(2,1)}, u32[]{:S(2)}, u32[]{:S(2)}) collective-permute-start(bf16[1,1024,512]{2,1,0:T(8,128)(2,1)} %fusion.17), channel_id=1, source_target_pairs={{0,2},{1,3},{2,0},{3,1},{4,6},{5,7},{6,4},{7,5},{8,10},{9,11},{10,... | collective-permute-start | bytes 3145736 | tf_op jit(solution)/shard_map/ppermute | solution.py:656
  224.9 191.8 %collective-permute-start.22 = (bf16[4,2,128,1024]{3,2,1,0:T(8,128)(2,1)}, bf16[4,2,128,1024]{3,2,1,0:T(8,128)(2,1)}, u32[]{:S(2)}, u32[]{:S(2)}) collective-permute-start(bf16[4,2,128,1024]{3,2,1,0:T(8,128)(2,1)} %constant_dynamic-slice_fusion.19), channel_id=1, source_target_pairs={{0,1},{1,0},{2,3},{3,2},{4,5},{5,4},{6,7},{7,6},{8,9},{9,8},{10,11... | collective-permute-start | bytes 6291464 | tf_op jit(solution)/shard_map/ppermute | solution.py:656
  344.6 5.1 slice-start
  344.6 33.1 %collective-permute-start.38 = (bf16[512,512]{1,0:T(8,128)(2,1)S(1)}, bf16[512,512]{1,0:T(8,128)(2,1)S(1)}, u32[]{:S(2)}, u32[]{:S(2)}) collective-permute-start(bf16[512,512]{1,0:T(8,128)(2,1)S(1)} %add_convert_fusion.7), channel_id=1, source_target_pairs={{0,16},{4,20},{8,24},{12,28},{16,0},{20,4},{24,8},{28,12},{1,17},{... | collective-permute-start | bytes 1572872 | tf_op jit(solution)/shard_map/ppermute | solution.py:656
  346.4 39.6 %copy-start.4 = (bf16[1024,512]{1,0:T(8,128)(2,1)S(1)}, bf16[1024,512]{1,0:T(8,128)(2,1)}, u32[]{:S(2)}) copy-start(bf16[1024,512]{1,0:T(8,128)(2,1)} %get-tuple-element.64) | copy-start | bytes 3145732
  346.5 39.6 %copy-start.5 = (bf16[1024,512]{1,0:T(8,128)(2,1)S(1)}, bf16[1024,512]{1,0:T(8,128)(2,1)}, u32[]{:S(2)}) copy-start(bf16[1024,512]{1,0:T(8,128)(2,1)} %get-tuple-element.65) | copy-start | bytes 3145732
  346.5 39.4 %collective-permute-start.33 = (bf16[3,256,256]{2,1,0:T(8,128)(2,1)S(1)}, bf16[3,256,256]{2,1,0:T(8,128)(2,1)S(1)}, u32[]{:S(2)}, u32[]{:S(2)}) collective-permute-start(bf16[3,256,256]{2,1,0:T(8,128)(2,1)S(1)} %constant_dynamic-slice_fusion.7), channel_id=1, source_target_pairs={{0,16},{4,20},{8,24},{12,28},{16,0},{20,4},{24,8},{28,12},{1,17},{... | collective-permute-start | bytes 1179656 | tf_op jit(solution)/shard_map/ppermute | solution.py:656
  377.9 29.8 %collective-permute-start.39 = (bf16[512,512]{1,0:T(8,128)(2,1)S(1)}, bf16[512,512]{1,0:T(8,128)(2,1)S(1)}, u32[]{:S(2)}, u32[]{:S(2)}) collective-permute-start(bf16[512,512]{1,0:T(8,128)(2,1)S(1)} %add_convert_fusion.6), channel_id=1, source_target_pairs={{0,8},{4,12},{8,0},{12,4},{16,24},{20,28},{24,16},{28,20},{1,9},{5... | collective-permute-start | bytes 1572872 | tf_op jit(solution)/shard_map/ppermute | solution.py:656
  386.0 20.1 %collective-permute-start.34 = (bf16[3,128,256]{2,1,0:T(8,128)(2,1)S(1)}, bf16[3,128,256]{2,1,0:T(8,128)(2,1)S(1)}, u32[]{:S(2)}, u32[]{:S(2)}) collective-permute-start(bf16[3,128,256]{2,1,0:T(8,128)(2,1)S(1)} %constant_dynamic-slice_fusion.6), channel_id=1, source_target_pairs={{0,8},{4,12},{8,0},{12,4},{16,24},{20,28},{24,16},{28,20},{1,9},{5... | collective-permute-start | bytes 589832 | tf_op jit(solution)/shard_map/ppermute | solution.py:656
  387.9 25.7 %collective-permute-start.29 = (bf16[512,512]{1,0:T(8,128)(2,1)S(1)}, bf16[512,512]{1,0:T(8,128)(2,1)S(1)}, u32[]{:S(2)}, u32[]{:S(2)}) collective-permute-start(bf16[512,512]{1,0:T(8,128)(2,1)S(1)} %dynamic-slice_bitcast_fusion), channel_id=1, source_target_pairs={{0,16},{4,20},{8,24},{12,28},{16,0},{20,4},{24,8},{28,12},{1,17},{... | collective-permute-start | bytes 1572872 | tf_op jit(solution)/shard_map/ppermute | solution.py:656
  406.2 5.5 collective-permute-start.35
  407.9 8.7 %collective-permute-start.40 = (bf16[256,512]{1,0:T(8,128)(2,1)S(1)}, bf16[256,512]{1,0:T(8,128)(2,1)S(1)}, u32[]{:S(2)}, u32[]{:S(2)}) collective-permute-start(bf16[256,512]{1,0:T(8,128)(2,1)S(1)} %constant_dynamic-slice_fusion.1), channel_id=1, source_target_pairs={{0,4},{4,0},{8,12},{12,8},{16,20},{20,16},{24,28},{28,24},{1,5},{5... | collective-permute-start | bytes 786440 | tf_op jit(solution)/shard_map/ppermute | solution.py:656
  411.8 2.1 collective-permute-start.36
  413.8 10.6 %collective-permute-start.30 = (bf16[256,512]{1,0:T(8,128)(2,1)S(1)}, bf16[256,512]{1,0:T(8,128)(2,1)S(1)}, u32[]{:S(2)}, u32[]{:S(2)}) collective-permute-start(bf16[256,512]{1,0:T(8,128)(2,1)S(1)} %constant_dynamic-slice_fusion.11), channel_id=1, source_target_pairs={{0,8},{4,12},{8,0},{12,4},{16,24},{20,28},{24,16},{28,20},{1,9},{5... | collective-permute-start | bytes 786440 | tf_op jit(solution)/shard_map/ppermute | solution.py:656
  416.7 9.4 %collective-permute-start.41 = (bf16[256,256]{1,0:T(8,128)(2,1)S(1)}, bf16[256,256]{1,0:T(8,128)(2,1)S(1)}, u32[]{:S(2)}, u32[]{:S(2)}) collective-permute-start(bf16[256,256]{1,0:T(8,128)(2,1)S(1)} %constant_dynamic-slice_fusion), channel_id=1, source_target_pairs={{0,1},{1,0},{2,3},{3,2},{4,5},{5,4},{6,7},{7,6},{8,9},{9,8},{10,11... | collective-permute-start | bytes 393224 | tf_op jit(solution)/shard_map/ppermute | solution.py:656
  419.6 51.8 %collective-permute-start.23 = (bf16[4,1,128,1024]{3,2,1,0:T(8,128)(2,1)S(1)}, bf16[4,1,128,1024]{3,2,1,0:T(8,128)(2,1)S(1)}, u32[]{:S(2)}, u32[]{:S(2)}) collective-permute-start(bf16[4,1,128,1024]{3,2,1,0:T(8,128)(2,1)S(1)} %constant_dynamic-slice_fusion.18), channel_id=1, source_target_pairs={{0,4},{4,0},{8,12},{12,8},{16,20},{20,16},{24,28},{28,24},{1,5},{5... | collective-permute-start | bytes 3145736 | tf_op jit(solution)/shard_map/ppermute | solution.py:656
  423.8 52.5 %collective-permute-start.9 = (bf16[4,1,128,1024]{3,2,1,0:T(8,128)(2,1)S(1)}, bf16[4,1,128,1024]{3,2,1,0:T(8,128)(2,1)S(1)}, u32[]{:S(2)}, u32[]{:S(2)}) collective-permute-start(bf16[4,1,128,1024]{3,2,1,0:T(8,128)(2,1)S(1)} %constant_dynamic-slice_fusion.30), channel_id=1, source_target_pairs={{0,4},{4,0},{8,12},{12,8},{16,20},{20,16},{24,28},{28,24},{1,5},{5... | collective-permute-start | bytes 3145736 | tf_op jit(solution)/shard_map/ppermute | solution.py:656
  424.5 45.9 %collective-permute-start.31 = (bf16[128,512]{1,0:T(8,128)(2,1)S(1)}, bf16[128,512]{1,0:T(8,128)(2,1)S(1)}, u32[]{:S(2)}, u32[]{:S(2)}) collective-permute-start(bf16[128,512]{1,0:T(8,128)(2,1)S(1)} %get-tuple-element.126), channel_id=1, source_target_pairs={{0,4},{4,0},{8,12},{12,8},{16,20},{20,16},{24,28},{28,24},{1,5},{5... | collective-permute-start | bytes 393224 | tf_op jit(solution)/shard_map/ppermute | solution.py:656
  471.9 11.2 %collective-permute-start.26 = (bf16[128,1024]{1,0:T(8,128)(2,1)S(1)}, bf16[128,1024]{1,0:T(8,128)(2,1)S(1)}, u32[]{:S(2)}, u32[]{:S(2)}) collective-permute-start(bf16[128,1024]{1,0:T(8,128)(2,1)S(1)} %get-tuple-element.98), channel_id=1, source_target_pairs={{0,24},{4,28},{8,16},{12,20},{16,8},{20,12},{24,0},{28,4},{1,25},{... | collective-permute-start | bytes 786440 | tf_op jit(solution)/shard_map/ppermute | solution.py:656
  473.0 35.8 %collective-permute-start.25 = (bf16[128,1024]{1,0:T(8,128)(2,1)S(1)}, bf16[128,1024]{1,0:T(8,128)(2,1)S(1)}, u32[]{:S(2)}, u32[]{:S(2)}) collective-permute-start(bf16[128,1024]{1,0:T(8,128)(2,1)S(1)} %get-tuple-element.99), channel_id=1, source_target_pairs={{0,16},{4,20},{8,24},{12,28},{16,0},{20,4},{24,8},{28,12},{1,17},{... | collective-permute-start | bytes 786440 | tf_op jit(solution)/shard_map/ppermute | solution.py:656
  473.5 35.3 %collective-permute-start.24 = (bf16[128,1024]{1,0:T(8,128)(2,1)S(1)}, bf16[128,1024]{1,0:T(8,128)(2,1)S(1)}, u32[]{:S(2)}, u32[]{:S(2)}) collective-permute-start(bf16[128,1024]{1,0:T(8,128)(2,1)S(1)} %get-tuple-element.100), channel_id=1, source_target_pairs={{0,8},{4,12},{8,0},{12,4},{16,24},{20,28},{24,16},{28,20},{1,9},{5... | collective-permute-start | bytes 786440 | tf_op jit(solution)/shard_map/ppermute | solution.py:656
  476.8 32.5 %collective-permute-start.12 = (bf16[128,1024]{1,0:T(8,128)(2,1)S(1)}, bf16[128,1024]{1,0:T(8,128)(2,1)S(1)}, u32[]{:S(2)}, u32[]{:S(2)}) collective-permute-start(bf16[128,1024]{1,0:T(8,128)(2,1)S(1)} %get-tuple-element.112), channel_id=1, source_target_pairs={{0,24},{4,28},{8,16},{12,20},{16,8},{20,12},{24,0},{28,4},{1,25},{... | collective-permute-start | bytes 786440 | tf_op jit(solution)/shard_map/ppermute | solution.py:656
  478.0 40.7 %collective-permute-start.11 = (bf16[128,1024]{1,0:T(8,128)(2,1)S(1)}, bf16[128,1024]{1,0:T(8,128)(2,1)S(1)}, u32[]{:S(2)}, u32[]{:S(2)}) collective-permute-start(bf16[128,1024]{1,0:T(8,128)(2,1)S(1)} %get-tuple-element.113), channel_id=1, source_target_pairs={{0,16},{4,20},{8,24},{12,28},{16,0},{20,4},{24,8},{28,12},{1,17},{... | collective-permute-start | bytes 786440 | tf_op jit(solution)/shard_map/ppermute | solution.py:656
  483.1 35.7 %collective-permute-start.10 = (bf16[128,1024]{1,0:T(8,128)(2,1)S(1)}, bf16[128,1024]{1,0:T(8,128)(2,1)S(1)}, u32[]{:S(2)}, u32[]{:S(2)}) collective-permute-start(bf16[128,1024]{1,0:T(8,128)(2,1)S(1)} %get-tuple-element.114), channel_id=1, source_target_pairs={{0,8},{4,12},{8,0},{12,4},{16,24},{20,28},{24,16},{28,20},{1,9},{5... | collective-permute-start | bytes 786440 | tf_op jit(solution)/shard_map/ppermute | solution.py:656
  509.3 10.9 %collective-permute-start.27 = (bf16[2,128,1024]{2,1,0:T(8,128)(2,1)S(1)}, bf16[2,128,1024]{2,1,0:T(8,128)(2,1)S(1)}, u32[]{:S(2)}, u32[]{:S(2)}) collective-permute-start(bf16[2,128,1024]{2,1,0:T(8,128)(2,1)S(1)} %get-tuple-element.92), channel_id=1, source_target_pairs={{0,1},{1,0},{2,3},{3,2},{4,5},{5,4},{6,7},{7,6},{8,9},{9,8},{10,11... | collective-permute-start | bytes 1572872 | tf_op jit(solution)/shard_map/ppermute | solution.py:656
  519.1 39.9 %copy-start.9 = (bf16[2,1,256,1024]{3,2,1,0:T(8,128)(2,1)S(1)}, bf16[2,1,256,1024]{3,2,1,0:T(8,128)(2,1)}, u32[]{:S(2)}) copy-start(bf16[2,1,256,1024]{3,2,1,0:T(8,128)(2,1)} %param.27) | copy-start | bytes 3145732
  520.1 38.9 %collective-permute-start.13 = (bf16[2,128,1024]{2,1,0:T(8,128)(2,1)}, bf16[2,128,1024]{2,1,0:T(8,128)(2,1)}, u32[]{:S(2)}, u32[]{:S(2)}) collective-permute-start(bf16[2,128,1024]{2,1,0:T(8,128)(2,1)} %get-tuple-element.106), channel_id=1, source_target_pairs={{0,1},{1,0},{2,3},{3,2},{4,5},{5,4},{6,7},{7,6},{8,9},{9,8},{10,11... | collective-permute-start | bytes 1572872 | tf_op jit(solution)/shard_map/ppermute | solution.py:656
  (13 other events, 45.1 us)
Sparse Core Ops, SparseCore 0:
  218.8 123.6 all-reduce.1

commit v2 on v1

--- a/solution.py
+++ b/solution.py
@@ -362,26 +362,30 @@
     )
     d_log = d_log + keep * held
     sub = lax.broadcasted_iota(jnp.int32, (8, length), 0)
-    gate_out[...] = jnp.where(sub == 0, d_in, d_log * rows_ref[1:2, :])
+    d_pre = d_log * rows_ref[1:2, :]
+    gate_out[...] = jnp.where(sub == 0, d_in, d_pre)
+    g_gain[2:3, :] += jnp.broadcast_to(jnp.sum(d_pre, axis=1, keepdims=True), (1, head_size))
 
     @pl.when(pl.program_id(0) == pl.num_programs(0) - 1)
     def _():
         if chained:
             final[0][...] = d_state[...]
             final[1][...] = d_norm[...]
-        g_down_out[...] = g_down[...].astype(bf16)
+        half = g_down.shape[1] // 2
+        g_down_out[0] = g_down[:, :half].astype(bf16)
+        g_down_out[1] = g_down[:, half:].astype(bf16)
         g_gain_out[...] = g_gain[...]
 
 
 def lower_kernel(
     chained, head_ref, d_gate, dq_ref, dk_ref, dv_ref, dskip_ref, dz_ref, mix_ref, mix_before, conv_ref,
-    q_ref, k_ref, v_ref, normed, w_q, w_k, w_v, w_mix, w_gate, conv_w, conv_b, gate_w, *refs
+    q_ref, k_ref, v_ref, normed, w_q, w_k, w_v, w_mix, w_gate, conv_w, conv_b, gate_w, g_gain, *refs
 ):
     if chained:
         first_halo, first_later, *refs = refs
-        later_out = refs.pop(7)
-    part_out, gq_out, gk_out, gv_out, gm_out, gz_out, small_out = refs[:7]
-    g_q, g_k, g_v, g_m, g_z, g_small, later = refs[7:]
+        later_out = refs.pop(4)
+    part_out, square_out, up_out, small_out = refs[:4]
+    g_q, g_k, g_v, g_m, g_z, g_small, later = refs[4:]
     length = q_ref.shape[0]
     step = pl.program_id(0)
 
@@ -431,15 +435,21 @@
     rows = normed[...]
     g_m[...] += mm_tn(rows, d_mix)
     g_z[...] += mm_tn(rows, d_z)
-    part_out[...] = (mm_nt(d_mix, w_mix[...]) + mm_nt(d_z, w_gate[...])).astype(bf16)
+    d_normed = mm_nt(d_mix, w_mix[...]) + mm_nt(d_z, w_gate[...])
+    part_out[...] = d_normed.astype(bf16)
+    g_ln = jnp.sum(d_normed * rows.astype(f32), axis=0, keepdims=True)
+    g_small[32:33, :] += g_ln[:, :size]
+    g_small[33:34, :] += g_ln[:, size:]
 
     @pl.when(step == pl.num_programs(0) - 1)
     def _():
-        gq_out[...] = g_q[...].astype(bf16)
-        gk_out[...] = g_k[...].astype(bf16)
-        gv_out[...] = g_v[...].astype(bf16)
-        gm_out[...] = g_m[...].astype(bf16)
-        gz_out[...] = g_z[...].astype(bf16)
+        half = size // 2
+        for at, ref in enumerate((g_q, g_k, g_v)):
+            square_out[0, :, half * at : half * at + half] = ref[:, :half].astype(bf16)
+            square_out[1, :, half * at : half * at + half] = ref[:, half:].astype(bf16)
+        up_out[0] = g_m[...].astype(bf16)
+        up_out[1] = g_z[...].astype(bf16)
+        g_small[29:32, :] = g_gain[0:3, :]
         small_out[...] = g_small[...]
         if chained:
             later_out[...] = later[...]
@@ -577,14 +587,14 @@
         + [
             struct((tokens, size), bf16),
             struct((8, tokens), f32),
-            struct((size, width), bf16),
+            struct((2, size, width // 2), bf16),
             struct((8, size), f32),
         ]
         + carried,
         [by_row(size)] * 5
         + [
             pl.BlockSpec((8, length), lambda g, h: (0, end - g)),
-            whole((size, width)),
+            pl.BlockSpec((2, size, width // 2), lambda g, h: (0, 0, 0)),
             whole((8, size)),
         ]
         + carried_specs,
@@ -600,7 +610,7 @@
 
 def lower(
     head, d_gate, dq, dk, dv, dskip, dz, mix, conv, q, k, v, normed,
-    w_query, w_key, w_value, w_up, conv_w, conv_b, gate_pairs, *first,
+    w_query, w_key, w_value, w_up, conv_w, conv_b, gate_pairs, g_gain, *first,
 ):
     tokens, size = q.shape
     width = normed.shape[1]
@@ -615,7 +625,7 @@
     return run_kernel(
         partial(lower_kernel, chained), head, steps,
         (d_gate, dq, dk, dv, dskip, dz, mix, mix, conv, q, k, v, normed,
-         w_query, w_key, w_value, w_up, w_up, conv_w, conv_b, gate_pairs, *first),
+         w_query, w_key, w_value, w_up, w_up, conv_w, conv_b, gate_pairs, g_gain, *first),
         [pl.BlockSpec((8, length), lambda g, h: (0, end - g))]
         + [by_row(size)] * 6
         + [
@@ -632,23 +642,559 @@
             pl.BlockSpec((4, size), lambda g, h: (0, h[0])),
             pl.BlockSpec((1, size), lambda g, h: (0, h[0])),
             whole(gate_pairs.shape),
+            whole(g_gain.shape),
         ]
         + [whole(value.shape) for value in first],
         [struct((tokens, width), bf16)]
-        + [struct((size, size), bf16)] * 3
-        + [struct((width, size), bf16)] * 2
-        + [struct((32, size), f32)]
+        + [struct((2, size, 3 * size // 2), bf16), struct((2, width, size), bf16)]
+        + [struct((40, size), f32)]
         + [struct((8, size), f32)] * chained,
         [by_row(width)]
-        + [whole((size, size))] * 3
-        + [whole((width, size))] * 2
-        + [whole((32, size))]
+        + [
+            pl.BlockSpec((2, size, 3 * size // 2), lambda g, h: (0, 0, 0)),
+            pl.BlockSpec((2, width, size), lambda g, h: (0, 0, 0)),
+        ]
+        + [whole((40, size))]
         + [whole((8, size))] * chained,
         [pltpu.VMEM((size, size), f32)] * 3
         + [pltpu.VMEM((width, size), f32)] * 2
-        + [pltpu.VMEM((32, size), f32), pltpu.VMEM((8, size), f32)],
+        + [pltpu.VMEM((40, size), f32), pltpu.VMEM((8, size), f32)],
         "lower", 2 * tokens * size * (6 * size + 4 * width), 48 * 2**20,
     )
+MESH_ID = pl.DeviceIdType.MESH
+
+
+def where_am_i():
+    at_seq, at_batch = lax.axis_index("seq"), lax.axis_index("batch")
+    within = lax.rem(at_seq, 8)
+    first = at_seq - within
+    return first, within // 2, lax.rem(within, 2), at_batch // 2, lax.rem(at_batch, 2)
+
+
+def greet(others):
+    barrier = pltpu.get_barrier_semaphore()
+    for other in others:
+        pl.semaphore_signal(barrier, 1, device_id=other, device_id_type=MESH_ID)
+    pl.semaphore_wait(barrier, len(others))
+
+
+def remote(src, dst, sent, landed, device):
+    return pltpu.make_async_remote_copy(src, dst, sent, landed, device_id=device, device_id_type=MESH_ID)
+
+
+def normalize(rows):
+    centre = rows - jnp.mean(rows, axis=-1, keepdims=True)
+    rstd = lax.rsqrt(jnp.mean(centre * centre, axis=-1, keepdims=True) + norm_epsilon)
+    return centre * rstd, rstd
+
+
+def gather_kernel(
+    rows_ref, gain_ref, out_ref, staged, kept, z_sent, z_landed, y_sent, y_landed, c_sent, c_landed
+):
+    first, z, y, x, c = where_am_i()
+    parts = z_landed.shape[1]
+    block = rows_ref.shape[1]
+    size = block // parts
+
+    def device(zz, yy, cc):
+        return (first + 2 * zz + yy, 2 * x + cc)
+
+    def rows(zz, yy, part):
+        return out_ref.at[pl.ds(pl.multiple_of((2 * zz + yy) * block + part * size, size), size)]
+
+    others = [device(lax.rem(z + k, 4), y, c) for k in range(1, 4)]
+    greet(others + [device(z, 1 - y, c), device(z, y, 1 - c)])
+    enters = z // 2 == c
+
+    def to_column(m, part):
+        return remote(
+            staged.at[m, pl.ds(part * size, size)], rows(z, y, part),
+            z_sent.at[m, part], z_landed.at[z, part], device(2 * c + m, y, c),
+        )
+
+    def keep(m, part):
+        return pltpu.make_async_copy(
+            staged.at[m, pl.ds(part * size, size)], rows(z, y, part), kept.at[part]
+        )
+
+    def from_column(zz, part):
+        return remote(
+            rows(zz, y, part), rows(zz, y, part), z_sent.at[0, part], z_landed.at[zz, part],
+            device(zz, y, c),
+        )
+
+    def to_row(zz, k, part):
+        return remote(
+            rows(zz, y, part), rows(zz, y, part), y_sent.at[k, part], y_landed.at[zz, part],
+            device(z, 1 - y, c),
+        )
+
+    def from_row(zz, k, part):
+        return remote(
+            rows(zz, 1 - y, part), rows(zz, 1 - y, part), y_sent.at[k, part],
+            y_landed.at[zz, part], device(z, 1 - y, c),
+        )
+
+    def to_core(zz, yy, k, part):
+        return remote(
+            rows(zz, yy, part), rows(zz, yy, part), c_sent.at[k, part],
+            c_landed.at[2 * zz + yy, part], device(z, y, 1 - c),
+        )
+
+    for m in range(2):
+        staged[m] = (normalize(rows_ref[m].astype(f32))[0] * gain_ref[...]).astype(bf16)
+        away = 2 * c + m != z
+        for part in range(parts):
+            pl.when(away)(lambda m=m, part=part: to_column(m, part).start())
+            pl.when(jnp.logical_not(away))(lambda m=m, part=part: keep(m, part).start())
+
+    @pl.when(enters)
+    def _():
+        for k in range(4):
+            zz = lax.rem(z + k, 4)
+            for part in range(parts):
+                if k == 0:
+                    keep(0, part).wait()
+                else:
+                    from_column(zz, part).wait_recv()
+                to_row(zz, k, part).start()
+                to_core(zz, y, k, part).start()
+        for k in range(4):
+            zz = lax.rem(z + k, 4)
+            for part in range(parts):
+                from_row(zz, k, part).wait_recv()
+                to_core(zz, 1 - y, 4 + k, part).start()
+        for k in range(4):
+            zz = lax.rem(z + k, 4)
+            for part in range(parts):
+                to_row(zz, k, part).wait_send()
+                to_core(zz, y, k, part).wait_send()
+                to_core(zz, 1 - y, 4 + k, part).wait_send()
+
+    @pl.when(jnp.logical_not(enters))
+    def _():
+        for zz in range(4):
+            for yy in range(2):
+                for part in range(parts):
+                    to_core(zz, yy, 0, part).wait_recv()
+
+    for m in range(2):
+        for part in range(parts):
+            pl.when(2 * c + m != z)(lambda m=m, part=part: to_column(m, part).wait_send())
+
+
+def gather_normed(rows, gain):
+    micro, block, width = rows.shape
+    parts = 2
+    sems = [(parts,), (2, parts), (4, parts), (4, parts), (4, parts), (8, parts), (8, parts)]
+    return pl.pallas_call(
+        gather_kernel,
+        out_shape=struct((8 * block, width), bf16),
+        in_specs=[pl.BlockSpec(memory_space=pltpu.VMEM)] * 2,
+        out_specs=pl.BlockSpec(memory_space=pl.ANY),
+        scratch_shapes=[pltpu.VMEM((micro, block, width), bf16)]
+        + [pltpu.SemaphoreType.DMA(shape) for shape in sems],
+        compiler_params=pltpu.CompilerParams(
+            collective_id=0, has_side_effects=True, vmem_limit_bytes=32 * 2**20
+        ),
+        name="gather_normed",
+    )(rows, gain)
+
+
+def finish_kernel(
+    part_ref, up_ref, square_ref, down_ref, small_ref, rows_ref, cot_ref, gain_ref,
+    grad_out, up_out, query_out, key_out, value_out, down_out, small_out,
+    own, from_core, to_row, from_row, to_owner, owned,
+    up_x, up_sum, up_send, up_left, up_right, sq_x, sq_sum, sq_send, sq_left, sq_right,
+    dn_x, dn_sum, dn_send, dn_left, dn_right,
+    up_go, up_got, sq_go, sq_got, dn_go, dn_got, small_x, small_sum, small_z, small_all,
+    own_sem, c_sent, c_landed, y_sent, y_landed, o_sent, o_landed,
+    x_sent, x_landed, r_sent, r_landed, l_sent, l_landed,
+    up_sem, sq_sent, sq_landed, dn_sent, dn_landed, sx_sem, sz_sent, sz_landed, sh_sent, sh_landed,
+):
+    first, z, y, x, c = where_am_i()
+    head = 2 * c + y
+
+    def device(zz, yy, cc, xx=x):
+        return (first + 2 * zz + yy, 2 * xx + cc)
+
+    around = [lax.rem(z + k, 4) for k in range(1, 4)]
+    group = [(1 - y, c), (y, 1 - c), (1 - y, 1 - c)]
+    others = [device(z, yy, cc) for yy, cc in group] + [device(z, y, c, 1 - x)]
+    for zz in around:
+        others += [device(zz, yy, cc) for yy, cc in [(y, c)] + group]
+    greet(others)
+
+    sources = (up_ref, square_ref, down_ref)
+    from_x = (up_x, sq_x, dn_x)
+    totals = (up_sum, sq_sum, dn_sum)
+    sends = (up_send, sq_send, dn_send)
+    from_left = (up_left, sq_left, dn_left)
+    from_right = (up_right, sq_right, dn_right)
+    half = own.shape[1]
+
+    def to_x(p, zz):
+        size = totals[p].shape[1]
+        here = pl.ds(zz * size, size)
+        return remote(
+            sources[p].at[1 - x, here], from_x[p].at[here], x_sent.at[p, zz], x_landed.at[p, zz],
+            device(z, y, c, 1 - x),
+        )
+
+    def block(zz, yy, cc):
+        start = ((2 * zz + yy) * 2 + cc) * half
+        return part_ref.at[pl.ds(pl.multiple_of(start, half), half)]
+
+    def load(zz, yy, k):
+        return pltpu.make_async_copy(block(zz, yy, c), own.at[k], own_sem.at[k])
+
+    def to_c(zz, yy, k):
+        return remote(
+            block(zz, yy, 1 - c), from_core.at[2 * zz + yy], c_sent.at[k],
+            c_landed.at[2 * zz + yy], device(z, y, 1 - c),
+        )
+
+    def to_y(zz):
+        return remote(
+            to_row.at[zz], from_row.at[zz], y_sent.at[zz], y_landed.at[zz], device(z, 1 - y, c)
+        )
+
+    def to_o(zz):
+        return remote(
+            to_owner.at[zz], owned.at[lax.rem(z, 2), c], o_sent.at[zz],
+            o_landed.at[lax.rem(z, 2), c], device(zz, y, z // 2),
+        )
+
+    def right(p, zz):
+        return remote(
+            sends[p].at[zz], from_left[p].at[zz - 1], r_sent.at[p, zz - 1],
+            r_landed.at[p, zz - 1], device(lax.rem(z + 1, 4), y, c),
+        )
+
+    def left(p, zz):
+        return remote(
+            sends[p].at[zz], from_right[p].at[zz], l_sent.at[p, zz], l_landed.at[p, zz],
+            device(lax.rem(z + 3, 4), y, c),
+        )
+
+    order = (3, 0, 2, 1)
+    small_to_x = remote(
+        small_ref, small_x, sx_sem.at[0], sx_sem.at[1], device(z, y, c, 1 - x)
+    )
+    small_to_x.start()
+    for p in range(3):
+        for zz in order:
+            to_x(p, zz).start()
+    for yy, at in ((1 - y, 0), (y, 4)):
+        for zz in range(4):
+            to_c(zz, yy, at + zz).start()
+            load(zz, yy, at + zz).start()
+
+    def core_sum(zz, yy, k):
+        load(zz, yy, k).wait()
+        to_c(zz, yy, k).wait_recv()
+        return (own[k].astype(f32) + from_core[2 * zz + yy].astype(f32)).astype(bf16)
+
+    for zz in range(4):
+        to_row[zz] = core_sum(zz, 1 - y, zz)
+        to_y(zz).start()
+    for zz in range(4):
+        own[4 + zz] = core_sum(zz, y, 4 + zz)
+
+    def row_step(zz):
+        to_y(zz).wait_recv()
+        to_owner[zz] = (own[4 + zz].astype(f32) + from_row[zz].astype(f32)).astype(bf16)
+        stays = jnp.logical_and(z == zz, z // 2 == c)
+
+        @pl.when(stays)
+        def _():
+            owned[lax.rem(z, 2), c] = to_owner[zz]
+
+        pl.when(jnp.logical_not(stays))(lambda: to_o(zz).start())
+
+    def x_step(p, zz):
+        size = totals[p].shape[1]
+        here = pl.ds(zz * size, size)
+        to_x(p, zz).wait_recv()
+        totals[p][zz] = (
+            sources[p][x, here].astype(f32) + from_x[p][here].astype(f32)
+        ).astype(bf16)
+
+    def chain_step(p, zz):
+        if zz > 0:
+
+            @pl.when(z == 0)
+            def _():
+                sends[p][zz] = totals[p][zz]
+                right(p, zz).start()
+
+        if zz > 1:
+
+            @pl.when(jnp.logical_and(z > 0, z < zz))
+            def _():
+                right(p, zz).wait_recv()
+                sends[p][zz] = (
+                    totals[p][zz].astype(f32) + from_left[p][zz - 1].astype(f32)
+                ).astype(bf16)
+                right(p, zz).start()
+
+        if zz < 3:
+
+            @pl.when(z == 3)
+            def _():
+                sends[p][zz] = totals[p][zz]
+                left(p, zz).start()
+
+        if zz < 2:
+
+            @pl.when(jnp.logical_and(z < 3, z > zz))
+            def _():
+                left(p, zz).wait_recv()
+                sends[p][zz] = (
+                    totals[p][zz].astype(f32) + from_right[p][zz].astype(f32)
+                ).astype(bf16)
+                left(p, zz).start()
+
+    def end_step(p, use):
+        for zz in range(4):
+
+            @pl.when(z == zz)
+            def _():
+                value = totals[p][zz].astype(f32)
+                if zz > 0:
+                    right(p, zz).wait_recv()
+                    value = value + from_left[p][zz - 1].astype(f32)
+                if zz < 3:
+                    left(p, zz).wait_recv()
+                    value = value + from_right[p][zz].astype(f32)
+                use(value)
+
+    def passed(p):
+        for zz in range(4):
+            if zz > 0:
+                pl.when(z < zz)(lambda: right(p, zz).wait_send())
+            if zz < 3:
+                pl.when(z > zz)(lambda: left(p, zz).wait_send())
+
+    for p in range(3):
+        row_step(p)
+        for zz in order:
+            x_step(p, zz)
+            chain_step(p, zz)
+    row_step(3)
+
+    small_to_x.wait_recv()
+    small_sum[...] = small_ref[...] + small_x[...]
+    small_z[z] = small_sum[...]
+
+    def small_to_z(k):
+        return remote(
+            small_sum, small_z.at[z], sz_sent.at[k], sz_landed.at[z], device(around[k], y, c)
+        )
+
+    def small_from_z(k):
+        return remote(
+            small_sum, small_z.at[around[k]], sz_sent.at[k], sz_landed.at[around[k]],
+            device(around[k], y, c),
+        )
+
+    for k in range(3):
+        small_to_z(k).start()
+
+    rows = up_go.shape[0]
+    cols = up_go.shape[1]
+
+    def use_up(value):
+        mine = jnp.where(y == 0, value[:rows], value[rows:])
+        up_go[...] = jnp.where(y == 0, value[rows:], value[:rows]).astype(bf16)
+        for yy in range(2):
+
+            @pl.when(y == yy)
+            def _():
+                up_out[:, cols * yy : cols * yy + cols] = mine
+
+    end_step(0, use_up)
+    up_to_y = remote(up_go, up_got, up_sem.at[0], up_sem.at[1], device(z, 1 - y, c))
+    up_to_y.start()
+
+    for k in range(3):
+        small_from_z(k).wait_recv()
+    total = small_z[0]
+    for zz in range(1, 4):
+        total = total + small_z[zz]
+    small_all[head] = total
+
+    def to_group(k, src, dst, sent, landed):
+        yy, cc = group[k]
+        return remote(src, dst, sent.at[k], landed, device(z, yy, cc))
+
+    def small_to_head(k):
+        return to_group(k, small_all.at[head], small_all.at[head], sh_sent, sh_landed.at[head])
+
+    def small_from_head(k):
+        at = 2 * group[k][1] + group[k][0]
+        return to_group(k, small_all.at[at], small_all.at[at], sh_sent, sh_landed.at[at])
+
+    for k in range(3):
+        small_to_head(k).start()
+
+    tall, wide = sq_got.shape[1], sq_got.shape[2] // 3
+
+    def use_square(value):
+        for yy in range(2):
+            for cc in range(2):
+                for a in range(3):
+                    sq_go[yy, cc, :, wide * a : wide * a + wide] = value[
+                        tall * yy : tall * yy + tall,
+                        (2 * a + cc) * wide : (2 * a + cc) * wide + wide,
+                    ].astype(bf16)
+
+    end_step(1, use_square)
+    sq_got[head] = sq_go[y, c]
+
+    def square_to(k):
+        yy, cc = group[k]
+        return to_group(k, sq_go.at[yy, cc], sq_got.at[head], sq_sent, sq_landed.at[head])
+
+    def square_from(k):
+        at = 2 * group[k][1] + group[k][0]
+        return to_group(k, sq_go.at[0, 0], sq_got.at[at], sq_sent, sq_landed.at[at])
+
+    for k in range(3):
+        square_to(k).start()
+
+    span = dn_go.shape[2]
+
+    def use_down(value):
+        for cc in range(2):
+            dn_go[cc] = value[:, span * cc : span * cc + span].astype(bf16)
+
+    end_step(2, use_down)
+
+    def down_to(cc):
+        return remote(
+            dn_go.at[cc], dn_got.at[lax.rem(z, 2)], dn_sent.at[cc], dn_landed.at[lax.rem(z, 2)],
+            device(head, z // 2, cc),
+        )
+
+    def down_from(k):
+        return remote(
+            dn_go.at[0], dn_got.at[k], dn_sent.at[0], dn_landed.at[k],
+            device(2 * y + k, lax.rem(z, 2), z // 2),
+        )
+
+    home = jnp.logical_and(head == z, z // 2 == y)
+    for cc in range(2):
+        stays = jnp.logical_and(home, c == cc)
+
+        @pl.when(stays)
+        def _():
+            dn_got[lax.rem(z, 2)] = dn_go[cc]
+
+        pl.when(jnp.logical_not(stays))(lambda: down_to(cc).start())
+
+    for m in range(2):
+        for cc in range(2):
+            own_part = jnp.logical_and(2 * c + m == z, c == cc)
+            landed = remote(
+                to_owner.at[0], owned.at[m, cc], o_sent.at[0], o_landed.at[m, cc],
+                device(2 * c + m, y, cc),
+            )
+            pl.when(jnp.logical_not(own_part))(lambda landed=landed: landed.wait_recv())
+        for cc in range(2):
+            here = pl.ds(cc * half, half)
+            row_hat, rstd = normalize(rows_ref[m, here].astype(f32))
+            scaled = owned[m, cc].astype(f32) * gain_ref[...]
+            d_row = rstd * (
+                scaled
+                - jnp.mean(scaled, axis=-1, keepdims=True)
+                - row_hat * jnp.mean(scaled * row_hat, axis=-1, keepdims=True)
+            )
+            grad_out[m, here] = (cot_ref[m, here].astype(f32) + d_row).astype(bf16)
+
+    up_to_y.wait_recv()
+    for yy in range(2):
+
+        @pl.when(y == yy)
+        def _():
+            up_out[:, cols * (1 - yy) : cols * (1 - yy) + cols] = up_got[...].astype(f32)
+
+    for k in range(3):
+        small_from_head(k).wait_recv()
+    small_out[...] = small_all[...]
+    for k in range(3):
+        square_from(k).wait_recv()
+    for a, ref in enumerate((query_out, key_out, value_out)):
+        ref[...] = sq_got[:, :, wide * a : wide * a + wide].astype(f32)
+    for k in range(2):
+        mine = jnp.logical_and(home, jnp.logical_and(lax.rem(z, 2) == k, z // 2 == c))
+        pl.when(jnp.logical_not(mine))(lambda: down_from(k).wait_recv())
+        tall = dn_got.shape[1]
+        down_out[tall * k : tall * k + tall] = dn_got[k].astype(f32)
+
+    small_to_x.wait_send()
+    up_to_y.wait_send()
+    for p in range(3):
+        for zz in range(4):
+            to_x(p, zz).wait_send()
+        passed(p)
+    for yy, at in ((1 - y, 0), (y, 4)):
+        for zz in range(4):
+            to_c(zz, yy, at + zz).wait_send()
+    for zz in range(4):
+        to_y(zz).wait_send()
+        stays = jnp.logical_and(z == zz, z // 2 == c)
+        pl.when(jnp.logical_not(stays))(lambda: to_o(zz).wait_send())
+    for k in range(3):
+        small_to_z(k).wait_send()
+        small_to_head(k).wait_send()
+        square_to(k).wait_send()
+    for cc in range(2):
+        stays = jnp.logical_and(home, c == cc)
+        pl.when(jnp.logical_not(stays))(lambda: down_to(cc).wait_send())
+
+
+def finish(part, up, square, down, small, rows, cot, gain):
+    micro, block, width = rows.shape
+    half = block // 2
+    size = down.shape[1]
+    lines = small.shape[0]
+    scratch = [
+        ((8, half, width), bf16), ((8, half, width), bf16), ((4, half, width), bf16),
+        ((4, half, width), bf16), ((4, half, width), bf16), ((2, 2, half, width), bf16),
+    ]
+    for piece in (up, square, down):
+        _, tall, wide = piece.shape
+        scratch += [((tall, wide), bf16), ((4, tall // 4, wide), bf16), ((4, tall // 4, wide), bf16)]
+        scratch += [((3, tall // 4, wide), bf16)] * 2
+    scratch += [
+        ((width // 8, size), bf16), ((width // 8, size), bf16),
+        ((2, 2, size // 8, 3 * size // 4), bf16), ((4, size // 8, 3 * size // 4), bf16),
+        ((2, size // 4, width // 4), bf16), ((2, size // 4, width // 4), bf16),
+        ((lines, size), f32), ((lines, size), f32), ((4, lines, size), f32), ((4, lines, size), f32),
+    ]
+    sems = [
+        (8,), (8,), (8,), (4,), (4,), (4,), (2, 2), (3, 4), (3, 4), (3, 3), (3, 3), (3, 3), (3, 3),
+        (2,), (3,), (4,), (2,), (2,), (2,), (3,), (4,), (3,), (4,),
+    ]
+    vmem = pl.BlockSpec(memory_space=pltpu.VMEM)
+    square_shape = struct((4, size // 8, size // 4), f32)
+    return pl.pallas_call(
+        finish_kernel,
+        out_shape=[
+            struct(rows.shape, bf16), struct((width // 8, 2 * size), f32),
+            square_shape, square_shape, square_shape,
+            struct((size // 2, width // 4), f32), struct((4, lines, size), f32),
+        ],
+        in_specs=[pl.BlockSpec(memory_space=pl.ANY)] + [vmem] * 7,
+        out_specs=[vmem] * 7,
+        scratch_shapes=[pltpu.VMEM(shape, dtype) for shape, dtype in scratch]
+        + [pltpu.SemaphoreType.DMA(shape) for shape in sems],
+        compiler_params=pltpu.CompilerParams(
+            collective_id=1, has_side_effects=True, vmem_limit_bytes=vmem_bytes
+        ),
+        name="finish",
+    )(part, up, square, down, small, rows, cot, gain)
 
 
 def swap(value, axis, mask):
@@ -708,36 +1254,6 @@
 def total_over_heads(value):
     value = value + swap(value, "batch", 1)
     return value + swap(value, "seq", 1)
-
-
-def reduce_up(pair):
-    z, y, x, c = place()
-    kept = halved(pair, x, 0, "batch", 2)[0].astype(bf16)
-    kept = halved(kept, z // 2, 0, "seq", 4).astype(bf16)
-    kept = halved(kept, z % 2, 0, "seq", 2).astype(bf16)
-    other = swap(part_of(kept, 1 - y, 2, 0), "seq", 1)
-    return paired(part_of(kept, y, 2, 0), other, y, 1).astype(f32)
-
-
-def reduce_square(stack):
-    z, y, x, c = place()
-    kept = halved(stack, x, 2, "batch", 2).astype(bf16)
-    kept = halved(kept, z // 2, 1, "seq", 4).astype(bf16)
-    kept = halved(kept, z % 2, 1, "seq", 2).astype(bf16)
-    other = swap(part_of(kept, 1 - y, 2, 1), "seq", 1)
-    kept = paired(part_of(kept, y, 2, 1)[None], other[None], y, 0)
-    other = swap(part_of(kept, 1 - c, 2, 3), "batch", 1)
-    return paired(part_of(kept, c, 2, 3), other, c, 0).astype(f32)
-
-
-def reduce_down(value):
-    z, y, x, c = place()
-    kept = halved(value, x, 1, "batch", 2).astype(bf16)
-    kept = (kept.astype(f32) + swap(kept, "seq", 4).astype(f32)).astype(bf16)
-    kept = kept.astype(f32) + swap(kept, "seq", 2).astype(f32)
-    kept = jnp.where(z == 2 * c + y, kept, 0.0).astype(bf16)
-    kept = halved(kept, y, 0, "seq", 1).astype(bf16)
-    return halved(kept, c, 1, "batch", 1)
 
 
 def over_ranges(value, count):
@@ -773,9 +1289,16 @@
     return after
 
 
-def reduce_blocks(at, g_m, g_z, squares, g_down, heads):
+def reduce_blocks(at, up, square, down, heads):
     count, batch_count = lax.axis_size("seq"), lax.axis_size("batch")
+    g_m, g_z = up
     width, size = g_m.shape
+    half = size // 2
+    squares = [
+        jnp.concatenate([square[0, :, k : k + half], square[1, :, k : k + half]], 1)
+        for k in range(0, 3 * half, half)
+    ]
+    g_down = jnp.concatenate([down[0], down[1]], 1)
     inner = heads * size
     up = jnp.zeros((width, 2 * inner), f32)
     up = lax.dynamic_update_slice_in_dim(up, g_m.astype(f32), at * size, 1)
@@ -811,11 +1334,7 @@
     out_row = out_gain.reshape(1, inner)
     skip_row = skip_gain.reshape(1, inner)
 
-    row_f = tokens[:, 0].astype(f32)
-    centre = row_f - jnp.mean(row_f, axis=-1, keepdims=True)
-    rstd = lax.rsqrt(jnp.mean(centre * centre, axis=-1, keepdims=True) + norm_epsilon)
-    row_hat = centre * rstd
-    normed = gather_sequence((row_hat * ln_gain).astype(bf16))
+    normed = gather_normed(tokens[:, 0], ln_gain[None])
     cot = gather_sequence(d_out[:, 0])
 
     gate_own = lax.dynamic_index_in_dim(
@@ -859,7 +1378,7 @@
     part, head_normed, states, norms, weights, cols, rows, *last = cell_forward(
         head, gates, q, k, v, conv, gate_z, out_row, skip_row, w_down, *first
     )
-    block_rows = (row_f + scatter_sequence(part)).astype(bf16)
+    block_rows = (tokens[:, 0].astype(f32) + scatter_sequence(part)).astype(bf16)
     after = ()
     if ranges > 1:
         after = (jnp.zeros((size, size), f32), jnp.zeros((8, size), f32))
@@ -873,8 +1392,6 @@
         head, rows, q, k, v, conv, gate_z, head_normed, states, norms, weights, cols, cot,
         out_row, skip_row, w_down, *after,
     )
-    if direct:
-        s_down = reduce_down(g_down)
     index = jnp.arange(2 * heads)[:, None]
     d_gate = jnp.where(index == at, d_rows[0:1], jnp.where(index == heads + at, d_rows[1:2], 0.0))
     d_gate = total_over_heads(d_gate)
@@ -882,32 +1399,36 @@
     if ranges > 1:
         *_, later = lower(
             head, d_gate, dq, dk, dv, dskip, dz, mix, conv, q, k, v, normed,
-            w_query, w_key, w_value, w_up, conv_w, conv_row, gate_pairs,
+            w_query, w_key, w_value, w_up, conv_w, conv_row, gate_pairs, g_gain,
             halo[0], jnp.zeros((8, size), f32),
         )
         first = (halo[0], shifted(later, "seq", -8))
-    d_part, g_q, g_k, g_v, g_m, g_z, small, *_ = lower(
+    d_part, square, up, small, *_ = lower(
         head, d_gate, dq, dk, dv, dskip, dz, mix, conv, q, k, v, normed,
-        w_query, w_key, w_value, w_up, conv_w, conv_row, gate_pairs, *first,
-    )
-    d_normed = scatter_sequence(d_part)
-    scaled = d_normed * ln_gain
-    d_row = rstd * (
-        scaled
-        - jnp.mean(scaled, axis=-1, keepdims=True)
-        - row_hat * jnp.mean(scaled * row_hat, axis=-1, keepdims=True)
-    )
-    grad_rows = (d_out[:, 0].astype(f32) + d_row).astype(bf16)
-    g_ln = jnp.sum(d_normed * row_hat, axis=(0, 1))
+        w_query, w_key, w_value, w_up, conv_w, conv_row, gate_pairs, g_gain, *first,
+    )
     if direct:
-        s_up = reduce_up(jnp.stack([g_m, g_z]))
-        squares = reduce_square(jnp.stack([g_q, g_k, g_v]))
+        grad_rows, s_up, s_query, s_key, s_value, s_down, small = finish(
+            d_part, up, square, g_down, small, tokens[:, 0], d_out[:, 0], ln_gain[None]
+        )
     else:
-        s_up, squares, s_down = reduce_blocks(at, g_m, g_z, (g_q, g_k, g_v), g_down, heads)
-    bias = jnp.broadcast_to(jnp.sum(d_rows[1]), (1, size))
-    small = jnp.concatenate([small[:29], g_gain[0:2], bias])[None]
-    small = jnp.where(jnp.arange(heads)[:, None, None] == at, small, 0.0)
-    small, s_ln = lax.psum((small, g_ln), ("seq", "batch"))
+        d_normed = scatter_sequence(d_part)
+        row_f = tokens[:, 0].astype(f32)
+        centre = row_f - jnp.mean(row_f, axis=-1, keepdims=True)
+        rstd = lax.rsqrt(jnp.mean(centre * centre, axis=-1, keepdims=True) + norm_epsilon)
+        row_hat = centre * rstd
+        scaled = d_normed * ln_gain
+        d_row = rstd * (
+            scaled
+            - jnp.mean(scaled, axis=-1, keepdims=True)
+            - row_hat * jnp.mean(scaled * row_hat, axis=-1, keepdims=True)
+        )
+        grad_rows = (d_out[:, 0].astype(f32) + d_row).astype(bf16)
+        s_up, squares, s_down = reduce_blocks(at, up, square, g_down, heads)
+        s_query, s_key, s_value = squares[:, 0], squares[:, 1], squares[:, 2]
+        small = jnp.where(jnp.arange(heads)[:, None, None] == at, small, 0.0)
+        small = lax.psum(small, ("seq", "batch"))
+    s_ln = jnp.sum(small[:, 32:34], 0).reshape(-1) / ln_gain
     s_gate_w = small[:, :24].reshape(heads, 3, 8, size).transpose(1, 0, 3, 2).reshape(3 * inner, 8)
     s_conv_w = small[:, 24:28].transpose(1, 0, 2).reshape(4, inner)
     return (
@@ -917,9 +1438,9 @@
         s_up,
         s_conv_w,
         small[:, 28].reshape(inner),
-        squares[:, 0],
-        squares[:, 1],
-        squares[:, 2],
+        s_query,
+        s_key,
+        s_value,
         s_gate_w,
         small[:, 31, 0],
         small[:, 29].reshape(inner),

time: 574 us -> 394 us (0.69)
  waiting for transfers between devices: 310 us -> 80.4 us
  Pallas kernels: 89.8 us -> 246 us
  blocking collectives: 37.8 us -> 0 us
  starting transfers between devices: 45.1 us -> 17.4 us
  other arithmetic: 48.3 us -> 21.1 us
  between operations: 15 us -> 0.94 us
    pallas_call x0 -> x2, Pallas kernels: none -> 154 us  [the longest x1 115 us: finish(): pl.pallas_call(finish_kernel, out_shape=[struct(rows.shape, bf16), struct...]
    psum x1 -> x0, waiting for transfers between devices: 118 us -> none  [head_device(): small, s_ln = lax.psum((small, g_ln), ('seq', 'batch'))]
    ppermute x42 -> x16, waiting for transfers between devices: 193 us -> 80.4 us  [swap(): return lax.ppermute(value, axis, [(s, s ^ mask) for s in range(count)])]
    psum x1 -> x0, blocking collectives: 37.8 us -> none  [head_device(): small, s_ln = lax.psum((small, g_ln), ('seq', 'batch'))]
    ppermute x42 -> x16, starting transfers between devices: 45.1 us -> 17.4 us  [swap(): return lax.ppermute(value, axis, [(s, s ^ mask) for s in range(count)])]
    select_n x7 -> x3, other arithmetic: 15.4 us -> 6.33 us  [paired(): jnp.where(bit == 0, jnp.concatenate([mine, other], dim), jnp.concatenate(...]
    convert_element_type x14 -> x1, other arithmetic: 9.08 us -> 1.62 us  [head_device(): (tokens[:, 0].astype(f32) + scatter_sequence(part)).astype(bf16)]
    unnamed x43 -> x34, local copies, waits for them, and re-layouts: 3.3 us -> 9.64 us
  transfers between devices with their start and end apart: 43 -> 16, of which waited for: 19 -> 10; matrix products, arithmetic and copies ran while one was open for 11% -> 7% of each run, Pallas kernels for 8% -> 11%
where the time goes in v2:
time: 394 us; the launch traced here: 392 us
  Pallas kernels  246 us (62%)
  waiting for transfers between devices  80.4 us (20%)
  local copies, waits for them, and re-layouts  26.6 us (7%)
  other arithmetic  21.1 us (5%)
  starting transfers between devices  17.4 us (4%)
    pallas_call x1, Pallas kernels, finish(): pl.pallas_call(finish_kernel, out_shape=[struct(rows.shape, bf16), struct...  115 us
    pallas_call x4, Pallas kernels, run_kernel(): pl.pallas_call(body, grid_spec=pltpu.PrefetchScalarGridSpec(num_scalar_pr...  91.1 us
    ppermute x16, waiting for transfers between devices, swap(): return lax.ppermute(value, axis, [(s, s ^ mask) for s in range(count)])  80.4 us
    pallas_call x1, Pallas kernels, gather_normed(): pl.pallas_call(gather_kernel, out_shape=struct((8 * block, width), bf16),...  39.1 us
    ppermute x16, starting transfers between devices, swap(): return lax.ppermute(value, axis, [(s, s ^ mask) for s in range(count)])  17.4 us
    unnamed x34, local copies, waits for them, and re-layouts  9.64 us
  transfers between devices with their start and end apart: 16, of which 10 were waited for; matrix products, arithmetic and copies ran while one was open for 7% of the time, Pallas kernels for 11%

profile of v2, /device:TPU:24, one launch (start us, length us, event | category | flops | bytes accessed | tf_op | source)
XLA Modules:
  0.0 391.9 jit_solution(11646005230650229970)
XLA Ops:
  0.7 0.8 constant_dynamic-update-slice_fusion.5
  1.5 0.8 constant_dynamic-update-slice_fusion.2
  2.3 0.8 constant_dynamic-update-slice_fusion
  3.1 1.2 copy-done.1
  5.0 39.1 %gather_normed.1.normed = bf16[2048,1024]{1,0:T(8,128)(2,1)S(1)} custom-call(bf16[2,256,1024]{2,1,0:T(8,128)(2,1)S(1)} %bitcast.73, f32[1,1024]{1,0:T(1,128)S(1)} %bitcast.75), custom_call_target="tpu_custom_call" | custom-call | tf_op jit(solution)/shard_map/gather_normed/pallas_call | solution.py:790
  44.2 2.0 copy-done
  46.2 0.7 maximum_maximum_fusion.gate_w
  47.0 14.1 %lift.1 = (bf16[2048,512]{1,0:T(8,128)(2,1)}, bf16[2048,512]{1,0:T(8,128)(2,1)}, bf16[2048,512]{1,0:T(8,128)(2,1)}, bf16[2048,512]{1,0:T(8,128)(2,1)}, bf16[2048...) custom-call(s32[1]{0:T(128)} %bitcast.head_ref, bf16[2048,1024]{1,0:T(8,128)(2,1)} %copy-done, ...), custom_call_target="tpu_custom_call" | custom-call | flops 7516192768 | bytes 25165824 | tf_op jit(solution)/shard_map/lift/pallas_call | solution.py:463
  61.3 1.3 collective-permute-done
  62.6 0.8 add.130
  64.6 3.2 collective-permute-done.1
  69.1 16.6 %cell_forward.1 = (bf16[2048,1024]{1,0:T(8,128)(2,1)}, f32[2048,512]{1,0:T(8,128)}, bf16[8,512,512]{2,1,0:T(8,128)(2,1)}, f32[8,8,512]{2,1,0:T(8,128)}, bf16[204...) custom-call(s32[1]{0:T(128)} %bitcast.head_ref, f32[2,2048]{1,0:T(2,128)} %pad_maximum_fusion.3.gates, ...), custom_call_target="tpu_custom_call" | custom-call | flops 5368709120 | bytes 29360128 | tf_op jit(solution)/shard_map/cell_forward/pallas_call | solution.py:463
  85.7 3.2 constant_dynamic-slice_fusion.11
  89.7 2.2 collective-permute-start.11
  91.9 5.6 %collective-permute-start.10 = (bf16[256,512]{1,0:T(8,128)(2,1)S(1)}, bf16[256,512]{1,0:T(8,128)(2,1)S(1)}, u32[]{:S(2)}, u32[]{:S(2)}) collective-permute-start(bf16[256,512]{1,0:T(8,128)(2,1)S(1)} %get-tuple-element.116), channel_id=1, source_target_pairs={{0,16},{4,20},{8,24},{12,28},{16,0},{20,4},{24,8},{28,12},{1,17},{... | collective-permute-start | bytes 786440 | tf_op jit(solution)/shard_map/ppermute | solution.py:1202
  98.0 2.4 collective-permute-done.11
  100.4 16.7 %collective-permute-done.10 = bf16[256,512]{1,0:T(8,128)(2,1)S(1)} collective-permute-done((bf16[256,512]{1,0:T(8,128)(2,1)S(1)}, bf16[256,512]{1,0:T(8,128)(2,1)S(1)}, u32[]{:S(2)}, u32[]{:S(2)}) %collective-permute-start.10) | collective-permute-done | bytes 262176 | tf_op jit(solution)/shard_map/ppermute | solution.py:1202
  118.1 3.2 add_convert_fusion
  121.4 1.1 constant_dynamic-slice_fusion.10
  122.5 1.5 collective-permute-start.3
  124.0 19.7 %collective-permute-done.12 = bf16[4,1,256,512]{3,2,0,1:T(8,128)(2,1)} collective-permute-done((bf16[4,1,256,512]{3,2,0,1:T(8,128)(2,1)S(1)}, bf16[4,1,256,512]{3,2,0,1:T(8,128)(2,1)}, u32[]{:S(2)}, u32[]{:S(2)}) %collective-permute-start.12) | collective-permute-done | bytes 1048608 | tf_op jit(solution)/shard_map/ppermute | solution.py:1202
  143.7 3.3 maximum_select_fusion.2
  147.0 18.3 %collective-permute-done.3 = bf16[4,1,128,1024]{3,2,1,0:T(8,128)(2,1)} collective-permute-done((bf16[4,1,128,1024]{3,2,1,0:T(8,128)(2,1)}, bf16[4,1,128,1024]{3,2,1,0:T(8,128)(2,1)}, u32[]{:S(2)}, u32[]{:S(2)}) %collective-permute-start.3) | collective-permute-done | bytes 1048608 | tf_op jit(solution)/shard_map/ppermute | solution.py:1202
  165.3 1.6 add_convert_fusion.2
  167.1 2.2 collective-permute-start.6
  169.3 2.3 collective-permute-start.4
  171.5 1.7 copy.33
  173.3 5.0 %collective-permute-done.6 = bf16[128,1024]{1,0:T(8,128)(2,1)S(1)} collective-permute-done((bf16[128,1024]{1,0:T(8,128)(2,1)S(1)}, bf16[128,1024]{1,0:T(8,128)(2,1)S(1)}, u32[]{:S(2)}, u32[]{:S(2)}) %collective-permute-start.6) | collective-permute-done | bytes 262176 | tf_op jit(solution)/shard_map/ppermute | solution.py:1202
  178.3 11.9 %collective-permute-done.5 = bf16[128,1024]{1,0:T(8,128)(2,1)S(1)} collective-permute-done((bf16[128,1024]{1,0:T(8,128)(2,1)S(1)}, bf16[128,1024]{1,0:T(8,128)(2,1)S(1)}, u32[]{:S(2)}, u32[]{:S(2)}) %collective-permute-start.5) | collective-permute-done | bytes 262176 | tf_op jit(solution)/shard_map/ppermute | solution.py:1202
  190.7 1.7 copy.34
  192.4 2.7 maximum_select_fusion.cot_ref
  195.2 27.6 %cell_backward.1 = (f32[2048,512]{1,0:T(8,128)}, f32[2048,512]{1,0:T(8,128)}, f32[2048,512]{1,0:T(8,128)}, f32[2048,512]{1,0:T(8,128)}, bf16[2048,512]{1,0:T(8,1...) custom-call(s32[1]{0:T(128)} %bitcast.head_ref, ...), custom_call_target="tpu_custom_call" | custom-call | flops 10737418240 | bytes 46137344 | tf_op jit(solution)/shard_map/cell_backward/pallas_call | solution.py:463
  222.8 0.9 fusion.5
  225.3 1.1 collective-permute-start.15
  226.4 1.6 add_convert_fusion.1
  228.1 1.7 collective-permute-done.15
  229.7 0.7 fusion.6.d_gate
  230.4 32.8 %lower.1 = (bf16[2048,1024]{1,0:T(8,128)(2,1)}, bf16[2,512,768]{2,1,0:T(8,128)(2,1)}, bf16[2,1024,512]{2,1,0:T(8,128)(2,1)}, f32[40,512]{1,0:T(8,128)}) custom-call(s32[1]{0:T(128)} %bitcast.head_ref, f32[8,2048]{1,0:T(8,128)} %fusion.6.d_gate, f32[2048,512]{1,0:T(8,128)} %get-tuple-element.61.dq_ref, f32[2048,512]{1,0:T(8,128)} %get-tuple-element.62.dk_ref, ...), custom_call_target="tpu_custom_call" | custom-call | flops 15032385536 | bytes 50331648 | tf_op jit(solution)/shard_map/lower/pallas_call | solution.py:463
  263.3 115.3 %finish.1 = (bf16[2,256,1024]{2,1,0:T(8,128)(2,1)}, f32[128,1024]{1,0:T(8,128)}, f32[4,64,128]{2,1,0:T(8,128)}, f32[4,64,128]{2,1,0:T(8,128)}, f32[4,64,128]{2,1...) custom-call(bf16[2048,1024]{1,0:T(8,128)(2,1)} %get-tuple-element.68.part_ref, ...), custom_call_target="tpu_custom_call" | custom-call | tf_op jit(solution)/shard_map/finish/pallas_call | solution.py:1182
  378.6 0.9 slice_reduce_fusion
  379.5 1.5 slice.30
  381.0 1.6 fusion.4
  382.5 1.0 slice_bitcast_fusion
  383.5 1.4 slice_reduce_fusion.1
  385.5 0.7 copy.36
  386.2 2.3 copy.52
  388.5 0.8 copy.53
  391.2 0.7 copy.57
  (68 shorter events, 10.6 us)
Async XLA Ops:
  3.1 1.2 copy-start.1
  4.4 0.7 copy-start.3
  44.2 2.0 copy-start
  47.0 17.1 %copy-start.5 = (bf16[2,1,256,1024]{3,2,1,0:T(8,128)(2,1)S(1)}, bf16[2,1,256,1024]{3,2,1,0:T(8,128)(2,1)}, u32[]{:S(2)}) copy-start(bf16[2,1,256,1024]{3,2,1,0:T(8,128)(2,1)} %param.27) | copy-start | bytes 3145732
  47.0 17.1 %copy-start.11 = (f32[4]{0:T(128)S(1)}, f32[4]{0:T(128)}, u32[]{:S(2)}) copy-start(f32[4]{0:T(128)} %param.23) | copy-start | bytes 52
  61.1 1.5 collective-permute-start
  63.5 4.3 %collective-permute-start.1 = (f32[8,2048]{1,0:T(8,128)S(1)}, f32[8,2048]{1,0:T(8,128)S(1)}, u32[]{:S(2)}, u32[]{:S(2)}) collective-permute-start(f32[8,2048]{1,0:T(8,128)S(1)} %add.130), channel_id=1, source_target_pairs={{0,4},{4,0},{8,12},{12,8},{16,20},{20,16},{24,28},{28,24},{1,5},{5... | collective-permute-start | bytes 196616 | tf_op jit(solution)/shard_map/ppermute | solution.py:1202
  64.0 24.8 %collective-permute-start.8 = (bf16[2,256,1024]{2,1,0:T(8,128)(2,1)S(1)}, bf16[2,256,1024]{2,1,0:T(8,128)(2,1)S(1)}, u32[]{:S(2)}, u32[]{:S(2)}) collective-permute-start(bf16[2,256,1024]{2,1,0:T(8,128)(2,1)S(1)} %bitcast.79), channel_id=1, source_target_pairs={{0,1},{1,0},{2,3},{3,2},{4,5},{5,4},{6,7},{7,6},{8,9},{9,8},{10,11... | collective-permute-start | bytes 3145736 | tf_op jit(solution)/shard_map/ppermute | solution.py:1202
  88.8 29.3 %collective-permute-start.2 = (bf16[4,2,128,1024]{3,2,1,0:T(8,128)(2,1)}, bf16[4,2,128,1024]{3,2,1,0:T(8,128)(2,1)}, u32[]{:S(2)}, u32[]{:S(2)}) collective-permute-start(bf16[4,2,128,1024]{3,2,1,0:T(8,128)(2,1)} %constant_dynamic-slice_fusion.11), channel_id=1, source_target_pairs={{0,1},{1,0},{2,3},{3,2},{4,5},{5,4},{6,7},{7,6},{8,9},{9,8},{10,11... | collective-permute-start | bytes 6291464 | tf_op jit(solution)/shard_map/ppermute | solution.py:1202
  89.7 10.7 %collective-permute-start.11 = (bf16[256,512]{1,0:T(8,128)(2,1)S(1)}, bf16[256,512]{1,0:T(8,128)(2,1)S(1)}, u32[]{:S(2)}, u32[]{:S(2)}) collective-permute-start(bf16[256,512]{1,0:T(8,128)(2,1)S(1)} %get-tuple-element.115), channel_id=1, source_target_pairs={{0,24},{4,28},{8,16},{12,20},{16,8},{20,12},{24,0},{28,4},{1,25},{... | collective-permute-start | bytes 786440 | tf_op jit(solution)/shard_map/ppermute | solution.py:1202
  91.9 25.2 %collective-permute-start.10 = (bf16[256,512]{1,0:T(8,128)(2,1)S(1)}, bf16[256,512]{1,0:T(8,128)(2,1)S(1)}, u32[]{:S(2)}, u32[]{:S(2)}) collective-permute-start(bf16[256,512]{1,0:T(8,128)(2,1)S(1)} %get-tuple-element.116), channel_id=1, source_target_pairs={{0,16},{4,20},{8,24},{12,28},{16,0},{20,4},{24,8},{28,12},{1,17},{... | collective-permute-start | bytes 786440 | tf_op jit(solution)/shard_map/ppermute | solution.py:1202
  97.6 19.6 %collective-permute-start.9 = (bf16[256,512]{1,0:T(8,128)(2,1)S(1)}, bf16[256,512]{1,0:T(8,128)(2,1)S(1)}, u32[]{:S(2)}, u32[]{:S(2)}) collective-permute-start(bf16[256,512]{1,0:T(8,128)(2,1)S(1)} %get-tuple-element.117), channel_id=1, source_target_pairs={{0,8},{4,12},{8,0},{12,4},{16,24},{20,28},{24,16},{28,20},{1,9},{5... | collective-permute-start | bytes 786440 | tf_op jit(solution)/shard_map/ppermute | solution.py:1202
  117.5 26.2 %collective-permute-start.12 = (bf16[4,1,256,512]{3,2,0,1:T(8,128)(2,1)S(1)}, bf16[4,1,256,512]{3,2,0,1:T(8,128)(2,1)}, u32[]{:S(2)}, u32[]{:S(2)}) collective-permute-start(bf16[4,1,256,512]{3,2,0,1:T(8,128)(2,1)S(1)} %maximum_bitcast_fusion), channel_id=1, source_target_pairs={{0,4},{4,0},{8,12},{12,8},{16,20},{20,16},{24,28},{28,24},{1,5},{5... | collective-permute-start | bytes 3145736 | tf_op jit(solution)/shard_map/ppermute | solution.py:1202
  122.5 42.9 %collective-permute-start.3 = (bf16[4,1,128,1024]{3,2,1,0:T(8,128)(2,1)}, bf16[4,1,128,1024]{3,2,1,0:T(8,128)(2,1)}, u32[]{:S(2)}, u32[]{:S(2)}) collective-permute-start(bf16[4,1,128,1024]{3,2,1,0:T(8,128)(2,1)} %constant_dynamic-slice_fusion.10), channel_id=1, source_target_pairs={{0,4},{4,0},{8,12},{12,8},{16,20},{20,16},{24,28},{28,24},{1,5},{5... | collective-permute-start | bytes 3145736 | tf_op jit(solution)/shard_map/ppermute | solution.py:1202
  147.0 43.7 %collective-permute-start.13 = (bf16[4,2,256,512]{3,2,0,1:T(8,128)(2,1)}, bf16[4,2,256,512]{3,2,0,1:T(8,128)(2,1)}, u32[]{:S(2)}, u32[]{:S(2)}) collective-permute-start(bf16[4,2,256,512]{3,2,0,1:T(8,128)(2,1)} %maximum_select_fusion.2), channel_id=1, source_target_pairs={{0,1},{1,0},{2,3},{3,2},{4,5},{5,4},{6,7},{7,6},{8,9},{9,8},{10,11... | collective-permute-start | bytes 6291464 | tf_op jit(solution)/shard_map/ppermute | solution.py:1202
  167.1 11.2 %collective-permute-start.6 = (bf16[128,1024]{1,0:T(8,128)(2,1)S(1)}, bf16[128,1024]{1,0:T(8,128)(2,1)S(1)}, u32[]{:S(2)}, u32[]{:S(2)}) collective-permute-start(bf16[128,1024]{1,0:T(8,128)(2,1)S(1)} %get-tuple-element.129), channel_id=1, source_target_pairs={{0,24},{4,28},{8,16},{12,20},{16,8},{20,12},{24,0},{28,4},{1,25},{... | collective-permute-start | bytes 786440 | tf_op jit(solution)/shard_map/ppermute | solution.py:1202
  169.3 20.9 %collective-permute-start.5 = (bf16[128,1024]{1,0:T(8,128)(2,1)S(1)}, bf16[128,1024]{1,0:T(8,128)(2,1)S(1)}, u32[]{:S(2)}, u32[]{:S(2)}) collective-permute-start(bf16[128,1024]{1,0:T(8,128)(2,1)S(1)} %get-tuple-element.130), channel_id=1, source_target_pairs={{0,16},{4,20},{8,24},{12,28},{16,0},{20,4},{24,8},{28,12},{1,17},{... | collective-permute-start | bytes 786440 | tf_op jit(solution)/shard_map/ppermute | solution.py:1202
  169.3 20.9 %collective-permute-start.4 = (bf16[128,1024]{1,0:T(8,128)(2,1)S(1)}, bf16[128,1024]{1,0:T(8,128)(2,1)S(1)}, u32[]{:S(2)}, u32[]{:S(2)}) collective-permute-start(bf16[128,1024]{1,0:T(8,128)(2,1)S(1)} %get-tuple-element.131), channel_id=1, source_target_pairs={{0,8},{4,12},{8,0},{12,4},{16,24},{20,28},{24,16},{28,20},{1,9},{5... | collective-permute-start | bytes 786440 | tf_op jit(solution)/shard_map/ppermute | solution.py:1202
  190.6 35.8 %collective-permute-start.7 = (bf16[2,128,1024]{2,1,0:T(8,128)(2,1)S(1)}, bf16[2,128,1024]{2,1,0:T(8,128)(2,1)S(1)}, u32[]{:S(2)}, u32[]{:S(2)}) collective-permute-start(bf16[2,128,1024]{2,1,0:T(8,128)(2,1)S(1)} %get-tuple-element.123), channel_id=1, source_target_pairs={{0,1},{1,0},{2,3},{3,2},{4,5},{5,4},{6,7},{7,6},{8,9},{9,8},{10,11... | collective-permute-start | bytes 1572872 | tf_op jit(solution)/shard_map/ppermute | solution.py:1202
  195.2 31.3 %copy-start.2 = (bf16[2,1,256,1024]{3,2,1,0:T(8,128)(2,1)S(1)}, bf16[2,1,256,1024]{3,2,1,0:T(8,128)(2,1)}, u32[]{:S(2)}) copy-start(bf16[2,1,256,1024]{3,2,1,0:T(8,128)(2,1)} %param.14) | copy-start | bytes 3145732
  223.8 1.4 collective-permute-start.14
  225.3 4.4 %collective-permute-start.15 = (f32[8,2048]{1,0:T(8,128)S(1)}, f32[8,2048]{1,0:T(8,128)S(1)}, u32[]{:S(2)}, u32[]{:S(2)}) collective-permute-start(f32[8,2048]{1,0:T(8,128)S(1)} %fusion.2), channel_id=1, source_target_pairs={{0,4},{4,0},{8,12},{12,8},{16,20},{20,16},{24,28},{28,24},{1,5},{5... | collective-permute-start | bytes 196616 | tf_op jit(solution)/shard_map/ppermute | solution.py:1202
  263.2 121.7 %copy-start.4 = (f32[1024]{0:T(1024)S(1)}, f32[1024]{0:T(1024)}, u32[]{:S(2)}) copy-start(f32[1024]{0:T(1024)} %param.15) | copy-start | bytes 12292
  378.6 9.9 %copy-start.6 = (f32[128,1024]{1,0:T(8,128)S(1)}, f32[128,1024]{1,0:T(8,128)}, u32[]{:S(2)}) copy-start(f32[128,1024]{1,0:T(8,128)} %get-tuple-element.156) | copy-start | bytes 1572868
  378.6 10.7 %copy-start.10 = (f32[4,64,128]{2,1,0:T(8,128)S(1)}, f32[4,64,128]{2,1,0:T(8,128)}, u32[]{:S(2)}) copy-start(f32[4,64,128]{2,1,0:T(8,128)} %get-tuple-element.159) | copy-start | bytes 393220
  382.5 7.4 %copy-start.9 = (f32[4,64,128]{2,1,0:T(8,128)S(1)}, f32[4,64,128]{2,1,0:T(8,128)}, u32[]{:S(2)}) copy-start(f32[4,64,128]{2,1,0:T(8,128)} %get-tuple-element.160) | copy-start | bytes 393220
  383.5 7.1 %copy-start.8 = (f32[4,64,128]{2,1,0:T(8,128)S(1)}, f32[4,64,128]{2,1,0:T(8,128)}, u32[]{:S(2)}) copy-start(f32[4,64,128]{2,1,0:T(8,128)} %get-tuple-element.161) | copy-start | bytes 393220
  385.5 5.7 %copy-start.7 = (f32[256,256]{1,0:T(8,128)S(1)}, f32[256,256]{1,0:T(8,128)}, u32[]{:S(2)}) copy-start(f32[256,256]{1,0:T(8,128)} %get-tuple-element.166) | copy-start | bytes 786436

commit v3 on v2

--- a/solution.py
+++ b/solution.py
@@ -741,29 +741,36 @@
             c_landed.at[2 * zz + yy, part], device(z, y, 1 - c),
         )
 
-    for m in range(2):
-        staged[m] = (normalize(rows_ref[m].astype(f32))[0] * gain_ref[...]).astype(bf16)
-        away = 2 * c + m != z
-        for part in range(parts):
+    for part in range(parts):
+        here = pl.ds(part * size, size)
+        for m in range(2):
+            staged[m, here] = (
+                normalize(rows_ref[m, here].astype(f32))[0] * gain_ref[...]
+            ).astype(bf16)
+            away = 2 * c + m != z
             pl.when(away)(lambda m=m, part=part: to_column(m, part).start())
             pl.when(jnp.logical_not(away))(lambda m=m, part=part: keep(m, part).start())
 
     @pl.when(enters)
     def _():
-        for k in range(4):
-            zz = lax.rem(z + k, 4)
-            for part in range(parts):
+        for part in range(parts):
+            for k in range(4):
+                zz = lax.rem(z + k, 4)
                 if k == 0:
                     keep(0, part).wait()
                 else:
                     from_column(zz, part).wait_recv()
                 to_row(zz, k, part).start()
                 to_core(zz, y, k, part).start()
+            if part > 0:
+                for k in range(4):
+                    zz = lax.rem(z + k, 4)
+                    from_row(zz, k, part - 1).wait_recv()
+                    to_core(zz, 1 - y, 4 + k, part - 1).start()
         for k in range(4):
             zz = lax.rem(z + k, 4)
-            for part in range(parts):
-                from_row(zz, k, part).wait_recv()
-                to_core(zz, 1 - y, 4 + k, part).start()
+            from_row(zz, k, parts - 1).wait_recv()
+            to_core(zz, 1 - y, 4 + k, parts - 1).start()
         for k in range(4):
             zz = lax.rem(z + k, 4)
             for part in range(parts):
@@ -785,7 +792,7 @@
 
 def gather_normed(rows, gain):
     micro, block, width = rows.shape
-    parts = 2
+    parts = 4
     sems = [(parts,), (2, parts), (4, parts), (4, parts), (4, parts), (8, parts), (8, parts)]
     return pl.pallas_call(
         gather_kernel,
@@ -805,11 +812,11 @@
     part_ref, up_ref, square_ref, down_ref, small_ref, rows_ref, cot_ref, gain_ref,
     grad_out, up_out, query_out, key_out, value_out, down_out, small_out,
     own, from_core, to_row, from_row, to_owner, owned,
-    up_x, up_sum, up_send, up_left, up_right, sq_x, sq_sum, sq_send, sq_left, sq_right,
-    dn_x, dn_sum, dn_send, dn_left, dn_right,
+    up_x, up_sum, up_near, up_pair, up_far, up_end, sq_x, sq_sum, sq_near, sq_pair, sq_far, sq_end,
+    dn_x, dn_sum, dn_near, dn_pair, dn_far, dn_end,
     up_go, up_got, sq_go, sq_got, dn_go, dn_got, small_x, small_sum, small_z, small_all,
     own_sem, c_sent, c_landed, y_sent, y_landed, o_sent, o_landed,
-    x_sent, x_landed, r_sent, r_landed, l_sent, l_landed,
+    x_sent, x_landed, near_sent, near_landed, far_sent, far_landed,
     up_sem, sq_sent, sq_landed, dn_sent, dn_landed, sx_sem, sz_sent, sz_landed, sh_sent, sh_landed,
 ):
     first, z, y, x, c = where_am_i()
@@ -828,17 +835,38 @@
     sources = (up_ref, square_ref, down_ref)
     from_x = (up_x, sq_x, dn_x)
     totals = (up_sum, sq_sum, dn_sum)
-    sends = (up_send, sq_send, dn_send)
-    from_left = (up_left, sq_left, dn_left)
-    from_right = (up_right, sq_right, dn_right)
+    from_near = (up_near, sq_near, dn_near)
+    pairs = (up_pair, sq_pair, dn_pair)
+    from_far = (up_far, sq_far, dn_far)
+    ends = (up_end, sq_end, dn_end)
+    high, low = z // 2, lax.rem(z, 2)
+    cut = up_sum.shape[2] // 2
+    items = [(0, k, pl.ds(m * cut, cut)) for m in range(2) for k in range(2)]
+    items += [(p, k, slice(None)) for p in (2, 1) for k in range(2)]
+    count = len(items)
     half = own.shape[1]
 
-    def to_x(p, zz):
-        size = totals[p].shape[1]
-        here = pl.ds(zz * size, size)
+    def to_x(n):
+        p, k, lanes = items[n]
+        size = 2 * totals[p].shape[1]
+        here = (pl.ds(k * size, size), lanes)
         return remote(
-            sources[p].at[1 - x, here], from_x[p].at[here], x_sent.at[p, zz], x_landed.at[p, zz],
+            sources[p].at[(1 - x, *here)], from_x[p].at[here], x_sent.at[n], x_landed.at[n],
             device(z, y, c, 1 - x),
+        )
+
+    def to_near(n):
+        p, k, lanes = items[n]
+        return remote(
+            totals[p].at[2 * k + 1 - low, :, lanes], from_near[p].at[k, :, lanes],
+            near_sent.at[n], near_landed.at[n], device(z + 1 - 2 * low, y, c),
+        )
+
+    def to_far(n):
+        p, k, lanes = items[n]
+        return remote(
+            pairs[p].at[k, :, lanes], from_far[p].at[:, lanes], far_sent.at[n], far_landed.at[n],
+            device(z + 2 - 4 * high, y, c),
         )
 
     def block(zz, yy, cc):
@@ -865,26 +893,13 @@
             o_landed.at[lax.rem(z, 2), c], device(zz, y, z // 2),
         )
 
-    def right(p, zz):
-        return remote(
-            sends[p].at[zz], from_left[p].at[zz - 1], r_sent.at[p, zz - 1],
-            r_landed.at[p, zz - 1], device(lax.rem(z + 1, 4), y, c),
-        )
-
-    def left(p, zz):
-        return remote(
-            sends[p].at[zz], from_right[p].at[zz], l_sent.at[p, zz], l_landed.at[p, zz],
-            device(lax.rem(z + 3, 4), y, c),
-        )
-
-    order = (3, 0, 2, 1)
+    ahead = 2
     small_to_x = remote(
         small_ref, small_x, sx_sem.at[0], sx_sem.at[1], device(z, y, c, 1 - x)
     )
     small_to_x.start()
-    for p in range(3):
-        for zz in order:
-            to_x(p, zz).start()
+    for n in range(ahead):
+        to_x(n).start()
     for yy, at in ((1 - y, 0), (y, 4)):
         for zz in range(4):
             to_c(zz, yy, at + zz).start()
@@ -897,12 +912,15 @@
 
     for zz in range(4):
         to_row[zz] = core_sum(zz, 1 - y, zz)
-        to_y(zz).start()
+        if zz < ahead:
+            to_y(zz).start()
     for zz in range(4):
         own[4 + zz] = core_sum(zz, y, 4 + zz)
 
     def row_step(zz):
         to_y(zz).wait_recv()
+        if zz + ahead < 4:
+            to_y(zz + ahead).start()
         to_owner[zz] = (own[4 + zz].astype(f32) + from_row[zz].astype(f32)).astype(bf16)
         stays = jnp.logical_and(z == zz, z // 2 == c)
 
@@ -912,80 +930,34 @@
 
         pl.when(jnp.logical_not(stays))(lambda: to_o(zz).start())
 
-    def x_step(p, zz):
+    def x_step(n):
+        p, k, lanes = items[n]
         size = totals[p].shape[1]
-        here = pl.ds(zz * size, size)
-        to_x(p, zz).wait_recv()
-        totals[p][zz] = (
-            sources[p][x, here].astype(f32) + from_x[p][here].astype(f32)
+        to_x(n).wait_recv()
+        if n + ahead < count:
+            to_x(n + ahead).start()
+        for at in (2 * k, 2 * k + 1):
+            here = (pl.ds(at * size, size), lanes)
+            totals[p][at, :, lanes] = (
+                sources[p][(x, *here)].astype(f32) + from_x[p][here].astype(f32)
+            ).astype(bf16)
+        to_near(n).start()
+
+    def near_step(n):
+        p, k, lanes = items[n]
+        to_near(n).wait_recv()
+        pairs[p][k, :, lanes] = (
+            totals[p][2 * k + low, :, lanes].astype(f32) + from_near[p][k, :, lanes].astype(f32)
         ).astype(bf16)
-
-    def chain_step(p, zz):
-        if zz > 0:
-
-            @pl.when(z == 0)
-            def _():
-                sends[p][zz] = totals[p][zz]
-                right(p, zz).start()
-
-        if zz > 1:
-
-            @pl.when(jnp.logical_and(z > 0, z < zz))
-            def _():
-                right(p, zz).wait_recv()
-                sends[p][zz] = (
-                    totals[p][zz].astype(f32) + from_left[p][zz - 1].astype(f32)
-                ).astype(bf16)
-                right(p, zz).start()
-
-        if zz < 3:
-
-            @pl.when(z == 3)
-            def _():
-                sends[p][zz] = totals[p][zz]
-                left(p, zz).start()
-
-        if zz < 2:
-
-            @pl.when(jnp.logical_and(z < 3, z > zz))
-            def _():
-                left(p, zz).wait_recv()
-                sends[p][zz] = (
-                    totals[p][zz].astype(f32) + from_right[p][zz].astype(f32)
-                ).astype(bf16)
-                left(p, zz).start()
-
-    def end_step(p, use):
-        for zz in range(4):
-
-            @pl.when(z == zz)
-            def _():
-                value = totals[p][zz].astype(f32)
-                if zz > 0:
-                    right(p, zz).wait_recv()
-                    value = value + from_left[p][zz - 1].astype(f32)
-                if zz < 3:
-                    left(p, zz).wait_recv()
-                    value = value + from_right[p][zz].astype(f32)
-                use(value)
-
-    def passed(p):
-        for zz in range(4):
-            if zz > 0:
-                pl.when(z < zz)(lambda: right(p, zz).wait_send())
-            if zz < 3:
-                pl.when(z > zz)(lambda: left(p, zz).wait_send())
-
-    for p in range(3):
-        row_step(p)
-        for zz in order:
-            x_step(p, zz)
-            chain_step(p, zz)
-    row_step(3)
-
-    small_to_x.wait_recv()
-    small_sum[...] = small_ref[...] + small_x[...]
-    small_z[z] = small_sum[...]
+        pl.when(high != k)(lambda: to_far(n).start())
+
+    def far_step(n):
+        p, k, lanes = items[n]
+
+        @pl.when(high == k)
+        def _():
+            to_far(n).wait_recv()
+            ends[p][:, lanes] = pairs[p][k, :, lanes].astype(f32) + from_far[p][:, lanes].astype(f32)
 
     def small_to_z(k):
         return remote(
@@ -998,8 +970,41 @@
             device(around[k], y, c),
         )
 
-    for k in range(3):
-        small_to_z(k).start()
+    def to_group(k, src, dst, sent, landed):
+        yy, cc = group[k]
+        return remote(src, dst, sent.at[k], landed, device(z, yy, cc))
+
+    def small_to_head(k):
+        return to_group(k, small_all.at[head], small_all.at[head], sh_sent, sh_landed.at[head])
+
+    def small_from_head(k):
+        at = 2 * group[k][1] + group[k][0]
+        return to_group(k, small_all.at[at], small_all.at[at], sh_sent, sh_landed.at[at])
+
+    for n in range(count + 3):
+        if n < 4:
+            row_step(n)
+        if n < count:
+            x_step(n)
+        if 1 <= n <= count:
+            near_step(n - 1)
+        if n >= 3:
+            far_step(n - 3)
+        if n == 2:
+            small_to_x.wait_recv()
+            small_sum[...] = small_ref[...] + small_x[...]
+            small_z[z] = small_sum[...]
+            for k in range(3):
+                small_to_z(k).start()
+        if n == 5:
+            for k in range(3):
+                small_from_z(k).wait_recv()
+            total = small_z[0]
+            for zz in range(1, 4):
+                total = total + small_z[zz]
+            small_all[head] = total
+            for k in range(3):
+                small_to_head(k).start()
 
     rows = up_go.shape[0]
     cols = up_go.shape[1]
@@ -1013,30 +1018,9 @@
             def _():
                 up_out[:, cols * yy : cols * yy + cols] = mine
 
-    end_step(0, use_up)
+    use_up(up_end[...])
     up_to_y = remote(up_go, up_got, up_sem.at[0], up_sem.at[1], device(z, 1 - y, c))
     up_to_y.start()
-
-    for k in range(3):
-        small_from_z(k).wait_recv()
-    total = small_z[0]
-    for zz in range(1, 4):
-        total = total + small_z[zz]
-    small_all[head] = total
-
-    def to_group(k, src, dst, sent, landed):
-        yy, cc = group[k]
-        return remote(src, dst, sent.at[k], landed, device(z, yy, cc))
-
-    def small_to_head(k):
-        return to_group(k, small_all.at[head], small_all.at[head], sh_sent, sh_landed.at[head])
-
-    def small_from_head(k):
-        at = 2 * group[k][1] + group[k][0]
-        return to_group(k, small_all.at[at], small_all.at[at], sh_sent, sh_landed.at[at])
-
-    for k in range(3):
-        small_to_head(k).start()
 
     tall, wide = sq_got.shape[1], sq_got.shape[2] // 3
 
@@ -1049,7 +1033,7 @@
                         (2 * a + cc) * wide : (2 * a + cc) * wide + wide,
                     ].astype(bf16)
 
-    end_step(1, use_square)
+    use_square(sq_end[...])
     sq_got[head] = sq_go[y, c]
 
     def square_to(k):
@@ -1069,7 +1053,7 @@
         for cc in range(2):
             dn_go[cc] = value[:, span * cc : span * cc + span].astype(bf16)
 
-    end_step(2, use_down)
+    use_down(dn_end[...])
 
     def down_to(cc):
         return remote(
@@ -1134,10 +1118,10 @@
 
     small_to_x.wait_send()
     up_to_y.wait_send()
-    for p in range(3):
-        for zz in range(4):
-            to_x(p, zz).wait_send()
-        passed(p)
+    for n in range(count):
+        to_x(n).wait_send()
+        to_near(n).wait_send()
+        pl.when(high != items[n][1])(lambda: to_far(n).wait_send())
     for yy, at in ((1 - y, 0), (y, 4)):
         for zz in range(4):
             to_c(zz, yy, at + zz).wait_send()
@@ -1165,8 +1149,9 @@
     ]
     for piece in (up, square, down):
         _, tall, wide = piece.shape
-        scratch += [((tall, wide), bf16), ((4, tall // 4, wide), bf16), ((4, tall // 4, wide), bf16)]
-        scratch += [((3, tall // 4, wide), bf16)] * 2
+        scratch += [((tall, wide), bf16), ((4, tall // 4, wide), bf16)]
+        scratch += [((2, tall // 4, wide), bf16)] * 2
+        scratch += [((tall // 4, wide), bf16), ((tall // 4, wide), f32)]
     scratch += [
         ((width // 8, size), bf16), ((width // 8, size), bf16),
         ((2, 2, size // 8, 3 * size // 4), bf16), ((4, size // 8, 3 * size // 4), bf16),
@@ -1174,7 +1159,7 @@
         ((lines, size), f32), ((lines, size), f32), ((4, lines, size), f32), ((4, lines, size), f32),
     ]
     sems = [
-        (8,), (8,), (8,), (4,), (4,), (4,), (2, 2), (3, 4), (3, 4), (3, 3), (3, 3), (3, 3), (3, 3),
+        (8,), (8,), (8,), (4,), (4,), (4,), (2, 2), (8,), (8,), (8,), (8,), (8,), (8,),
         (2,), (3,), (4,), (2,), (2,), (2,), (3,), (4,), (3,), (4,),
     ]
     vmem = pl.BlockSpec(memory_space=pltpu.VMEM)
@@ -1223,32 +1208,52 @@
     return (at_seq % 8) // 2, at_seq % 2, at_batch // 2, at_batch % 2
 
 
-def across(blocks, z):
+def sent_across(blocks, z):
     got = [lax.dynamic_index_in_dim(blocks, z, 0, keepdims=False)]
     for k in range(1, 4):
         got.append(swap(lax.dynamic_index_in_dim(blocks, z ^ k, 0, keepdims=False), "seq", 2 * k))
+    return got
+
+
+def in_order(got, z):
     got = jnp.stack(got)
     return jnp.stack([lax.dynamic_index_in_dim(got, z ^ k, 0, keepdims=False) for k in range(4)])
 
 
-def gather_sequence(own):
+def hold(value, *done):
+    return lax.optimization_barrier((value, *done))
+
+
+def gather_first(own):
     z, y, x, c = place()
-    micro, rows, width = own.shape
     slots = paired(own, swap(own, "batch", 1), c, 0)
-    blocks = across(part_of(slots, c, 2, 2), z)[:, None]
-    both = paired(blocks, swap(blocks, "seq", 1), y, 1)
-    return paired(both, swap(both, "batch", 1), c, 3).reshape(8 * rows, width)
+    return part_of(slots, c, 2, 2)
+
+
+def gather_last(blocks, other):
+    z, y, x, c = place()
+    rows, width = blocks.shape[2:]
+    both = paired(blocks, other, y, 1)
+    return paired(both, swap(both, "batch", 1), c, 3).reshape(8 * rows, 2 * width)
+
+
+def scatter_first(parts):
+    z, y, x, c = place()
+    blocks = parts.reshape(4, 2, -1, parts.shape[1])
+    return halved(blocks, c, 2, "batch", 1).astype(bf16)
+
+
+def scatter_last(slots):
+    z, y, x, c = place()
+    other = swap(part_of(slots, 1 - c, 2, 0), "batch", 1)
+    return paired(part_of(slots, c, 2, 0), other, c, 1).astype(f32)
 
 
 def scatter_sequence(parts):
     z, y, x, c = place()
-    width = parts.shape[1]
-    blocks = parts.reshape(4, 2, -1, width)
-    blocks = halved(blocks, c, 2, "batch", 1).astype(bf16)
+    blocks = scatter_first(parts)
     blocks = halved(blocks, y, 1, "seq", 1).astype(bf16)[:, 0]
-    slots = across(blocks, z)
-    other = swap(part_of(slots, 1 - c, 2, 0), "batch", 1)
-    return paired(part_of(slots, c, 2, 0), other, c, 1).astype(f32)
+    return scatter_last(in_order(sent_across(blocks, z), z))
 
 
 def total_over_heads(value):
@@ -1335,7 +1340,8 @@
     skip_row = skip_gain.reshape(1, inner)
 
     normed = gather_normed(tokens[:, 0], ln_gain[None])
-    cot = gather_sequence(d_out[:, 0])
+    cot_half, normed = hold(gather_first(d_out[:, 0]), normed)
+    cot_across = sent_across(cot_half, z)
 
     gate_own = lax.dynamic_index_in_dim(
         gate_w.reshape(3, heads, size, 8), at, 1, keepdims=False
@@ -1355,7 +1361,11 @@
     mix, conv, q, k, v, gate_z, gates, *halo = lift(
         head, normed, w_up, w_query, w_key, w_value, conv_w, conv_row, gate_parts, *first
     )
+    cot_across, gates = hold(cot_across, gates)
+    cot_blocks = in_order(cot_across, z)[:, None]
     gates = total_over_heads(gates)
+    cot_blocks, gates = hold(cot_blocks, gates)
+    cot_row = swap(cot_blocks, "seq", 1)
     gates = jnp.concatenate(
         [
             lax.dynamic_slice_in_dim(gates, at, 1, 0),
@@ -1378,7 +1388,11 @@
     part, head_normed, states, norms, weights, cols, rows, *last = cell_forward(
         head, gates, q, k, v, conv, gate_z, out_row, skip_row, w_down, *first
     )
-    block_rows = (tokens[:, 0].astype(f32) + scatter_sequence(part)).astype(bf16)
+    cot_row, part = hold(cot_row, part)
+    cot = gather_last(cot_blocks, cot_row)
+    part = scatter_first(part)
+    part, cot = hold(part, cot)
+    part_row = swap(part_of(part, 1 - y, 2, 1), "seq", 1)
     after = ()
     if ranges > 1:
         after = (jnp.zeros((size, size), f32), jnp.zeros((8, size), f32))
@@ -1392,9 +1406,13 @@
         head, rows, q, k, v, conv, gate_z, head_normed, states, norms, weights, cols, cot,
         out_row, skip_row, w_down, *after,
     )
+    part_row, d_rows = hold(part_row, d_rows)
+    part = (part_of(part, y, 2, 1).astype(f32) + part_row.astype(f32)).astype(bf16)[:, 0]
     index = jnp.arange(2 * heads)[:, None]
     d_gate = jnp.where(index == at, d_rows[0:1], jnp.where(index == heads + at, d_rows[1:2], 0.0))
     d_gate = total_over_heads(d_gate)
+    part, d_gate = hold(part, d_gate)
+    part_across = sent_across(part, z)
     first = ()
     if ranges > 1:
         *_, later = lower(
@@ -1407,6 +1425,9 @@
         head, d_gate, dq, dk, dv, dskip, dz, mix, conv, q, k, v, normed,
         w_query, w_key, w_value, w_up, conv_w, conv_row, gate_pairs, g_gain, *first,
     )
+    part_across, small = hold(part_across, small)
+    block_rows = scatter_last(in_order(part_across, z))
+    block_rows = (tokens[:, 0].astype(f32) + block_rows).astype(bf16)
     if direct:
         grad_rows, s_up, s_query, s_key, s_value, s_down, small = finish(
             d_part, up, square, g_down, small, tokens[:, 0], d_out[:, 0], ln_gain[None]

time: 394 us -> 307 us (0.78)
  waiting for transfers between devices: 80.4 us -> 18.3 us
  Pallas kernels: 246 us -> 226 us
  local copies, waits for them, and re-layouts: 26.6 us -> 21.4 us
  other arithmetic: 21.1 us -> 16.9 us
    ppermute x16, waiting for transfers between devices: 80.4 us -> 18.3 us  [swap(): return lax.ppermute(value, axis, [(s, s ^ mask) for s in range(count)])]
    pallas_call x1, Pallas kernels: 115 us -> 98.8 us  [finish(): pl.pallas_call(finish_kernel, out_shape=[struct(rows.shape, bf16), struct...]
    unnamed x34 -> x44, local copies, waits for them, and re-layouts: 9.64 us -> 9.39 us
  transfers between devices with their start and end apart: 16 -> 16, of which waited for: 10 -> 7; matrix products, arithmetic and copies ran while one was open for 7% -> 7% of each run, Pallas kernels for 11% -> 74%
where the time goes in v3:
time: 307 us; the launch traced here: 304 us
  Pallas kernels  226 us (74%)
  local copies, waits for them, and re-layouts  21.4 us (7%)
  starting transfers between devices  19.8 us (6%)
  waiting for transfers between devices  18.3 us (6%)
  other arithmetic  16.9 us (6%)
    pallas_call x1, Pallas kernels, finish(): pl.pallas_call(finish_kernel, out_shape=[struct(rows.shape, bf16), struct...  98.8 us
    pallas_call x4, Pallas kernels, run_kernel(): pl.pallas_call(body, grid_spec=pltpu.PrefetchScalarGridSpec(num_scalar_pr...  91.2 us
    pallas_call x1, Pallas kernels, gather_normed(): pl.pallas_call(gather_kernel, out_shape=struct((8 * block, width), bf16),...  36.2 us
    ppermute x16, starting transfers between devices, swap(): return lax.ppermute(value, axis, [(s, s ^ mask) for s in range(count)])  19.8 us
    ppermute x16, waiting for transfers between devices, swap(): return lax.ppermute(value, axis, [(s, s ^ mask) for s in range(count)])  18.3 us
    unnamed x44, local copies, waits for them, and re-layouts  9.39 us
    select_n x3, other arithmetic, paired(): jnp.where(bit == 0, jnp.concatenate([mine, other], dim), jnp.concatenate(...  7.39 us
  transfers between devices with their start and end apart: 16, of which 7 were waited for; matrix products, arithmetic and copies ran while one was open for 7% of the time, Pallas kernels for 74%

profile of v3, /device:TPU:24, one launch (start us, length us, event | category | flops | bytes accessed | tf_op | source)
XLA Modules:
  0.0 303.8 jit_solution(3490361554324798135)
XLA Ops:
  0.9 1.2 copy-done.1
  2.1 0.7 copy-done.3
  2.8 36.2 %gather_normed.1.normed = bf16[2048,1024]{1,0:T(8,128)(2,1)S(1)} custom-call(bf16[2,256,1024]{2,1,0:T(8,128)(2,1)S(1)} %bitcast.81, f32[1,1024]{1,0:T(1,128)S(1)} %bitcast.83), custom_call_target="tpu_custom_call" | custom-call | tf_op jit(solution)/shard_map/gather_normed/pallas_call | solution.py:797
  39.1 2.0 copy-done
  41.1 0.7 maximum_maximum_fusion.gate_w
  42.3 6.5 %collective-permute-start.2 = (bf16[256,512]{1,0:T(8,128)(2,1)S(1)}, bf16[256,512]{1,0:T(8,128)(2,1)S(1)}, u32[]{:S(2)}, u32[]{:S(2)}) collective-permute-start(bf16[256,512]{1,0:T(8,128)(2,1)S(1)} %get-tuple-element.173), channel_id=1, source_target_pairs={{0,16},{4,20},{8,24},{12,28},{16,0},{20,4},{24,8},{28,12},{1,17},{... | collective-permute-start | bytes 786440 | tf_op jit(solution)/shard_map/ppermute | solution.py:1187
  48.9 1.4 collective-permute-start.3
  50.3 14.3 %lift.1 = (bf16[2048,512]{1,0:T(8,128)(2,1)}, bf16[2048,512]{1,0:T(8,128)(2,1)}, bf16[2048,512]{1,0:T(8,128)(2,1)}, bf16[2048,512]{1,0:T(8,128)(2,1)}, bf16[2048...) custom-call(s32[1]{0:T(128)} %bitcast.7.head_ref, bf16[2048,1024]{1,0:T(8,128)(2,1)} %copy-done, ...), custom_call_target="tpu_custom_call" | custom-call | flops 7516192768 | bytes 25165824 | tf_op jit(solution)/shard_map/lift/pallas_call | solution.py:463
  64.5 3.7 %collective-permute-done.3 = bf16[256,512]{1,0:T(8,128)(2,1)S(1)} collective-permute-done((bf16[256,512]{1,0:T(8,128)(2,1)S(1)}, bf16[256,512]{1,0:T(8,128)(2,1)S(1)}, u32[]{:S(2)}, u32[]{:S(2)}) %collective-permute-start.3) | collective-permute-done | bytes 262176 | tf_op jit(solution)/shard_map/ppermute | solution.py:1187
  68.5 1.2 collective-permute-done.4
  69.9 4.1 %collective-permute-done.5 = f32[8,2048]{1,0:T(8,128)S(1)} collective-permute-done((f32[8,2048]{1,0:T(8,128)S(1)}, f32[8,2048]{1,0:T(8,128)S(1)}, u32[]{:S(2)}, u32[]{:S(2)}) %collective-permute-start.5) | collective-permute-done | bytes 65568 | tf_op jit(solution)/shard_map/ppermute | solution.py:1187
  74.3 0.6 dynamic_slice.96
  74.9 0.7 constant_dynamic-slice_fusion.7
  75.5 0.6 pad_maximum_fusion.4.gates
  76.2 16.6 %cell_forward.1 = (bf16[2048,1024]{1,0:T(8,128)(2,1)}, f32[2048,512]{1,0:T(8,128)}, bf16[8,512,512]{2,1,0:T(8,128)(2,1)}, f32[8,8,512]{2,1,0:T(8,128)}, bf16[204...) custom-call(s32[1]{0:T(128)} %bitcast.7.head_ref, f32[2,2048]{1,0:T(2,128)} %pad_maximum_fusion.4.gates, ...), custom_call_target="tpu_custom_call" | custom-call | flops 5368709120 | bytes 29360128 | tf_op jit(solution)/shard_map/cell_forward/pallas_call | solution.py:463
  92.7 5.5 %collective-permute-done.6 = bf16[4,1,256,512]{3,2,0,1:T(8,128)(2,1)S(1)} collective-permute-done((bf16[4,1,256,512]{3,2,0,1:T(8,128)(2,1)S(1)}, bf16[4,1,256,512]{3,2,0,1:T(8,128)(2,1)S(1)}, u32[]{:S(2)}, u32[]{:S(2)}) %collective-permute-start.6) | collective-permute-done | bytes 1048608 | tf_op jit(solution)/shard_map/ppermute | solution.py:1187
  98.2 1.0 copy-done.5
  99.2 2.1 maximum_select_fusion.1
  101.4 3.2 %constant_dynamic-slice_fusion.6 = bf16[4,2,128,1024]{3,2,1,0:T(8,128)(2,1)} fusion(bf16[4,2,256,1024]{3,2,1,0:T(8,128)(2,1)} %bitcast.88, s32[]{:T(128)S(6)} %select_n.155), kind=kLoop, calls=%fused_computation.52 | loop fusion | bytes 4194308 | tf_op jit(solution)/shard_map/dynamic_slice | solution.py:1192
  105.1 0.6 collective-permute-done.8
  105.7 5.0 %maximum_select_fusion.cot_ref = bf16[2048,1024]{1,0:T(8,128)(2,1)} fusion(bf16[2048,512]{1,0:T(8,128)(2,1)} %bitcast.25, bf16[2048,512]{1,0:T(8,128)(2,1)S(1)} %bitcast.86, pred[]{:T(512)S(6)} %eq.39), kind=kLoop, calls=%fused_computation | loop fusion | flops 18874368 | bytes 8388609 | tf_op jit(solution)/shard_map/jit(_where)/select_n | solution.py:1201
  110.7 2.6 add_convert_fusion
  113.3 0.9 collective-permute-start.9
  114.2 27.4 %cell_backward.1 = (f32[2048,512]{1,0:T(8,128)}, f32[2048,512]{1,0:T(8,128)}, f32[2048,512]{1,0:T(8,128)}, f32[2048,512]{1,0:T(8,128)}, bf16[2048,512]{1,0:T(8,1...) custom-call(s32[1]{0:T(128)} %bitcast.7.head_ref, ...), custom_call_target="tpu_custom_call" | custom-call | flops 10737418240 | bytes 46137344 | tf_op jit(solution)/shard_map/cell_backward/pallas_call | solution.py:463
  141.6 0.9 fusion.9
  142.7 0.7 copy.45
  144.0 1.3 collective-permute-start.11
  145.7 2.6 collective-permute-done.11
  148.3 0.7 fusion.10.d_gate
  149.1 5.2 %collective-permute-start.12 = (bf16[128,1024]{1,0:T(8,128)(2,1)S(1)}, bf16[128,1024]{1,0:T(8,128)(2,1)S(1)}, u32[]{:S(2)}, u32[]{:S(2)}) collective-permute-start(bf16[128,1024]{1,0:T(8,128)(2,1)S(1)} %get-tuple-element.166), channel_id=1, source_target_pairs={{0,8},{4,12},{8,0},{12,4},{16,24},{20,28},{24,16},{28,20},{1,9},{5... | collective-permute-start | bytes 786440 | tf_op jit(solution)/shard_map/ppermute | solution.py:1187
  154.3 2.0 collective-permute-start.13
  156.3 1.4 collective-permute-start.14
  157.7 33.0 %lower.1 = (bf16[2048,1024]{1,0:T(8,128)(2,1)}, bf16[2,512,768]{2,1,0:T(8,128)(2,1)}, bf16[2,1024,512]{2,1,0:T(8,128)(2,1)}, f32[40,512]{1,0:T(8,128)}) custom-call(s32[1]{0:T(128)} %bitcast.7.head_ref, f32[8,2048]{1,0:T(8,128)} %fusion.10.d_gate, f32[2048,512]{1,0:T(8,128)} %get-tuple-element.100.dq_ref, f32[2048,512]{1,0:T(8,128)} %get-tuple-element.101.dk_ref, ...), custom_call_target="tpu_custom_call" | custom-call | flops 15032385536 | bytes 50331648 | tf_op jit(solution)/shard_map/lower/pallas_call | solution.py:463
  191.3 98.8 %finish.1 = (bf16[2,256,1024]{2,1,0:T(8,128)(2,1)}, f32[128,1024]{1,0:T(8,128)}, f32[4,64,128]{2,1,0:T(8,128)}, f32[4,64,128]{2,1,0:T(8,128)}, f32[4,64,128]{2,1...) custom-call(bf16[2048,1024]{1,0:T(8,128)(2,1)} %get-tuple-element.112.part_ref, ...), custom_call_target="tpu_custom_call" | custom-call | tf_op jit(solution)/shard_map/finish/pallas_call | solution.py:1167
  290.1 1.0 slice_bitcast_fusion
  291.1 1.5 slice.30
  292.6 0.7 copy.42
  293.3 0.9 slice_reduce_fusion
  294.2 0.6 div.14
  294.8 1.3 slice_reduce_fusion.1
  296.1 1.6 fusion.8
  297.7 1.6 add_convert_fusion.1
  299.4 1.0 copy.59
  300.3 0.8 copy.60
  301.1 0.7 copy.61
  301.8 0.7 copy.62
  302.4 0.7 copy.63
  303.1 0.7 copy.64
  (76 shorter events, 3.8 us)
Async XLA Ops:
  0.6 41.2 %collective-permute-start = (bf16[2,256,1024]{2,1,0:T(8,128)(2,1)}, bf16[2,256,1024]{2,1,0:T(8,128)(2,1)S(1)}, u32[]{:S(2)}, u32[]{:S(2)}) collective-permute-start(bf16[2,256,1024]{2,1,0:T(8,128)(2,1)} %bitcast.90), channel_id=1, source_target_pairs={{0,1},{1,0},{2,3},{3,2},{4,5},{5,4},{6,7},{7,6},{8,9},{9,8},{10,11... | collective-permute-start | bytes 3145736 | tf_op jit(solution)/shard_map/ppermute | solution.py:1187
  0.9 1.2 copy-start.1
  2.1 0.7 copy-start.3
  2.8 38.2 %copy-start.14 = (f32[6144,8]{0,1:T(8,128)S(1)}, f32[6144,8]{0,1:T(8,128)}, u32[]{:S(2)}) copy-start(f32[6144,8]{0,1:T(8,128)} %param.22) | copy-start | bytes 589828
  2.8 39.1 %copy-start.7 = (bf16[2,1,256,1024]{3,2,1,0:T(8,128)(2,1)S(1)}, bf16[2,1,256,1024]{3,2,1,0:T(8,128)(2,1)}, u32[]{:S(2)}) copy-start(bf16[2,1,256,1024]{3,2,1,0:T(8,128)(2,1)} %param.27) | copy-start | bytes 3145732
  39.1 2.0 copy-start
  42.2 22.3 %collective-permute-start.1 = (bf16[256,512]{1,0:T(8,128)(2,1)S(1)}, bf16[256,512]{1,0:T(8,128)(2,1)S(1)}, u32[]{:S(2)}, u32[]{:S(2)}) collective-permute-start(bf16[256,512]{1,0:T(8,128)(2,1)S(1)} %get-tuple-element.174), channel_id=1, source_target_pairs={{0,8},{4,12},{8,0},{12,4},{16,24},{20,28},{24,16},{28,20},{1,9},{5... | collective-permute-start | bytes 786440 | tf_op jit(solution)/shard_map/ppermute | solution.py:1187
  42.3 22.2 %collective-permute-start.2 = (bf16[256,512]{1,0:T(8,128)(2,1)S(1)}, bf16[256,512]{1,0:T(8,128)(2,1)S(1)}, u32[]{:S(2)}, u32[]{:S(2)}) collective-permute-start(bf16[256,512]{1,0:T(8,128)(2,1)S(1)} %get-tuple-element.173), channel_id=1, source_target_pairs={{0,16},{4,20},{8,24},{12,28},{16,0},{20,4},{24,8},{28,12},{1,17},{... | collective-permute-start | bytes 786440 | tf_op jit(solution)/shard_map/ppermute | solution.py:1187
  48.9 19.3 %collective-permute-start.3 = (bf16[256,512]{1,0:T(8,128)(2,1)S(1)}, bf16[256,512]{1,0:T(8,128)(2,1)S(1)}, u32[]{:S(2)}, u32[]{:S(2)}) collective-permute-start(bf16[256,512]{1,0:T(8,128)(2,1)S(1)} %get-tuple-element.172), channel_id=1, source_target_pairs={{0,24},{4,28},{8,16},{12,20},{16,8},{20,12},{24,0},{28,4},{1,25},{... | collective-permute-start | bytes 786440 | tf_op jit(solution)/shard_map/ppermute | solution.py:1187
  68.2 1.5 collective-permute-start.4
  68.2 1.5 copy-start.15
  68.4 5.9 %copy-start.16 = (f32[4]{0:T(128)S(1)}, f32[4]{0:T(128)}, u32[]{:S(2)}) copy-start(f32[4]{0:T(128)} %param.23) | copy-start | bytes 52
  69.7 4.3 %collective-permute-start.5 = (f32[8,2048]{1,0:T(8,128)S(1)}, f32[8,2048]{1,0:T(8,128)S(1)}, u32[]{:S(2)}, u32[]{:S(2)}) collective-permute-start(f32[8,2048]{1,0:T(8,128)S(1)} %add.124), channel_id=1, source_target_pairs={{0,4},{4,0},{8,12},{12,8},{16,20},{20,16},{24,28},{28,24},{1,5},{5... | collective-permute-start | bytes 196616 | tf_op jit(solution)/shard_map/ppermute | solution.py:1187
  74.0 24.1 %collective-permute-start.6 = (bf16[4,1,256,512]{3,2,0,1:T(8,128)(2,1)S(1)}, bf16[4,1,256,512]{3,2,0,1:T(8,128)(2,1)S(1)}, u32[]{:S(2)}, u32[]{:S(2)}) collective-permute-start(bf16[4,1,256,512]{3,2,0,1:T(8,128)(2,1)S(1)} %bitcast.84), channel_id=1, source_target_pairs={{0,4},{4,0},{8,12},{12,8},{16,20},{20,16},{24,28},{28,24},{1,5},{5... | collective-permute-start | bytes 3145736 | tf_op jit(solution)/shard_map/ppermute | solution.py:1187
  98.2 1.0 copy-start.5
  101.3 4.4 %collective-permute-start.8 = (bf16[4,2,256,512]{3,2,1,0:T(8,128)(2,1)S(1)}, bf16[4,2,256,512]{3,2,1,0:T(8,128)(2,1)}, u32[]{:S(2)}, u32[]{:S(2)}) collective-permute-start(bf16[4,2,256,512]{3,2,1,0:T(8,128)(2,1)S(1)} %maximum_select_fusion.1), channel_id=1, source_target_pairs={{0,1},{1,0},{2,3},{3,2},{4,5},{5,4},{6,7},{7,6},{8,9},{9,8},{10,11... | collective-permute-start | bytes 6291464 | tf_op jit(solution)/shard_map/ppermute | solution.py:1187
  104.6 6.1 %collective-permute-start.7 = (bf16[4,2,128,1024]{3,2,1,0:T(8,128)(2,1)}, bf16[4,2,128,1024]{3,2,1,0:T(8,128)(2,1)}, u32[]{:S(2)}, u32[]{:S(2)}) collective-permute-start(bf16[4,2,128,1024]{3,2,1,0:T(8,128)(2,1)} %constant_dynamic-slice_fusion.6), channel_id=1, source_target_pairs={{0,1},{1,0},{2,3},{3,2},{4,5},{5,4},{6,7},{7,6},{8,9},{9,8},{10,11... | collective-permute-start | bytes 6291464 | tf_op jit(solution)/shard_map/ppermute | solution.py:1187
  105.7 5.0 %copy-start.6 = (bf16[2048,1024]{1,0:T(8,128)(2,1)S(1)}, bf16[2048,1024]{1,0:T(8,128)(2,1)}, u32[]{:S(2)}) copy-start(bf16[2048,1024]{1,0:T(8,128)(2,1)} %get-tuple-element.85) | copy-start | bytes 12582916
  113.3 28.2 %collective-permute-start.9 = (bf16[4,1,128,1024]{3,2,1,0:T(8,128)(2,1)S(1)}, bf16[4,1,128,1024]{3,2,1,0:T(8,128)(2,1)S(1)}, u32[]{:S(2)}, u32[]{:S(2)}) collective-permute-start(bf16[4,1,128,1024]{3,2,1,0:T(8,128)(2,1)S(1)} %constant_dynamic-slice_fusion.5), channel_id=1, source_target_pairs={{0,4},{4,0},{8,12},{12,8},{16,20},{20,16},{24,28},{28,24},{1,5},{5... | collective-permute-start | bytes 3145736 | tf_op jit(solution)/shard_map/ppermute | solution.py:1187
  142.6 1.3 collective-permute-start.10
  144.0 4.3 %collective-permute-start.11 = (f32[8,2048]{1,0:T(8,128)S(1)}, f32[8,2048]{1,0:T(8,128)S(1)}, u32[]{:S(2)}, u32[]{:S(2)}) collective-permute-start(f32[8,2048]{1,0:T(8,128)S(1)} %fusion.6), channel_id=1, source_target_pairs={{0,4},{4,0},{8,12},{12,8},{16,20},{20,16},{24,28},{28,24},{1,5},{5... | collective-permute-start | bytes 196616 | tf_op jit(solution)/shard_map/ppermute | solution.py:1187
  149.1 41.6 %collective-permute-start.12 = (bf16[128,1024]{1,0:T(8,128)(2,1)S(1)}, bf16[128,1024]{1,0:T(8,128)(2,1)S(1)}, u32[]{:S(2)}, u32[]{:S(2)}) collective-permute-start(bf16[128,1024]{1,0:T(8,128)(2,1)S(1)} %get-tuple-element.166), channel_id=1, source_target_pairs={{0,8},{4,12},{8,0},{12,4},{16,24},{20,28},{24,16},{28,20},{1,9},{5... | collective-permute-start | bytes 786440 | tf_op jit(solution)/shard_map/ppermute | solution.py:1187
  154.3 36.4 %collective-permute-start.13 = (bf16[128,1024]{1,0:T(8,128)(2,1)S(1)}, bf16[128,1024]{1,0:T(8,128)(2,1)S(1)}, u32[]{:S(2)}, u32[]{:S(2)}) collective-permute-start(bf16[128,1024]{1,0:T(8,128)(2,1)S(1)} %get-tuple-element.165), channel_id=1, source_target_pairs={{0,16},{4,20},{8,24},{12,28},{16,0},{20,4},{24,8},{28,12},{1,17},{... | collective-permute-start | bytes 786440 | tf_op jit(solution)/shard_map/ppermute | solution.py:1187
  156.3 34.5 %collective-permute-start.14 = (bf16[128,1024]{1,0:T(8,128)(2,1)S(1)}, bf16[128,1024]{1,0:T(8,128)(2,1)S(1)}, u32[]{:S(2)}, u32[]{:S(2)}) collective-permute-start(bf16[128,1024]{1,0:T(8,128)(2,1)S(1)} %get-tuple-element.164), channel_id=1, source_target_pairs={{0,24},{4,28},{8,16},{12,20},{16,8},{20,12},{24,0},{28,4},{1,25},{... | collective-permute-start | bytes 786440 | tf_op jit(solution)/shard_map/ppermute | solution.py:1187
  191.2 106.5 %collective-permute-start.15 = (bf16[2,128,1024]{2,1,0:T(8,128)(2,1)S(1)}, bf16[2,128,1024]{2,1,0:T(8,128)(2,1)S(1)}, u32[]{:S(2)}, u32[]{:S(2)}) collective-permute-start(bf16[2,128,1024]{2,1,0:T(8,128)(2,1)S(1)} %get-tuple-element.159), channel_id=1, source_target_pairs={{0,1},{1,0},{2,3},{3,2},{4,5},{5,4},{6,7},{7,6},{8,9},{9,8},{10,11... | collective-permute-start | bytes 1572872 | tf_op jit(solution)/shard_map/ppermute | solution.py:1187
  191.3 102.9 %copy-start.4 = (f32[1024]{0:T(1024)S(1)}, f32[1024]{0:T(1024)}, u32[]{:S(2)}) copy-start(f32[1024]{0:T(1024)} %param.15) | copy-start | bytes 12292
  191.3 106.4 %copy-start.2 = (bf16[2,1,256,1024]{3,2,1,0:T(8,128)(2,1)S(1)}, bf16[2,1,256,1024]{3,2,1,0:T(8,128)(2,1)}, u32[]{:S(2)}) copy-start(bf16[2,1,256,1024]{3,2,1,0:T(8,128)(2,1)} %param.14) | copy-start | bytes 3145732
  290.1 9.3 %copy-start.8 = (bf16[2,256,1024]{2,1,0:T(8,128)(2,1)S(1)}, bf16[2,256,1024]{2,1,0:T(8,128)(2,1)}, u32[]{:S(2)}) copy-start(bf16[2,256,1024]{2,1,0:T(8,128)(2,1)} %get-tuple-element.117) | copy-start | bytes 3145732
  297.7 2.6 copy-start.9
  299.3 1.8 copy-start.13
  299.3 2.4 copy-start.12
  299.3 3.1 %copy-start.11 = (f32[4,64,128]{2,1,0:T(8,128)S(1)}, f32[4,64,128]{2,1,0:T(8,128)}, u32[]{:S(2)}) copy-start(f32[4,64,128]{2,1,0:T(8,128)} %get-tuple-element.205) | copy-start | bytes 393220
  299.3 3.8 %copy-start.10 = (f32[256,256]{1,0:T(8,128)S(1)}, f32[256,256]{1,0:T(8,128)}, u32[]{:S(2)}) copy-start(f32[256,256]{1,0:T(8,128)} %get-tuple-element.210) | copy-start | bytes 786436

commit v4 on v3

--- a/solution.py
+++ b/solution.py
@@ -272,14 +272,12 @@
 
 def cell_backward_kernel(
     chained, head_ref, rows_ref, q_ref, k_ref, v_ref, conv_ref, z_ref, normed_ref, state_ref, norm_ref,
-    weight_ref, col_ref, cot_ref, out_gain, skip_gain, w_down, *refs
+    weight_ref, col_ref, cot_ref, rows_in, out_gain, skip_gain, w_down, *refs
 ):
     if chained:
-        *first, dq_out, dk_out, dv_out, dskip_out, dz_out, gate_out, g_down_out, g_gain_out = refs[:10]
-        *final, d_state, d_norm, g_down, g_gain = refs[10:]
-    else:
-        dq_out, dk_out, dv_out, dskip_out, dz_out, gate_out, g_down_out, g_gain_out = refs[:8]
-        d_state, d_norm, g_down, g_gain = refs[8:]
+        first, refs = refs[:2], refs[2:]
+    dq_out, dk_out, dv_out, dskip_out, dz_out, gate_out, g_down_out, g_z_out, g_gain_out, *refs = refs
+    *final, d_state, d_norm, g_down, g_z, g_gain = refs
     length = q_ref.shape[0]
     head_size = q_ref.shape[1]
     scale = head_size ** (-0.5)
@@ -293,6 +291,7 @@
             d_state[...] = jnp.zeros_like(d_state)
             d_norm[...] = jnp.zeros_like(d_norm)
         g_down[...] = jnp.zeros_like(g_down)
+        g_z[...] = jnp.zeros_like(g_z)
         g_gain[...] = jnp.zeros_like(g_gain)
 
     causal, diagonal = masks(length)
@@ -316,7 +315,9 @@
     head_in = normed * out_gain[...] + skip_gain[...] * conv
     g_down[...] += mm_tn((head_in * silu).astype(bf16), cot)
     d_gated = mm_nt(cot, w_down[...])
-    dz_out[...] = (d_gated * head_in * (opened * (1.0 + gate_z * (1.0 - opened)))).astype(bf16)
+    d_z = (d_gated * head_in * (opened * (1.0 + gate_z * (1.0 - opened)))).astype(bf16)
+    dz_out[...] = d_z
+    g_z[...] += mm_tn(rows_in[...], d_z)
     d_head = d_gated * silu
     g_gain[0:1, :] += jnp.sum(d_head * normed, axis=0, keepdims=True)
     g_gain[1:2, :] += jnp.sum(d_head * conv, axis=0, keepdims=True)
@@ -374,28 +375,12 @@
         half = g_down.shape[1] // 2
         g_down_out[0] = g_down[:, :half].astype(bf16)
         g_down_out[1] = g_down[:, half:].astype(bf16)
+        g_z_out[...] = g_z[...].astype(bf16)
         g_gain_out[...] = g_gain[...]
 
 
-def lower_kernel(
-    chained, head_ref, d_gate, dq_ref, dk_ref, dv_ref, dskip_ref, dz_ref, mix_ref, mix_before, conv_ref,
-    q_ref, k_ref, v_ref, normed, w_q, w_k, w_v, w_mix, w_gate, conv_w, conv_b, gate_w, g_gain, *refs
-):
-    if chained:
-        first_halo, first_later, *refs = refs
-        later_out = refs.pop(4)
-    part_out, square_out, up_out, small_out = refs[:4]
-    g_q, g_k, g_v, g_m, g_z, g_small, later = refs[4:]
-    length = q_ref.shape[0]
-    step = pl.program_id(0)
-
-    @pl.when(step == 0)
-    def _():
-        for ref in (g_q, g_k, g_v, g_m, g_z, g_small, later):
-            ref[...] = jnp.zeros_like(ref)
-        if chained:
-            later[...] = first_later[...]
-
+def lower_first(d_gate, dq_ref, dk_ref, dv_ref, mix_ref, conv_ref, q_ref, k_ref, v_ref, gate_w,
+                g_q, g_k, g_v, g_small):
     high, middle, low = split_three(d_gate[...])
     left = jnp.concatenate([high, middle, low, high, middle, high], axis=0)
     d_joined = mm_tn(left, gate_w[...])
@@ -404,18 +389,25 @@
     key_low = (dk_ref[...] + d_joined[:, size : 2 * size]).astype(bf16)
     value_low = (dv_ref[...] + d_joined[:, 2 * size :]).astype(bf16)
     conv = conv_ref[...]
-    mix = mix_ref[...]
     g_q[...] += mm_tn(conv, query_low)
     g_k[...] += mm_tn(conv, key_low)
-    g_v[...] += mm_tn(mix, value_low)
+    g_v[...] += mm_tn(mix_ref[...], value_low)
     three = jnp.concatenate([high, middle, low], axis=0)
     for at, ref in enumerate((q_ref, k_ref, v_ref)):
         got = mm(three, ref[...])
         g_small[8 * at : 8 * at + 8, :] += got[0:8] + got[8:16] + got[16:24]
-    d_conv = dskip_ref[...] + mm_nt(query_low, w_q[0]) + mm_nt(key_low, w_k[0])
-    halo = mix_before[8:16, :].astype(f32)
-    edge = first_halo[8:16, :].astype(f32) if chained else 0.0
-    halo = jnp.where(step == pl.num_programs(0) - 1, edge, halo)
+    return query_low, key_low, value_low
+
+
+def lower_second(
+    edge, last, lows, dskip_ref, dz_ref, mix_ref, mix_before, normed, w_q, w_k, w_v, w_mix, w_gate,
+    conv_w, conv_b, g_gain, g_small, later,
+):
+    query_low, key_low, value_low = lows
+    length, size = mix_ref.shape
+    mix = mix_ref[...]
+    d_conv = dskip_ref[...] + mm_nt(query_low, w_q[...]) + mm_nt(key_low, w_k[...])
+    halo = jnp.where(last, edge, mix_before[8:16, :].astype(f32))
     taps = conv_taps(jnp.concatenate([halo, mix.astype(f32)], axis=0), length)
     summed = conv_b[...]
     for j in range(4):
@@ -430,16 +422,50 @@
     d_mix = conv_w[3:4, :] * d_summed
     for j in range(3):
         d_mix = d_mix + conv_w[j : j + 1, :] * pltpu.roll(ext, length + 8 - (3 - j), 0)[0:length]
-    d_mix = (d_mix + mm_nt(value_low, w_v[0])).astype(bf16)
+    d_mix = (d_mix + mm_nt(value_low, w_v[...])).astype(bf16)
     d_z = dz_ref[...]
     rows = normed[...]
-    g_m[...] += mm_tn(rows, d_mix)
-    g_z[...] += mm_tn(rows, d_z)
     d_normed = mm_nt(d_mix, w_mix[...]) + mm_nt(d_z, w_gate[...])
-    part_out[...] = d_normed.astype(bf16)
     g_ln = jnp.sum(d_normed * rows.astype(f32), axis=0, keepdims=True)
     g_small[32:33, :] += g_ln[:, :size]
     g_small[33:34, :] += g_ln[:, size:]
+
+    @pl.when(last)
+    def _():
+        g_small[29:32, :] = g_gain[0:3, :]
+
+    return rows, d_mix, d_z, d_normed
+
+
+def lower_kernel(chained, head_ref, *refs):
+    ins, refs = refs[:22], list(refs[22:])
+    edge = 0.0
+    if chained:
+        first_halo, first_later, *refs = refs
+        edge = first_halo[8:16, :].astype(f32)
+        later_out = refs.pop(4)
+    part_out, square_out, up_out, small_out = refs[:4]
+    g_q, g_k, g_v, g_m, g_z, g_small, later = refs[4:]
+    step = pl.program_id(0)
+    size = g_q.shape[0]
+
+    @pl.when(step == 0)
+    def _():
+        for ref in (g_q, g_k, g_v, g_m, g_z, g_small, later):
+            ref[...] = jnp.zeros_like(ref)
+        if chained:
+            later[...] = first_later[...]
+
+    (d_gate, dq, dk, dv, dskip, dz, mix, mix_before, conv, q, k, v, normed,
+     w_q, w_k, w_v, w_mix, w_gate, conv_w, conv_b, gate_w, g_gain) = ins
+    lows = lower_first(d_gate, dq, dk, dv, mix, conv, q, k, v, gate_w, g_q, g_k, g_v, g_small)
+    rows, d_mix, d_z, d_normed = lower_second(
+        edge, step == pl.num_programs(0) - 1, lows, dskip, dz, mix, mix_before, normed,
+        w_q.at[0], w_k.at[0], w_v.at[0], w_mix, w_gate, conv_w, conv_b, g_gain, g_small, later,
+    )
+    g_m[...] += mm_tn(rows, d_mix)
+    g_z[...] += mm_tn(rows, d_z)
+    part_out[...] = d_normed.astype(bf16)
 
     @pl.when(step == pl.num_programs(0) - 1)
     def _():
@@ -449,7 +475,6 @@
             square_out[1, :, half * at : half * at + half] = ref[:, half:].astype(bf16)
         up_out[0] = g_m[...].astype(bf16)
         up_out[1] = g_z[...].astype(bf16)
-        g_small[29:32, :] = g_gain[0:3, :]
         small_out[...] = g_small[...]
         if chained:
             later_out[...] = later[...]
@@ -554,7 +579,7 @@
 
 
 def cell_backward(
-    head, rows, q, k, v, conv, gate_z, normed, states, norms, weights, cols, cot,
+    head, rows, q, k, v, conv, gate_z, normed, states, norms, weights, cols, cot, rows_in,
     out_gain, skip_gain, w_down, *first,
 ):
     tokens, size = q.shape
@@ -569,7 +594,7 @@
     carried_specs = [whole(value.shape) for value in first]
     return run_kernel(
         partial(cell_backward_kernel, len(first) > 0), head, steps,
-        (rows, q, k, v, conv, gate_z, normed, states, norms, weights, cols, cot,
+        (rows, q, k, v, conv, gate_z, normed, states, norms, weights, cols, cot, rows_in,
          out_gain, skip_gain, w_down, *first),
         [pl.BlockSpec((8, length), lambda g, h: (0, end - g))]
         + [by_row(size)] * 6
@@ -578,6 +603,7 @@
             pl.BlockSpec((1, 8, size), lambda g, h: (end - g, 0, 0)),
             by_row(length),
             by_row(128),
+            by_row(width),
             by_row(width),
             gain, gain,
             pl.BlockSpec((size, width), lambda g, h: (h[0], 0)),
@@ -588,6 +614,7 @@
             struct((tokens, size), bf16),
             struct((8, tokens), f32),
             struct((2, size, width // 2), bf16),
+            struct((width, size), bf16),
             struct((8, size), f32),
         ]
         + carried,
@@ -595,6 +622,7 @@
         + [
             pl.BlockSpec((8, length), lambda g, h: (0, end - g)),
             pl.BlockSpec((2, size, width // 2), lambda g, h: (0, 0, 0)),
+            whole((width, size)),
             whole((8, size)),
         ]
         + carried_specs,
@@ -602,49 +630,62 @@
             pltpu.VMEM((size, size), f32),
             pltpu.VMEM((8, size), f32),
             pltpu.VMEM((size, width), f32),
+            pltpu.VMEM((width, size), f32),
             pltpu.VMEM((8, size), f32),
         ],
         "cell_backward", 2 * tokens * size * (4 * length + 4 * size + 2 * width), 44 * 2**20,
     )
 
 
-def lower(
-    head, d_gate, dq, dk, dv, dskip, dz, mix, conv, q, k, v, normed,
-    w_query, w_key, w_value, w_up, conv_w, conv_b, gate_pairs, g_gain, *first,
+def lower_inputs(
+    length, d_gate, dq, dk, dv, dskip, dz, mix, conv, q, k, v, normed,
+    w_query, w_key, w_value, w_up, conv_w, conv_b, gate_pairs, g_gain,
 ):
     tokens, size = q.shape
     width = normed.shape[1]
     heads = w_query.shape[0]
+    end = tokens // length - 1
+    by_row = lambda n: pl.BlockSpec((length, n), lambda g, h: (end - g, 0))
+    kept = lambda shape, index: pl.BlockSpec(shape, index, pipeline_mode=pl.Buffered(1))
+    weight = kept((1, size, size), lambda g, h: (h[0], 0, 0))
+    inputs = (
+        d_gate, dq, dk, dv, dskip, dz, mix, mix, conv, q, k, v, normed,
+        w_query, w_key, w_value, w_up, w_up, conv_w, conv_b, gate_pairs, g_gain,
+    )
+    specs = [pl.BlockSpec((8, length), lambda g, h: (0, end - g))]
+    specs += [by_row(size)] * 6
+    specs += [
+        pl.BlockSpec(
+            (16, size), lambda g, h: (jnp.maximum((end - g) * (length // 16) - 1, 0), 0)
+        )
+    ]
+    specs += [by_row(size)] * 4
+    specs += [by_row(width), weight, weight, weight]
+    specs += [
+        kept((width, size), lambda g, h: (0, h[0])),
+        kept((width, size), lambda g, h: (0, heads + h[0])),
+        kept((4, size), lambda g, h: (0, h[0])),
+        kept((1, size), lambda g, h: (0, h[0])),
+        kept(gate_pairs.shape, lambda g, h: (0, 0)),
+        kept(g_gain.shape, lambda g, h: (0, 0)),
+    ]
+    return inputs, specs
+
+
+def lower(head, *inputs):
+    inputs, first = inputs[:20], inputs[20:]
+    tokens, size = inputs[1].shape
+    width = inputs[11].shape[1]
     length = wide_len
-    steps = tokens // length
-    end = steps - 1
+    end = tokens // length - 1
     by_row = lambda n: pl.BlockSpec((length, n), lambda g, h: (end - g, 0))
-    weight = pl.BlockSpec((1, size, size), lambda g, h: (h[0], 0, 0))
     whole = lambda shape: pl.BlockSpec(shape, lambda g, h: (0, 0))
     chained = len(first) > 0
+    inputs, specs = lower_inputs(length, *inputs)
     return run_kernel(
-        partial(lower_kernel, chained), head, steps,
-        (d_gate, dq, dk, dv, dskip, dz, mix, mix, conv, q, k, v, normed,
-         w_query, w_key, w_value, w_up, w_up, conv_w, conv_b, gate_pairs, g_gain, *first),
-        [pl.BlockSpec((8, length), lambda g, h: (0, end - g))]
-        + [by_row(size)] * 6
-        + [
-            pl.BlockSpec(
-                (16, size),
-                lambda g, h: (jnp.maximum((end - g) * (length // 16) - 1, 0), 0),
-            )
-        ]
-        + [by_row(size)] * 4
-        + [by_row(width), weight, weight, weight]
-        + [
-            pl.BlockSpec((width, size), lambda g, h: (0, h[0])),
-            pl.BlockSpec((width, size), lambda g, h: (0, heads + h[0])),
-            pl.BlockSpec((4, size), lambda g, h: (0, h[0])),
-            pl.BlockSpec((1, size), lambda g, h: (0, h[0])),
-            whole(gate_pairs.shape),
-            whole(g_gain.shape),
-        ]
-        + [whole(value.shape) for value in first],
+        partial(lower_kernel, chained), head, tokens // length,
+        (*inputs, *first),
+        specs + [whole(value.shape) for value in first],
         [struct((tokens, width), bf16)]
         + [struct((2, size, 3 * size // 2), bf16), struct((2, width, size), bf16)]
         + [struct((40, size), f32)]
@@ -808,78 +849,101 @@
     )(rows, gain)
 
 
-def finish_kernel(
-    part_ref, up_ref, square_ref, down_ref, small_ref, rows_ref, cot_ref, gain_ref,
-    grad_out, up_out, query_out, key_out, value_out, down_out, small_out,
-    own, from_core, to_row, from_row, to_owner, owned,
-    up_x, up_sum, up_near, up_pair, up_far, up_end, sq_x, sq_sum, sq_near, sq_pair, sq_far, sq_end,
-    dn_x, dn_sum, dn_near, dn_pair, dn_far, dn_end,
-    up_go, up_got, sq_go, sq_got, dn_go, dn_got, small_x, small_sum, small_z, small_all,
-    own_sem, c_sent, c_landed, y_sent, y_landed, o_sent, o_landed,
-    x_sent, x_landed, near_sent, near_landed, far_sent, far_landed,
-    up_sem, sq_sent, sq_landed, dn_sent, dn_landed, sx_sem, sz_sent, sz_landed, sh_sent, sh_landed,
+def drain_kernel(
+    d_gate, dq, dk, dv, mix_ref, conv, q_ref, k_ref, v_ref, dskip, dz, mix_before, normed,
+    gate_pairs, g_gain, w_query, w_key, w_value, w_up, conv_w, conv_b,
+    down_ref, lifted_ref, rows_ref, cot_ref, gain_ref, *refs
 ):
+    grad_out, up_out, query_out, key_out, value_out, down_out, small_out, *refs = refs
+    w_q, w_k, w_v, w_mix, w_gate, taps_w, taps_b, q_all, k_all, v_all, *refs = refs
+    g_q, g_k, g_v, g_small, later, rows_all, lifted_all, part_all, *refs = refs
+    from_core, kept, to_row, from_row, to_owner, owned, *refs = refs
+    give_up, give_square, *refs = refs
+    from_x, totals, from_near, pairs, from_far, ends = (refs[k : 18 : 6] for k in range(6))
+    refs = refs[18:]
+    up_go, up_got, sq_go, sq_got, dn_go, dn_got, small_x, small_sum, small_z, small_all, *refs = refs
+    c_sent, c_landed, y_sent, y_landed, o_sent, o_landed, *refs = refs
+    x_sent, x_landed, near_sent, near_landed, far_sent, far_landed, *refs = refs
+    w_sem, up_sem, sq_sent, sq_landed, dn_sent, dn_landed, sx_sem, sz_sent, sz_landed, *refs = refs
+    sh_sent, sh_landed = refs
+    step = pl.program_id(0)
+    blocks, block, width = part_all.shape
+    half = block // 2
+    size = g_q.shape[0]
     first, z, y, x, c = where_am_i()
     head = 2 * c + y
+    high, low = z // 2, lax.rem(z, 2)
 
     def device(zz, yy, cc, xx=x):
         return (first + 2 * zz + yy, 2 * xx + cc)
 
     around = [lax.rem(z + k, 4) for k in range(1, 4)]
     group = [(1 - y, c), (y, 1 - c), (1 - y, 1 - c)]
-    others = [device(z, yy, cc) for yy, cc in group] + [device(z, y, c, 1 - x)]
-    for zz in around:
-        others += [device(zz, yy, cc) for yy, cc in [(y, c)] + group]
-    greet(others)
-
-    sources = (up_ref, square_ref, down_ref)
-    from_x = (up_x, sq_x, dn_x)
-    totals = (up_sum, sq_sum, dn_sum)
-    from_near = (up_near, sq_near, dn_near)
-    pairs = (up_pair, sq_pair, dn_pair)
-    from_far = (up_far, sq_far, dn_far)
-    ends = (up_end, sq_end, dn_end)
-    high, low = z // 2, lax.rem(z, 2)
-    cut = up_sum.shape[2] // 2
-    items = [(0, k, pl.ds(m * cut, cut)) for m in range(2) for k in range(2)]
-    items += [(p, k, slice(None)) for p in (2, 1) for k in range(2)]
-    count = len(items)
-    half = own.shape[1]
-
-    def to_x(n):
-        p, k, lanes = items[n]
-        size = 2 * totals[p].shape[1]
-        here = (pl.ds(k * size, size), lanes)
+
+    def down_rows(q):
+        tall = down_ref.shape[1] // 4
+        return pl.ds(q * tall, tall)
+
+    def up_rows(q):
+        tall = lifted_ref.shape[0] // 4
+        return pl.ds(q * tall, tall)
+
+    def to_x(p, q):
+        give = (give_up, give_square)[p].at[q] if p < 2 else down_ref.at[1 - x, down_rows(q)]
         return remote(
-            sources[p].at[(1 - x, *here)], from_x[p].at[here], x_sent.at[n], x_landed.at[n],
-            device(z, y, c, 1 - x),
-        )
-
-    def to_near(n):
-        p, k, lanes = items[n]
+            give, from_x[p].at[q], x_sent.at[p, q], x_landed.at[p, q], device(z, y, c, 1 - x)
+        )
+
+    def to_near(p, q):
         return remote(
-            totals[p].at[2 * k + 1 - low, :, lanes], from_near[p].at[k, :, lanes],
-            near_sent.at[n], near_landed.at[n], device(z + 1 - 2 * low, y, c),
-        )
-
-    def to_far(n):
-        p, k, lanes = items[n]
+            totals[p].at[q], from_near[p].at[q // 2], near_sent.at[p, q], near_landed.at[p, q],
+            device(z + 1 - 2 * low, y, c),
+        )
+
+    def to_far(p, q):
         return remote(
-            pairs[p].at[k, :, lanes], from_far[p].at[:, lanes], far_sent.at[n], far_landed.at[n],
+            pairs[p].at[q // 2], from_far[p], far_sent.at[p, q], far_landed.at[p, q],
             device(z + 2 - 4 * high, y, c),
         )
 
-    def block(zz, yy, cc):
-        start = ((2 * zz + yy) * 2 + cc) * half
-        return part_ref.at[pl.ds(pl.multiple_of(start, half), half)]
-
-    def load(zz, yy, k):
-        return pltpu.make_async_copy(block(zz, yy, c), own.at[k], own_sem.at[k])
-
-    def to_c(zz, yy, k):
+    def x_step(p, q):
+        to_x(p, q).wait_recv()
+        own = totals[p][q] if p < 2 else down_ref[x, down_rows(q)]
+        totals[p][q] = (own.astype(f32) + from_x[p][q].astype(f32)).astype(bf16)
+        pl.when(low != q % 2)(lambda: to_near(p, q).start())
+
+    def near_step(p, q):
+        @pl.when(low == q % 2)
+        def _():
+            to_near(p, q).wait_recv()
+            pairs[p][q // 2] = (
+                totals[p][q].astype(f32) + from_near[p][q // 2].astype(f32)
+            ).astype(bf16)
+            pl.when(high != q // 2)(lambda: to_far(p, q).start())
+
+    def far_step(p, q):
+        @pl.when(z == q)
+        def _():
+            to_far(p, q).wait_recv()
+            ends[p][...] = pairs[p][q // 2].astype(f32) + from_far[p][...].astype(f32)
+
+    def weight_copies():
+        lanes = pl.ds(pl.multiple_of(head * size, size), size)
+        gate_lanes = pl.ds(pl.multiple_of((w_query.shape[0] + head) * size, size), size)
+        pairs_of = [
+            (w_query.at[head], w_q), (w_key.at[head], w_k), (w_value.at[head], w_v),
+            (w_up.at[:, lanes], w_mix), (w_up.at[:, gate_lanes], w_gate),
+            (conv_w.at[:, lanes], taps_w), (conv_b.at[:, lanes], taps_b),
+        ]
+        return [
+            pltpu.make_async_copy(src, dst, w_sem.at[k]) for k, (src, dst) in enumerate(pairs_of)
+        ]
+
+    def to_c(at):
+        there = pl.ds(pl.multiple_of((1 - c) * half, half), half)
         return remote(
-            block(zz, yy, 1 - c), from_core.at[2 * zz + yy], c_sent.at[k],
-            c_landed.at[2 * zz + yy], device(z, y, 1 - c),
+            part_all.at[at, there], from_core.at[at], c_sent.at[at], c_landed.at[at],
+            device(z, y, 1 - c),
         )
 
     def to_y(zz):
@@ -889,75 +953,44 @@
 
     def to_o(zz):
         return remote(
-            to_owner.at[zz], owned.at[lax.rem(z, 2), c], o_sent.at[zz],
-            o_landed.at[lax.rem(z, 2), c], device(zz, y, z // 2),
-        )
-
-    ahead = 2
-    small_to_x = remote(
-        small_ref, small_x, sx_sem.at[0], sx_sem.at[1], device(z, y, c, 1 - x)
-    )
-    small_to_x.start()
-    for n in range(ahead):
-        to_x(n).start()
-    for yy, at in ((1 - y, 0), (y, 4)):
-        for zz in range(4):
-            to_c(zz, yy, at + zz).start()
-            load(zz, yy, at + zz).start()
-
-    def core_sum(zz, yy, k):
-        load(zz, yy, k).wait()
-        to_c(zz, yy, k).wait_recv()
-        return (own[k].astype(f32) + from_core[2 * zz + yy].astype(f32)).astype(bf16)
-
-    for zz in range(4):
-        to_row[zz] = core_sum(zz, 1 - y, zz)
-        if zz < ahead:
+            to_owner.at[zz], owned.at[low, c], o_sent.at[zz], o_landed.at[low, c],
+            device(zz, y, z // 2),
+        )
+
+    def stays(zz):
+        return jnp.logical_and(z == zz, z // 2 == c)
+
+    def core_step(at):
+        zz, yy = at // 2, lax.rem(at, 2)
+        to_c(at).wait_recv()
+        here = pl.ds(pl.multiple_of(c * half, half), half)
+        value = (part_all[at, here].astype(f32) + from_core[at].astype(f32)).astype(bf16)
+
+        @pl.when(yy == y)
+        def _():
+            kept[zz] = value
+
+        @pl.when(yy != y)
+        def _():
+            to_row[zz] = value
             to_y(zz).start()
-    for zz in range(4):
-        own[4 + zz] = core_sum(zz, y, 4 + zz)
 
     def row_step(zz):
         to_y(zz).wait_recv()
-        if zz + ahead < 4:
-            to_y(zz + ahead).start()
-        to_owner[zz] = (own[4 + zz].astype(f32) + from_row[zz].astype(f32)).astype(bf16)
-        stays = jnp.logical_and(z == zz, z // 2 == c)
-
-        @pl.when(stays)
+        to_owner[zz] = (kept[zz].astype(f32) + from_row[zz].astype(f32)).astype(bf16)
+
+        @pl.when(stays(zz))
         def _():
-            owned[lax.rem(z, 2), c] = to_owner[zz]
-
-        pl.when(jnp.logical_not(stays))(lambda: to_o(zz).start())
-
-    def x_step(n):
-        p, k, lanes = items[n]
-        size = totals[p].shape[1]
-        to_x(n).wait_recv()
-        if n + ahead < count:
-            to_x(n + ahead).start()
-        for at in (2 * k, 2 * k + 1):
-            here = (pl.ds(at * size, size), lanes)
-            totals[p][at, :, lanes] = (
-                sources[p][(x, *here)].astype(f32) + from_x[p][here].astype(f32)
-            ).astype(bf16)
-        to_near(n).start()
-
-    def near_step(n):
-        p, k, lanes = items[n]
-        to_near(n).wait_recv()
-        pairs[p][k, :, lanes] = (
-            totals[p][2 * k + low, :, lanes].astype(f32) + from_near[p][k, :, lanes].astype(f32)
-        ).astype(bf16)
-        pl.when(high != k)(lambda: to_far(n).start())
-
-    def far_step(n):
-        p, k, lanes = items[n]
-
-        @pl.when(high == k)
-        def _():
-            to_far(n).wait_recv()
-            ends[p][:, lanes] = pairs[p][k, :, lanes].astype(f32) + from_far[p][:, lanes].astype(f32)
+            owned[low, c] = to_owner[zz]
+
+        pl.when(jnp.logical_not(stays(zz)))(lambda: to_o(zz).start())
+
+    def to_group(k, src, dst, sent, landed):
+        yy, cc = group[k]
+        return remote(src, dst, sent.at[k], landed, device(z, yy, cc))
+
+    def small_to_x():
+        return remote(g_small, small_x, sx_sem.at[0], sx_sem.at[1], device(z, y, c, 1 - x))
 
     def small_to_z(k):
         return remote(
@@ -970,10 +1003,6 @@
             device(around[k], y, c),
         )
 
-    def to_group(k, src, dst, sent, landed):
-        yy, cc = group[k]
-        return remote(src, dst, sent.at[k], landed, device(z, yy, cc))
-
     def small_to_head(k):
         return to_group(k, small_all.at[head], small_all.at[head], sh_sent, sh_landed.at[head])
 
@@ -981,205 +1010,310 @@
         at = 2 * group[k][1] + group[k][0]
         return to_group(k, small_all.at[at], small_all.at[at], sh_sent, sh_landed.at[at])
 
-    for n in range(count + 3):
-        if n < 4:
-            row_step(n)
-        if n < count:
-            x_step(n)
-        if 1 <= n <= count:
-            near_step(n - 1)
-        if n >= 3:
-            far_step(n - 3)
-        if n == 2:
-            small_to_x.wait_recv()
-            small_sum[...] = small_ref[...] + small_x[...]
-            small_z[z] = small_sum[...]
-            for k in range(3):
-                small_to_z(k).start()
-        if n == 5:
-            for k in range(3):
-                small_from_z(k).wait_recv()
-            total = small_z[0]
-            for zz in range(1, 4):
-                total = total + small_z[zz]
-            small_all[head] = total
-            for k in range(3):
-                small_to_head(k).start()
-
-    rows = up_go.shape[0]
-    cols = up_go.shape[1]
-
-    def use_up(value):
-        mine = jnp.where(y == 0, value[:rows], value[rows:])
-        up_go[...] = jnp.where(y == 0, value[rows:], value[:rows]).astype(bf16)
-        for yy in range(2):
-
-            @pl.when(y == yy)
+    def up_to_y():
+        return remote(up_go, up_got, up_sem.at[0], up_sem.at[1], device(z, 1 - y, c))
+
+    def square_to(k):
+        yy, cc = group[k]
+        return to_group(k, sq_go.at[yy, cc], sq_got.at[head], sq_sent, sq_landed.at[head])
+
+    def square_from(k):
+        at = 2 * group[k][1] + group[k][0]
+        return to_group(k, sq_go.at[0, 0], sq_got.at[at], sq_sent, sq_landed.at[at])
+
+    def down_to(cc):
+        return remote(
+            dn_go.at[cc], dn_got.at[low], dn_sent.at[cc], dn_landed.at[low],
+            device(head, z // 2, cc),
+        )
+
+    def down_from(k):
+        return remote(
+            dn_go.at[0], dn_got.at[k], dn_sent.at[0], dn_landed.at[k],
+            device(2 * y + k, low, z // 2),
+        )
+
+    home = jnp.logical_and(head == z, z // 2 == y)
+
+    @pl.when(step == 0)
+    def _():
+        others = [device(z, yy, cc) for yy, cc in group] + [device(z, y, c, 1 - x)]
+        for zz in around:
+            others += [device(zz, yy, cc) for yy, cc in [(y, c)] + group]
+        greet(others)
+        for q in range(4):
+            to_x(2, q).start()
+        for copy in weight_copies():
+            copy.start()
+        for ref in (g_q, g_k, g_v, g_small, later):
+            ref[...] = jnp.zeros_like(ref)
+
+    tall, wide = size // 4, size // 2
+
+    @pl.when(step < blocks)
+    def _():
+        lows = lower_first(
+            d_gate, dq, dk, dv, mix_ref, conv, q_ref, k_ref, v_ref, gate_pairs, g_q, g_k, g_v, g_small
+        )
+        here = pl.ds(pl.multiple_of(step * block, block), block)
+        for ref, value in zip((q_all, k_all, v_all), lows):
+            ref[here] = value
+
+    @pl.when(step == blocks - 1)
+    def _():
+        for q in range(4):
+            rows_q = slice(tall * q, tall * q + tall)
+            for at, ref in enumerate((g_q, g_k, g_v)):
+                lanes = slice(wide * at, wide * at + wide)
+                left, right = ref[rows_q, :wide], ref[rows_q, wide:]
+                totals[1][q, :, lanes] = jnp.where(x == 0, left, right).astype(bf16)
+                give_square[q, :, lanes] = jnp.where(x == 0, right, left).astype(bf16)
+            to_x(1, q).start()
+        for copy in weight_copies():
+            copy.wait()
+
+    @pl.when(step >= blocks)
+    def _():
+        now = 2 * blocks - 1 - step
+        here = pl.ds(pl.multiple_of(now * block, block), block)
+        lows = (q_all[here], k_all[here], v_all[here])
+        rows, d_mix, d_z, d_normed = lower_second(
+            0.0, now == 0, lows, dskip, dz, mix_ref, mix_before, normed,
+            w_q, w_k, w_v, w_mix, w_gate, taps_w, taps_b, g_gain, g_small, later,
+        )
+        rows_all[here] = rows
+        lifted_all[here] = d_mix
+        part_all[now] = d_normed.astype(bf16)
+        to_c(now).start()
+        pl.when(now < blocks - 1)(lambda: core_step(now + 1))
+
+    def at_end(when, *work):
+        @pl.when(step == blocks + when)
+        def _():
+            for do in work:
+                do()
+
+    def spread_down():
+        span = dn_go.shape[2]
+        for cc in range(2):
+            dn_go[cc] = ends[2][:, span * cc : span * cc + span].astype(bf16)
+            left_here = jnp.logical_and(home, c == cc)
+
+            @pl.when(left_here)
             def _():
-                up_out[:, cols * yy : cols * yy + cols] = mine
-
-    use_up(up_end[...])
-    up_to_y = remote(up_go, up_got, up_sem.at[0], up_sem.at[1], device(z, 1 - y, c))
-    up_to_y.start()
-
-    tall, wide = sq_got.shape[1], sq_got.shape[2] // 3
-
-    def use_square(value):
+                dn_got[low] = dn_go[cc]
+
+            pl.when(jnp.logical_not(left_here))(lambda: down_to(cc).start())
+
+    def every(do, p):
+        return [partial(do, p, q) for q in range(4)]
+
+    at_end(1, *every(x_step, 2))
+    at_end(3, partial(x_step, 1, 0))
+    at_end(4, *every(near_step, 2))
+    at_end(5, partial(x_step, 1, 1), partial(near_step, 1, 0))
+    at_end(6, partial(row_step, 3))
+    at_end(7, partial(x_step, 1, 2), partial(near_step, 1, 1), *every(far_step, 2), spread_down)
+
+    @pl.when(step == 2 * blocks - 1)
+    def _():
+        small_to_x().start()
+        for q in range(4):
+            got = mm_tn(rows_all[:, block * q : block * q + block], lifted_all[...]).astype(bf16)
+            given = lifted_ref[up_rows(q)]
+            totals[0][q] = jnp.where(x == 0, got, given)
+            give_up[q] = jnp.where(x == 0, given, got)
+            if q < 2:
+                to_x(0, q).start()
+            if q == 0:
+                core_step(0)
+        row_step(2)
+        x_step(1, 3)
+        near_step(1, 2)
+        row_step(1)
+        x_step(0, 0)
+        to_x(0, 2).start()
+        near_step(1, 3)
+        far_step(1, 0)
+        far_step(1, 1)
+        small_to_x().wait_recv()
+        small_sum[...] = g_small[...] + small_x[...]
+        small_z[z] = small_sum[...]
+        for k in range(3):
+            small_to_z(k).start()
+        row_step(0)
+        x_step(0, 1)
+        to_x(0, 3).start()
+        near_step(0, 0)
+        far_step(1, 2)
+        far_step(1, 3)
         for yy in range(2):
             for cc in range(2):
                 for a in range(3):
-                    sq_go[yy, cc, :, wide * a : wide * a + wide] = value[
-                        tall * yy : tall * yy + tall,
-                        (2 * a + cc) * wide : (2 * a + cc) * wide + wide,
+                    sq_go[yy, cc, :, tall * a : tall * a + tall] = ends[1][
+                        tall // 2 * yy : tall // 2 * yy + tall // 2,
+                        (2 * a + cc) * tall : (2 * a + cc) * tall + tall,
                     ].astype(bf16)
-
-    use_square(sq_end[...])
-    sq_got[head] = sq_go[y, c]
-
-    def square_to(k):
-        yy, cc = group[k]
-        return to_group(k, sq_go.at[yy, cc], sq_got.at[head], sq_sent, sq_landed.at[head])
-
-    def square_from(k):
-        at = 2 * group[k][1] + group[k][0]
-        return to_group(k, sq_go.at[0, 0], sq_got.at[at], sq_sent, sq_landed.at[at])
-
-    for k in range(3):
-        square_to(k).start()
-
-    span = dn_go.shape[2]
-
-    def use_down(value):
+        sq_got[head] = sq_go[y, c]
+        for k in range(3):
+            square_to(k).start()
+        for k in range(3):
+            small_from_z(k).wait_recv()
+        total = small_z[0]
+        for zz in range(1, 4):
+            total = total + small_z[zz]
+        small_all[head] = total
+        for k in range(3):
+            small_to_head(k).start()
+        x_step(0, 2)
+        near_step(0, 1)
+        far_step(0, 0)
+        x_step(0, 3)
+        near_step(0, 2)
+        far_step(0, 1)
+        near_step(0, 3)
+        far_step(0, 2)
+        far_step(0, 3)
+        value = ends[0][...]
+        mine = jnp.where(y == 0, value[:half], value[half:])
+        up_go[...] = jnp.where(y == 0, value[half:], value[:half]).astype(bf16)
+        up_to_y().start()
+        for yy in range(2):
+
+            @pl.when(y == yy)
+            def _():
+                up_out[:, size * yy : size * yy + size] = mine
+
+        for m in range(2):
+            for cc in range(2):
+                own_part = jnp.logical_and(2 * c + m == z, c == cc)
+                landed = remote(
+                    to_owner.at[0], owned.at[m, cc], o_sent.at[0], o_landed.at[m, cc],
+                    device(2 * c + m, y, cc),
+                )
+                pl.when(jnp.logical_not(own_part))(lambda: landed.wait_recv())
+                rows_here = pl.ds(cc * half, half)
+                row_hat, rstd = normalize(rows_ref[m, rows_here].astype(f32))
+                scaled = owned[m, cc].astype(f32) * gain_ref[...]
+                d_row = rstd * (
+                    scaled
+                    - jnp.mean(scaled, axis=-1, keepdims=True)
+                    - row_hat * jnp.mean(scaled * row_hat, axis=-1, keepdims=True)
+                )
+                grad_out[m, rows_here] = (cot_ref[m, rows_here].astype(f32) + d_row).astype(bf16)
+
+        for k in range(3):
+            small_from_head(k).wait_recv()
+        small_out[...] = small_all[...]
+        for k in range(3):
+            square_from(k).wait_recv()
+        for a, ref in enumerate((query_out, key_out, value_out)):
+            ref[...] = sq_got[:, :, tall * a : tall * a + tall].astype(f32)
+        for k in range(2):
+            mine = jnp.logical_and(home, jnp.logical_and(low == k, z // 2 == c))
+            pl.when(jnp.logical_not(mine))(lambda: down_from(k).wait_recv())
+            deep = dn_got.shape[1]
+            down_out[deep * k : deep * k + deep] = dn_got[k].astype(f32)
+        up_to_y().wait_recv()
+        for yy in range(2):
+
+            @pl.when(y == yy)
+            def _():
+                up_out[:, size * (1 - yy) : size * (1 - yy) + size] = up_got[...].astype(f32)
+
+        small_to_x().wait_send()
+        up_to_y().wait_send()
+        for p in range(3):
+            for q in range(4):
+                to_x(p, q).wait_send()
+                pl.when(low != q % 2)(lambda: to_near(p, q).wait_send())
+                passes = jnp.logical_and(low == q % 2, high != q // 2)
+                pl.when(passes)(lambda: to_far(p, q).wait_send())
+        for at in range(blocks):
+            to_c(at).wait_send()
+        for zz in range(4):
+            to_y(zz).wait_send()
+            pl.when(jnp.logical_not(stays(zz)))(lambda: to_o(zz).wait_send())
+        for k in range(3):
+            small_to_z(k).wait_send()
+            small_to_head(k).wait_send()
+            square_to(k).wait_send()
         for cc in range(2):
-            dn_go[cc] = value[:, span * cc : span * cc + span].astype(bf16)
-
-    use_down(dn_end[...])
-
-    def down_to(cc):
-        return remote(
-            dn_go.at[cc], dn_got.at[lax.rem(z, 2)], dn_sent.at[cc], dn_landed.at[lax.rem(z, 2)],
-            device(head, z // 2, cc),
-        )
-
-    def down_from(k):
-        return remote(
-            dn_go.at[0], dn_got.at[k], dn_sent.at[0], dn_landed.at[k],
-            device(2 * y + k, lax.rem(z, 2), z // 2),
-        )
-
-    home = jnp.logical_and(head == z, z // 2 == y)
-    for cc in range(2):
-        stays = jnp.logical_and(home, c == cc)
-
-        @pl.when(stays)
-        def _():
-            dn_got[lax.rem(z, 2)] = dn_go[cc]
-
-        pl.when(jnp.logical_not(stays))(lambda: down_to(cc).start())
-
-    for m in range(2):
-        for cc in range(2):
-            own_part = jnp.logical_and(2 * c + m == z, c == cc)
-            landed = remote(
-                to_owner.at[0], owned.at[m, cc], o_sent.at[0], o_landed.at[m, cc],
-                device(2 * c + m, y, cc),
-            )
-            pl.when(jnp.logical_not(own_part))(lambda landed=landed: landed.wait_recv())
-        for cc in range(2):
-            here = pl.ds(cc * half, half)
-            row_hat, rstd = normalize(rows_ref[m, here].astype(f32))
-            scaled = owned[m, cc].astype(f32) * gain_ref[...]
-            d_row = rstd * (
-                scaled
-                - jnp.mean(scaled, axis=-1, keepdims=True)
-                - row_hat * jnp.mean(scaled * row_hat, axis=-1, keepdims=True)
-            )
-            grad_out[m, here] = (cot_ref[m, here].astype(f32) + d_row).astype(bf16)
-
-    up_to_y.wait_recv()
-    for yy in range(2):
-
-        @pl.when(y == yy)
-        def _():
-            up_out[:, cols * (1 - yy) : cols * (1 - yy) + cols] = up_got[...].astype(f32)
-
-    for k in range(3):
-        small_from_head(k).wait_recv()
-    small_out[...] = small_all[...]
-    for k in range(3):
-        square_from(k).wait_recv()
-    for a, ref in enumerate((query_out, key_out, value_out)):
-        ref[...] = sq_got[:, :, wide * a : wide * a + wide].astype(f32)
-    for k in range(2):
-        mine = jnp.logical_and(home, jnp.logical_and(lax.rem(z, 2) == k, z // 2 == c))
-        pl.when(jnp.logical_not(mine))(lambda: down_from(k).wait_recv())
-        tall = dn_got.shape[1]
-        down_out[tall * k : tall * k + tall] = dn_got[k].astype(f32)
-
-    small_to_x.wait_send()
-    up_to_y.wait_send()
-    for n in range(count):
-        to_x(n).wait_send()
-        to_near(n).wait_send()
-        pl.when(high != items[n][1])(lambda: to_far(n).wait_send())
-    for yy, at in ((1 - y, 0), (y, 4)):
-        for zz in range(4):
-            to_c(zz, yy, at + zz).wait_send()
-    for zz in range(4):
-        to_y(zz).wait_send()
-        stays = jnp.logical_and(z == zz, z // 2 == c)
-        pl.when(jnp.logical_not(stays))(lambda: to_o(zz).wait_send())
-    for k in range(3):
-        small_to_z(k).wait_send()
-        small_to_head(k).wait_send()
-        square_to(k).wait_send()
-    for cc in range(2):
-        stays = jnp.logical_and(home, c == cc)
-        pl.when(jnp.logical_not(stays))(lambda: down_to(cc).wait_send())
-
-
-def finish(part, up, square, down, small, rows, cot, gain):
+            left_here = jnp.logical_and(home, c == cc)
+            pl.when(jnp.logical_not(left_here))(lambda: down_to(cc).wait_send())
+
+
+def drain(inputs, down, lifted, rows, cot, gain):
+    (d_gate, dq, dk, dv, dskip, dz, mix, conv, q, k, v, normed,
+     w_query, w_key, w_value, w_up, conv_w, conv_b, gate_pairs, g_gain) = inputs
+    tokens, size = q.shape
     micro, block, width = rows.shape
     half = block // 2
-    size = down.shape[1]
-    lines = small.shape[0]
-    scratch = [
-        ((8, half, width), bf16), ((8, half, width), bf16), ((4, half, width), bf16),
+    lines = 40
+    steps = tokens // block
+    early = lambda g: jnp.minimum(g, steps - 1)
+    late = lambda g: jnp.minimum(2 * steps - 1 - g, steps - 1)
+    both = lambda g: jnp.where(g < steps, g, 2 * steps - 1 - g)
+    by_row = lambda n, at: pl.BlockSpec((block, n), lambda g: (at(g), 0))
+    kept = lambda value: pl.BlockSpec(
+        value.shape, lambda g: (0,) * value.ndim, pipeline_mode=pl.Buffered(1)
+    )
+    anywhere = pl.BlockSpec(memory_space=pl.ANY)
+    arguments = (
+        d_gate, dq, dk, dv, mix, conv, q, k, v, dskip, dz, mix, normed, gate_pairs, g_gain,
+        w_query, w_key, w_value, w_up, conv_w, conv_b, down, lifted, rows, cot, gain,
+    )
+    specs = [pl.BlockSpec((8, block), lambda g: (0, early(g)))] + [by_row(size, early)] * 3
+    specs += [by_row(size, both)] + [by_row(size, early)] * 4 + [by_row(size, late)] * 2
+    specs += [
+        pl.BlockSpec((16, size), lambda g: (jnp.maximum(late(g) * (block // 16) - 1, 0), 0)),
+        by_row(width, late), kept(gate_pairs), kept(g_gain),
+    ]
+    specs += [anywhere] * 6 + [kept(value) for value in (down, lifted, rows, cot, gain)]
+    scratch = [((size, size), bf16)] * 3 + [((width, size), bf16)] * 2
+    scratch += [((4, size), f32), ((1, size), f32)] + [((tokens, size), bf16)] * 3
+    scratch += [((size, size), f32)] * 3 + [((lines, size), f32), ((8, size), f32)]
+    scratch += [((tokens, width), bf16), ((tokens, size), bf16), ((8, block, width), bf16)]
+    scratch += [
+        ((8, half, width), bf16), ((4, half, width), bf16), ((4, half, width), bf16),
         ((4, half, width), bf16), ((4, half, width), bf16), ((2, 2, half, width), bf16),
     ]
-    for piece in (up, square, down):
-        _, tall, wide = piece.shape
-        scratch += [((tall, wide), bf16), ((4, tall // 4, wide), bf16)]
-        scratch += [((2, tall // 4, wide), bf16)] * 2
-        scratch += [((tall // 4, wide), bf16), ((tall // 4, wide), f32)]
+    pieces = [(width // 4, size), (size // 4, 3 * size // 2), (size // 4, width // 2)]
+    scratch += [((4, *piece), bf16) for piece in pieces[:2]]
+    for piece in pieces:
+        scratch += [((4, *piece), bf16)] * 2 + [((2, *piece), bf16)] * 2
+        scratch += [(piece, bf16), (piece, f32)]
     scratch += [
         ((width // 8, size), bf16), ((width // 8, size), bf16),
         ((2, 2, size // 8, 3 * size // 4), bf16), ((4, size // 8, 3 * size // 4), bf16),
         ((2, size // 4, width // 4), bf16), ((2, size // 4, width // 4), bf16),
         ((lines, size), f32), ((lines, size), f32), ((4, lines, size), f32), ((4, lines, size), f32),
     ]
-    sems = [
-        (8,), (8,), (8,), (4,), (4,), (4,), (2, 2), (8,), (8,), (8,), (8,), (8,), (8,),
-        (2,), (3,), (4,), (2,), (2,), (2,), (3,), (4,), (3,), (4,),
+    sems = [(8,), (8,), (4,), (4,), (4,), (2, 2)] + [(3, 4)] * 6
+    sems += [(7,), (2,), (3,), (4,), (2,), (2,), (2,), (3,), (4,), (3,), (4,)]
+    square = struct((4, size // 8, size // 4), f32)
+    outs = [
+        struct(rows.shape, bf16), struct((width // 8, 2 * size), f32), square, square, square,
+        struct((size // 2, width // 4), f32), struct((4, lines, size), f32),
     ]
-    vmem = pl.BlockSpec(memory_space=pltpu.VMEM)
-    square_shape = struct((4, size // 8, size // 4), f32)
     return pl.pallas_call(
-        finish_kernel,
-        out_shape=[
-            struct(rows.shape, bf16), struct((width // 8, 2 * size), f32),
-            square_shape, square_shape, square_shape,
-            struct((size // 2, width // 4), f32), struct((4, lines, size), f32),
-        ],
-        in_specs=[pl.BlockSpec(memory_space=pl.ANY)] + [vmem] * 7,
-        out_specs=[vmem] * 7,
+        drain_kernel,
+        grid=(2 * steps,),
+        in_specs=specs,
+        out_specs=[kept(value) for value in outs],
         scratch_shapes=[pltpu.VMEM(shape, dtype) for shape, dtype in scratch]
         + [pltpu.SemaphoreType.DMA(shape) for shape in sems],
+        out_shape=outs,
         compiler_params=pltpu.CompilerParams(
-            collective_id=1, has_side_effects=True, vmem_limit_bytes=vmem_bytes
+            dimension_semantics=("arbitrary",), collective_id=1, has_side_effects=True,
+            vmem_limit_bytes=60 * 2**20,
         ),
-        name="finish",
-    )(part, up, square, down, small, rows, cot, gain)
+        cost_estimate=pl.CostEstimate(
+            flops=2 * tokens * size * (6 * size + 4 * width), bytes_accessed=48 * 2**20,
+            transcendentals=0,
+        ),
+        name="drain",
+    )(*arguments)
 
 
 def swap(value, axis, mask):
@@ -1397,13 +1531,13 @@
     if ranges > 1:
         after = (jnp.zeros((size, size), f32), jnp.zeros((8, size), f32))
         *_, d_state, d_norm = cell_backward(
-            head, rows, q, k, v, conv, gate_z, head_normed, states, norms, weights, cols, cot,
+            head, rows, q, k, v, conv, gate_z, head_normed, states, norms, weights, cols, cot, normed,
             out_row, skip_row, w_down, *after,
         )
         keep = jnp.exp(total + first[2][0, 0] - last[2][0, 0])
         after = cotangent_after(d_state, d_norm, keep, ranges)
-    dq, dk, dv, dskip, dz, d_rows, g_down, g_gain, *_ = cell_backward(
-        head, rows, q, k, v, conv, gate_z, head_normed, states, norms, weights, cols, cot,
+    dq, dk, dv, dskip, dz, d_rows, g_down, g_z, g_gain, *_ = cell_backward(
+        head, rows, q, k, v, conv, gate_z, head_normed, states, norms, weights, cols, cot, normed,
         out_row, skip_row, w_down, *after,
     )
     part_row, d_rows = hold(part_row, d_rows)
@@ -1413,26 +1547,24 @@
     d_gate = total_over_heads(d_gate)
     part, d_gate = hold(part, d_gate)
     part_across = sent_across(part, z)
-    first = ()
-    if ranges > 1:
-        *_, later = lower(
-            head, d_gate, dq, dk, dv, dskip, dz, mix, conv, q, k, v, normed,
-            w_query, w_key, w_value, w_up, conv_w, conv_row, gate_pairs, g_gain,
-            halo[0], jnp.zeros((8, size), f32),
-        )
-        first = (halo[0], shifted(later, "seq", -8))
-    d_part, square, up, small, *_ = lower(
-        head, d_gate, dq, dk, dv, dskip, dz, mix, conv, q, k, v, normed,
-        w_query, w_key, w_value, w_up, conv_w, conv_row, gate_pairs, g_gain, *first,
-    )
+    lower_args = (
+        d_gate, dq, dk, dv, dskip, dz, mix, conv, q, k, v, normed,
+        w_query, w_key, w_value, w_up, conv_w, conv_row, gate_pairs, g_gain,
+    )
+    if direct:
+        grad_rows, s_up, s_query, s_key, s_value, s_down, small = drain(
+            lower_args, g_down, g_z, tokens[:, 0], d_out[:, 0], ln_gain[None]
+        )
+    else:
+        first = ()
+        if ranges > 1:
+            *_, later = lower(head, *lower_args, halo[0], jnp.zeros((8, size), f32))
+            first = (halo[0], shifted(later, "seq", -8))
+        d_part, square, up, small, *_ = lower(head, *lower_args, *first)
     part_across, small = hold(part_across, small)
     block_rows = scatter_last(in_order(part_across, z))
     block_rows = (tokens[:, 0].astype(f32) + block_rows).astype(bf16)
-    if direct:
-        grad_rows, s_up, s_query, s_key, s_value, s_down, small = finish(
-            d_part, up, square, g_down, small, tokens[:, 0], d_out[:, 0], ln_gain[None]
-        )
-    else:
+    if not direct:
         d_normed = scatter_sequence(d_part)
         row_f = tokens[:, 0].astype(f32)
         centre = row_f - jnp.mean(row_f, axis=-1, keepdims=True)

time: 307 us -> 285 us (0.928)
  Pallas kernels: 226 us -> 211 us
    pallas_call x4 -> x3, Pallas kernels: 91.2 us -> 60.5 us  [run_kernel(): pl.pallas_call(body, grid_spec=pltpu.PrefetchScalarGridSpec(num_scalar_pr...]
    pallas_call x1, Pallas kernels: 98.8 us -> 114 us  [drain(): pl.pallas_call(drain_kernel, grid=(2 * steps,), in_specs=specs, out_specs...]
    unnamed x44 -> x46, local copies, waits for them, and re-layouts: 9.39 us -> 10 us
  transfers between devices with their start and end apart: 16 -> 16, of which waited for: 7 -> 7; matrix products, arithmetic and copies ran while one was open for 7% -> 5% of each run, Pallas kernels for 74% -> 74%
where the time goes in v4:
time: 285 us; the launch traced here: 284 us
  Pallas kernels  211 us (74%)
  starting transfers between devices  19.8 us (7%)
  local copies, waits for them, and re-layouts  18.4 us (6%)
  waiting for transfers between devices  18.4 us (6%)
  other arithmetic  16.1 us (6%)
    pallas_call x1, Pallas kernels, drain(): pl.pallas_call(drain_kernel, grid=(2 * steps,), in_specs=specs, out_specs...  114 us
    pallas_call x3, Pallas kernels, run_kernel(): pl.pallas_call(body, grid_spec=pltpu.PrefetchScalarGridSpec(num_scalar_pr...  60.5 us
    pallas_call x1, Pallas kernels, gather_normed(): pl.pallas_call(gather_kernel, out_shape=struct((8 * block, width), bf16),...  36.2 us
    ppermute x16, starting transfers between devices, swap(): return lax.ppermute(value, axis, [(s, s ^ mask) for s in range(count)])  19.8 us
    ppermute x16, waiting for transfers between devices, swap(): return lax.ppermute(value, axis, [(s, s ^ mask) for s in range(count)])  18.4 us
    unnamed x46, local copies, waits for them, and re-layouts  10 us
    select_n x3, other arithmetic, paired(): jnp.where(bit == 0, jnp.concatenate([mine, other], dim), jnp.concatenate(...  7.37 us
  transfers between devices with their start and end apart: 16, of which 7 were waited for; matrix products, arithmetic and copies ran while one was open for 5% of the time, Pallas kernels for 74%

profile of v4, /device:TPU:24, one launch (start us, length us, event | category | flops | bytes accessed | tf_op | source)
XLA Modules:
  0.0 284.4 jit_solution(634811752551341819)
XLA Ops:
  0.9 1.2 copy-done.1
  2.1 0.7 copy-done.3
  2.8 36.2 %gather_normed.1.normed.rows_in = bf16[2048,1024]{1,0:T(8,128)(2,1)S(1)} custom-call(bf16[2,256,1024]{2,1,0:T(8,128)(2,1)S(1)} %bitcast.81, f32[1,1024]{1,0:T(1,128)S(1)} %bitcast.83), custom_call_target="tpu_custom_call" | custom-call | tf_op jit(solution)/shard_map/gather_normed/pallas_call | solution.py:838
  39.1 2.0 copy-done
  41.1 0.7 maximum_maximum_fusion.gate_w
  42.3 6.5 %collective-permute-start.2 = (bf16[256,512]{1,0:T(8,128)(2,1)S(1)}, bf16[256,512]{1,0:T(8,128)(2,1)S(1)}, u32[]{:S(2)}, u32[]{:S(2)}) collective-permute-start(bf16[256,512]{1,0:T(8,128)(2,1)S(1)} %get-tuple-element.167), channel_id=1, source_target_pairs={{0,16},{4,20},{8,24},{12,28},{16,0},{20,4},{24,8},{28,12},{1,17},{... | collective-permute-start | bytes 786440 | tf_op jit(solution)/shard_map/ppermute | solution.py:1321
  48.9 1.4 collective-permute-start.3
  50.3 14.3 %lift.1 = (bf16[2048,512]{1,0:T(8,128)(2,1)}, bf16[2048,512]{1,0:T(8,128)(2,1)}, bf16[2048,512]{1,0:T(8,128)(2,1)}, bf16[2048,512]{1,0:T(8,128)(2,1)}, bf16[2048...) custom-call(s32[1]{0:T(128)} %bitcast.7.head_ref, bf16[2048,1024]{1,0:T(8,128)(2,1)} %copy-done, ...), custom_call_target="tpu_custom_call" | custom-call | flops 7516192768 | bytes 25165824 | tf_op jit(solution)/shard_map/lift/pallas_call | solution.py:488
  64.5 3.7 %collective-permute-done.3 = bf16[256,512]{1,0:T(8,128)(2,1)S(1)} collective-permute-done((bf16[256,512]{1,0:T(8,128)(2,1)S(1)}, bf16[256,512]{1,0:T(8,128)(2,1)S(1)}, u32[]{:S(2)}, u32[]{:S(2)}) %collective-permute-start.3) | collective-permute-done | bytes 262176 | tf_op jit(solution)/shard_map/ppermute | solution.py:1321
  68.5 1.2 collective-permute-done.4
  69.9 4.1 %collective-permute-done.5 = f32[8,2048]{1,0:T(8,128)S(1)} collective-permute-done((f32[8,2048]{1,0:T(8,128)S(1)}, f32[8,2048]{1,0:T(8,128)S(1)}, u32[]{:S(2)}, u32[]{:S(2)}) %collective-permute-start.5) | collective-permute-done | bytes 65568 | tf_op jit(solution)/shard_map/ppermute | solution.py:1321
  74.3 0.6 dynamic_slice.96
  74.9 0.7 constant_dynamic-slice_fusion.7
  75.5 0.6 pad_maximum_fusion.4.gates
  76.2 16.6 %cell_forward.1 = (bf16[2048,1024]{1,0:T(8,128)(2,1)}, f32[2048,512]{1,0:T(8,128)}, bf16[8,512,512]{2,1,0:T(8,128)(2,1)}, f32[8,8,512]{2,1,0:T(8,128)}, bf16[204...) custom-call(s32[1]{0:T(128)} %bitcast.7.head_ref, f32[2,2048]{1,0:T(2,128)} %pad_maximum_fusion.4.gates, ...), custom_call_target="tpu_custom_call" | custom-call | flops 5368709120 | bytes 29360128 | tf_op jit(solution)/shard_map/cell_forward/pallas_call | solution.py:488
  92.7 5.4 %collective-permute-done.6 = bf16[4,1,256,512]{3,2,0,1:T(8,128)(2,1)S(1)} collective-permute-done((bf16[4,1,256,512]{3,2,0,1:T(8,128)(2,1)S(1)}, bf16[4,1,256,512]{3,2,0,1:T(8,128)(2,1)S(1)}, u32[]{:S(2)}, u32[]{:S(2)}) %collective-permute-start.6) | collective-permute-done | bytes 1048608 | tf_op jit(solution)/shard_map/ppermute | solution.py:1321
  98.2 1.0 copy-done.5
  99.2 2.1 maximum_select_fusion.1
  101.4 3.1 %constant_dynamic-slice_fusion.6 = bf16[4,2,128,1024]{3,2,1,0:T(8,128)(2,1)} fusion(bf16[4,2,256,1024]{3,2,1,0:T(8,128)(2,1)} %bitcast.88, s32[]{:T(128)S(6)} %select_n.155), kind=kLoop, calls=%fused_computation.52 | loop fusion | bytes 4194308 | tf_op jit(solution)/shard_map/dynamic_slice | solution.py:1326
  104.5 0.5 collective-permute-start.7
  105.0 0.7 collective-permute-done.8
  105.7 5.0 %maximum_select_fusion.cot_ref = bf16[2048,1024]{1,0:T(8,128)(2,1)} fusion(bf16[2048,512]{1,0:T(8,128)(2,1)} %bitcast.25, bf16[2048,512]{1,0:T(8,128)(2,1)S(1)} %bitcast.86, pred[]{:T(512)S(6)} %eq.39), kind=kLoop, calls=%fused_computation | loop fusion | flops 18874368 | bytes 8388609 | tf_op jit(solution)/shard_map/jit(_where)/select_n | solution.py:1335
  110.7 2.6 add_convert_fusion
  113.3 0.9 collective-permute-start.9
  114.2 29.7 %cell_backward.1 = (f32[2048,512]{1,0:T(8,128)}, f32[2048,512]{1,0:T(8,128)}, f32[2048,512]{1,0:T(8,128)}, f32[2048,512]{1,0:T(8,128)}, bf16[2048,512]{1,0:T(8,1...) custom-call(s32[1]{0:T(128)} %bitcast.7.head_ref, ...), custom_call_target="tpu_custom_call" | custom-call | flops 10737418240 | bytes 46137344 | tf_op jit(solution)/shard_map/cell_backward/pallas_call | solution.py:488
  143.9 0.9 fusion.9
  145.0 0.7 copy.45
  145.7 0.5 collective-permute-done.10
  146.3 1.3 collective-permute-start.11
  148.0 2.6 collective-permute-done.11
  150.6 0.7 fusion.10.d_gate
  151.4 5.2 %collective-permute-start.12 = (bf16[128,1024]{1,0:T(8,128)(2,1)S(1)}, bf16[128,1024]{1,0:T(8,128)(2,1)S(1)}, u32[]{:S(2)}, u32[]{:S(2)}) collective-permute-start(bf16[128,1024]{1,0:T(8,128)(2,1)S(1)} %get-tuple-element.160), channel_id=1, source_target_pairs={{0,8},{4,12},{8,0},{12,4},{16,24},{20,28},{24,16},{28,20},{1,9},{5... | collective-permute-start | bytes 786440 | tf_op jit(solution)/shard_map/ppermute | solution.py:1321
  156.7 2.0 collective-permute-start.13
  158.6 1.4 collective-permute-start.14
  160.0 113.8 %drain.1 = (bf16[2,256,1024]{2,1,0:T(8,128)(2,1)}, f32[128,1024]{1,0:T(8,128)}, f32[4,64,128]{2,1,0:T(8,128)}, f32[4,64,128]{2,1,0:T(8,128)}, f32[4,64,128]{2,1,...) custom-call(f32[8,2048]{1,0:T(8,128)} %fusion.10.d_gate, f32[2048,512]{1,0:T(8,128)} %get-tuple-element.97.dq, ...), custom_call_target="tpu_custom_call" | custom-call | flops 15032385536 | bytes 50331648 | tf_op jit(solution)/shard_map/drain/pallas_call | solution.py:1299
  274.5 0.6 copy-done.11
  275.1 0.6 slice.30
  275.7 0.7 copy.42
  276.4 0.6 div.14
  277.0 0.6 slice_reduce_fusion.1
  277.7 0.6 fusion.8
  278.3 1.6 add_convert_fusion.1
  280.0 1.0 copy.59
  280.9 0.8 copy.60
  281.7 0.7 copy.61
  282.4 0.7 copy.62
  283.1 0.7 copy.63
  283.7 0.7 copy.64
  (77 shorter events, 2.8 us)
Async XLA Ops:
  0.6 41.2 %collective-permute-start = (bf16[2,256,1024]{2,1,0:T(8,128)(2,1)}, bf16[2,256,1024]{2,1,0:T(8,128)(2,1)S(1)}, u32[]{:S(2)}, u32[]{:S(2)}) collective-permute-start(bf16[2,256,1024]{2,1,0:T(8,128)(2,1)} %bitcast.90), channel_id=1, source_target_pairs={{0,1},{1,0},{2,3},{3,2},{4,5},{5,4},{6,7},{7,6},{8,9},{9,8},{10,11... | collective-permute-start | bytes 3145736 | tf_op jit(solution)/shard_map/ppermute | solution.py:1321
  0.9 1.2 copy-start.1
  2.1 0.7 copy-start.3
  2.8 38.2 %copy-start.15 = (f32[6144,8]{0,1:T(8,128)S(1)}, f32[6144,8]{0,1:T(8,128)}, u32[]{:S(2)}) copy-start(f32[6144,8]{0,1:T(8,128)} %param.22) | copy-start | bytes 589828
  2.8 39.1 %copy-start.7 = (bf16[2,1,256,1024]{3,2,1,0:T(8,128)(2,1)S(1)}, bf16[2,1,256,1024]{3,2,1,0:T(8,128)(2,1)}, u32[]{:S(2)}) copy-start(bf16[2,1,256,1024]{3,2,1,0:T(8,128)(2,1)} %param.27) | copy-start | bytes 3145732
  39.1 2.0 copy-start
  42.2 22.3 %collective-permute-start.1 = (bf16[256,512]{1,0:T(8,128)(2,1)S(1)}, bf16[256,512]{1,0:T(8,128)(2,1)S(1)}, u32[]{:S(2)}, u32[]{:S(2)}) collective-permute-start(bf16[256,512]{1,0:T(8,128)(2,1)S(1)} %get-tuple-element.168), channel_id=1, source_target_pairs={{0,8},{4,12},{8,0},{12,4},{16,24},{20,28},{24,16},{28,20},{1,9},{5... | collective-permute-start | bytes 786440 | tf_op jit(solution)/shard_map/ppermute | solution.py:1321
  42.3 22.2 %collective-permute-start.2 = (bf16[256,512]{1,0:T(8,128)(2,1)S(1)}, bf16[256,512]{1,0:T(8,128)(2,1)S(1)}, u32[]{:S(2)}, u32[]{:S(2)}) collective-permute-start(bf16[256,512]{1,0:T(8,128)(2,1)S(1)} %get-tuple-element.167), channel_id=1, source_target_pairs={{0,16},{4,20},{8,24},{12,28},{16,0},{20,4},{24,8},{28,12},{1,17},{... | collective-permute-start | bytes 786440 | tf_op jit(solution)/shard_map/ppermute | solution.py:1321
  48.9 19.3 %collective-permute-start.3 = (bf16[256,512]{1,0:T(8,128)(2,1)S(1)}, bf16[256,512]{1,0:T(8,128)(2,1)S(1)}, u32[]{:S(2)}, u32[]{:S(2)}) collective-permute-start(bf16[256,512]{1,0:T(8,128)(2,1)S(1)} %get-tuple-element.166), channel_id=1, source_target_pairs={{0,24},{4,28},{8,16},{12,20},{16,8},{20,12},{24,0},{28,4},{1,25},{... | collective-permute-start | bytes 786440 | tf_op jit(solution)/shard_map/ppermute | solution.py:1321
  68.2 1.5 collective-permute-start.4
  68.2 1.5 copy-start.16
  68.4 5.9 %copy-start.17 = (f32[4]{0:T(128)S(1)}, f32[4]{0:T(128)}, u32[]{:S(2)}) copy-start(f32[4]{0:T(128)} %param.23) | copy-start | bytes 52
  69.7 4.3 %collective-permute-start.5 = (f32[8,2048]{1,0:T(8,128)S(1)}, f32[8,2048]{1,0:T(8,128)S(1)}, u32[]{:S(2)}, u32[]{:S(2)}) collective-permute-start(f32[8,2048]{1,0:T(8,128)S(1)} %add.124), channel_id=1, source_target_pairs={{0,4},{4,0},{8,12},{12,8},{16,20},{20,16},{24,28},{28,24},{1,5},{5... | collective-permute-start | bytes 196616 | tf_op jit(solution)/shard_map/ppermute | solution.py:1321
  74.0 24.1 %collective-permute-start.6 = (bf16[4,1,256,512]{3,2,0,1:T(8,128)(2,1)S(1)}, bf16[4,1,256,512]{3,2,0,1:T(8,128)(2,1)S(1)}, u32[]{:S(2)}, u32[]{:S(2)}) collective-permute-start(bf16[4,1,256,512]{3,2,0,1:T(8,128)(2,1)S(1)} %bitcast.84), channel_id=1, source_target_pairs={{0,4},{4,0},{8,12},{12,8},{16,20},{20,16},{24,28},{28,24},{1,5},{5... | collective-permute-start | bytes 3145736 | tf_op jit(solution)/shard_map/ppermute | solution.py:1321
  98.2 1.0 copy-start.5
  101.3 4.4 %collective-permute-start.8 = (bf16[4,2,256,512]{3,2,1,0:T(8,128)(2,1)S(1)}, bf16[4,2,256,512]{3,2,1,0:T(8,128)(2,1)}, u32[]{:S(2)}, u32[]{:S(2)}) collective-permute-start(bf16[4,2,256,512]{3,2,1,0:T(8,128)(2,1)S(1)} %maximum_select_fusion.1), channel_id=1, source_target_pairs={{0,1},{1,0},{2,3},{3,2},{4,5},{5,4},{6,7},{7,6},{8,9},{9,8},{10,11... | collective-permute-start | bytes 6291464 | tf_op jit(solution)/shard_map/ppermute | solution.py:1321
  104.5 6.2 %collective-permute-start.7 = (bf16[4,2,128,1024]{3,2,1,0:T(8,128)(2,1)}, bf16[4,2,128,1024]{3,2,1,0:T(8,128)(2,1)}, u32[]{:S(2)}, u32[]{:S(2)}) collective-permute-start(bf16[4,2,128,1024]{3,2,1,0:T(8,128)(2,1)} %constant_dynamic-slice_fusion.6), channel_id=1, source_target_pairs={{0,1},{1,0},{2,3},{3,2},{4,5},{5,4},{6,7},{7,6},{8,9},{9,8},{10,11... | collective-permute-start | bytes 6291464 | tf_op jit(solution)/shard_map/ppermute | solution.py:1321
  105.7 5.0 %copy-start.6 = (bf16[2048,1024]{1,0:T(8,128)(2,1)S(1)}, bf16[2048,1024]{1,0:T(8,128)(2,1)}, u32[]{:S(2)}) copy-start(bf16[2048,1024]{1,0:T(8,128)(2,1)} %get-tuple-element.82) | copy-start | bytes 12582916
  113.3 30.6 %collective-permute-start.9 = (bf16[4,1,128,1024]{3,2,1,0:T(8,128)(2,1)S(1)}, bf16[4,1,128,1024]{3,2,1,0:T(8,128)(2,1)S(1)}, u32[]{:S(2)}, u32[]{:S(2)}) collective-permute-start(bf16[4,1,128,1024]{3,2,1,0:T(8,128)(2,1)S(1)} %constant_dynamic-slice_fusion.5), channel_id=1, source_target_pairs={{0,4},{4,0},{8,12},{12,8},{16,20},{20,16},{24,28},{28,24},{1,5},{5... | collective-permute-start | bytes 3145736 | tf_op jit(solution)/shard_map/ppermute | solution.py:1321
  144.9 1.3 collective-permute-start.10
  146.3 4.3 %collective-permute-start.11 = (f32[8,2048]{1,0:T(8,128)S(1)}, f32[8,2048]{1,0:T(8,128)S(1)}, u32[]{:S(2)}, u32[]{:S(2)}) collective-permute-start(f32[8,2048]{1,0:T(8,128)S(1)} %fusion.6), channel_id=1, source_target_pairs={{0,4},{4,0},{8,12},{12,8},{16,20},{20,16},{24,28},{28,24},{1,5},{5... | collective-permute-start | bytes 196616 | tf_op jit(solution)/shard_map/ppermute | solution.py:1321
  151.4 122.4 %collective-permute-start.12 = (bf16[128,1024]{1,0:T(8,128)(2,1)S(1)}, bf16[128,1024]{1,0:T(8,128)(2,1)S(1)}, u32[]{:S(2)}, u32[]{:S(2)}) collective-permute-start(bf16[128,1024]{1,0:T(8,128)(2,1)S(1)} %get-tuple-element.160), channel_id=1, source_target_pairs={{0,8},{4,12},{8,0},{12,4},{16,24},{20,28},{24,16},{28,20},{1,9},{5... | collective-permute-start | bytes 786440 | tf_op jit(solution)/shard_map/ppermute | solution.py:1321
  156.7 117.2 %collective-permute-start.13 = (bf16[128,1024]{1,0:T(8,128)(2,1)S(1)}, bf16[128,1024]{1,0:T(8,128)(2,1)S(1)}, u32[]{:S(2)}, u32[]{:S(2)}) collective-permute-start(bf16[128,1024]{1,0:T(8,128)(2,1)S(1)} %get-tuple-element.159), channel_id=1, source_target_pairs={{0,16},{4,20},{8,24},{12,28},{16,0},{20,4},{24,8},{28,12},{1,17},{... | collective-permute-start | bytes 786440 | tf_op jit(solution)/shard_map/ppermute | solution.py:1321
  158.6 115.2 %collective-permute-start.14 = (bf16[128,1024]{1,0:T(8,128)(2,1)S(1)}, bf16[128,1024]{1,0:T(8,128)(2,1)S(1)}, u32[]{:S(2)}, u32[]{:S(2)}) collective-permute-start(bf16[128,1024]{1,0:T(8,128)(2,1)S(1)} %get-tuple-element.158), channel_id=1, source_target_pairs={{0,24},{4,28},{8,16},{12,20},{16,8},{20,12},{24,0},{28,4},{1,25},{... | collective-permute-start | bytes 786440 | tf_op jit(solution)/shard_map/ppermute | solution.py:1321
  274.1 1.0 copy-start.11
  274.1 2.3 copy-start.4
  274.1 4.2 %copy-start.2 = (bf16[2,1,256,1024]{3,2,1,0:T(8,128)(2,1)S(1)}, bf16[2,1,256,1024]{3,2,1,0:T(8,128)(2,1)}, u32[]{:S(2)}) copy-start(bf16[2,1,256,1024]{3,2,1,0:T(8,128)(2,1)} %param.14) | copy-start | bytes 3145732
  274.4 5.6 %copy-start.8 = (bf16[2,256,1024]{2,1,0:T(8,128)(2,1)S(1)}, bf16[2,256,1024]{2,1,0:T(8,128)(2,1)}, u32[]{:S(2)}) copy-start(bf16[2,256,1024]{2,1,0:T(8,128)(2,1)} %get-tuple-element.111) | copy-start | bytes 3145732
  274.4 3.9 %collective-permute-start.15 = (bf16[2,128,1024]{2,1,0:T(8,128)(2,1)S(1)}, bf16[2,128,1024]{2,1,0:T(8,128)(2,1)S(1)}, u32[]{:S(2)}, u32[]{:S(2)}) collective-permute-start(bf16[2,128,1024]{2,1,0:T(8,128)(2,1)S(1)} %get-tuple-element.153), channel_id=1, source_target_pairs={{0,1},{1,0},{2,3},{3,2},{4,5},{5,4},{6,7},{7,6},{8,9},{9,8},{10,11... | collective-permute-start | bytes 1572872 | tf_op jit(solution)/shard_map/ppermute | solution.py:1321
  278.3 2.6 copy-start.9
  280.0 1.8 copy-start.14
  280.0 2.4 copy-start.13
  280.0 3.1 %copy-start.12 = (f32[4,64,128]{2,1,0:T(8,128)S(1)}, f32[4,64,128]{2,1,0:T(8,128)}, u32[]{:S(2)}) copy-start(f32[4,64,128]{2,1,0:T(8,128)} %get-tuple-element.199) | copy-start | bytes 393220
  280.0 3.8 %copy-start.10 = (f32[256,256]{1,0:T(8,128)S(1)}, f32[256,256]{1,0:T(8,128)}, u32[]{:S(2)}) copy-start(f32[256,256]{1,0:T(8,128)} %get-tuple-element.204) | copy-start | bytes 786436

commit v5 on v4

--- a/solution.py
+++ b/solution.py
@@ -187,7 +187,8 @@
 
 
 def cell_forward_kernel(
-    chained, head_ref, gates, q_ref, k_ref, v_ref, conv_ref, z_ref, out_gain, skip_gain, w_down, *refs
+    chained, head_ref, gates, q_ref, k_ref, v_ref, conv_ref, z_ref, out_gain, skip_gain, w_down, *refs,
+    start=0,
 ):
     if chained:
         *first, part_out, normed_out, state_out, norm_out, weight_out, col_out, row_out = refs[:10]
@@ -199,7 +200,7 @@
     head_size = q_ref.shape[1]
     scale = head_size ** (-0.5)
 
-    @pl.when(pl.program_id(0) == 0)
+    @pl.when(pl.program_id(0) == start)
     def _():
         if chained:
             for ref, value in zip((state, norm, level), first):
@@ -435,6 +436,45 @@
         g_small[29:32, :] = g_gain[0:3, :]
 
     return rows, d_mix, d_z, d_normed
+
+
+def lower_block(
+    at_start, at_end, lows, dskip_ref, dskip_next, dz_ref, mix_ref, mix_before, mix_next, normed,
+    w_q, w_k, w_v, w_mix, w_gate, conv_w, conv_b, g_small,
+):
+    query_low, key_low, value_low = lows
+    length, size = mix_ref.shape
+    extra = mix_next.shape[0]
+    halo = jnp.where(at_start, 0.0, mix_before[8:16, :].astype(f32))
+    ext = jnp.concatenate(
+        [halo, mix_ref[...].astype(f32), mix_next[...].astype(f32)], axis=0
+    )
+    taps = conv_taps(ext, length + extra)
+    summed = conv_b[...]
+    for j in range(4):
+        summed = summed + conv_w[j : j + 1, :] * taps[j]
+    opened = jax.nn.sigmoid(summed)
+    d_conv = jnp.concatenate([dskip_ref[...], dskip_next[...]], axis=0)
+    d_conv = d_conv + mm_nt(query_low, w_q[...]) + mm_nt(key_low, w_k[...])
+    d_summed = d_conv * (opened * (1.0 + summed * (1.0 - opened)))
+    for j in range(4):
+        g_small[24 + j : 25 + j, :] += jnp.sum(
+            d_summed[:length] * taps[j][:length], axis=0, keepdims=True
+        )
+    g_small[28:29, :] += jnp.sum(d_summed[:length], axis=0, keepdims=True)
+    row = lax.broadcasted_iota(jnp.int32, d_summed.shape, 0)
+    d_summed = jnp.where(jnp.logical_and(at_end, row >= length), 0.0, d_summed)
+    d_mix = conv_w[3:4, :] * d_summed[:length]
+    for j in range(3):
+        ahead = pltpu.roll(d_summed, length + extra - (3 - j), 0)[0:length]
+        d_mix = d_mix + conv_w[j : j + 1, :] * ahead
+    d_mix = (d_mix + mm_nt(value_low, w_v[...])).astype(bf16)
+    rows = normed[...]
+    d_normed = mm_nt(d_mix, w_mix[...]) + mm_nt(dz_ref[...], w_gate[...])
+    g_ln = jnp.sum(d_normed * rows.astype(f32), axis=0, keepdims=True)
+    g_small[32:33, :] += g_ln[:, :size]
+    g_small[33:34, :] += g_ln[:, size:]
+    return rows, d_mix, d_normed
 
 
 def lower_kernel(chained, head_ref, *refs):
@@ -705,11 +745,25 @@
 MESH_ID = pl.DeviceIdType.MESH
 
 
+def halves_of(value, count):
+    whole = jnp.int32(0)
+    for bound in range(2, count, 2):
+        whole = whole + jnp.where(value >= bound, 1, 0)
+    return whole, value - 2 * whole
+
+
 def where_am_i():
     at_seq, at_batch = lax.axis_index("seq"), lax.axis_index("batch")
-    within = lax.rem(at_seq, 8)
-    first = at_seq - within
-    return first, within // 2, lax.rem(within, 2), at_batch // 2, lax.rem(at_batch, 2)
+    first = jnp.int32(0)
+    for bound in range(8, lax.axis_size("seq"), 8):
+        first = first + jnp.where(at_seq >= bound, 8, 0)
+    z, y = halves_of(at_seq - first, 8)
+    x, c = halves_of(at_batch, lax.axis_size("batch"))
+    return first, z, y, x, c
+
+
+def turn(value, count):
+    return jnp.where(value >= count, value - count, value)
 
 
 def greet(others):
@@ -729,119 +783,154 @@
     return centre * rstd, rstd
 
 
-def gather_kernel(
-    rows_ref, gain_ref, out_ref, staged, kept, z_sent, z_landed, y_sent, y_landed, c_sent, c_landed
-):
-    first, z, y, x, c = where_am_i()
-    parts = z_landed.shape[1]
+class Gather:
+    def __init__(self, source, out_ref, block, parts, sems):
+        self.source, self.out_ref, self.block, self.parts = source, out_ref, block, parts
+        self.kept, self.z_sent, self.z_landed, self.y_sent, self.y_landed, *sems = sems
+        self.c_sent, self.c_landed = sems
+        self.first, self.z, self.y, self.x, self.c = where_am_i()
+        self.size = block // parts
+        self.enters = halves_of(self.z, 4)[0] == self.c
+
+    def device(self, zz, yy, cc):
+        return (self.first + 2 * zz + yy, 2 * self.x + cc)
+
+    def others(self):
+        others = [self.device(turn(self.z + k, 4), self.y, self.c) for k in range(1, 4)]
+        return others + [self.device(self.z, 1 - self.y, self.c), self.device(self.z, self.y, 1 - self.c)]
+
+    def rows(self, zz, yy, part):
+        start = (2 * zz + yy) * self.block + part * self.size
+        return self.out_ref.at[pl.ds(pl.multiple_of(start, self.size), self.size)]
+
+    def away(self, m):
+        return 2 * self.c + m != self.z
+
+    def to_column(self, m, part):
+        return remote(
+            self.source(m, part), self.rows(self.z, self.y, part), self.z_sent.at[m, part],
+            self.z_landed.at[self.z, part], self.device(2 * self.c + m, self.y, self.c),
+        )
+
+    def keep(self, m, part):
+        return pltpu.make_async_copy(
+            self.source(m, part), self.rows(self.z, self.y, part), self.kept.at[part]
+        )
+
+    def from_column(self, zz, part):
+        here = self.rows(zz, self.y, part)
+        return remote(
+            here, here, self.z_sent.at[0, part], self.z_landed.at[zz, part],
+            self.device(zz, self.y, self.c),
+        )
+
+    def to_row(self, zz, k, part):
+        here = self.rows(zz, self.y, part)
+        return remote(
+            here, here, self.y_sent.at[k, part], self.y_landed.at[zz, part],
+            self.device(self.z, 1 - self.y, self.c),
+        )
+
+    def from_row(self, zz, k, part):
+        here = self.rows(zz, 1 - self.y, part)
+        return remote(
+            here, here, self.y_sent.at[k, part], self.y_landed.at[zz, part],
+            self.device(self.z, 1 - self.y, self.c),
+        )
+
+    def to_core(self, zz, yy, k, part):
+        here = self.rows(zz, yy, part)
+        return remote(
+            here, here, self.c_sent.at[k, part], self.c_landed.at[2 * zz + yy, part],
+            self.device(self.z, self.y, 1 - self.c),
+        )
+
+    def start(self, part):
+        for m in range(2):
+            pl.when(self.away(m))(lambda: self.to_column(m, part).start())
+            pl.when(jnp.logical_not(self.away(m)))(lambda: self.keep(m, part).start())
+
+    def at(self, k):
+        high, low = halves_of(self.z, 4)
+        far = 2 * high if k < 2 else 2 - 2 * high
+        return far + (low if k % 2 == 0 else 1 - low)
+
+    def pass_column(self, k, part):
+        @pl.when(self.enters)
+        def _():
+            if k == 0:
+                self.keep(0, part).wait()
+            else:
+                self.from_column(self.at(k), part).wait_recv()
+            self.to_row(self.at(k), k, part).start()
+            self.to_core(self.at(k), self.y, k, part).start()
+
+    def pass_row(self, k, part):
+        @pl.when(self.enters)
+        def _():
+            self.from_row(self.at(k), k, part).wait_recv()
+            self.to_core(self.at(k), 1 - self.y, 4 + k, part).start()
+
+    def finish(self):
+        @pl.when(self.enters)
+        def _():
+            for k in range(4):
+                for part in range(self.parts):
+                    self.to_row(self.at(k), k, part).wait_send()
+                    self.to_core(self.at(k), self.y, k, part).wait_send()
+                    self.to_core(self.at(k), 1 - self.y, 4 + k, part).wait_send()
+
+        @pl.when(jnp.logical_not(self.enters))
+        def _():
+            for zz in range(4):
+                for yy in range(2):
+                    for part in range(self.parts):
+                        self.to_core(zz, yy, 0, part).wait_recv()
+
+        for m in range(2):
+            for part in range(self.parts):
+                pl.when(self.away(m))(lambda: self.to_column(m, part).wait_send())
+
+
+def gather_sems(parts):
+    shapes = [(parts,), (2, parts), (4, parts), (4, parts), (4, parts), (8, parts), (8, parts)]
+    return [pltpu.SemaphoreType.DMA(shape) for shape in shapes]
+
+
+def gather_kernel(rows_ref, gain_ref, out_ref, staged, *sems):
+    parts = sems[0].shape[0]
     block = rows_ref.shape[1]
     size = block // parts
-
-    def device(zz, yy, cc):
-        return (first + 2 * zz + yy, 2 * x + cc)
-
-    def rows(zz, yy, part):
-        return out_ref.at[pl.ds(pl.multiple_of((2 * zz + yy) * block + part * size, size), size)]
-
-    others = [device(lax.rem(z + k, 4), y, c) for k in range(1, 4)]
-    greet(others + [device(z, 1 - y, c), device(z, y, 1 - c)])
-    enters = z // 2 == c
-
-    def to_column(m, part):
-        return remote(
-            staged.at[m, pl.ds(part * size, size)], rows(z, y, part),
-            z_sent.at[m, part], z_landed.at[z, part], device(2 * c + m, y, c),
-        )
-
-    def keep(m, part):
-        return pltpu.make_async_copy(
-            staged.at[m, pl.ds(part * size, size)], rows(z, y, part), kept.at[part]
-        )
-
-    def from_column(zz, part):
-        return remote(
-            rows(zz, y, part), rows(zz, y, part), z_sent.at[0, part], z_landed.at[zz, part],
-            device(zz, y, c),
-        )
-
-    def to_row(zz, k, part):
-        return remote(
-            rows(zz, y, part), rows(zz, y, part), y_sent.at[k, part], y_landed.at[zz, part],
-            device(z, 1 - y, c),
-        )
-
-    def from_row(zz, k, part):
-        return remote(
-            rows(zz, 1 - y, part), rows(zz, 1 - y, part), y_sent.at[k, part],
-            y_landed.at[zz, part], device(z, 1 - y, c),
-        )
-
-    def to_core(zz, yy, k, part):
-        return remote(
-            rows(zz, yy, part), rows(zz, yy, part), c_sent.at[k, part],
-            c_landed.at[2 * zz + yy, part], device(z, y, 1 - c),
-        )
-
+    gather = Gather(
+        lambda m, part: staged.at[m, pl.ds(part * size, size)], out_ref, block, parts, sems
+    )
+    greet(gather.others())
     for part in range(parts):
         here = pl.ds(part * size, size)
         for m in range(2):
             staged[m, here] = (
                 normalize(rows_ref[m, here].astype(f32))[0] * gain_ref[...]
             ).astype(bf16)
-            away = 2 * c + m != z
-            pl.when(away)(lambda m=m, part=part: to_column(m, part).start())
-            pl.when(jnp.logical_not(away))(lambda m=m, part=part: keep(m, part).start())
-
-    @pl.when(enters)
-    def _():
-        for part in range(parts):
+        gather.start(part)
+    for part in range(parts):
+        for k in range(4):
+            gather.pass_column(k, part)
+        if part > 0:
             for k in range(4):
-                zz = lax.rem(z + k, 4)
-                if k == 0:
-                    keep(0, part).wait()
-                else:
-                    from_column(zz, part).wait_recv()
-                to_row(zz, k, part).start()
-                to_core(zz, y, k, part).start()
-            if part > 0:
-                for k in range(4):
-                    zz = lax.rem(z + k, 4)
-                    from_row(zz, k, part - 1).wait_recv()
-                    to_core(zz, 1 - y, 4 + k, part - 1).start()
-        for k in range(4):
-            zz = lax.rem(z + k, 4)
-            from_row(zz, k, parts - 1).wait_recv()
-            to_core(zz, 1 - y, 4 + k, parts - 1).start()
-        for k in range(4):
-            zz = lax.rem(z + k, 4)
-            for part in range(parts):
-                to_row(zz, k, part).wait_send()
-                to_core(zz, y, k, part).wait_send()
-                to_core(zz, 1 - y, 4 + k, part).wait_send()
-
-    @pl.when(jnp.logical_not(enters))
-    def _():
-        for zz in range(4):
-            for yy in range(2):
-                for part in range(parts):
-                    to_core(zz, yy, 0, part).wait_recv()
-
-    for m in range(2):
-        for part in range(parts):
-            pl.when(2 * c + m != z)(lambda m=m, part=part: to_column(m, part).wait_send())
+                gather.pass_row(k, part - 1)
+    for k in range(4):
+        gather.pass_row(k, parts - 1)
+    gather.finish()
 
 
 def gather_normed(rows, gain):
     micro, block, width = rows.shape
-    parts = 4
-    sems = [(parts,), (2, parts), (4, parts), (4, parts), (4, parts), (8, parts), (8, parts)]
     return pl.pallas_call(
         gather_kernel,
         out_shape=struct((8 * block, width), bf16),
         in_specs=[pl.BlockSpec(memory_space=pltpu.VMEM)] * 2,
         out_specs=pl.BlockSpec(memory_space=pl.ANY),
-        scratch_shapes=[pltpu.VMEM((micro, block, width), bf16)]
-        + [pltpu.SemaphoreType.DMA(shape) for shape in sems],
+        scratch_shapes=[pltpu.VMEM((micro, block, width), bf16)] + gather_sems(4),
         compiler_params=pltpu.CompilerParams(
             collective_id=0, has_side_effects=True, vmem_limit_bytes=32 * 2**20
         ),
@@ -849,22 +938,403 @@
     )(rows, gain)
 
 
+def rise_kernel(
+    normed, w_mix, w_gate, w_q, w_k, w_v, conv_w, conv_b, gate_parts, gate_b, out_gain, skip_gain,
+    w_down, cot_ref, *refs
+):
+    lift_outs, cell_outs, (cot_out, *refs) = refs[:6], refs[6:13], refs[13:]
+    q_all, k_all, v_all, conv_all, z_all, carry, gate_mine, gate_all, gates, *refs = refs
+    state, h_sent, h_landed, *sems = refs[:3], *refs[3:]
+    parts = sems[0].shape[0]
+    step = pl.program_id(0)
+    blocks = pl.num_programs(0) // 2
+    block = normed.shape[0]
+    size = cot_ref.shape[1] // parts
+    gather = Gather(
+        lambda m, part: cot_ref.at[m, pl.ds(part * size, size)], cot_out, cot_ref.shape[1], parts,
+        sems,
+    )
+    z, y, c = gather.z, gather.y, gather.c
+    head = 2 * c + y
+    heads = gate_all.shape[0]
+    group = [(1 - y, c), (y, 1 - c), (1 - y, 1 - c)]
+    span = gate_mine.shape[1] // 2
+
+    def gate_to(k, part):
+        lanes = pl.ds(part * span, span)
+        return remote(
+            gate_mine.at[:, lanes], gate_all.at[head, :, lanes], h_sent.at[k, part],
+            h_landed.at[head, part], gather.device(z, *group[k]),
+        )
+
+    def gate_from(k, part):
+        lanes = pl.ds(part * span, span)
+        at = 2 * group[k][1] + group[k][0]
+        return remote(
+            gate_mine.at[:, lanes], gate_all.at[at, :, lanes], h_sent.at[k, part],
+            h_landed.at[at, part], gather.device(z, *group[k]),
+        )
+
+    @pl.when(step == 0)
+    def _():
+        greet(gather.others() + [gather.device(z, 1 - y, 1 - c)])
+        for part in range(parts):
+            gather.start(part)
+
+    @pl.when(step < blocks)
+    def _():
+        here = pl.ds(pl.multiple_of(step * block, block), block)
+        lift_kernel(
+            False, None, normed, w_mix, w_gate, w_q, w_k, w_v, conv_w, conv_b, gate_parts,
+            *lift_outs, gate_mine.at[:, here], carry,
+        )
+        for ref, made in zip((conv_all, q_all, k_all, v_all, z_all), lift_outs[1:]):
+            ref[here] = made[...]
+        gate_all[head, :, here] = gate_mine[:, here]
+
+    for part in range(2):
+
+        @pl.when(step == (blocks // 2) * (part + 1) - 1)
+        def _():
+            for k in range(3):
+                gate_to(k, part).start()
+
+        @pl.when(step == blocks + (blocks // 2) * part)
+        def _():
+            for k in range(3):
+                gate_from(k, part).wait_recv()
+
+    @pl.when(step >= blocks)
+    def _():
+        here = pl.ds(pl.multiple_of((step - blocks) * block, block), block)
+        for row, at in enumerate((head, heads + head)):
+            total = gate_all[0, pl.ds(at, 1), here]
+            for h in range(1, heads):
+                total = total + gate_all[h, pl.ds(at, 1), here]
+            if row == 1:
+                total = total + gate_b[pl.ds(head, 1), :]
+            gates[row : row + 1, :] = total
+        cell_forward_kernel(
+            False, None, gates, q_all.at[here], k_all.at[here], v_all.at[here], conv_all.at[here],
+            z_all.at[here], out_gain, skip_gain, w_down, *cell_outs, *state, start=blocks,
+        )
+
+    def columns(part, ks=(1, 2, 3)):
+        return [partial(gather.pass_column, k, part) for k in ks]
+
+    def rows(part, ks=(0, 1, 2, 3)):
+        return [partial(gather.pass_row, k, part) for k in ks]
+
+    plan = {
+        0: [do for part in range(parts) for do in columns(part, (0,))],
+        4: columns(0) + [do for part in range(parts) for do in rows(part, (0,))],
+        7: columns(1),
+        8: rows(0, (1, 2, 3)),
+        10: columns(2),
+        11: rows(1, (1, 2, 3)),
+        13: columns(3),
+        14: rows(2, (1, 2, 3)),
+        15: rows(3, (1, 2, 3)),
+    }
+    for when, work in plan.items():
+
+        @pl.when(step == when)
+        def _():
+            for do in work:
+                do()
+
+    @pl.when(step == 2 * blocks - 1)
+    def _():
+        gather.finish()
+        for k in range(3):
+            for part in range(2):
+                gate_to(k, part).wait_send()
+
+
+def rise(
+    normed, w_up, w_query, w_key, w_value, conv_w, conv_b, gate_parts, gate_b, out_gain, skip_gain,
+    w_down, cot,
+):
+    tokens, width = normed.shape
+    heads, size, _ = w_query.shape
+    micro, block, _ = cot.shape
+    steps = tokens // block
+    early = lambda g: jnp.minimum(g, steps - 1)
+    late = lambda g: jnp.maximum(g - steps, 0)
+    by_row = lambda n, at: pl.BlockSpec((block, n), lambda g: (at(g), 0))
+    kept = lambda shape, index: pl.BlockSpec(shape, index, pipeline_mode=pl.Buffered(1))
+    weight = kept((1, size, size), lambda g: (own_head(), 0, 0))
+    lanes = lambda rows: kept((rows, size), lambda g: (0, own_head()))
+    anywhere = pl.BlockSpec(memory_space=pl.ANY)
+    specs = [
+        by_row(width, early), lanes(width), kept((width, size), lambda g: (0, heads + own_head())),
+        weight, weight, weight, lanes(4), lanes(1), kept(gate_parts.shape, lambda g: (0, 0, 0)),
+        kept(gate_b.shape, lambda g: (0, 0)), lanes(1), lanes(1),
+        kept((size, width), lambda g: (own_head(), 0)), kept(cot.shape, lambda g: (0, 0, 0)),
+    ]
+    outs = [struct((tokens, size), bf16)] * 5 + [struct((tokens, size), f32)]
+    out_specs = [by_row(size, early)] * 6
+    outs += [
+        struct((tokens, width), bf16), struct((tokens, size), f32),
+        struct((steps, size, size), bf16), struct((steps, 8, size), f32),
+        struct((tokens, block), bf16), struct((tokens, 128), f32), struct((8, tokens), f32),
+        struct((tokens, width), bf16),
+    ]
+    out_specs += [
+        by_row(width, late), by_row(size, late),
+        pl.BlockSpec((1, size, size), lambda g: (late(g), 0, 0)),
+        pl.BlockSpec((1, 8, size), lambda g: (late(g), 0, 0)),
+        by_row(block, late), by_row(128, late),
+        pl.BlockSpec((8, block), lambda g: (0, late(g))), anywhere,
+    ]
+    scratch = [((tokens, size), bf16)] * 4 + [((tokens, size), f32), ((8, size), f32)]
+    scratch += [((8, tokens), f32), ((heads, 8, tokens), f32), ((8, block), f32)]
+    scratch += [((size, size), f32), ((8, size), f32), ((8, 128), f32)]
+    return pl.pallas_call(
+        rise_kernel,
+        grid=(2 * steps,),
+        in_specs=specs,
+        out_specs=out_specs,
+        out_shape=outs,
+        scratch_shapes=[pltpu.VMEM(shape, dtype) for shape, dtype in scratch]
+        + [pltpu.SemaphoreType.DMA((3, 2)), pltpu.SemaphoreType.DMA((4, 2))] + gather_sems(4),
+        compiler_params=pltpu.CompilerParams(
+            dimension_semantics=("arbitrary",), collective_id=3, has_side_effects=True,
+            vmem_limit_bytes=vmem_bytes,
+        ),
+        name="rise",
+    )(
+        normed, w_up, w_up, w_query, w_key, w_value, conv_w, conv_b, gate_parts, gate_b, out_gain,
+        skip_gain, w_down, cot,
+    )
+
+
+def own_head():
+    first, z, y, x, c = where_am_i()
+    return 2 * c + y
+
+
+def settle_kernel(*refs):
+    ins, refs = refs[:16], refs[16:]
+    part_ref, tokens_ref, *refs = refs
+    (dq_out, dk_out, dv_out, dskip_out, dz_out, g_down_out, g_z_out, g_gain_out,
+     block_out, gate_out, *refs) = refs
+    state, (gate_rows, gate_all, own, from_core, kept, to_row, from_row, to_owner, owned, *sems) = (
+        refs[:5], refs[5:],
+    )
+    own_sem, c_sent, c_landed, y_sent, y_landed, o_sent, o_landed, h_sent, h_landed = sems
+    step = pl.program_id(0)
+    first, z, y, x, c = where_am_i()
+    head = 2 * c + y
+    high, low = halves_of(z, 4)
+    half = own.shape[1]
+    block = ins[1].shape[0]
+
+    def device(zz, yy, cc):
+        return (first + 2 * zz + yy, 2 * x + cc)
+
+    around = [turn(z + k, 4) for k in range(1, 4)]
+    order = around + [z]
+    group = [(1 - y, c), (y, 1 - c), (1 - y, 1 - c)]
+
+    def rows_of(at, cc):
+        return part_ref.at[pl.ds(pl.multiple_of((2 * at + cc) * half, half), half)]
+
+    def load(at):
+        return pltpu.make_async_copy(rows_of(at, c), own.at[at], own_sem.at[at])
+
+    def to_c(at):
+        return remote(
+            rows_of(at, 1 - c), from_core.at[at], c_sent.at[at], c_landed.at[at],
+            device(z, y, 1 - c),
+        )
+
+    def to_y(zz):
+        return remote(
+            to_row.at[zz], from_row.at[zz], y_sent.at[zz], y_landed.at[zz], device(z, 1 - y, c)
+        )
+
+    def to_o(zz):
+        return remote(
+            to_owner.at[zz], owned.at[low, c], o_sent.at[zz], o_landed.at[low, c],
+            device(zz, y, high),
+        )
+
+    def core_sum(at):
+        load(at).wait()
+        to_c(at).wait_recv()
+        return (own[at].astype(f32) + from_core[at].astype(f32)).astype(bf16)
+
+    def core_step(zz):
+        to_row[zz] = core_sum(2 * zz + 1 - y)
+        to_y(zz).start()
+        kept[zz] = core_sum(2 * zz + y)
+
+    def row_sum(zz):
+        to_y(zz).wait_recv()
+        return (kept[zz].astype(f32) + from_row[zz].astype(f32)).astype(bf16)
+
+    enters = high == c
+
+    def row_step(zz):
+        to_owner[zz] = row_sum(zz)
+        to_o(zz).start()
+
+    def gate_to(k):
+        yy, cc = group[k]
+        return remote(
+            gate_rows, gate_all.at[head], h_sent.at[k], h_landed.at[head], device(z, yy, cc)
+        )
+
+    def gate_from(k):
+        at = 2 * group[k][1] + group[k][0]
+        return remote(
+            gate_rows, gate_all.at[at], h_sent.at[k], h_landed.at[at], device(z, *group[k])
+        )
+
+    @pl.when(step == 0)
+    def _():
+        others = [device(z, yy, cc) for yy, cc in group]
+        for zz in around:
+            others += [device(zz, y, c), device(zz, y, 1 - c)]
+        greet(others)
+        for zz in order:
+            for yy in (1 - y, y):
+                to_c(2 * zz + yy).start()
+                load(2 * zz + yy).start()
+
+    now = pl.num_programs(0) - 1 - step
+    lanes = pl.ds(pl.multiple_of(now * block, block), block)
+    cell_backward_kernel(
+        False, None, *ins, dq_out, dk_out, dv_out, dskip_out, dz_out, gate_rows.at[:, lanes],
+        g_down_out, g_z_out, g_gain_out, *state,
+    )
+
+    for k in range(4):
+        pl.when(step == k)(lambda: core_step(order[k]))
+    for k, when in enumerate((2, 4, 5)):
+        pl.when(step == when)(lambda: row_step(order[k]))
+
+    @pl.when(step == pl.num_programs(0) - 1)
+    def _():
+        for k in range(3):
+            gate_to(k).start()
+        gate_all[head] = gate_rows[...]
+
+        @pl.when(enters)
+        def _():
+            owned[low, c] = row_sum(z)
+
+        @pl.when(jnp.logical_not(enters))
+        def _():
+            row_step(z)
+
+        for m in range(2):
+            for cc in range(2):
+                own_part = jnp.logical_and(2 * c + m == z, c == cc)
+                landed = remote(
+                    to_owner.at[0], owned.at[m, cc], o_sent.at[0], o_landed.at[m, cc],
+                    device(2 * c + m, y, cc),
+                )
+                pl.when(jnp.logical_not(own_part))(lambda: landed.wait_recv())
+                here = pl.ds(cc * half, half)
+                block_out[m, here] = (
+                    tokens_ref[m, here].astype(f32) + owned[m, cc].astype(f32)
+                ).astype(bf16)
+        for k in range(3):
+            gate_from(k).wait_recv()
+        heads = gate_all.shape[0]
+        for h in range(heads):
+            gate_out[h : h + 1, :] = gate_all[h, 0:1, :]
+            gate_out[heads + h : heads + h + 1, :] = gate_all[h, 1:2, :]
+        for k in range(3):
+            gate_to(k).wait_send()
+            to_o(order[k]).wait_send()
+        pl.when(jnp.logical_not(enters))(lambda: to_o(z).wait_send())
+        for zz in range(4):
+            to_y(zz).wait_send()
+        for at in range(8):
+            to_c(at).wait_send()
+
+
+def settle(
+    part, tokens, rows, q, k, v, conv, gate_z, normed, states, norms, weights, cols, cot, rows_in,
+    out_gain, skip_gain, w_down,
+):
+    count, size = q.shape
+    width = w_down.shape[1]
+    micro, block, _ = tokens.shape
+    half = block // 2
+    length = chunk_len
+    end = count // length - 1
+    by_row = lambda n: pl.BlockSpec((length, n), lambda g: (end - g, 0))
+    gain = pl.BlockSpec((1, size), lambda g: (0, own_head()), pipeline_mode=pl.Buffered(1))
+    kept = lambda value: pl.BlockSpec(
+        value.shape, lambda g: (0,) * len(value.shape), pipeline_mode=pl.Buffered(1)
+    )
+    specs = [pl.BlockSpec((8, length), lambda g: (0, end - g))] + [by_row(size)] * 6
+    specs += [
+        pl.BlockSpec((1, size, size), lambda g: (end - g, 0, 0)),
+        pl.BlockSpec((1, 8, size), lambda g: (end - g, 0, 0)),
+        by_row(length), by_row(128), by_row(width), by_row(width), gain, gain,
+        pl.BlockSpec((size, width), lambda g: (own_head(), 0), pipeline_mode=pl.Buffered(1)),
+        pl.BlockSpec(memory_space=pl.ANY), kept(tokens),
+    ]
+    whole = [
+        struct((2, size, width // 2), bf16), struct((width, size), bf16), struct((8, size), f32),
+        struct(tokens.shape, bf16), struct((8, count), f32),
+    ]
+    outs = [struct((count, size), f32)] * 4 + [struct((count, size), bf16)] + whole
+    scratch = [
+        ((size, size), f32), ((8, size), f32), ((size, width), f32), ((width, size), f32),
+        ((8, size), f32), ((8, count), f32), ((4, 8, count), f32),
+        ((8, half, width), bf16), ((8, half, width), bf16), ((4, half, width), bf16),
+        ((4, half, width), bf16), ((4, half, width), bf16), ((4, half, width), bf16),
+        ((2, 2, half, width), bf16),
+    ]
+    sems = [(8,), (8,), (8,), (4,), (4,), (4,), (2, 2), (3,), (4,)]
+    return pl.pallas_call(
+        settle_kernel,
+        grid=(count // length,),
+        in_specs=specs,
+        out_specs=[by_row(size)] * 5 + [kept(value) for value in whole],
+        out_shape=outs,
+        scratch_shapes=[pltpu.VMEM(shape, dtype) for shape, dtype in scratch]
+        + [pltpu.SemaphoreType.DMA(shape) for shape in sems],
+        compiler_params=pltpu.CompilerParams(
+            dimension_semantics=("arbitrary",), collective_id=2, has_side_effects=True,
+            vmem_limit_bytes=60 * 2**20,
+        ),
+        cost_estimate=pl.CostEstimate(
+            flops=2 * count * size * (4 * length + 4 * size + 3 * width),
+            bytes_accessed=48 * 2**20, transcendentals=0,
+        ),
+        name="settle",
+    )(
+        rows, q, k, v, conv, gate_z, normed, states, norms, weights, cols, cot, rows_in,
+        out_gain, skip_gain, w_down, part, tokens,
+    )
+
+
 def drain_kernel(
-    d_gate, dq, dk, dv, mix_ref, conv, q_ref, k_ref, v_ref, dskip, dz, mix_before, normed,
+    d_gate, dq, dk, dv, mix_ref, conv, q_ref, k_ref, v_ref,
+    dskip, dskip_next, dz, mix_before, mix_next, normed,
     gate_pairs, g_gain, w_query, w_key, w_value, w_up, conv_w, conv_b,
     down_ref, lifted_ref, rows_ref, cot_ref, gain_ref, *refs
 ):
     grad_out, up_out, query_out, key_out, value_out, down_out, small_out, *refs = refs
     w_q, w_k, w_v, w_mix, w_gate, taps_w, taps_b, q_all, k_all, v_all, *refs = refs
-    g_q, g_k, g_v, g_small, later, rows_all, lifted_all, part_all, *refs = refs
+    g_q, g_k, g_v, g_small, rows_all, lifted_all, part_all, *refs = refs
     from_core, kept, to_row, from_row, to_owner, owned, *refs = refs
     give_up, give_square, *refs = refs
-    from_x, totals, from_near, pairs, from_far, ends = (refs[k : 18 : 6] for k in range(6))
-    refs = refs[18:]
+    cross_go, cross_got, *refs = refs
+    from_x, totals, refs = refs[:3], (*refs[3:6], None, refs[6]), refs[7:]
+    from_near, pairs, from_far, ends = (refs[k : 20 : 4] for k in range(4))
+    refs = refs[20:]
     up_go, up_got, sq_go, sq_got, dn_go, dn_got, small_x, small_sum, small_z, small_all, *refs = refs
     c_sent, c_landed, y_sent, y_landed, o_sent, o_landed, *refs = refs
     x_sent, x_landed, near_sent, near_landed, far_sent, far_landed, *refs = refs
-    w_sem, up_sem, sq_sent, sq_landed, dn_sent, dn_landed, sx_sem, sz_sent, sz_landed, *refs = refs
+    cross_sem, w_sem, up_sem, sq_sent, sq_landed, dn_sent, dn_landed, sx_sem, sz_sent, sz_landed, *refs = refs
     sh_sent, sh_landed = refs
     step = pl.program_id(0)
     blocks, block, width = part_all.shape
@@ -872,12 +1342,12 @@
     size = g_q.shape[0]
     first, z, y, x, c = where_am_i()
     head = 2 * c + y
-    high, low = z // 2, lax.rem(z, 2)
+    high, low = halves_of(z, 4)
 
     def device(zz, yy, cc, xx=x):
         return (first + 2 * zz + yy, 2 * xx + cc)
 
-    around = [lax.rem(z + k, 4) for k in range(1, 4)]
+    around = [turn(z + k, 4) for k in range(1, 4)]
     group = [(1 - y, c), (y, 1 - c), (1 - y, 1 - c)]
 
     def down_rows(q):
@@ -894,11 +1364,19 @@
             give, from_x[p].at[q], x_sent.at[p, q], x_landed.at[p, q], device(z, y, c, 1 - x)
         )
 
+    def before_near(p, q):
+        if p == 3:
+            return lifted_ref.at[up_rows(q), pl.ds(size // 2, size // 2)]
+        return totals[p].at[q]
+
     def to_near(p, q):
         return remote(
-            totals[p].at[q], from_near[p].at[q // 2], near_sent.at[p, q], near_landed.at[p, q],
+            before_near(p, q), from_near[p].at[q // 2], near_sent.at[p, q], near_landed.at[p, q],
             device(z + 1 - 2 * low, y, c),
         )
+
+    def start_near(p, q):
+        pl.when(low != q % 2)(lambda: to_near(p, q).start())
 
     def to_far(p, q):
         return remote(
@@ -910,14 +1388,14 @@
         to_x(p, q).wait_recv()
         own = totals[p][q] if p < 2 else down_ref[x, down_rows(q)]
         totals[p][q] = (own.astype(f32) + from_x[p][q].astype(f32)).astype(bf16)
-        pl.when(low != q % 2)(lambda: to_near(p, q).start())
+        start_near(p, q)
 
     def near_step(p, q):
         @pl.when(low == q % 2)
         def _():
             to_near(p, q).wait_recv()
             pairs[p][q // 2] = (
-                totals[p][q].astype(f32) + from_near[p][q // 2].astype(f32)
+                before_near(p, q)[...].astype(f32) + from_near[p][q // 2].astype(f32)
             ).astype(bf16)
             pl.when(high != q // 2)(lambda: to_far(p, q).start())
 
@@ -925,7 +1403,15 @@
         @pl.when(z == q)
         def _():
             to_far(p, q).wait_recv()
-            ends[p][...] = pairs[p][q // 2].astype(f32) + from_far[p][...].astype(f32)
+            total = pairs[p][q // 2].astype(f32) + from_far[p][...].astype(f32)
+            ends[p][:, : total.shape[1]] = total
+
+    def to_cross():
+        return remote(cross_go, cross_got, cross_sem.at[0], cross_sem.at[1], device(z, y, c, 1 - x))
+
+    def cross(p):
+        cross_go[...] = ends[p][...].astype(bf16)
+        to_cross().start()
 
     def weight_copies():
         lanes = pl.ds(pl.multiple_of(head * size, size), size)
@@ -954,14 +1440,14 @@
     def to_o(zz):
         return remote(
             to_owner.at[zz], owned.at[low, c], o_sent.at[zz], o_landed.at[low, c],
-            device(zz, y, z // 2),
+            device(zz, y, high),
         )
 
     def stays(zz):
-        return jnp.logical_and(z == zz, z // 2 == c)
+        return jnp.logical_and(z == zz, high == c)
 
     def core_step(at):
-        zz, yy = at // 2, lax.rem(at, 2)
+        zz, yy = halves_of(at, 8)
         to_c(at).wait_recv()
         here = pl.ds(pl.multiple_of(c * half, half), half)
         value = (part_all[at, here].astype(f32) + from_core[at].astype(f32)).astype(bf16)
@@ -1024,16 +1510,16 @@
     def down_to(cc):
         return remote(
             dn_go.at[cc], dn_got.at[low], dn_sent.at[cc], dn_landed.at[low],
-            device(head, z // 2, cc),
+            device(head, high, cc),
         )
 
     def down_from(k):
         return remote(
             dn_go.at[0], dn_got.at[k], dn_sent.at[0], dn_landed.at[k],
-            device(2 * y + k, low, z // 2),
-        )
-
-    home = jnp.logical_and(head == z, z // 2 == y)
+            device(2 * y + k, low, high),
+        )
+
+    home = jnp.logical_and(head == z, high == y)
 
     @pl.when(step == 0)
     def _():
@@ -1043,11 +1529,16 @@
         greet(others)
         for q in range(4):
             to_x(2, q).start()
+        for q in range(4):
+            start_near(3, q)
         for copy in weight_copies():
             copy.start()
-        for ref in (g_q, g_k, g_v, g_small, later):
+        for ref in (g_q, g_k, g_v, g_small):
             ref[...] = jnp.zeros_like(ref)
-
+        for ref in (q_all, k_all, v_all):
+            ref[blocks * block :] = jnp.zeros_like(ref[blocks * block :])
+
+    order = around + [z]
     tall, wide = size // 4, size // 2
 
     @pl.when(step < blocks)
@@ -1074,18 +1565,19 @@
 
     @pl.when(step >= blocks)
     def _():
-        now = 2 * blocks - 1 - step
+        now = drain_order(step, blocks)
         here = pl.ds(pl.multiple_of(now * block, block), block)
-        lows = (q_all[here], k_all[here], v_all[here])
-        rows, d_mix, d_z, d_normed = lower_second(
-            0.0, now == 0, lows, dskip, dz, mix_ref, mix_before, normed,
-            w_q, w_k, w_v, w_mix, w_gate, taps_w, taps_b, g_gain, g_small, later,
+        more = pl.ds(pl.multiple_of(now * block, block), block + mix_next.shape[0])
+        rows, d_mix, d_normed = lower_block(
+            now == 0, now == blocks - 1, (q_all[more], k_all[more], v_all[here]),
+            dskip, dskip_next, dz, mix_ref, mix_before, mix_next, normed,
+            w_q, w_k, w_v, w_mix, w_gate, taps_w, taps_b, g_small,
         )
         rows_all[here] = rows
         lifted_all[here] = d_mix
         part_all[now] = d_normed.astype(bf16)
         to_c(now).start()
-        pl.when(now < blocks - 1)(lambda: core_step(now + 1))
+        pl.when(step > blocks)(lambda: core_step(drain_order(step - 1, blocks)))
 
     def at_end(when, *work):
         @pl.when(step == blocks + when)
@@ -1108,45 +1600,55 @@
     def every(do, p):
         return [partial(do, p, q) for q in range(4)]
 
+    def early_cross():
+        pl.when(x == 0)(lambda: cross(3))
+
+    at_end(0, *every(near_step, 3))
     at_end(1, *every(x_step, 2))
     at_end(3, partial(x_step, 1, 0))
-    at_end(4, *every(near_step, 2))
-    at_end(5, partial(x_step, 1, 1), partial(near_step, 1, 0))
-    at_end(6, partial(row_step, 3))
-    at_end(7, partial(x_step, 1, 2), partial(near_step, 1, 1), *every(far_step, 2), spread_down)
+    at_end(4, *every(far_step, 3), early_cross)
+    at_end(5, *every(near_step, 2), partial(x_step, 1, 1), partial(near_step, 1, 0))
+    at_end(7, partial(row_step, order[0]), partial(x_step, 1, 2), partial(near_step, 1, 1))
 
     @pl.when(step == 2 * blocks - 1)
     def _():
+        g_small[29:32, :] = g_gain[0:3, :]
         small_to_x().start()
         for q in range(4):
             got = mm_tn(rows_all[:, block * q : block * q + block], lifted_all[...]).astype(bf16)
-            given = lifted_ref[up_rows(q)]
-            totals[0][q] = jnp.where(x == 0, got, given)
-            give_up[q] = jnp.where(x == 0, given, got)
-            if q < 2:
-                to_x(0, q).start()
+            given = lifted_ref[up_rows(q), :wide]
+            totals[0][q] = jnp.where(x == 0, got[:, :wide], given)
+            give_up[q] = jnp.where(x == 0, given, got[:, :wide])
+            totals[4][q] = got[:, wide:]
+            to_x(0, q).start()
+            start_near(4, q)
             if q == 0:
-                core_step(0)
-        row_step(2)
+                core_step(2 * z + y)
+        for q in range(4):
+            far_step(2, q)
+        spread_down()
+        row_step(order[1])
         x_step(1, 3)
         near_step(1, 2)
-        row_step(1)
         x_step(0, 0)
-        to_x(0, 2).start()
+        row_step(order[2])
+        near_step(4, 0)
+        near_step(4, 1)
         near_step(1, 3)
-        far_step(1, 0)
-        far_step(1, 1)
+        x_step(0, 1)
+        near_step(0, 0)
         small_to_x().wait_recv()
         small_sum[...] = g_small[...] + small_x[...]
         small_z[z] = small_sum[...]
         for k in range(3):
             small_to_z(k).start()
-        row_step(0)
-        x_step(0, 1)
-        to_x(0, 3).start()
-        near_step(0, 0)
-        far_step(1, 2)
-        far_step(1, 3)
+        near_step(4, 2)
+        near_step(4, 3)
+        x_step(0, 2)
+        near_step(0, 1)
+        row_step(z)
+        for q in range(4):
+            far_step(1, q)
         for yy in range(2):
             for cc in range(2):
                 for a in range(3):
@@ -1157,6 +1659,12 @@
         sq_got[head] = sq_go[y, c]
         for k in range(3):
             square_to(k).start()
+        x_step(0, 3)
+        near_step(0, 2)
+        for q in range(4):
+            far_step(4, q)
+        pl.when(x == 1)(lambda: cross(4))
+        near_step(0, 3)
         for k in range(3):
             small_from_z(k).wait_recv()
         total = small_z[0]
@@ -1165,15 +1673,11 @@
         small_all[head] = total
         for k in range(3):
             small_to_head(k).start()
-        x_step(0, 2)
-        near_step(0, 1)
-        far_step(0, 0)
-        x_step(0, 3)
-        near_step(0, 2)
-        far_step(0, 1)
-        near_step(0, 3)
-        far_step(0, 2)
-        far_step(0, 3)
+        for q in range(4):
+            far_step(0, q)
+        to_cross().wait_recv()
+        kept_half = jnp.where(x == 0, ends[4][...], ends[3][...])
+        ends[0][:, wide:] = kept_half + cross_got[...].astype(f32)
         value = ends[0][...]
         mine = jnp.where(y == 0, value[:half], value[half:])
         up_go[...] = jnp.where(y == 0, value[half:], value[:half]).astype(bf16)
@@ -1210,7 +1714,7 @@
         for a, ref in enumerate((query_out, key_out, value_out)):
             ref[...] = sq_got[:, :, tall * a : tall * a + tall].astype(f32)
         for k in range(2):
-            mine = jnp.logical_and(home, jnp.logical_and(low == k, z // 2 == c))
+            mine = jnp.logical_and(home, jnp.logical_and(low == k, high == c))
             pl.when(jnp.logical_not(mine))(lambda: down_from(k).wait_recv())
             deep = dn_got.shape[1]
             down_out[deep * k : deep * k + deep] = dn_got[k].astype(f32)
@@ -1223,9 +1727,11 @@
 
         small_to_x().wait_send()
         up_to_y().wait_send()
-        for p in range(3):
+        to_cross().wait_send()
+        for p in range(5):
             for q in range(4):
-                to_x(p, q).wait_send()
+                if p < 3:
+                    to_x(p, q).wait_send()
                 pl.when(low != q % 2)(lambda: to_near(p, q).wait_send())
                 passes = jnp.logical_and(low == q % 2, high != q // 2)
                 pl.when(passes)(lambda: to_far(p, q).wait_send())
@@ -1243,6 +1749,12 @@
             pl.when(jnp.logical_not(left_here))(lambda: down_to(cc).wait_send())
 
 
+def drain_order(step, blocks):
+    first, z, y, x, c = where_am_i()
+    k, odd = halves_of(jnp.maximum(step - blocks, 0), blocks)
+    return 2 * turn(z + 1 + k, 4) + jnp.where(odd == 0, 1 - y, y)
+
+
 def drain(inputs, down, lifted, rows, cot, gain):
     (d_gate, dq, dk, dv, dskip, dz, mix, conv, q, k, v, normed,
      w_query, w_key, w_value, w_up, conv_w, conv_b, gate_pairs, g_gain) = inputs
@@ -1252,45 +1764,50 @@
     lines = 40
     steps = tokens // block
     early = lambda g: jnp.minimum(g, steps - 1)
-    late = lambda g: jnp.minimum(2 * steps - 1 - g, steps - 1)
-    both = lambda g: jnp.where(g < steps, g, 2 * steps - 1 - g)
+    late = lambda g: drain_order(g, steps)
+    both = lambda g: jnp.where(g < steps, g, drain_order(g, steps))
+    edge = lambda at: pl.BlockSpec(
+        (16, size), lambda g: (jnp.clip(at(g), 0, tokens // 16 - 1), 0)
+    )
+    before = edge(lambda g: late(g) * (block // 16) - 1)
+    behind = edge(lambda g: (late(g) + 1) * (block // 16))
     by_row = lambda n, at: pl.BlockSpec((block, n), lambda g: (at(g), 0))
     kept = lambda value: pl.BlockSpec(
         value.shape, lambda g: (0,) * value.ndim, pipeline_mode=pl.Buffered(1)
     )
     anywhere = pl.BlockSpec(memory_space=pl.ANY)
     arguments = (
-        d_gate, dq, dk, dv, mix, conv, q, k, v, dskip, dz, mix, normed, gate_pairs, g_gain,
+        d_gate, dq, dk, dv, mix, conv, q, k, v, dskip, dskip, dz, mix, mix, normed, gate_pairs, g_gain,
         w_query, w_key, w_value, w_up, conv_w, conv_b, down, lifted, rows, cot, gain,
     )
     specs = [pl.BlockSpec((8, block), lambda g: (0, early(g)))] + [by_row(size, early)] * 3
-    specs += [by_row(size, both)] + [by_row(size, early)] * 4 + [by_row(size, late)] * 2
-    specs += [
-        pl.BlockSpec((16, size), lambda g: (jnp.maximum(late(g) * (block // 16) - 1, 0), 0)),
-        by_row(width, late), kept(gate_pairs), kept(g_gain),
-    ]
+    specs += [by_row(size, both)] + [by_row(size, early)] * 4
+    specs += [by_row(size, late), behind, by_row(size, late), before, behind, by_row(width, late)]
+    specs += [kept(gate_pairs), kept(g_gain)]
     specs += [anywhere] * 6 + [kept(value) for value in (down, lifted, rows, cot, gain)]
     scratch = [((size, size), bf16)] * 3 + [((width, size), bf16)] * 2
-    scratch += [((4, size), f32), ((1, size), f32)] + [((tokens, size), bf16)] * 3
-    scratch += [((size, size), f32)] * 3 + [((lines, size), f32), ((8, size), f32)]
+    scratch += [((4, size), f32), ((1, size), f32)] + [((tokens + 16, size), bf16)] * 3
+    scratch += [((size, size), f32)] * 3 + [((lines, size), f32)]
     scratch += [((tokens, width), bf16), ((tokens, size), bf16), ((8, block, width), bf16)]
     scratch += [
         ((8, half, width), bf16), ((4, half, width), bf16), ((4, half, width), bf16),
         ((4, half, width), bf16), ((4, half, width), bf16), ((2, 2, half, width), bf16),
     ]
-    pieces = [(width // 4, size), (size // 4, 3 * size // 2), (size // 4, width // 2)]
-    scratch += [((4, *piece), bf16) for piece in pieces[:2]]
+    up = (width // 4, size // 2)
+    pieces = [up, (size // 4, 3 * size // 2), (size // 4, width // 2), up, up]
+    scratch += [((4, *piece), bf16) for piece in pieces[:2]] + [(up, bf16)] * 2
+    scratch += [((4, *piece), bf16) for piece in pieces[:3] + pieces[:3] + pieces[4:]]
     for piece in pieces:
-        scratch += [((4, *piece), bf16)] * 2 + [((2, *piece), bf16)] * 2
-        scratch += [(piece, bf16), (piece, f32)]
+        scratch += [((2, *piece), bf16)] * 2 + [(piece, bf16), (piece, f32)]
+    scratch[-17] = ((up[0], size), f32)
     scratch += [
         ((width // 8, size), bf16), ((width // 8, size), bf16),
         ((2, 2, size // 8, 3 * size // 4), bf16), ((4, size // 8, 3 * size // 4), bf16),
         ((2, size // 4, width // 4), bf16), ((2, size // 4, width // 4), bf16),
         ((lines, size), f32), ((lines, size), f32), ((4, lines, size), f32), ((4, lines, size), f32),
     ]
-    sems = [(8,), (8,), (4,), (4,), (4,), (2, 2)] + [(3, 4)] * 6
-    sems += [(7,), (2,), (3,), (4,), (2,), (2,), (2,), (3,), (4,), (3,), (4,)]
+    sems = [(8,), (8,), (4,), (4,), (4,), (2, 2)] + [(5, 4)] * 6
+    sems += [(2,), (7,), (2,), (3,), (4,), (2,), (2,), (2,), (3,), (4,), (3,), (4,)]
     square = struct((4, size // 8, size // 4), f32)
     outs = [
         struct(rows.shape, bf16), struct((width // 8, 2 * size), f32), square, square, square,
@@ -1354,21 +1871,13 @@
     return jnp.stack([lax.dynamic_index_in_dim(got, z ^ k, 0, keepdims=False) for k in range(4)])
 
 
-def hold(value, *done):
-    return lax.optimization_barrier((value, *done))
-
-
-def gather_first(own):
+def gather_sequence(own):
     z, y, x, c = place()
+    micro, rows, width = own.shape
     slots = paired(own, swap(own, "batch", 1), c, 0)
-    return part_of(slots, c, 2, 2)
-
-
-def gather_last(blocks, other):
-    z, y, x, c = place()
-    rows, width = blocks.shape[2:]
-    both = paired(blocks, other, y, 1)
-    return paired(both, swap(both, "batch", 1), c, 3).reshape(8 * rows, 2 * width)
+    blocks = in_order(sent_across(part_of(slots, c, 2, 2), z), z)[:, None]
+    both = paired(blocks, swap(blocks, "seq", 1), y, 1)
+    return paired(both, swap(both, "batch", 1), c, 3).reshape(8 * rows, width)
 
 
 def scatter_first(parts):
@@ -1474,9 +1983,6 @@
     skip_row = skip_gain.reshape(1, inner)
 
     normed = gather_normed(tokens[:, 0], ln_gain[None])
-    cot_half, normed = hold(gather_first(d_out[:, 0]), normed)
-    cot_across = sent_across(cot_half, z)
-
     gate_own = lax.dynamic_index_in_dim(
         gate_w.reshape(3, heads, size, 8), at, 1, keepdims=False
     ).transpose(0, 2, 1)
@@ -1491,62 +1997,64 @@
         .reshape(48, 3 * size)
     )
 
-    first = () if ranges == 1 else (shifted(normed[-16:], "seq", 8),)
-    mix, conv, q, k, v, gate_z, gates, *halo = lift(
-        head, normed, w_up, w_query, w_key, w_value, conv_w, conv_row, gate_parts, *first
-    )
-    cot_across, gates = hold(cot_across, gates)
-    cot_blocks = in_order(cot_across, z)[:, None]
-    gates = total_over_heads(gates)
-    cot_blocks, gates = hold(cot_blocks, gates)
-    cot_row = swap(cot_blocks, "seq", 1)
-    gates = jnp.concatenate(
-        [
-            lax.dynamic_slice_in_dim(gates, at, 1, 0),
-            lax.dynamic_slice_in_dim(gates, heads + at, 1, 0)
-            + lax.dynamic_slice_in_dim(gate_b, at, 1, 0)[:, None],
-        ]
-    )
-    first = ()
-    if ranges > 1:
-        first = (
-            jnp.zeros((size, size), f32),
-            jnp.zeros((8, size), f32),
-            jnp.full((8, 128), floor_value, f32),
-        )
-        *_, state, norm, level = cell_forward(
+    if direct:
+        (mix, conv, q, k, v, gate_z, part, head_normed, states, norms, weights, cols, rows, cot) = rise(
+            normed, w_up, w_query, w_key, w_value, conv_w, conv_row, gate_parts, gate_b[:, None],
+            out_row, skip_row, w_down, d_out[:, 0],
+        )
+    else:
+        cot = gather_sequence(d_out[:, 0])
+        first = () if ranges == 1 else (shifted(normed[-16:], "seq", 8),)
+        mix, conv, q, k, v, gate_z, gates, *halo = lift(
+            head, normed, w_up, w_query, w_key, w_value, conv_w, conv_row, gate_parts, *first
+        )
+        gates = total_over_heads(gates)
+        gates = jnp.concatenate(
+            [
+                lax.dynamic_slice_in_dim(gates, at, 1, 0),
+                lax.dynamic_slice_in_dim(gates, heads + at, 1, 0)
+                + lax.dynamic_slice_in_dim(gate_b, at, 1, 0)[:, None],
+            ]
+        )
+        first = ()
+        if ranges > 1:
+            first = (
+                jnp.zeros((size, size), f32),
+                jnp.zeros((8, size), f32),
+                jnp.full((8, 128), floor_value, f32),
+            )
+            *_, state, norm, level = cell_forward(
+                head, gates, q, k, v, conv, gate_z, out_row, skip_row, w_down, *first
+            )
+            total = jnp.sum(jax.nn.log_sigmoid(gates[1]))
+            first = state_before(state, norm, level, total, ranges)
+        part, head_normed, states, norms, weights, cols, rows, *last = cell_forward(
             head, gates, q, k, v, conv, gate_z, out_row, skip_row, w_down, *first
         )
-        total = jnp.sum(jax.nn.log_sigmoid(gates[1]))
-        first = state_before(state, norm, level, total, ranges)
-    part, head_normed, states, norms, weights, cols, rows, *last = cell_forward(
-        head, gates, q, k, v, conv, gate_z, out_row, skip_row, w_down, *first
-    )
-    cot_row, part = hold(cot_row, part)
-    cot = gather_last(cot_blocks, cot_row)
-    part = scatter_first(part)
-    part, cot = hold(part, cot)
-    part_row = swap(part_of(part, 1 - y, 2, 1), "seq", 1)
-    after = ()
-    if ranges > 1:
-        after = (jnp.zeros((size, size), f32), jnp.zeros((8, size), f32))
-        *_, d_state, d_norm = cell_backward(
-            head, rows, q, k, v, conv, gate_z, head_normed, states, norms, weights, cols, cot, normed,
-            out_row, skip_row, w_down, *after,
-        )
-        keep = jnp.exp(total + first[2][0, 0] - last[2][0, 0])
-        after = cotangent_after(d_state, d_norm, keep, ranges)
-    dq, dk, dv, dskip, dz, d_rows, g_down, g_z, g_gain, *_ = cell_backward(
-        head, rows, q, k, v, conv, gate_z, head_normed, states, norms, weights, cols, cot, normed,
-        out_row, skip_row, w_down, *after,
-    )
-    part_row, d_rows = hold(part_row, d_rows)
-    part = (part_of(part, y, 2, 1).astype(f32) + part_row.astype(f32)).astype(bf16)[:, 0]
-    index = jnp.arange(2 * heads)[:, None]
-    d_gate = jnp.where(index == at, d_rows[0:1], jnp.where(index == heads + at, d_rows[1:2], 0.0))
-    d_gate = total_over_heads(d_gate)
-    part, d_gate = hold(part, d_gate)
-    part_across = sent_across(part, z)
+    cell_args = (
+        rows, q, k, v, conv, gate_z, head_normed, states, norms, weights, cols, cot, normed,
+        out_row, skip_row, w_down,
+    )
+    if direct:
+        dq, dk, dv, dskip, dz, g_down, g_z, g_gain, block_rows, d_gate = settle(
+            part, tokens[:, 0], *cell_args
+        )
+    else:
+        block_rows = (tokens[:, 0].astype(f32) + scatter_sequence(part)).astype(bf16)
+        after = ()
+        if ranges > 1:
+            after = (jnp.zeros((size, size), f32), jnp.zeros((8, size), f32))
+            *_, d_state, d_norm = cell_backward(head, *cell_args, *after)
+            keep = jnp.exp(total + first[2][0, 0] - last[2][0, 0])
+            after = cotangent_after(d_state, d_norm, keep, ranges)
+        dq, dk, dv, dskip, dz, d_rows, g_down, g_z, g_gain, *_ = cell_backward(
+            head, *cell_args, *after
+        )
+        index = jnp.arange(2 * heads)[:, None]
+        d_gate = jnp.where(
+            index == at, d_rows[0:1], jnp.where(index == heads + at, d_rows[1:2], 0.0)
+        )
+        d_gate = total_over_heads(d_gate)
     lower_args = (
         d_gate, dq, dk, dv, dskip, dz, mix, conv, q, k, v, normed,
         w_query, w_key, w_value, w_up, conv_w, conv_row, gate_pairs, g_gain,
@@ -1561,9 +2069,6 @@
             *_, later = lower(head, *lower_args, halo[0], jnp.zeros((8, size), f32))
             first = (halo[0], shifted(later, "seq", -8))
         d_part, square, up, small, *_ = lower(head, *lower_args, *first)
-    part_across, small = hold(part_across, small)
-    block_rows = scatter_last(in_order(part_across, z))
-    block_rows = (tokens[:, 0].astype(f32) + block_rows).astype(bf16)
     if not direct:
         d_normed = scatter_sequence(d_part)
         row_f = tokens[:, 0].astype(f32)

time: 285 us -> 264 us (0.926)
  Pallas kernels: 211 us -> 240 us
  starting transfers between devices: 19.8 us -> 0 us
  waiting for transfers between devices: 18.4 us -> 0 us
  other arithmetic: 16.1 us -> 4.61 us
    pallas_call x3 -> x2, Pallas kernels: 60.5 us -> 93.2 us  [the longest x1 49.6 us: rise(): pl.pallas_call(rise_kernel, grid=(2 * steps,), in_specs=specs, out_specs=...]
    ppermute x16 -> x0, starting transfers between devices: 19.8 us -> none  [swap(): return lax.ppermute(value, axis, [(s, s ^ mask) for s in range(count)])]
    ppermute x16 -> x0, waiting for transfers between devices: 18.4 us -> none  [swap(): return lax.ppermute(value, axis, [(s, s ^ mask) for s in range(count)])]
    select_n x4 -> x0, other arithmetic: 7.45 us -> none  [the longest x3 7.37 us: paired(): jnp.where(bit == 0, jnp.concatenate([mine, other], dim), jnp.concatenate(...]
    convert_element_type x2 -> x0, other arithmetic: 4.2 us -> none  [the longest x1 2.56 us: scatter_first(): return halved(blocks, c, 2, 'batch', 1).astype(bf16)]
    dynamic_slice x5 -> x0, local copies, waits for them, and re-layouts: 3.92 us -> none  [the longest x2 3.15 us: part_of(): return lax.dynamic_slice_in_dim(value, at * size, size, axis)]
    pallas_call x1, Pallas kernels: 114 us -> 111 us  [drain(): pl.pallas_call(drain_kernel, grid=(2 * steps,), in_specs=specs, out_specs...]
    unnamed x46 -> x31, local copies, waits for them, and re-layouts: 10 us -> 10.6 us
  transfers between devices with their start and end apart: 16 -> 0, of which waited for: 7 -> 0; matrix products, arithmetic and copies ran while one was open for 5% -> 0% of each run, Pallas kernels for 74% -> 0%
where the time goes in v5:
time: 264 us
  Pallas kernels  240 us (91%)
  local copies, waits for them, and re-layouts  18.8 us (7%)
  other arithmetic  4.61 us (2%)
    pallas_call x1, Pallas kernels, drain(): pl.pallas_call(drain_kernel, grid=(2 * steps,), in_specs=specs, out_specs...  111 us
    pallas_call x1, Pallas kernels, rise(): pl.pallas_call(rise_kernel, grid=(2 * steps,), in_specs=specs, out_specs=...  49.6 us
    pallas_call x1, Pallas kernels, settle(): pl.pallas_call(settle_kernel, grid=(count // length,), in_specs=specs, ou...  43.6 us
    pallas_call x1, Pallas kernels, gather_normed(): pl.pallas_call(gather_kernel, out_shape=struct((8 * block, width), bf16),...  35.7 us
    unnamed x31, local copies, waits for them, and re-layouts  10.6 us

profile of v5, /device:TPU:24, one launch (start us, length us, event | category | flops | bytes accessed | tf_op | source)
XLA Modules:
  0.0 263.8 jit_solution(1643401632654112367)
XLA Ops:
  0.7 0.1 pad.3.clone
  0.8 1.3 copy.35.gate_b
  2.1 0.8 constant_dynamic-update-slice_fusion.5
  2.9 0.8 constant_dynamic-update-slice_fusion.2
  3.7 0.8 constant_dynamic-update-slice_fusion
  4.5 0.7 copy.41
  5.2 0.7 maximum_maximum_fusion.gate_parts
  5.9 0.0 copy-start.1
  5.9 1.2 copy-done.1
  7.1 0.0 copy-start.2
  7.1 0.7 copy-done.2
  7.8 35.7 %gather_normed.1.normed.refs_12_ = bf16[2048,1024]{1,0:T(8,128)(2,1)S(1)} custom-call(bf16[2,256,1024]{2,1,0:T(8,128)(2,1)S(1)} %bitcast.46, f32[1,1024]{1,0:T(1,128)S(1)} %bitcast.48), custom_call_target="tpu_custom_call" | custom-call | tf_op jit(solution)/shard_map/gather_normed/pallas_call | solution.py:928
  43.5 0.0 copy-start
  43.6 1.9 copy-done
  45.5 49.6 %rise.1 = (bf16[2048,512]{1,0:T(8,128)(2,1)}, bf16[2048,512]{1,0:T(8,128)(2,1)}, bf16[2048,512]{1,0:T(8,128)(2,1)}, bf16[2048,512]{1,0:T(8,128)(2,1)}, bf16[2048...) custom-call(bf16[2048,1024]{1,0:T(8,128)(2,1)} %copy-done, ...), custom_call_target="tpu_custom_call" | custom-call | tf_op jit(solution)/shard_map/rise/pallas_call | solution.py:1093
  95.1 43.6 %settle.1 = (f32[2048,512]{1,0:T(8,128)}, f32[2048,512]{1,0:T(8,128)}, f32[2048,512]{1,0:T(8,128)}, f32[2048,512]{1,0:T(8,128)}, bf16[2048,512]{1,0:T(8,128)(2,1...) custom-call(f32[8,2048]{1,0:T(8,128)} %get-tuple-element.45.refs_0_,, ...), custom_call_target="tpu_custom_call" | custom-call | flops 12884901888 | bytes 50331648 | tf_op jit(solution)/shard_map/settle/pallas_call | solution.py:1296
  138.7 0.0 copy-start.3
  138.7 0.0 copy-start.4
  138.7 110.7 %drain.1 = (bf16[2,256,1024]{2,1,0:T(8,128)(2,1)}, f32[128,1024]{1,0:T(8,128)}, f32[4,64,128]{2,1,0:T(8,128)}, f32[4,64,128]{2,1,0:T(8,128)}, f32[4,64,128]{2,1,...) custom-call(f32[8,2048]{1,0:T(8,128)} %get-tuple-element.59.d_gate, f32[2048,512]{1,0:T(8,128)} %get-tuple-element.60.dq, ...), custom_call_target="tpu_custom_call" | custom-call | flops 15032385536 | bytes 50331648 | tf_op jit(solution)/shard_map/drain/pallas_call | solution.py:1816
  249.4 0.0 copy-start.5
  249.4 0.0 copy-start.9
  249.5 0.0 copy-start.8
  249.5 0.0 copy-start.7
  249.5 0.0 copy-start.6
  249.5 1.4 slice_reduce_fusion.1
  250.9 0.9 slice_reduce_fusion
  251.8 0.0 copy-done.3
  251.8 0.6 div.3
  252.4 1.6 fusion.3
  254.0 1.5 slice.22
  255.4 0.9 slice_bitcast_fusion
  256.4 0.7 copy.37
  257.1 0.0 copy-done.4
  257.1 1.0 copy.55
  258.0 2.3 copy.56
  260.3 0.0 copy-done.5
  260.3 0.8 copy.57
  261.1 0.0 copy-done.9
  261.1 0.7 copy.58
  261.7 0.0 copy-done.8
  261.8 0.7 copy.59
  262.4 0.0 copy-done.7
  262.4 0.7 copy.60
  263.1 0.0 copy-done.6
  263.1 0.7 copy.61
  (5 shorter events, 0.0 us)
Async XLA Ops:
  5.9 1.2 copy-start.1
  7.1 0.7 copy-start.2
  43.5 2.0 copy-start
  138.7 113.1 %copy-start.3 = (f32[1024]{0:T(1024)S(1)}, f32[1024]{0:T(1024)}, u32[]{:S(2)}) copy-start(f32[1024]{0:T(1024)} %param.15) | copy-start | bytes 12292
  138.7 118.3 %copy-start.4 = (bf16[2,256,1024]{2,1,0:T(8,128)(2,1)S(1)}, bf16[2,256,1024]{2,1,0:T(8,128)(2,1)}, u32[]{:S(2)}) copy-start(bf16[2,256,1024]{2,1,0:T(8,128)(2,1)} %get-tuple-element.58) | copy-start | bytes 3145732
  249.4 10.9 %copy-start.5 = (f32[128,1024]{1,0:T(8,128)S(1)}, f32[128,1024]{1,0:T(8,128)}, u32[]{:S(2)}) copy-start(f32[128,1024]{1,0:T(8,128)} %get-tuple-element.130) | copy-start | bytes 1572868
  249.4 11.6 %copy-start.9 = (f32[4,64,128]{2,1,0:T(8,128)S(1)}, f32[4,64,128]{2,1,0:T(8,128)}, u32[]{:S(2)}) copy-start(f32[4,64,128]{2,1,0:T(8,128)} %get-tuple-element.133) | copy-start | bytes 393220
  249.5 12.3 %copy-start.8 = (f32[4,64,128]{2,1,0:T(8,128)S(1)}, f32[4,64,128]{2,1,0:T(8,128)}, u32[]{:S(2)}) copy-start(f32[4,64,128]{2,1,0:T(8,128)} %get-tuple-element.134) | copy-start | bytes 393220
  249.5 12.9 %copy-start.7 = (f32[4,64,128]{2,1,0:T(8,128)S(1)}, f32[4,64,128]{2,1,0:T(8,128)}, u32[]{:S(2)}) copy-start(f32[4,64,128]{2,1,0:T(8,128)} %get-tuple-element.135) | copy-start | bytes 393220
  249.5 13.6 %copy-start.6 = (f32[256,256]{1,0:T(8,128)S(1)}, f32[256,256]{1,0:T(8,128)}, u32[]{:S(2)}) copy-start(f32[256,256]{1,0:T(8,128)} %get-tuple-element.140) | copy-start | bytes 786436

commit v6 on v5

--- a/solution.py
+++ b/solution.py
@@ -871,7 +871,7 @@
             self.from_row(self.at(k), k, part).wait_recv()
             self.to_core(self.at(k), 1 - self.y, 4 + k, part).start()
 
-    def finish(self):
+    def finish(self, wait_core):
         @pl.when(self.enters)
         def _():
             for k in range(4):
@@ -880,12 +880,14 @@
                     self.to_core(self.at(k), self.y, k, part).wait_send()
                     self.to_core(self.at(k), 1 - self.y, 4 + k, part).wait_send()
 
-        @pl.when(jnp.logical_not(self.enters))
-        def _():
-            for zz in range(4):
-                for yy in range(2):
-                    for part in range(self.parts):
-                        self.to_core(zz, yy, 0, part).wait_recv()
+        if wait_core:
+
+            @pl.when(jnp.logical_not(self.enters))
+            def _():
+                for zz in range(4):
+                    for yy in range(2):
+                        for part in range(self.parts):
+                            self.to_core(zz, yy, 0, part).wait_recv()
 
         for m in range(2):
             for part in range(self.parts):
@@ -920,7 +922,7 @@
                 gather.pass_row(k, part - 1)
     for k in range(4):
         gather.pass_row(k, parts - 1)
-    gather.finish()
+    gather.finish(True)
 
 
 def gather_normed(rows, gain):
@@ -938,21 +940,38 @@
     )(rows, gain)
 
 
+def lift_rest(rows, before, w_q, w_k, w_v, conv_w, conv_b, gate_parts):
+    length = rows.shape[0]
+    taps = conv_taps(jnp.concatenate([before, rows.astype(f32)], axis=0), length)
+    summed = conv_b[...]
+    for j in range(4):
+        summed = summed + conv_w[j : j + 1, :] * taps[j]
+    conv = (summed * jax.nn.sigmoid(summed)).astype(bf16)
+    q = mm(conv, w_q[0]).astype(bf16)
+    k = mm(conv, w_k[0]).astype(bf16)
+    v = mm(rows, w_v[0]).astype(bf16)
+    parts = mm_nt(gate_parts[0], q) + mm_nt(gate_parts[1], k) + mm_nt(gate_parts[2], v)
+    return conv, q, k, v, parts[0:8] + parts[8:16] + parts[16:24]
+
+
 def rise_kernel(
-    normed, w_mix, w_gate, w_q, w_k, w_v, conv_w, conv_b, gate_parts, gate_b, out_gain, skip_gain,
-    w_down, cot_ref, *refs
+    tokens, ln_gain, w_mix, w_gate, w_q, w_k, w_v, conv_w, conv_b, gate_own, gate_b, out_gain,
+    skip_gain, w_down, cot_ref, *refs
 ):
-    lift_outs, cell_outs, (cot_out, *refs) = refs[:6], refs[6:13], refs[13:]
-    q_all, k_all, v_all, conv_all, z_all, carry, gate_mine, gate_all, gates, *refs = refs
-    state, h_sent, h_landed, *sems = refs[:3], *refs[3:]
+    kept_outs, cell_outs, (cot_out, *refs) = refs[:7], refs[7:14], refs[14:]
+    rows_all, mix_all, conv_all, q_all, k_all, v_all, z_all, *refs = refs
+    staged, gate_mine, gate_all, gates, gate_parts, *refs = refs
+    state, h_sent, h_landed, out_sem, *sems = refs[:3], *refs[3:]
     parts = sems[0].shape[0]
     step = pl.program_id(0)
     blocks = pl.num_programs(0) // 2
-    block = normed.shape[0]
-    size = cot_ref.shape[1] // parts
+    micro, block, width = cot_ref.shape
+    size = block // parts
+    normed = Gather(
+        lambda m, part: staged.at[m, pl.ds(part * size, size)], rows_all, block, parts, sems[:7]
+    )
     gather = Gather(
-        lambda m, part: cot_ref.at[m, pl.ds(part * size, size)], cot_out, cot_ref.shape[1], parts,
-        sems,
+        lambda m, part: cot_ref.at[m, pl.ds(part * size, size)], cot_out, block, parts, sems[7:]
     )
     z, y, c = gather.z, gather.y, gather.c
     head = 2 * c + y
@@ -975,22 +994,78 @@
             h_landed.at[at, part], gather.device(z, *group[k]),
         )
 
+    def keep_out(k):
+        made = (rows_all, mix_all, conv_all, q_all, k_all, v_all, z_all)[k]
+        return pltpu.make_async_copy(made, kept_outs[k], out_sem.at[k])
+
+    def lift_up(yy, part):
+        here = [
+            pl.ds(pl.multiple_of((2 * zz + yy) * block + part * size, size), size)
+            for zz in range(4)
+        ]
+        rows = jnp.concatenate([rows_all[at] for at in here], axis=0)
+        mix = mm(rows, w_mix[...]).astype(bf16)
+        gate_z = mm(rows, w_gate[...])
+        for k, at in enumerate(here):
+            mix_all[at] = mix[size * k : size * k + size]
+            z_all[at] = gate_z[size * k : size * k + size]
+
+    def arrived(yy, part):
+        @pl.when(jnp.logical_not(normed.enters))
+        def _():
+            for zz in range(4):
+                normed.to_core(zz, yy, 0, part).wait_recv()
+
     @pl.when(step == 0)
     def _():
-        greet(gather.others() + [gather.device(z, 1 - y, 1 - c)])
+        greet(normed.others() + [gather.device(z, 1 - y, 1 - c)])
+        for p in range(3):
+            gate_parts[p, 0:24] = jnp.concatenate(split_three(gate_own[8 * p : 8 * p + 8, :]), axis=0)
+            gate_parts[p, 24:32] = jnp.zeros_like(gate_parts[p, 24:32])
         for part in range(parts):
-            gather.start(part)
+            here = pl.ds(part * size, size)
+            for m in range(2):
+                staged[m, here] = (
+                    normalize(tokens[m, here].astype(f32))[0] * ln_gain[...]
+                ).astype(bf16)
+            normed.start(part)
+        for part in range(parts):
+            for k in range(4):
+                normed.pass_column(k, part)
+            if part == parts - 1:
+                for later in range(parts):
+                    gather.start(later)
+            arrived(y, part)
+            lift_up(y, part)
+            if part > 0:
+                for k in range(4):
+                    normed.pass_row(k, part - 1)
+                arrived(1 - y, part - 1)
+                lift_up(1 - y, part - 1)
+        for k in range(4):
+            normed.pass_row(k, parts - 1)
+        arrived(1 - y, parts - 1)
+        lift_up(1 - y, parts - 1)
+        for k in (0, 1, 6):
+            keep_out(k).start()
 
     @pl.when(step < blocks)
     def _():
         here = pl.ds(pl.multiple_of(step * block, block), block)
-        lift_kernel(
-            False, None, normed, w_mix, w_gate, w_q, w_k, w_v, conv_w, conv_b, gate_parts,
-            *lift_outs, gate_mine.at[:, here], carry,
-        )
-        for ref, made in zip((conv_all, q_all, k_all, v_all, z_all), lift_outs[1:]):
-            ref[here] = made[...]
-        gate_all[head, :, here] = gate_mine[:, here]
+        edge = pl.ds(pl.multiple_of(jnp.maximum(step * block - 16, 0), 16), 16)
+        before = jnp.where(step == 0, 0.0, mix_all[edge][8:16].astype(f32))
+        conv, q, k, v, gate = lift_rest(
+            mix_all[here], before, w_q, w_k, w_v, conv_w, conv_b, gate_parts
+        )
+        for ref, made in zip((conv_all, q_all, k_all, v_all), (conv, q, k, v)):
+            ref[here] = made
+        gate_mine[:, here] = gate
+        gate_all[head, :, here] = gate
+
+    @pl.when(step == blocks - 1)
+    def _():
+        for k in (2, 3, 4, 5):
+            keep_out(k).start()
 
     for part in range(2):
 
@@ -1012,7 +1087,7 @@
             for h in range(1, heads):
                 total = total + gate_all[h, pl.ds(at, 1), here]
             if row == 1:
-                total = total + gate_b[pl.ds(head, 1), :]
+                total = total + gate_b[head]
             gates[row : row + 1, :] = total
         cell_forward_kernel(
             False, None, gates, q_all.at[here], k_all.at[here], v_all.at[here], conv_all.at[here],
@@ -1027,14 +1102,12 @@
 
     plan = {
         0: [do for part in range(parts) for do in columns(part, (0,))],
-        4: columns(0) + [do for part in range(parts) for do in rows(part, (0,))],
-        7: columns(1),
-        8: rows(0, (1, 2, 3)),
-        10: columns(2),
-        11: rows(1, (1, 2, 3)),
-        13: columns(3),
-        14: rows(2, (1, 2, 3)),
-        15: rows(3, (1, 2, 3)),
+        2: columns(0),
+        5: columns(1) + [do for part in range(parts) for do in rows(part, (0,))],
+        7: columns(2) + rows(0, (1, 2, 3)),
+        9: columns(3) + rows(1, (1, 2, 3)),
+        11: rows(2, (1, 2, 3)),
+        13: rows(3, (1, 2, 3)),
     }
     for when, work in plan.items():
 
@@ -1045,40 +1118,45 @@
 
     @pl.when(step == 2 * blocks - 1)
     def _():
-        gather.finish()
+        for k in range(7):
+            keep_out(k).wait()
+        normed.finish(False)
+        gather.finish(True)
         for k in range(3):
             for part in range(2):
                 gate_to(k, part).wait_send()
 
 
 def rise(
-    normed, w_up, w_query, w_key, w_value, conv_w, conv_b, gate_parts, gate_b, out_gain, skip_gain,
-    w_down, cot,
+    tokens, ln_gain, w_up, w_query, w_key, w_value, conv_w, conv_b, gate_own, gate_b, out_gain,
+    skip_gain, w_down, cot,
 ):
-    tokens, width = normed.shape
     heads, size, _ = w_query.shape
-    micro, block, _ = cot.shape
-    steps = tokens // block
-    early = lambda g: jnp.minimum(g, steps - 1)
+    micro, block, width = cot.shape
+    steps = 8
+    count = steps * block
     late = lambda g: jnp.maximum(g - steps, 0)
     by_row = lambda n, at: pl.BlockSpec((block, n), lambda g: (at(g), 0))
     kept = lambda shape, index: pl.BlockSpec(shape, index, pipeline_mode=pl.Buffered(1))
     weight = kept((1, size, size), lambda g: (own_head(), 0, 0))
     lanes = lambda rows: kept((rows, size), lambda g: (0, own_head()))
     anywhere = pl.BlockSpec(memory_space=pl.ANY)
+    own = kept(cot.shape, lambda g: (0, 0, 0))
     specs = [
-        by_row(width, early), lanes(width), kept((width, size), lambda g: (0, heads + own_head())),
-        weight, weight, weight, lanes(4), lanes(1), kept(gate_parts.shape, lambda g: (0, 0, 0)),
-        kept(gate_b.shape, lambda g: (0, 0)), lanes(1), lanes(1),
-        kept((size, width), lambda g: (own_head(), 0)), kept(cot.shape, lambda g: (0, 0, 0)),
+        own, kept(ln_gain.shape, lambda g: (0, 0)), lanes(width),
+        kept((width, size), lambda g: (0, heads + own_head())),
+        weight, weight, weight, lanes(4), lanes(1), kept(gate_own.shape, lambda g: (0, 0)),
+        pl.BlockSpec(memory_space=pltpu.SMEM), lanes(1), lanes(1),
+        kept((size, width), lambda g: (own_head(), 0)), own,
     ]
-    outs = [struct((tokens, size), bf16)] * 5 + [struct((tokens, size), f32)]
-    out_specs = [by_row(size, early)] * 6
+    whole = [((count, width), bf16)] + [((count, size), bf16)] * 5 + [((count, size), f32)]
+    outs = [struct(*value) for value in whole]
+    out_specs = [anywhere] * 7
     outs += [
-        struct((tokens, width), bf16), struct((tokens, size), f32),
+        struct((count, width), bf16), struct((count, size), f32),
         struct((steps, size, size), bf16), struct((steps, 8, size), f32),
-        struct((tokens, block), bf16), struct((tokens, 128), f32), struct((8, tokens), f32),
-        struct((tokens, width), bf16),
+        struct((count, block), bf16), struct((count, 128), f32), struct((8, count), f32),
+        struct((count, width), bf16),
     ]
     out_specs += [
         by_row(width, late), by_row(size, late),
@@ -1087,8 +1165,9 @@
         by_row(block, late), by_row(128, late),
         pl.BlockSpec((8, block), lambda g: (0, late(g))), anywhere,
     ]
-    scratch = [((tokens, size), bf16)] * 4 + [((tokens, size), f32), ((8, size), f32)]
-    scratch += [((8, tokens), f32), ((heads, 8, tokens), f32), ((8, block), f32)]
+    scratch = whole + [((micro, block, width), bf16)]
+    scratch += [((8, count), f32), ((heads, 8, count), f32), ((8, block), f32)]
+    scratch += [((3, 32, size), bf16)]
     scratch += [((size, size), f32), ((8, size), f32), ((8, 128), f32)]
     return pl.pallas_call(
         rise_kernel,
@@ -1097,15 +1176,16 @@
         out_specs=out_specs,
         out_shape=outs,
         scratch_shapes=[pltpu.VMEM(shape, dtype) for shape, dtype in scratch]
-        + [pltpu.SemaphoreType.DMA((3, 2)), pltpu.SemaphoreType.DMA((4, 2))] + gather_sems(4),
+        + [pltpu.SemaphoreType.DMA(shape) for shape in ((3, 2), (4, 2), (7,))]
+        + gather_sems(4) * 2,
         compiler_params=pltpu.CompilerParams(
             dimension_semantics=("arbitrary",), collective_id=3, has_side_effects=True,
             vmem_limit_bytes=vmem_bytes,
         ),
         name="rise",
     )(
-        normed, w_up, w_up, w_query, w_key, w_value, conv_w, conv_b, gate_parts, gate_b, out_gain,
-        skip_gain, w_down, cot,
+        tokens, ln_gain, w_up, w_up, w_query, w_key, w_value, conv_w, conv_b, gate_own, gate_b,
+        out_gain, skip_gain, w_down, cot,
     )
 
 
@@ -1319,11 +1399,11 @@
 def drain_kernel(
     d_gate, dq, dk, dv, mix_ref, conv, q_ref, k_ref, v_ref,
     dskip, dskip_next, dz, mix_before, mix_next, normed,
-    gate_pairs, g_gain, w_query, w_key, w_value, w_up, conv_w, conv_b,
+    gate_own, g_gain, w_query, w_key, w_value, w_up, conv_w, conv_b,
     down_ref, lifted_ref, rows_ref, cot_ref, gain_ref, *refs
 ):
     grad_out, up_out, query_out, key_out, value_out, down_out, small_out, *refs = refs
-    w_q, w_k, w_v, w_mix, w_gate, taps_w, taps_b, q_all, k_all, v_all, *refs = refs
+    w_q, w_k, w_v, w_mix, w_gate, taps_w, taps_b, gate_pairs, q_all, k_all, v_all, *refs = refs
     g_q, g_k, g_v, g_small, rows_all, lifted_all, part_all, *refs = refs
     from_core, kept, to_row, from_row, to_owner, owned, *refs = refs
     give_up, give_square, *refs = refs
@@ -1531,6 +1611,11 @@
             to_x(2, q).start()
         for q in range(4):
             start_near(3, q)
+        for p in range(3):
+            one, two, three = split_three(gate_own[8 * p : 8 * p + 8, :])
+            gate_pairs[:, size * p : size * p + size] = jnp.concatenate(
+                [one, one, one, two, two, three], axis=0
+            )
         for copy in weight_copies():
             copy.start()
         for ref in (g_q, g_k, g_v, g_small):
@@ -1603,12 +1688,60 @@
     def early_cross():
         pl.when(x == 0)(lambda: cross(3))
 
-    at_end(0, *every(near_step, 3))
-    at_end(1, *every(x_step, 2))
-    at_end(3, partial(x_step, 1, 0))
-    at_end(4, *every(far_step, 3), early_cross)
-    at_end(5, *every(near_step, 2), partial(x_step, 1, 1), partial(near_step, 1, 0))
-    at_end(7, partial(row_step, order[0]), partial(x_step, 1, 2), partial(near_step, 1, 1))
+    at_end(-3, *every(near_step, 3))
+    at_end(-1, *every(x_step, 2))
+    at_end(1, *every(far_step, 3), early_cross)
+    at_end(2, *every(near_step, 2), partial(x_step, 1, 0))
+    at_end(4, partial(x_step, 1, 1), partial(near_step, 1, 0), *every(far_step, 2), spread_down)
+    at_end(5, partial(row_step, order[0]))
+    at_end(6, partial(x_step, 1, 2), partial(near_step, 1, 1))
+    at_end(7, partial(row_step, order[1]), partial(x_step, 1, 3))
+
+    def norm_back(m, cc):
+        own_part = jnp.logical_and(2 * c + m == z, c == cc)
+        landed = remote(
+            to_owner.at[0], owned.at[m, cc], o_sent.at[0], o_landed.at[m, cc],
+            device(2 * c + m, y, cc),
+        )
+        pl.when(jnp.logical_not(own_part))(lambda: landed.wait_recv())
+        rows_here = pl.ds(cc * half, half)
+        row_hat, rstd = normalize(rows_ref[m, rows_here].astype(f32))
+        scaled = owned[m, cc].astype(f32) * gain_ref[...]
+        d_row = rstd * (
+            scaled
+            - jnp.mean(scaled, axis=-1, keepdims=True)
+            - row_hat * jnp.mean(scaled * row_hat, axis=-1, keepdims=True)
+        )
+        grad_out[m, rows_here] = (cot_ref[m, rows_here].astype(f32) + d_row).astype(bf16)
+
+    def small_after_x():
+        small_to_x().wait_recv()
+        small_sum[...] = g_small[...] + small_x[...]
+        small_z[z] = small_sum[...]
+        for k in range(3):
+            small_to_z(k).start()
+
+    def small_after_z():
+        for k in range(3):
+            small_from_z(k).wait_recv()
+        total = small_z[0]
+        for zz in range(1, 4):
+            total = total + small_z[zz]
+        small_all[head] = total
+        for k in range(3):
+            small_to_head(k).start()
+
+    def spread_square():
+        for yy in range(2):
+            for cc in range(2):
+                for a in range(3):
+                    sq_go[yy, cc, :, tall * a : tall * a + tall] = ends[1][
+                        tall // 2 * yy : tall // 2 * yy + tall // 2,
+                        (2 * a + cc) * tall : (2 * a + cc) * tall + tall,
+                    ].astype(bf16)
+        sq_got[head] = sq_go[y, c]
+        for k in range(3):
+            square_to(k).start()
 
     @pl.when(step == 2 * blocks - 1)
     def _():
@@ -1624,55 +1757,35 @@
             start_near(4, q)
             if q == 0:
                 core_step(2 * z + y)
-        for q in range(4):
-            far_step(2, q)
-        spread_down()
-        row_step(order[1])
-        x_step(1, 3)
+        small_after_x()
+        row_step(order[2])
         near_step(1, 2)
+        near_step(1, 3)
         x_step(0, 0)
-        row_step(order[2])
         near_step(4, 0)
         near_step(4, 1)
-        near_step(1, 3)
+        far_step(1, 0)
+        far_step(1, 1)
+        row_step(z)
         x_step(0, 1)
-        near_step(0, 0)
-        small_to_x().wait_recv()
-        small_sum[...] = g_small[...] + small_x[...]
-        small_z[z] = small_sum[...]
-        for k in range(3):
-            small_to_z(k).start()
         near_step(4, 2)
         near_step(4, 3)
+        small_after_z()
         x_step(0, 2)
+        near_step(0, 0)
         near_step(0, 1)
-        row_step(z)
-        for q in range(4):
-            far_step(1, q)
-        for yy in range(2):
-            for cc in range(2):
-                for a in range(3):
-                    sq_go[yy, cc, :, tall * a : tall * a + tall] = ends[1][
-                        tall // 2 * yy : tall // 2 * yy + tall // 2,
-                        (2 * a + cc) * tall : (2 * a + cc) * tall + tall,
-                    ].astype(bf16)
-        sq_got[head] = sq_go[y, c]
-        for k in range(3):
-            square_to(k).start()
+        far_step(1, 2)
+        far_step(1, 3)
+        spread_square()
         x_step(0, 3)
-        near_step(0, 2)
         for q in range(4):
             far_step(4, q)
         pl.when(x == 1)(lambda: cross(4))
+        near_step(0, 2)
+        for m in range(2):
+            for cc in range(2):
+                norm_back(m, cc)
         near_step(0, 3)
-        for k in range(3):
-            small_from_z(k).wait_recv()
-        total = small_z[0]
-        for zz in range(1, 4):
-            total = total + small_z[zz]
-        small_all[head] = total
-        for k in range(3):
-            small_to_head(k).start()
         for q in range(4):
             far_step(0, q)
         to_cross().wait_recv()
@@ -1687,24 +1800,6 @@
             @pl.when(y == yy)
             def _():
                 up_out[:, size * yy : size * yy + size] = mine
-
-        for m in range(2):
-            for cc in range(2):
-                own_part = jnp.logical_and(2 * c + m == z, c == cc)
-                landed = remote(
-                    to_owner.at[0], owned.at[m, cc], o_sent.at[0], o_landed.at[m, cc],
-                    device(2 * c + m, y, cc),
-                )
-                pl.when(jnp.logical_not(own_part))(lambda: landed.wait_recv())
-                rows_here = pl.ds(cc * half, half)
-                row_hat, rstd = normalize(rows_ref[m, rows_here].astype(f32))
-                scaled = owned[m, cc].astype(f32) * gain_ref[...]
-                d_row = rstd * (
-                    scaled
-                    - jnp.mean(scaled, axis=-1, keepdims=True)
-                    - row_hat * jnp.mean(scaled * row_hat, axis=-1, keepdims=True)
-                )
-                grad_out[m, rows_here] = (cot_ref[m, rows_here].astype(f32) + d_row).astype(bf16)
 
         for k in range(3):
             small_from_head(k).wait_recv()
@@ -1757,7 +1852,7 @@
 
 def drain(inputs, down, lifted, rows, cot, gain):
     (d_gate, dq, dk, dv, dskip, dz, mix, conv, q, k, v, normed,
-     w_query, w_key, w_value, w_up, conv_w, conv_b, gate_pairs, g_gain) = inputs
+     w_query, w_key, w_value, w_up, conv_w, conv_b, gate_own, g_gain) = inputs
     tokens, size = q.shape
     micro, block, width = rows.shape
     half = block // 2
@@ -1777,16 +1872,17 @@
     )
     anywhere = pl.BlockSpec(memory_space=pl.ANY)
     arguments = (
-        d_gate, dq, dk, dv, mix, conv, q, k, v, dskip, dskip, dz, mix, mix, normed, gate_pairs, g_gain,
+        d_gate, dq, dk, dv, mix, conv, q, k, v, dskip, dskip, dz, mix, mix, normed, gate_own, g_gain,
         w_query, w_key, w_value, w_up, conv_w, conv_b, down, lifted, rows, cot, gain,
     )
     specs = [pl.BlockSpec((8, block), lambda g: (0, early(g)))] + [by_row(size, early)] * 3
     specs += [by_row(size, both)] + [by_row(size, early)] * 4
     specs += [by_row(size, late), behind, by_row(size, late), before, behind, by_row(width, late)]
-    specs += [kept(gate_pairs), kept(g_gain)]
+    specs += [kept(gate_own), kept(g_gain)]
     specs += [anywhere] * 6 + [kept(value) for value in (down, lifted, rows, cot, gain)]
     scratch = [((size, size), bf16)] * 3 + [((width, size), bf16)] * 2
-    scratch += [((4, size), f32), ((1, size), f32)] + [((tokens + 16, size), bf16)] * 3
+    scratch += [((4, size), f32), ((1, size), f32), ((48, 3 * size), bf16)]
+    scratch += [((tokens + 16, size), bf16)] * 3
     scratch += [((size, size), f32)] * 3 + [((lines, size), f32)]
     scratch += [((tokens, width), bf16), ((tokens, size), bf16), ((8, block, width), bf16)]
     scratch += [
@@ -1833,6 +1929,43 @@
     )(*arguments)
 
 
+def spread_kernel(small, gain, *refs):
+    count = (len(refs) - 7) // 2
+    for k in range(count):
+        refs[count + 7 + k][...] = refs[k][...]
+    ln_out, conv_out, bias_out, gate_out, forget_out, out_gain, skip_gain = refs[count : count + 7]
+    heads, _, size = small.shape
+    total = small[0, 32:34, :]
+    for h in range(1, heads):
+        total = total + small[h, 32:34, :]
+    for k in range(2):
+        lanes = slice(size * k, size * k + size)
+        ln_out[:, lanes] = total[k : k + 1, :] / gain[:, lanes]
+    for h in range(heads):
+        lanes = slice(size * h, size * h + size)
+        conv_out[:, lanes] = small[h, 24:28, :]
+        bias_out[:, lanes] = small[h, 28:29, :]
+        out_gain[:, lanes] = small[h, 29:30, :]
+        skip_gain[:, lanes] = small[h, 30:31, :]
+        forget_out[:, h : h + 1] = small[h, 31:32, 0:1]
+        for p in range(3):
+            start = (heads * p + h) * size
+            gate_out[:, start : start + size] = small[h, 8 * p : 8 * p + 8, :]
+
+
+def spread(small, gain, *made):
+    heads, _, size = small.shape
+    inner = heads * size
+    shapes = [gain.shape, (4, inner), (1, inner), (8, 3 * inner), (1, heads), (1, inner), (1, inner)]
+    return pl.pallas_call(
+        spread_kernel,
+        out_shape=[struct(shape, f32) for shape in shapes]
+        + [struct(value.shape, value.dtype) for value in made],
+        name="spread",
+        compiler_params=pltpu.CompilerParams(vmem_limit_bytes=62 * 2**20),
+    )(small, gain, *made)
+
+
 def swap(value, axis, mask):
     count = lax.axis_size(axis)
     return lax.ppermute(value, axis, [(s, s ^ mask) for s in range(count)])
@@ -1982,10 +2115,10 @@
     out_row = out_gain.reshape(1, inner)
     skip_row = skip_gain.reshape(1, inner)
 
-    normed = gather_normed(tokens[:, 0], ln_gain[None])
     gate_own = lax.dynamic_index_in_dim(
         gate_w.reshape(3, heads, size, 8), at, 1, keepdims=False
     ).transpose(0, 2, 1)
+    gate_rows = gate_own.reshape(24, size)
     high = lax.reduce_precision(gate_own, 8, 7)
     middle = lax.reduce_precision(gate_own - high, 8, 7)
     low = lax.reduce_precision(gate_own - high - middle, 8, 7)
@@ -1998,11 +2131,13 @@
     )
 
     if direct:
-        (mix, conv, q, k, v, gate_z, part, head_normed, states, norms, weights, cols, rows, cot) = rise(
-            normed, w_up, w_query, w_key, w_value, conv_w, conv_row, gate_parts, gate_b[:, None],
+        (normed, mix, conv, q, k, v, gate_z,
+         part, head_normed, states, norms, weights, cols, rows, cot) = rise(
+            tokens[:, 0], ln_gain[None], w_up, w_query, w_key, w_value, conv_w, conv_row, gate_rows, gate_b,
             out_row, skip_row, w_down, d_out[:, 0],
         )
     else:
+        normed = gather_normed(tokens[:, 0], ln_gain[None])
         cot = gather_sequence(d_out[:, 0])
         first = () if ranges == 1 else (shifted(normed[-16:], "seq", 8),)
         mix, conv, q, k, v, gate_z, gates, *halo = lift(
@@ -2061,7 +2196,7 @@
     )
     if direct:
         grad_rows, s_up, s_query, s_key, s_value, s_down, small = drain(
-            lower_args, g_down, g_z, tokens[:, 0], d_out[:, 0], ln_gain[None]
+            (*lower_args[:18], gate_rows, g_gain), g_down, g_z, tokens[:, 0], d_out[:, 0], ln_gain[None]
         )
     else:
         first = ()
@@ -2086,23 +2221,24 @@
         s_query, s_key, s_value = squares[:, 0], squares[:, 1], squares[:, 2]
         small = jnp.where(jnp.arange(heads)[:, None, None] == at, small, 0.0)
         small = lax.psum(small, ("seq", "batch"))
-    s_ln = jnp.sum(small[:, 32:34], 0).reshape(-1) / ln_gain
-    s_gate_w = small[:, :24].reshape(heads, 3, 8, size).transpose(1, 0, 3, 2).reshape(3 * inner, 8)
-    s_conv_w = small[:, 24:28].transpose(1, 0, 2).reshape(4, inner)
+    (s_ln, s_conv_w, s_conv_b, s_gate_w, s_gate_b, s_out_gain, s_skip,
+     block_rows, grad_rows, s_up, s_query, s_key, s_value, s_down) = spread(
+        small, ln_gain[None], block_rows, grad_rows, s_up, s_query, s_key, s_value, s_down
+    )
     return (
         block_rows[:, None],
         grad_rows[:, None],
-        s_ln,
+        s_ln[0],
         s_up,
         s_conv_w,
-        small[:, 28].reshape(inner),
+        s_conv_b[0],
         s_query,
         s_key,
         s_value,
-        s_gate_w,
-        small[:, 31, 0],
-        small[:, 29].reshape(inner),
-        small[:, 30].reshape(inner),
+        s_gate_w.T,
+        s_gate_b[0],
+        s_out_gain[0],
+        s_skip[0],
         s_down,
     )
 

time: 264 us -> 228 us (0.86)
  local copies, waits for them, and re-layouts: 18.8 us -> 1.53 us
  Pallas kernels: 240 us -> 225 us
  other arithmetic: 4.61 us -> 0 us
    pallas_call x1, Pallas kernels: 35.7 us -> 3.77 us  [spread(): pl.pallas_call(spread_kernel, out_shape=[struct(shape, f32) for shape in...]
    pallas_call x1, Pallas kernels: 49.6 us -> 71.3 us  [rise(): pl.pallas_call(rise_kernel, grid=(2 * steps,), in_specs=specs, out_specs=...]
    pallas_call x1, Pallas kernels: 111 us -> 101 us  [drain(): pl.pallas_call(drain_kernel, grid=(2 * steps,), in_specs=specs, out_specs...]
    unnamed x31 -> x4, local copies, waits for them, and re-layouts: 10.6 us -> 0.91 us
    pallas_call x1, Pallas kernels: 43.6 us -> 49.5 us  [settle(): pl.pallas_call(settle_kernel, grid=(count // length,), in_specs=specs, ou...]
    slice x3 -> x0, local copies, waits for them, and re-layouts: 4.46 us -> none  [the longest x1 1.57 us: head_device(): small[:, 30].reshape(inner)]
where the time goes in v6:
time: 228 us
  Pallas kernels  225 us (99%)
    pallas_call x1, Pallas kernels, drain(): pl.pallas_call(drain_kernel, grid=(2 * steps,), in_specs=specs, out_specs...  101 us
    pallas_call x1, Pallas kernels, rise(): pl.pallas_call(rise_kernel, grid=(2 * steps,), in_specs=specs, out_specs=...  71.3 us
    pallas_call x1, Pallas kernels, settle(): pl.pallas_call(settle_kernel, grid=(count // length,), in_specs=specs, ou...  49.5 us

profile of v6, /device:TPU:24, one launch (start us, length us, event | category | flops | bytes accessed | tf_op | source)
XLA Modules:
  0.0 227.8 jit_solution(3932588806768294440)
XLA Ops:
  0.6 0.0 copy-start
  0.7 0.9 copy-done
  1.6 0.6 dynamic-slice_bitcast_fusion.gate_own
  2.2 71.3 %rise.1 = (bf16[2048,1024]{1,0:T(8,128)(2,1)}, bf16[2048,512]{1,0:T(8,128)(2,1)}, bf16[2048,512]{1,0:T(8,128)(2,1)}, bf16[2048,512]{1,0:T(8,128)(2,1)}, bf16[204...) custom-call(bf16[2,256,1024]{2,1,0:T(8,128)(2,1)} %bitcast.26, ...), custom_call_target="tpu_custom_call" | custom-call | tf_op jit(solution)/shard_map/rise/pallas_call | solution.py:1172
  73.5 49.5 %settle.1 = (f32[2048,512]{1,0:T(8,128)}, f32[2048,512]{1,0:T(8,128)}, f32[2048,512]{1,0:T(8,128)}, f32[2048,512]{1,0:T(8,128)}, bf16[2048,512]{1,0:T(8,128)(2,1...) custom-call(f32[8,2048]{1,0:T(8,128)} %get-tuple-element.60.refs_0_,, ...), custom_call_target="tpu_custom_call" | custom-call | flops 12884901888 | bytes 50331648 | tf_op jit(solution)/shard_map/settle/pallas_call | solution.py:1376
  123.1 0.0 copy-start.1
  123.1 100.8 %drain.1 = (bf16[2,256,1024]{2,1,0:T(8,128)(2,1)}, f32[128,1024]{1,0:T(8,128)}, f32[4,64,128]{2,1,0:T(8,128)}, f32[4,64,128]{2,1,0:T(8,128)}, f32[4,64,128]{2,1,...) custom-call(f32[8,2048]{1,0:T(8,128)} %get-tuple-element.74.d_gate, f32[2048,512]{1,0:T(8,128)} %get-tuple-element.75.dq, ...), custom_call_target="tpu_custom_call" | custom-call | flops 15032385536 | bytes 50331648 | tf_op jit(solution)/shard_map/drain/pallas_call | solution.py:1912
  223.9 3.8 %spread.1 = (f32[1,1024]{1,0:T(1,128)}, f32[4,2048]{1,0:T(4,128)}, f32[1,2048]{1,0:T(1,128)}, f32[8,6144]{1,0:T(8,128)}, f32[1,4]{1,0:T(1,128)}, /*index=5*/f32[...) custom-call(f32[4,40,512]{2,1,0:T(8,128)} %get-tuple-element.84.smal, ...), custom_call_target="tpu_custom_call" | custom-call | tf_op jit(solution)/shard_map/spread/pallas_call | solution.py:1960
  227.6 0.0 copy-done.1
Async XLA Ops:
  0.6 0.9 copy-start
  123.1 104.6 %copy-start.1 = (f32[6144,8]{0,1:T(8,128)S(1)}, f32[6144,8]{0,1:T(8,128)}, u32[]{:S(2)}) copy-start(f32[6144,8]{0,1:T(8,128)} %param.22) | copy-start | bytes 589828

commit v7 on v6

--- a/solution.py
+++ b/solution.py
@@ -186,30 +186,10 @@
     return row >= col, row == col
 
 
-def cell_forward_kernel(
-    chained, head_ref, gates, q_ref, k_ref, v_ref, conv_ref, z_ref, out_gain, skip_gain, w_down, *refs,
-    start=0,
-):
-    if chained:
-        *first, part_out, normed_out, state_out, norm_out, weight_out, col_out, row_out = refs[:10]
-        *final, state, norm, level = refs[10:]
-    else:
-        part_out, normed_out, state_out, norm_out, weight_out, col_out, row_out = refs[:7]
-        state, norm, level = refs[7:]
+def cell_recur(gates, q_ref, k_ref, v_ref, state_out, norm_out, weight_out, row_out, state, norm, level):
     length = q_ref.shape[0]
     head_size = q_ref.shape[1]
     scale = head_size ** (-0.5)
-
-    @pl.when(pl.program_id(0) == start)
-    def _():
-        if chained:
-            for ref, value in zip((state, norm, level), first):
-                ref[...] = value[...]
-        else:
-            state[...] = jnp.zeros_like(state)
-            norm[...] = jnp.zeros_like(norm)
-            level[...] = jnp.full_like(level, floor_value)
-
     causal, diagonal = masks(length)
     a_row, run_col, log_forget = gate_rows(gates[...], causal, diagonal)
     before = level[0:1, 0:1]
@@ -237,26 +217,9 @@
     size = jnp.abs(denominator)
     inverse = 1.0 / jnp.maximum(size, floor)
     hidden = numerator * inverse
-    centre = hidden - jnp.mean(hidden, axis=1, keepdims=True)
-    spread = jnp.mean(centre * centre, axis=1, keepdims=True)
-    rstd = lax.rsqrt(spread + norm_epsilon)
-    normed = centre * rstd
-    normed_out[...] = normed
-    gate_z = z_ref[...]
-    gated = (normed * out_gain[...] + skip_gain[...] * conv_ref[...].astype(f32)) * (
-        gate_z * jax.nn.sigmoid(gate_z)
-    )
-    part_out[...] = mm(gated.astype(bf16), w_down[...]).astype(bf16)
-    factor = jnp.where(
-        size > floor,
-        jnp.where(denominator > 0, 1.0, -1.0) * inverse * (norm_epsilon * rstd * rstd),
-        0.0,
-    )
-    lane = lax.broadcasted_iota(jnp.int32, (length, 128), 1)
-    packed = jnp.where(lane == 0, rstd, inverse)
-    packed = jnp.where(lane == 2, from_state, packed)
-    packed = jnp.where(lane == 3, top, packed)
-    col_out[...] = jnp.where(lane == 4, factor, packed)
+    slope = jnp.where(
+        size > floor, jnp.where(denominator > 0, 1.0, -1.0) * inverse * norm_epsilon, 0.0
+    )
     sub = lax.broadcasted_iota(jnp.int32, (8, length), 0)
     row_out[...] = jnp.where(sub == 0, a_row, 1.0 - jnp.exp(log_forget))
     last = top[length - 1 : length, :]
@@ -266,6 +229,54 @@
     state[...] = keep * state[...] + mm_tn(weighted.astype(bf16), v)
     norm[...] = keep * norm[...] + jnp.sum(weighted, axis=0, keepdims=True)
     level[...] = jnp.broadcast_to(run_col[length - 1 : length, :] + last, level.shape)
+    lane = lax.broadcasted_iota(jnp.int32, (length, 128), 1)
+    packed = jnp.where(lane == 1, inverse, slope)
+    packed = jnp.where(lane == 2, from_state, packed)
+    return hidden, jnp.where(lane == 3, top, packed)
+
+
+def cell_head(hidden, cols, conv_ref, z_ref, out_gain, skip_gain, w_down, part_out, normed_out, col_out):
+    centre = hidden - jnp.mean(hidden, axis=1, keepdims=True)
+    spread = jnp.mean(centre * centre, axis=1, keepdims=True)
+    rstd = lax.rsqrt(spread + norm_epsilon)
+    normed = centre * rstd
+    normed_out[...] = normed
+    gate_z = z_ref[...]
+    gated = (normed * out_gain[...] + skip_gain[...] * conv_ref[...].astype(f32)) * (
+        gate_z * jax.nn.sigmoid(gate_z)
+    )
+    part_out[...] = mm(gated.astype(bf16), w_down[...]).astype(bf16)
+    lane = lax.broadcasted_iota(jnp.int32, cols.shape, 1)
+    cols = jnp.where(lane == 0, rstd, cols)
+    col_out[...] = jnp.where(lane == 4, cols * (rstd * rstd), cols)
+
+
+def cell_forward_kernel(
+    chained, head_ref, gates, q_ref, k_ref, v_ref, conv_ref, z_ref, out_gain, skip_gain, w_down, *refs
+):
+    if chained:
+        *first, part_out, normed_out, state_out, norm_out, weight_out, col_out, row_out = refs[:10]
+        *final, state, norm, level = refs[10:]
+    else:
+        part_out, normed_out, state_out, norm_out, weight_out, col_out, row_out = refs[:7]
+        state, norm, level = refs[7:]
+
+    @pl.when(pl.program_id(0) == 0)
+    def _():
+        if chained:
+            for ref, value in zip((state, norm, level), first):
+                ref[...] = value[...]
+        else:
+            state[...] = jnp.zeros_like(state)
+            norm[...] = jnp.zeros_like(norm)
+            level[...] = jnp.full_like(level, floor_value)
+
+    hidden, cols = cell_recur(
+        gates, q_ref, k_ref, v_ref, state_out, norm_out, weight_out, row_out, state, norm, level
+    )
+    cell_head(
+        hidden, cols, conv_ref, z_ref, out_gain, skip_gain, w_down, part_out, normed_out, col_out
+    )
     if chained:
         for ref, value in zip(final, (state, norm, level)):
             ref[...] = value[...]
@@ -784,12 +795,12 @@
 
 
 class Gather:
-    def __init__(self, source, out_ref, block, parts, sems):
-        self.source, self.out_ref, self.block, self.parts = source, out_ref, block, parts
+    def __init__(self, source, out_ref, block, cuts, sems):
+        self.source, self.out_ref, self.block, self.cuts = source, out_ref, block, cuts
+        self.parts = len(cuts)
         self.kept, self.z_sent, self.z_landed, self.y_sent, self.y_landed, *sems = sems
         self.c_sent, self.c_landed = sems
         self.first, self.z, self.y, self.x, self.c = where_am_i()
-        self.size = block // parts
         self.enters = halves_of(self.z, 4)[0] == self.c
 
     def device(self, zz, yy, cc):
@@ -800,21 +811,23 @@
         return others + [self.device(self.z, 1 - self.y, self.c), self.device(self.z, self.y, 1 - self.c)]
 
     def rows(self, zz, yy, part):
-        start = (2 * zz + yy) * self.block + part * self.size
-        return self.out_ref.at[pl.ds(pl.multiple_of(start, self.size), self.size)]
+        start, size = self.cuts[part]
+        return self.out_ref.at[
+            pl.ds(pl.multiple_of((2 * zz + yy) * self.block + start, 16), size)
+        ]
 
     def away(self, m):
         return 2 * self.c + m != self.z
 
     def to_column(self, m, part):
         return remote(
-            self.source(m, part), self.rows(self.z, self.y, part), self.z_sent.at[m, part],
+            self.source(m, pl.ds(*self.cuts[part])), self.rows(self.z, self.y, part), self.z_sent.at[m, part],
             self.z_landed.at[self.z, part], self.device(2 * self.c + m, self.y, self.c),
         )
 
     def keep(self, m, part):
         return pltpu.make_async_copy(
-            self.source(m, part), self.rows(self.z, self.y, part), self.kept.at[part]
+            self.source(m, pl.ds(*self.cuts[part])), self.rows(self.z, self.y, part), self.kept.at[part]
         )
 
     def from_column(self, zz, part):
@@ -894,6 +907,16 @@
                 pl.when(self.away(m))(lambda: self.to_column(m, part).wait_send())
 
 
+def even_cuts(block, parts):
+    size = block // parts
+    return [(part * size, size) for part in range(parts)]
+
+
+def falling_cuts(block):
+    unit = block // 16
+    return [(0, 5 * unit), (5 * unit, 5 * unit), (10 * unit, 4 * unit), (14 * unit, 2 * unit)]
+
+
 def gather_sems(parts):
     shapes = [(parts,), (2, parts), (4, parts), (4, parts), (4, parts), (8, parts), (8, parts)]
     return [pltpu.SemaphoreType.DMA(shape) for shape in shapes]
@@ -902,13 +925,11 @@
 def gather_kernel(rows_ref, gain_ref, out_ref, staged, *sems):
     parts = sems[0].shape[0]
     block = rows_ref.shape[1]
-    size = block // parts
-    gather = Gather(
-        lambda m, part: staged.at[m, pl.ds(part * size, size)], out_ref, block, parts, sems
-    )
+    cuts = even_cuts(block, parts)
+    gather = Gather(lambda m, here: staged.at[m, here], out_ref, block, cuts, sems)
     greet(gather.others())
     for part in range(parts):
-        here = pl.ds(part * size, size)
+        here = pl.ds(*cuts[part])
         for m in range(2):
             staged[m, here] = (
                 normalize(rows_ref[m, here].astype(f32))[0] * gain_ref[...]
@@ -960,18 +981,16 @@
 ):
     kept_outs, cell_outs, (cot_out, *refs) = refs[:7], refs[7:14], refs[14:]
     rows_all, mix_all, conv_all, q_all, k_all, v_all, z_all, *refs = refs
-    staged, gate_mine, gate_all, gates, gate_parts, *refs = refs
+    staged, gate_mine, gate_all, gates, gate_parts, hidden_kept, cols_kept, *refs = refs
     state, h_sent, h_landed, out_sem, *sems = refs[:3], *refs[3:]
     parts = sems[0].shape[0]
     step = pl.program_id(0)
-    blocks = pl.num_programs(0) // 2
+    blocks = (pl.num_programs(0) - 1) // 2
     micro, block, width = cot_ref.shape
-    size = block // parts
-    normed = Gather(
-        lambda m, part: staged.at[m, pl.ds(part * size, size)], rows_all, block, parts, sems[:7]
-    )
+    cuts = falling_cuts(block)
+    normed = Gather(lambda m, here: staged.at[m, here], rows_all, block, cuts, sems[:7])
     gather = Gather(
-        lambda m, part: cot_ref.at[m, pl.ds(part * size, size)], cot_out, block, parts, sems[7:]
+        lambda m, here: cot_ref.at[m, here], cot_out, block, even_cuts(block, parts), sems[7:]
     )
     z, y, c = gather.z, gather.y, gather.c
     head = 2 * c + y
@@ -999,9 +1018,9 @@
         return pltpu.make_async_copy(made, kept_outs[k], out_sem.at[k])
 
     def lift_up(yy, part):
+        start, size = cuts[part]
         here = [
-            pl.ds(pl.multiple_of((2 * zz + yy) * block + part * size, size), size)
-            for zz in range(4)
+            pl.ds(pl.multiple_of((2 * zz + yy) * block + start, 16), size) for zz in range(4)
         ]
         rows = jnp.concatenate([rows_all[at] for at in here], axis=0)
         mix = mm(rows, w_mix[...]).astype(bf16)
@@ -1023,7 +1042,7 @@
             gate_parts[p, 0:24] = jnp.concatenate(split_three(gate_own[8 * p : 8 * p + 8, :]), axis=0)
             gate_parts[p, 24:32] = jnp.zeros_like(gate_parts[p, 24:32])
         for part in range(parts):
-            here = pl.ds(part * size, size)
+            here = pl.ds(*cuts[part])
             for m in range(2):
                 staged[m, here] = (
                     normalize(tokens[m, here].astype(f32))[0] * ln_gain[...]
@@ -1079,8 +1098,9 @@
             for k in range(3):
                 gate_from(k, part).wait_recv()
 
-    @pl.when(step >= blocks)
-    def _():
+    part_out, normed_out, state_out, norm_out, weight_out, col_out, row_out = cell_outs
+
+    def recur():
         here = pl.ds(pl.multiple_of((step - blocks) * block, block), block)
         for row, at in enumerate((head, heads + head)):
             total = gate_all[0, pl.ds(at, 1), here]
@@ -1089,10 +1109,31 @@
             if row == 1:
                 total = total + gate_b[head]
             gates[row : row + 1, :] = total
-        cell_forward_kernel(
-            False, None, gates, q_all.at[here], k_all.at[here], v_all.at[here], conv_all.at[here],
-            z_all.at[here], out_gain, skip_gain, w_down, *cell_outs, *state, start=blocks,
-        )
+        return cell_recur(
+            gates, q_all.at[here], k_all.at[here], v_all.at[here],
+            state_out, norm_out, weight_out, row_out, *state,
+        )
+
+    def head_of_last():
+        here = pl.ds(pl.multiple_of((step - blocks - 1) * block, block), block)
+        cell_head(
+            hidden_kept[...], cols_kept[...], conv_all.at[here], z_all.at[here],
+            out_gain, skip_gain, w_down, part_out, normed_out, col_out,
+        )
+
+    @pl.when(step == blocks)
+    def _():
+        state[0][...] = jnp.zeros_like(state[0])
+        state[1][...] = jnp.zeros_like(state[1])
+        state[2][...] = jnp.full_like(state[2], floor_value)
+        hidden_kept[...], cols_kept[...] = recur()
+
+    @pl.when(jnp.logical_and(step > blocks, step < 2 * blocks))
+    def _():
+        head_of_last()
+        hidden_kept[...], cols_kept[...] = recur()
+
+    pl.when(step == 2 * blocks)(head_of_last)
 
     def columns(part, ks=(1, 2, 3)):
         return [partial(gather.pass_column, k, part) for k in ks]
@@ -1116,7 +1157,7 @@
             for do in work:
                 do()
 
-    @pl.when(step == 2 * blocks - 1)
+    @pl.when(step == 2 * blocks)
     def _():
         for k in range(7):
             keep_out(k).wait()
@@ -1135,7 +1176,8 @@
     micro, block, width = cot.shape
     steps = 8
     count = steps * block
-    late = lambda g: jnp.maximum(g - steps, 0)
+    late = lambda g: jnp.clip(g - steps, 0, steps - 1)
+    after = lambda g: jnp.clip(g - steps - 1, 0, steps - 1)
     by_row = lambda n, at: pl.BlockSpec((block, n), lambda g: (at(g), 0))
     kept = lambda shape, index: pl.BlockSpec(shape, index, pipeline_mode=pl.Buffered(1))
     weight = kept((1, size, size), lambda g: (own_head(), 0, 0))
@@ -1159,19 +1201,19 @@
         struct((count, width), bf16),
     ]
     out_specs += [
-        by_row(width, late), by_row(size, late),
+        by_row(width, after), by_row(size, after),
         pl.BlockSpec((1, size, size), lambda g: (late(g), 0, 0)),
         pl.BlockSpec((1, 8, size), lambda g: (late(g), 0, 0)),
-        by_row(block, late), by_row(128, late),
+        by_row(block, late), by_row(128, after),
         pl.BlockSpec((8, block), lambda g: (0, late(g))), anywhere,
     ]
     scratch = whole + [((micro, block, width), bf16)]
     scratch += [((8, count), f32), ((heads, 8, count), f32), ((8, block), f32)]
-    scratch += [((3, 32, size), bf16)]
+    scratch += [((3, 32, size), bf16), ((block, size), f32), ((block, 128), f32)]
     scratch += [((size, size), f32), ((8, size), f32), ((8, 128), f32)]
     return pl.pallas_call(
         rise_kernel,
-        grid=(2 * steps,),
+        grid=(2 * steps + 1,),
         in_specs=specs,
         out_specs=out_specs,
         out_shape=outs,
@@ -1292,7 +1334,7 @@
 
     for k in range(4):
         pl.when(step == k)(lambda: core_step(order[k]))
-    for k, when in enumerate((2, 4, 5)):
+    for k, when in enumerate((1, 3, 5)):
         pl.when(step == when)(lambda: row_step(order[k]))
 
     @pl.when(step == pl.num_programs(0) - 1)

time: 228 us -> 228 us (level)
  no operation moved by 1% of the time
where the time goes in v7:
time: 228 us; the launch traced here: 227 us
  Pallas kernels  225 us (99%)
    pallas_call x1, Pallas kernels, drain(): pl.pallas_call(drain_kernel, grid=(2 * steps,), in_specs=specs, out_specs...  100 us
    pallas_call x1, Pallas kernels, rise(): pl.pallas_call(rise_kernel, grid=(2 * steps + 1,), in_specs=specs, out_sp...  72.5 us
    pallas_call x1, Pallas kernels, settle(): pl.pallas_call(settle_kernel, grid=(count // length,), in_specs=specs, ou...  48.7 us

profile of v7, /device:TPU:24, one launch (start us, length us, event | category | flops | bytes accessed | tf_op | source)
XLA Modules:
  0.0 227.5 jit_solution(1553841266659009361)
XLA Ops:
  0.6 0.0 copy-start
  0.7 0.9 copy-done
  1.6 0.6 dynamic-slice_bitcast_fusion.gate_own
  2.2 72.5 %rise.1 = (bf16[2048,1024]{1,0:T(8,128)(2,1)}, bf16[2048,512]{1,0:T(8,128)(2,1)}, bf16[2048,512]{1,0:T(8,128)(2,1)}, bf16[2048,512]{1,0:T(8,128)(2,1)}, bf16[204...) custom-call(bf16[2,256,1024]{2,1,0:T(8,128)(2,1)} %bitcast.26, ...), custom_call_target="tpu_custom_call" | custom-call | tf_op jit(solution)/shard_map/rise/pallas_call | solution.py:1214
  74.7 48.7 %settle.1 = (f32[2048,512]{1,0:T(8,128)}, f32[2048,512]{1,0:T(8,128)}, f32[2048,512]{1,0:T(8,128)}, f32[2048,512]{1,0:T(8,128)}, bf16[2048,512]{1,0:T(8,128)(2,1...) custom-call(f32[8,2048]{1,0:T(8,128)} %get-tuple-element.60.refs_0_,, ...), custom_call_target="tpu_custom_call" | custom-call | flops 12884901888 | bytes 50331648 | tf_op jit(solution)/shard_map/settle/pallas_call | solution.py:1418
  123.4 0.0 copy-start.1
  123.4 100.1 %drain.1 = (bf16[2,256,1024]{2,1,0:T(8,128)(2,1)}, f32[128,1024]{1,0:T(8,128)}, f32[4,64,128]{2,1,0:T(8,128)}, f32[4,64,128]{2,1,0:T(8,128)}, f32[4,64,128]{2,1,...) custom-call(f32[8,2048]{1,0:T(8,128)} %get-tuple-element.74.d_gate, f32[2048,512]{1,0:T(8,128)} %get-tuple-element.75.dq, ...), custom_call_target="tpu_custom_call" | custom-call | flops 15032385536 | bytes 50331648 | tf_op jit(solution)/shard_map/drain/pallas_call | solution.py:1954
  223.5 3.8 %spread.1 = (f32[1,1024]{1,0:T(1,128)}, f32[4,2048]{1,0:T(4,128)}, f32[1,2048]{1,0:T(1,128)}, f32[8,6144]{1,0:T(8,128)}, f32[1,4]{1,0:T(1,128)}, /*index=5*/f32[...) custom-call(f32[4,40,512]{2,1,0:T(8,128)} %get-tuple-element.84.smal, ...), custom_call_target="tpu_custom_call" | custom-call | tf_op jit(solution)/shard_map/spread/pallas_call | solution.py:2002
  227.3 0.0 copy-done.1
Async XLA Ops:
  0.6 0.9 copy-start
  123.4 103.9 %copy-start.1 = (f32[6144,8]{0,1:T(8,128)S(1)}, f32[6144,8]{0,1:T(8,128)}, u32[]{:S(2)}) copy-start(f32[6144,8]{0,1:T(8,128)} %param.22) | copy-start | bytes 589828

commit v8 on v7

--- a/solution.py
+++ b/solution.py
@@ -976,12 +976,13 @@
 
 
 def rise_kernel(
-    tokens, ln_gain, w_mix, w_gate, w_q, w_k, w_v, conv_w, conv_b, gate_own, gate_b, out_gain,
-    skip_gain, w_down, cot_ref, *refs
+    tokens, ln_gain, up_src, q_src, k_src, v_src, conv_w, conv_b, gate_own, gate_b, out_gain,
+    skip_gain, down_src, cot_src, *refs
 ):
     kept_outs, cell_outs, (cot_out, *refs) = refs[:7], refs[7:14], refs[14:]
     rows_all, mix_all, conv_all, q_all, k_all, v_all, z_all, *refs = refs
     staged, gate_mine, gate_all, gates, gate_parts, hidden_kept, cols_kept, *refs = refs
+    w_mix, w_gate, w_q, w_k, w_v, w_down, cot_ref, load_sem, *refs = refs
     state, h_sent, h_landed, out_sem, *sems = refs[:3], *refs[3:]
     parts = sems[0].shape[0]
     step = pl.program_id(0)
@@ -1012,6 +1013,18 @@
             gate_mine.at[:, lanes], gate_all.at[at, :, lanes], h_sent.at[k, part],
             h_landed.at[at, part], gather.device(z, *group[k]),
         )
+
+    wide = w_mix.shape[1]
+    own_lanes = pl.ds(pl.multiple_of(head * wide, wide), wide)
+    gate_lanes = pl.ds(pl.multiple_of((heads + head) * wide, wide), wide)
+    loads = [
+        (up_src.at[:, own_lanes], w_mix), (up_src.at[:, gate_lanes], w_gate),
+        (q_src.at[pl.ds(head, 1)], w_q), (k_src.at[pl.ds(head, 1)], w_k),
+        (v_src.at[pl.ds(head, 1)], w_v), (down_src.at[own_lanes], w_down), (cot_src, cot_ref),
+    ]
+
+    def load(k):
+        return pltpu.make_async_copy(*loads[k], load_sem.at[k])
 
     def keep_out(k):
         made = (rows_all, mix_all, conv_all, q_all, k_all, v_all, z_all)[k]
@@ -1048,9 +1061,14 @@
                     normalize(tokens[m, here].astype(f32))[0] * ln_gain[...]
                 ).astype(bf16)
             normed.start(part)
+        for k in range(7):
+            load(k).start()
         for part in range(parts):
             for k in range(4):
                 normed.pass_column(k, part)
+            if part == 0:
+                for k in range(7):
+                    load(k).wait()
             if part == parts - 1:
                 for later in range(parts):
                     gather.start(later)
@@ -1180,16 +1198,13 @@
     after = lambda g: jnp.clip(g - steps - 1, 0, steps - 1)
     by_row = lambda n, at: pl.BlockSpec((block, n), lambda g: (at(g), 0))
     kept = lambda shape, index: pl.BlockSpec(shape, index, pipeline_mode=pl.Buffered(1))
-    weight = kept((1, size, size), lambda g: (own_head(), 0, 0))
     lanes = lambda rows: kept((rows, size), lambda g: (0, own_head()))
     anywhere = pl.BlockSpec(memory_space=pl.ANY)
     own = kept(cot.shape, lambda g: (0, 0, 0))
     specs = [
-        own, kept(ln_gain.shape, lambda g: (0, 0)), lanes(width),
-        kept((width, size), lambda g: (0, heads + own_head())),
-        weight, weight, weight, lanes(4), lanes(1), kept(gate_own.shape, lambda g: (0, 0)),
+        own, kept(ln_gain.shape, lambda g: (0, 0)), anywhere, anywhere, anywhere, anywhere, lanes(4), lanes(1), kept(gate_own.shape, lambda g: (0, 0)),
         pl.BlockSpec(memory_space=pltpu.SMEM), lanes(1), lanes(1),
-        kept((size, width), lambda g: (own_head(), 0)), own,
+        anywhere, anywhere,
     ]
     whole = [((count, width), bf16)] + [((count, size), bf16)] * 5 + [((count, size), f32)]
     outs = [struct(*value) for value in whole]
@@ -1210,14 +1225,18 @@
     scratch = whole + [((micro, block, width), bf16)]
     scratch += [((8, count), f32), ((heads, 8, count), f32), ((8, block), f32)]
     scratch += [((3, 32, size), bf16), ((block, size), f32), ((block, 128), f32)]
-    scratch += [((size, size), f32), ((8, size), f32), ((8, 128), f32)]
+    loaded = [((width, size), bf16)] * 2 + [((1, size, size), bf16)] * 3
+    loaded += [((size, width), bf16), (cot.shape, bf16)]
+    states = [((size, size), f32), ((8, size), f32), ((8, 128), f32)]
     return pl.pallas_call(
         rise_kernel,
         grid=(2 * steps + 1,),
         in_specs=specs,
         out_specs=out_specs,
         out_shape=outs,
-        scratch_shapes=[pltpu.VMEM(shape, dtype) for shape, dtype in scratch]
+        scratch_shapes=[pltpu.VMEM(shape, dtype) for shape, dtype in scratch + loaded]
+        + [pltpu.SemaphoreType.DMA((7,))]
+        + [pltpu.VMEM(shape, dtype) for shape, dtype in states]
         + [pltpu.SemaphoreType.DMA(shape) for shape in ((3, 2), (4, 2), (7,))]
         + gather_sems(4) * 2,
         compiler_params=pltpu.CompilerParams(
@@ -1226,7 +1245,7 @@
         ),
         name="rise",
     )(
-        tokens, ln_gain, w_up, w_up, w_query, w_key, w_value, conv_w, conv_b, gate_own, gate_b,
+        tokens, ln_gain, w_up, w_query, w_key, w_value, conv_w, conv_b, gate_own, gate_b,
         out_gain, skip_gain, w_down, cot,
     )
 

time: 228 us -> 225 us (0.987)
  no operation moved by 1% of the time
where the time goes in v8:
time: 225 us
  Pallas kernels  223 us (99%)
    pallas_call x1, Pallas kernels, drain(): pl.pallas_call(drain_kernel, grid=(2 * steps,), in_specs=specs, out_specs...  100 us
    pallas_call x1, Pallas kernels, rise(): pl.pallas_call(rise_kernel, grid=(2 * steps + 1,), in_specs=specs, out_sp...  70.5 us
    pallas_call x1, Pallas kernels, settle(): pl.pallas_call(settle_kernel, grid=(count // length,), in_specs=specs, ou...  48.4 us

profile of v8, /device:TPU:24, one launch (start us, length us, event | category | flops | bytes accessed | tf_op | source)
XLA Modules:
  0.0 225.2 jit_solution(15615576655979557420)
XLA Ops:
  0.6 0.0 copy-start
  0.7 0.9 copy-done
  1.6 0.6 dynamic-slice_bitcast_fusion.gate_own
  2.2 70.5 %rise.1 = (bf16[2048,1024]{1,0:T(8,128)(2,1)}, bf16[2048,512]{1,0:T(8,128)(2,1)}, bf16[2048,512]{1,0:T(8,128)(2,1)}, bf16[2048,512]{1,0:T(8,128)(2,1)}, bf16[204...) custom-call(bf16[2,256,1024]{2,1,0:T(8,128)(2,1)} %bitcast.26, ...), custom_call_target="tpu_custom_call" | custom-call | tf_op jit(solution)/shard_map/rise/pallas_call | solution.py:1231
  72.7 48.4 %settle.1 = (f32[2048,512]{1,0:T(8,128)}, f32[2048,512]{1,0:T(8,128)}, f32[2048,512]{1,0:T(8,128)}, f32[2048,512]{1,0:T(8,128)}, bf16[2048,512]{1,0:T(8,128)(2,1...) custom-call(f32[8,2048]{1,0:T(8,128)} %get-tuple-element.60.refs_0_,, ...), custom_call_target="tpu_custom_call" | custom-call | flops 12884901888 | bytes 50331648 | tf_op jit(solution)/shard_map/settle/pallas_call | solution.py:1437
  121.1 0.0 copy-start.1
  121.1 100.1 %drain.1 = (bf16[2,256,1024]{2,1,0:T(8,128)(2,1)}, f32[128,1024]{1,0:T(8,128)}, f32[4,64,128]{2,1,0:T(8,128)}, f32[4,64,128]{2,1,0:T(8,128)}, f32[4,64,128]{2,1,...) custom-call(f32[8,2048]{1,0:T(8,128)} %get-tuple-element.74.d_gate, f32[2048,512]{1,0:T(8,128)} %get-tuple-element.75.dq, ...), custom_call_target="tpu_custom_call" | custom-call | flops 15032385536 | bytes 50331648 | tf_op jit(solution)/shard_map/drain/pallas_call | solution.py:1973
  221.2 3.8 %spread.1 = (f32[1,1024]{1,0:T(1,128)}, f32[4,2048]{1,0:T(4,128)}, f32[1,2048]{1,0:T(1,128)}, f32[8,6144]{1,0:T(8,128)}, f32[1,4]{1,0:T(1,128)}, /*index=5*/f32[...) custom-call(f32[4,40,512]{2,1,0:T(8,128)} %get-tuple-element.84.smal, ...), custom_call_target="tpu_custom_call" | custom-call | tf_op jit(solution)/shard_map/spread/pallas_call | solution.py:2021
  225.0 0.0 copy-done.1
Async XLA Ops:
  0.6 0.9 copy-start
  121.1 103.9 %copy-start.1 = (f32[6144,8]{0,1:T(8,128)S(1)}, f32[6144,8]{0,1:T(8,128)}, u32[]{:S(2)}) copy-start(f32[6144,8]{0,1:T(8,128)} %param.22) | copy-start | bytes 589828
